TPU v7x, 32 devices: a whole 2x2x4 slice. The times are simulated.
32 devices in a mesh: ctx: 8 (over z, x), wt: 4 (over y, core).
Axes of the slice: x: 2, y: 2, z: 4, core: 2. Of those that a mesh axis runs over, the one named last changes fastest.
Arguments:
- layer_input: bfloat16 [4, 2048, 2048], P('wt', 'ctx'), may hold values from -6 to 6
- cotangent: bfloat16 [4, 2048, 2048], P('wt', 'ctx'), may hold values from -6 to 6
- document_length: int32 [4, 8], replicated, may hold values from 1 to 1793, 2048 in all within a row
- adapter_choice_index: int32 [1], replicated, may hold values from 0 to 7
- query_weight: bfloat16 [2048, 2048], P(('ctx', 'wt')), may hold values from -0.125 to 0.125
- key_weight: bfloat16 [2048, 2048], P(('ctx', 'wt')), may hold values from -0.125 to 0.125
- value_weight: bfloat16 [2048, 2048], P(('ctx', 'wt')), may hold values from -0.125 to 0.125
- output_weight: bfloat16 [2048, 2048], P(('ctx', 'wt')), may hold values from -0.125 to 0.125
- gate_weight: bfloat16 [2048, 8192], P(('ctx', 'wt')), may hold values from -0.125 to 0.125
- up_weight: bfloat16 [2048, 8192], P(('ctx', 'wt')), may hold values from -0.125 to 0.125
- down_weight: bfloat16 [8192, 2048], P(('ctx', 'wt')), may hold values from -0.0625 to 0.0625
- query_norm_gain: float32 [2048], replicated, may hold values from 0.25 to 1.75
- key_norm_gain: float32 [2048], replicated, may hold values from 0.25 to 1.75
- attention_norm_gain: float32 [2048], replicated, may hold values from 0.25 to 1.75
- feedforward_norm_gain: float32 [2048], replicated, may hold values from 0.25 to 1.75
- adapter_model_input_maps: bfloat16 [8, 6, 16, 2048], replicated, may hold values from -0.125 to 0.125
- adapter_down_input_maps: bfloat16 [8, 16, 8192], replicated, may hold values from -0.0625 to 0.0625
- adapter_model_output_maps: bfloat16 [8, 5, 16, 2048], replicated, may hold values from -1.5 to 1.5
- adapter_hidden_output_maps: bfloat16 [8, 2, 16, 8192], replicated, may hold values from -1.5 to 1.5
Outputs:
- result: bfloat16 [4, 2048, 2048], P('wt', 'ctx')
- grad_input: float32 [4, 2048, 2048], P('wt', 'ctx')
- grad_a_model: float32 [8, 6, 16, 2048], P(None, None, None, ('ctx', 'wt'))
- grad_a_hidden: float32 [8, 16, 8192], P(None, None, ('ctx', 'wt'))
- grad_b_model: float32 [8, 5, 16, 2048], P(None, None, None, ('ctx', 'wt'))
- grad_b_hidden: float32 [8, 2, 16, 8192], P(None, None, None, ('ctx', 'wt'))
Inputs may be any that keep to these rules, and one draw needn't show every extreme that they name: `document_length`: each sequence's lengths sum to 2048; the longest of each is 1793.
All inputs are finite; a program needn't handle non-finite values.
Results may differ from a plain program's by a relative error of at most 0.015.
Values may be sent and summed in bfloat16 or wider, within the bound.
A program may use at most 512 MiB of HBM per device.

v0:
```python
import jax
import jax.numpy as jnp
from jax import lax
from jax.sharding import PartitionSpec as P

HD = 128
WINDOW = 1024


SCALE_ADAPT = 0.5
ROPE_BASE = 500000.0
EPS = 1e-06
NEG_FILL = -1e30
HIGHEST = lax.Precision.HIGHEST


def shifted(value, axis, by):
    length = lax.axis_size(axis)
    pairs = [(i, i + by) for i in range(length) if 0 <= i + by < length]
    return lax.ppermute(value, axis, pairs)


def rms_scale(values, gain):
    return values * lax.rsqrt(jnp.mean(values * values, axis=-1, keepdims=True) + EPS) * gain


def rope_tables(positions):
    half_dim = HD // 2
    inv_freq = ROPE_BASE ** (-(jnp.arange(half_dim, dtype=jnp.float32) * 2.0 / HD))
    angles = positions.astype(jnp.float32)[:, None] * inv_freq[None, :]
    return (jnp.cos(angles), jnp.sin(angles))


def rotate(values, cosines, sines):
    tok_rows = cosines.shape[0]
    half_dim = HD // 2
    shaped = values.reshape(-1, tok_rows, values.shape[-1] // HD, HD)
    front_half = shaped[..., :half_dim]
    back_half = shaped[..., half_dim:]
    cos_b = cosines[None, :, None, :]
    sin_b = sines[None, :, None, :]
    turned = jnp.concatenate(
        [front_half * cos_b - back_half * sin_b, back_half * cos_b + front_half * sin_b], axis=-1
    )
    return turned.reshape(values.shape)


def doc_index(positions, lengths):
    bounds = jnp.cumsum(lengths, axis=1)
    return jnp.sum((positions[None, :, None] >= bounds[:, None, :]).astype(jnp.int32), axis=2)


def project(inputs, weight, adapt_in, adapt_out):
    base_out = jnp.dot(inputs, weight, preferred_element_type=jnp.float32)
    narrow = jnp.einsum("ti,ri->tr", inputs, adapt_in, preferred_element_type=jnp.float32)
    return (
        base_out + SCALE_ADAPT * jnp.dot(narrow, adapt_out.astype(jnp.float32), precision=HIGHEST),
        narrow,
    )


def project_back(inputs, weight, adapt_in, adapt_out, grad_low, narrow):
    through = jnp.einsum("to,io->ti", grad_low, weight, preferred_element_type=jnp.float32)
    narrow_grad = jnp.einsum("to,ro->tr", grad_low, adapt_out, preferred_element_type=jnp.float32)
    grad_in = through + SCALE_ADAPT * jnp.dot(
        narrow_grad, adapt_in.astype(jnp.float32), precision=HIGHEST
    )
    grad_adapt_out = SCALE_ADAPT * jnp.dot(
        narrow.T, grad_low, precision=HIGHEST, preferred_element_type=jnp.float32
    )
    grad_adapt_in = SCALE_ADAPT * jnp.dot(
        narrow_grad.T, inputs, precision=HIGHEST, preferred_element_type=jnp.float32
    )
    return (grad_in, grad_adapt_in, grad_adapt_out)


def on_device(
    layer_input,
    cotangent,
    document_length,
    adapter_choice_index,
    query_weight,
    key_weight,
    value_weight,
    output_weight,
    gate_weight,
    up_weight,
    down_weight,
    query_norm_gain,
    key_norm_gain,
    attention_norm_gain,
    feedforward_norm_gain,
    adapter_model_input_maps,
    adapter_down_input_maps,
    adapter_model_output_maps,
    adapter_hidden_output_maps,
):
    tok_rows = layer_input.shape[1]
    model_dim = layer_input.shape[2]
    reach = WINDOW // tok_rows
    key_count = (reach + 1) * tok_rows
    score_scale = HD ** (-0.5)
    seq_count = 1
    lengths = lax.dynamic_slice_in_dim(document_length, lax.axis_index("wt"), 1, 0)

    def fetch_all():
        attn = (
            lax.all_gather(query_weight, ("ctx", "wt"), axis=0, tiled=True),
            lax.all_gather(key_weight, ("ctx", "wt"), axis=0, tiled=True),
            lax.all_gather(value_weight, ("ctx", "wt"), axis=0, tiled=True),
            lax.all_gather(output_weight, ("ctx", "wt"), axis=0, tiled=True),
        )
        feed = (
            lax.all_gather(gate_weight, ("ctx", "wt"), axis=0, tiled=True),
            lax.all_gather(up_weight, ("ctx", "wt"), axis=0, tiled=True),
            lax.all_gather(down_weight, ("ctx", "wt"), axis=0, tiled=True),
        )
        return (attn[0], attn[1], attn[2], attn[3], feed[0], feed[1], feed[2])

    heads_here = model_dim // HD
    block_start = lax.axis_index("ctx") * tok_rows
    positions = block_start + jnp.arange(tok_rows, dtype=jnp.int32)
    key_pos = block_start - reach * tok_rows + jnp.arange(key_count, dtype=jnp.int32)
    query_docs = doc_index(positions, lengths)
    key_docs = doc_index(key_pos, lengths)
    distance = positions[:, None] - key_pos[None, :]
    near = (key_pos[None, :] >= 0) & (distance >= 0) & (distance < WINDOW)
    allowed = (query_docs[:, :, None] == key_docs[:, None, :]) & near[None]
    cosines, sines = rope_tables(positions)
    selected_adapter = adapter_choice_index[0]
    select_model_input_map = lax.dynamic_index_in_dim(
        adapter_model_input_maps, selected_adapter, 0, keepdims=False
    )
    select_hidden_input_map = lax.dynamic_index_in_dim(
        adapter_down_input_maps, selected_adapter, 0, keepdims=False
    )
    select_model_output_map = lax.dynamic_index_in_dim(
        adapter_model_output_maps, selected_adapter, 0, keepdims=False
    )
    select_hidden_output_map = lax.dynamic_index_in_dim(
        adapter_hidden_output_maps, selected_adapter, 0, keepdims=False
    )
    b_query = select_model_output_map[0]
    b_key = select_model_output_map[1]
    b_value = select_model_output_map[2]
    a_output = select_model_input_map[3]
    b_gate = select_hidden_output_map[0]
    b_up = select_hidden_output_map[1]
    weights_now = fetch_all()
    own_inputs = layer_input[0]
    query_pre, query_narrow = project(
        own_inputs, weights_now[0], select_model_input_map[0], b_query
    )
    key_pre, key_narrow = project(own_inputs, weights_now[1], select_model_input_map[1], b_key)
    value_pre, value_narrow = project(
        own_inputs, weights_now[2], select_model_input_map[2], b_value
    )
    squares = (
        jnp.sum(query_pre * query_pre, axis=-1, keepdims=True),
        jnp.sum(key_pre * key_pre, axis=-1, keepdims=True),
    )
    query_inv = lax.rsqrt(squares[0] / model_dim + EPS)
    key_inv = lax.rsqrt(squares[1] / model_dim + EPS)
    query_low = rotate(query_pre * query_inv * query_norm_gain, cosines, sines).astype(jnp.bfloat16)
    key_low = rotate(key_pre * key_inv * key_norm_gain, cosines, sines).astype(jnp.bfloat16)
    value_low = value_pre.astype(jnp.bfloat16)
    blocks = [(key_low, value_low)]
    current = (key_low, value_low)
    for hop_index in range(reach):
        current = shifted((current[0], current[1]), "ctx", 1)
        blocks.append(current)
    key_all = jnp.concatenate(
        [
            blocks[reach - order_id][0].reshape(seq_count, tok_rows, model_dim)
            for order_id in range(reach + 1)
        ],
        axis=1,
    )
    value_all = jnp.concatenate(
        [
            blocks[reach - order_id][1].reshape(seq_count, tok_rows, model_dim)
            for order_id in range(reach + 1)
        ],
        axis=1,
    )
    query4 = query_low.reshape(seq_count, tok_rows, heads_here, HD)
    key4 = key_all.reshape(seq_count, key_count, heads_here, HD)
    value4 = value_all.reshape(seq_count, key_count, heads_here, HD)

    def masked_scores():
        raw_scores = (
            jnp.einsum("sqhd,skhd->shqk", query4, key4, preferred_element_type=jnp.float32)
            * score_scale
        )
        return jnp.where(allowed[:, None], raw_scores, NEG_FILL)

    scores = masked_scores()
    row_max = jnp.max(scores, axis=-1, keepdims=True)
    shifted_exp = jnp.exp(scores - row_max)
    row_total = jnp.sum(shifted_exp, axis=-1, keepdims=True)
    log_total = row_max + jnp.log(row_total)
    probs_low = (shifted_exp / row_total).astype(jnp.bfloat16)
    attended = jnp.einsum(
        "shqk,skhd->sqhd", probs_low, value4, preferred_element_type=jnp.float32
    ).reshape(seq_count * tok_rows, model_dim)
    attended_low = attended.astype(jnp.bfloat16)
    attn_part, output_narrow = project(
        attended_low, weights_now[3], a_output, select_model_output_map[3]
    )

    def attn_post(values):
        return rms_scale(values, attention_norm_gain)

    attn_normed, attn_pull = jax.vjp(attn_post, attn_part)
    middle = own_inputs.astype(jnp.float32) + attn_normed
    middle_low = middle.astype(jnp.bfloat16)
    gate_pre, gate_narrow = project(middle_low, weights_now[4], select_model_input_map[4], b_gate)
    up_pre, up_narrow = project(middle_low, weights_now[5], select_model_input_map[5], b_up)

    def gating(gate_in, up_in):
        return jax.nn.silu(gate_in) * up_in

    gated, gate_pull = jax.vjp(gating, gate_pre, up_pre)
    gated_low = gated.astype(jnp.bfloat16)
    feed_part, down_narrow = project(
        gated_low, weights_now[6], select_hidden_input_map, select_model_output_map[4]
    )

    def feed_post(values):
        return rms_scale(values, feedforward_norm_gain)

    feed_normed, feed_pull = jax.vjp(feed_post, feed_part)
    result = (middle + feed_normed).astype(jnp.bfloat16)
    grad_out = cotangent[0].astype(jnp.float32)
    weights_back = fetch_all()
    grad_feed = feed_pull(grad_out)[0].astype(jnp.bfloat16)
    grad_gated, ga_down_part, gb_down = project_back(
        gated_low,
        weights_back[6],
        select_hidden_input_map,
        select_model_output_map[4],
        grad_feed,
        down_narrow,
    )
    grad_gate, grad_up_in = gate_pull(grad_gated)
    grad_gate_side, ga_gate, gb_gate_part = project_back(
        middle_low,
        weights_back[4],
        select_model_input_map[4],
        b_gate,
        grad_gate.astype(jnp.bfloat16),
        gate_narrow,
    )
    grad_up_side, ga_up, gb_up_part = project_back(
        middle_low,
        weights_back[5],
        select_model_input_map[5],
        b_up,
        grad_up_in.astype(jnp.bfloat16),
        up_narrow,
    )
    grad_mid = grad_out + (grad_gate_side + grad_up_side)
    grad_attn = attn_pull(grad_mid)[0].astype(jnp.bfloat16)
    grad_attended, ga_out_part, gb_output = project_back(
        attended_low,
        weights_back[3],
        a_output,
        select_model_output_map[3],
        grad_attn,
        output_narrow,
    )
    grad_att4 = grad_attended.astype(jnp.bfloat16).reshape(seq_count, tok_rows, heads_here, HD)
    recomputed = masked_scores()
    back_probs = jnp.exp(recomputed - log_total)
    back_low = back_probs.astype(jnp.bfloat16)
    grad_probs = jnp.einsum(
        "sqhd,skhd->shqk", grad_att4, value4, preferred_element_type=jnp.float32
    )
    inner_sum = jnp.sum(back_probs * grad_probs, axis=-1, keepdims=True)
    grad_scores = (back_probs * (grad_probs - inner_sum)).astype(jnp.bfloat16)
    grad_query = (
        jnp.einsum(
            "shqk,skhd->sqhd", grad_scores, key4, preferred_element_type=jnp.float32
        ).reshape(seq_count * tok_rows, model_dim)
        * score_scale
    )
    grad_key_all = (
        jnp.einsum("shqk,sqhd->skhd", grad_scores, query4, preferred_element_type=jnp.float32)
        * score_scale
    ).reshape(seq_count, reach + 1, tok_rows, model_dim)
    grad_value_all = jnp.einsum(
        "shqk,sqhd->skhd", back_low, grad_att4, preferred_element_type=jnp.float32
    ).reshape(seq_count, reach + 1, tok_rows, model_dim)
    grad_key_own = grad_key_all[:, 0]
    grad_value_own = grad_value_all[:, 0]
    for hop_index in range(reach):
        moved = (
            shifted(grad_key_own.astype(jnp.bfloat16), "ctx", -1).astype(grad_key_own.dtype),
            shifted(grad_value_own.astype(jnp.bfloat16), "ctx", -1).astype(grad_value_own.dtype),
        )
        grad_key_own = moved[0] + grad_key_all[:, hop_index + 1]
        grad_value_own = moved[1] + grad_value_all[:, hop_index + 1]
    grad_key_rows = grad_key_own.reshape(seq_count * tok_rows, model_dim)
    grad_value_rows = grad_value_own.reshape(seq_count * tok_rows, model_dim)
    query_turn = rotate(grad_query, cosines, -sines) * query_norm_gain
    key_turn = rotate(grad_key_rows, cosines, -sines) * key_norm_gain
    inners = (
        jnp.sum(query_pre * query_turn, axis=-1, keepdims=True),
        jnp.sum(key_pre * key_turn, axis=-1, keepdims=True),
    )
    grad_query_pre = (
        query_inv * query_turn
        - query_pre * (query_inv * query_inv * query_inv) * (inners[0] / model_dim)
    ).astype(jnp.bfloat16)
    grad_key_pre = (
        key_inv * key_turn - key_pre * (key_inv * key_inv * key_inv) * (inners[1] / model_dim)
    ).astype(jnp.bfloat16)
    grad_value_low = grad_value_rows.astype(jnp.bfloat16)
    grad_in_query, ga_query, gb_query = project_back(
        own_inputs,
        weights_back[0],
        select_model_input_map[0],
        b_query,
        grad_query_pre,
        query_narrow,
    )
    grad_in_key, ga_key, gb_key = project_back(
        own_inputs, weights_back[1], select_model_input_map[1], b_key, grad_key_pre, key_narrow
    )
    grad_in_value, ga_value, gb_value = project_back(
        own_inputs,
        weights_back[2],
        select_model_input_map[2],
        b_value,
        grad_value_low,
        value_narrow,
    )
    grad_input = grad_mid + (grad_in_query + grad_in_key + grad_in_value)
    ga_model = jnp.stack([ga_query, ga_key, ga_value, ga_out_part, ga_gate, ga_up])
    gb_model = jnp.stack([gb_query, gb_key, gb_value, gb_output, gb_down])
    gb_hidden = jnp.stack([gb_gate_part, gb_up_part])
    adapter_selector = (
        jnp.arange(adapter_model_input_maps.shape[0], dtype=jnp.int32) == selected_adapter
    ).astype(jnp.float32)
    summed = (
        lax.psum_scatter(
            adapter_selector[:, None, None, None] * ga_model[None],
            ("ctx", "wt"),
            scatter_dimension=3,
            tiled=True,
        ),
        lax.psum_scatter(
            adapter_selector[:, None, None] * ga_down_part[None],
            ("ctx", "wt"),
            scatter_dimension=2,
            tiled=True,
        ),
        lax.psum_scatter(
            adapter_selector[:, None, None, None] * gb_model[None],
            ("ctx", "wt"),
            scatter_dimension=3,
            tiled=True,
        ),
        lax.psum_scatter(
            adapter_selector[:, None, None, None] * gb_hidden[None],
            ("ctx", "wt"),
            scatter_dimension=3,
            tiled=True,
        ),
    )
    sum_a_model, sum_a_hidden, sum_b_model, sum_b_hidden = summed
    return (result[None], grad_input[None], sum_a_model, sum_a_hidden, sum_b_model, sum_b_hidden)


def solution(mesh):
    placed = (
        P("wt", "ctx", None),
        P("wt", "ctx", None),
        P(),
        P(),
        P(("ctx", "wt"), None),
        P(("ctx", "wt"), None),
        P(("ctx", "wt"), None),
        P(("ctx", "wt"), None),
        P(("ctx", "wt"), None),
        P(("ctx", "wt"), None),
        P(("ctx", "wt"), None),
        P(),
        P(),
        P(),
        P(),
        P(),
        P(),
        P(),
        P(),
    )
    return jax.shard_map(
        on_device,
        mesh=mesh,
        in_specs=placed,
        out_specs=(
            P("wt", "ctx", None),
            P("wt", "ctx", None),
            P(None, None, None, ("ctx", "wt")),
            P(None, None, ("ctx", "wt")),
            P(None, None, None, ("ctx", "wt")),
            P(None, None, None, ("ctx", "wt")),
        ),
        check_vma=False,
    )
```

profile of v0, /device:TPU:0, one launch (start us, length us, event | category | flops | bytes accessed | tf_op | source)
XLA Modules:
  0.0 2224.2 jit_solution(9672759434266626897)
XLA Ops:
  17.1 74.1 %all-gather.8.cloned.1.call-done = bf16[2048,2048]{1,0:T(8,128)(2,1)} async-done(((bf16[64,2048]{1,0:T(8,128)(2,1)}), bf16[2048,2048]{1,0:T(8,128)(2,1)}) %all-gather.8.cloned.1.call-update) | async-done | bytes 8388624 | tf_op jit(solution)/shard_map/all_gather | solution.py:110
  91.2 6.0 fusion.113
  104.5 74.6 %all-gather.12.cloned.1.call-done = bf16[2048,2048]{1,0:T(8,128)(2,1)} async-done(((bf16[64,2048]{1,0:T(8,128)(2,1)}), bf16[2048,2048]{1,0:T(8,128)(2,1)}) %all-gather.12.cloned.1.call-update) | async-done | bytes 8388624 | tf_op jit(solution)/shard_map/all_gather | solution.py:109
  179.1 6.0 fusion.105
  196.3 4.3 collective-permute-start.4
  205.0 25.9 %collective-permute-done.4 = bf16[256,2048]{0,1:T(8,128)(2,1)} collective-permute-done((bf16[256,2048]{0,1:T(8,128)(2,1)}, bf16[256,2048]{0,1:T(8,128)(2,1)}, u32[]{:S(2)}, u32[]{:S(2)}) %collective-permute-start.4) | collective-permute-done | bytes 1048608 | tf_op jit(solution)/shard_map/ppermute | solution.py:20
  230.9 8.6 collective-permute-start.5
  244.9 23.4 %collective-permute-done.1 = bf16[256,2048]{1,0:T(8,128)(2,1)} collective-permute-done((bf16[256,2048]{1,0:T(8,128)(2,1)}, bf16[256,2048]{1,0:T(8,128)(2,1)}, u32[]{:S(2)}, u32[]{:S(2)}) %collective-permute-start.1) | collective-permute-done | bytes 1048608 | tf_op jit(solution)/shard_map/ppermute | solution.py:20
  268.3 10.5 collective-permute-start.2
  278.8 12.0 collective-permute-done.5
  290.8 18.1 collective-permute-start.6
  308.9 6.1 fusion.109
  317.8 26.6 %collective-permute-start.3 = (bf16[256,2048]{1,0:T(8,128)(2,1)}, bf16[256,2048]{1,0:T(8,128)(2,1)}, u32[]{:S(2)}, u32[]{:S(2)}) collective-permute-start(bf16[256,2048]{1,0:T(8,128)(2,1)} %collective-permute-done.2), channel_id=1, source_target_pairs={{0,4},{4,8},{8,12},{12,16},{16,20},{20,24},{24,28},{1,5},{5,9},{9,... | collective-permute-start | bytes 3145736 | tf_op jit(solution)/shard_map/ppermute | solution.py:20
  345.0 37.7 %collective-permute-start.7 = (bf16[256,2048]{0,1:T(8,128)(2,1)}, bf16[256,2048]{0,1:T(8,128)(2,1)}, u32[]{:S(2)}, u32[]{:S(2)}) collective-permute-start(bf16[256,2048]{0,1:T(8,128)(2,1)} %collective-permute-done.6), channel_id=1, source_target_pairs={{0,4},{4,8},{8,12},{12,16},{16,20},{20,24},{24,28},{1,5},{5,9},{9,... | collective-permute-start | bytes 3145736 | tf_op jit(solution)/shard_map/ppermute | solution.py:20
  420.1 9.8 fusion.170
  430.0 10.7 fusion
  440.6 9.5 fusion.85
  451.3 6.1 fusion.171
  474.3 139.5 %all-gather.16.cloned.1.call-done = bf16[2048,8192]{1,0:T(8,128)(2,1)} async-done(((bf16[64,8192]{1,0:T(8,128)(2,1)}), bf16[2048,8192]{1,0:T(8,128)(2,1)}) %all-gather.16.cloned.1.call-update) | async-done | bytes 33554448 | tf_op jit(solution)/shard_map/all_gather | solution.py:114
  613.8 18.5 fusion.172
  632.3 8.1 fusion.4
  640.4 169.2 %all-gather.18.cloned.1.call-done = bf16[2048,8192]{1,0:T(8,128)(2,1)} async-done(((bf16[64,8192]{1,0:T(8,128)(2,1)}), bf16[2048,8192]{1,0:T(8,128)(2,1)}) %all-gather.18.cloned.1.call-update) | async-done | bytes 33554448 | tf_op jit(solution)/shard_map/all_gather | solution.py:115
  809.5 18.7 fusion.173
  828.3 11.2 multiply_convert_fusion.2
  843.5 161.9 %all-gather.20.cloned.1.call-done = bf16[8192,2048]{1,0:T(8,128)(2,1)} async-done(((bf16[256,2048]{1,0:T(8,128)(2,1)}), bf16[8192,2048]{1,0:T(8,128)(2,1)}) %all-gather.20.cloned.1.call-update) | async-done | bytes 33554448 | tf_op jit(solution)/shard_map/all_gather | solution.py:116
  1005.4 16.8 fusion.174
  1028.3 18.5 fusion.175
  1046.9 13.6 multiply_convert_fusion.1
  1066.9 17.1 fusion.176
  1088.0 17.0 fusion.177
  1105.0 4.7 multiply_reduce_fusion.3
  1120.6 14.9 fusion.15
  1135.6 11.6 copy.151
  1154.8 15.9 multiply_reduce_fusion
  1170.7 14.6 multiply_convert_fusion
  1189.2 6.2 multiply_bitcast_fusion
  1195.5 11.6 copy.144
  1215.1 5.1 fusion.75
  1221.5 43.3 %collective-permute-done.8 = bf16[1,256,2048]{2,0,1:T(2,128)(2,1)S(1)} collective-permute-done((bf16[1,256,2048]{2,0,1:T(2,128)(2,1)}, bf16[1,256,2048]{2,0,1:T(2,128)(2,1)S(1)}, u32[]{:S(2)}, u32[]{:S(2)}) %collective-permute-start.8) | collective-permute-done | bytes 1048608 | tf_op jit(solution)/shard_map/ppermute | solution.py:20
  1264.8 4.5 fusion.82
  1270.5 39.2 %collective-permute-done.13 = bf16[1,256,2048]{2,0,1:T(2,128)(2,1)S(1)} collective-permute-done((bf16[1,256,2048]{2,0,1:T(2,128)(2,1)S(1)}, bf16[1,256,2048]{2,0,1:T(2,128)(2,1)S(1)}, u32[]{:S(2)}, u32[]{:S(2)}) %collective-permute-start.13) | collective-permute-done | bytes 1048608 | tf_op jit(solution)/shard_map/ppermute | solution.py:20
  1314.2 40.5 %collective-permute-done.9 = bf16[1,256,2048]{2,0,1:T(2,128)(2,1)} collective-permute-done((bf16[1,256,2048]{2,0,1:T(2,128)(2,1)S(1)}, bf16[1,256,2048]{2,0,1:T(2,128)(2,1)}, u32[]{:S(2)}, u32[]{:S(2)}) %collective-permute-start.9) | collective-permute-done | bytes 1048608 | tf_op jit(solution)/shard_map/ppermute | solution.py:20
  1354.8 6.4 fusion.80
  1362.5 37.2 %collective-permute-done.14 = bf16[1,256,2048]{2,0,1:T(2,128)(2,1)} collective-permute-done((bf16[1,256,2048]{2,0,1:T(2,128)(2,1)S(1)}, bf16[1,256,2048]{2,0,1:T(2,128)(2,1)}, u32[]{:S(2)}, u32[]{:S(2)}) %collective-permute-start.14) | collective-permute-done | bytes 1048608 | tf_op jit(solution)/shard_map/ppermute | solution.py:20
  1399.7 5.8 fusion.71
  1406.8 37.8 %collective-permute-done.10 = bf16[1,256,2048]{2,0,1:T(2,128)(2,1)} collective-permute-done((bf16[1,256,2048]{2,0,1:T(2,128)(2,1)}, bf16[1,256,2048]{2,0,1:T(2,128)(2,1)}, u32[]{:S(2)}, u32[]{:S(2)}) %collective-permute-start.10) | collective-permute-done | bytes 1048608 | tf_op jit(solution)/shard_map/ppermute | solution.py:20
  1444.6 6.4 fusion.78
  1452.8 6.8 multiply_bitcast_fusion.1
  1459.6 30.0 %collective-permute-done.15 = bf16[1,256,2048]{2,0,1:T(2,128)(2,1)} collective-permute-done((bf16[1,256,2048]{2,0,1:T(2,128)(2,1)}, bf16[1,256,2048]{2,0,1:T(2,128)(2,1)}, u32[]{:S(2)}, u32[]{:S(2)}) %collective-permute-start.15) | collective-permute-done | bytes 1048608 | tf_op jit(solution)/shard_map/ppermute | solution.py:20
  1489.6 4.5 fusion.69
  1497.0 36.8 %collective-permute-done.11 = bf16[1,256,2048]{2,0,1:T(2,128)(2,1)} collective-permute-done((bf16[1,256,2048]{2,0,1:T(2,128)(2,1)}, bf16[1,256,2048]{2,0,1:T(2,128)(2,1)}, u32[]{:S(2)}, u32[]{:S(2)}) %collective-permute-start.11) | collective-permute-done | bytes 1048608 | tf_op jit(solution)/shard_map/ppermute | solution.py:20
  1533.8 6.2 fusion.76
  1540.1 6.2 copy.146
  1555.9 4.7 multiply_subtract_fusion
  1578.4 50.3 %copy.161 = f32[8,6,16,2048]{2,1,0,3:T(8,128)} copy(f32[8,6,16,2048]{3,2,1,0:T(8,128)} %broadcast_multiply_fusion.1) | data formatting | bytes 12582912
  1628.7 41.0 %reshape.685 = f32[2048,768]{1,0:T(8,128)} reshape(f32[2048,8,6,16]{3,2,1,0:T(8,128)} %bitcast.72) | data formatting | bytes 12582912
  1680.9 50.3 %copy.163 = f32[8,5,16,2048]{2,1,0,3:T(8,128)} copy(f32[8,5,16,2048]{3,2,1,0:T(8,128)} %broadcast_multiply_fusion.2) | data formatting | bytes 10485760
  1731.2 39.7 %reshape.687 = f32[2048,640]{1,0:T(8,128)} reshape(f32[2048,8,5,16]{3,2,1,0:T(8,128)} %bitcast.74) | data formatting | bytes 10485760
  1784.6 4.4 broadcast_multiply_fusion
  1789.0 6.3 fusion.179
  1796.6 5.9 fusion.180
  1815.9 113.9 %reduce-scatter.15.cloned.1.call-done = f32[64,640]{1,0:T(8,128)} async-done(((f32[2048,640]{1,0:T(8,128)}), f32[64,640]{1,0:T(8,128)}) %reduce-scatter.15.cloned.1.call-update) | async-done | bytes 163856
  1935.7 134.1 %reduce-scatter.9.cloned.1.call-done = f32[8,16,256]{2,1,0:T(8,128)} async-done(((f32[8,16,8192]{2,1,0:T(8,128)}), f32[8,16,256]{2,1,0:T(8,128)}) %reduce-scatter.9.cloned.1.call-update) | async-done | bytes 131088 | tf_op jit(solution)/shard_map/reduce_scatter | solution.py:352
  2069.7 147.8 %reduce-scatter.11.cloned.1.call-done = f32[8,2,16,256]{3,2,1,0:T(8,128)} async-done(((f32[8,2,16,8192]{3,2,1,0:T(8,128)}), f32[8,2,16,256]{3,2,1,0:T(8,128)}) %reduce-scatter.11.cloned.1.call-update) | async-done | bytes 262160 | tf_op jit(solution)/shard_map/reduce_scatter | solution.py:364
  (364 shorter events, 233.6 us)
Async XLA Ops:
  7.2 6.7 copy-start
  7.2 84.0 %all-gather.8.cloned.1.call-start = ((), (), s32[]{:S(2)}) async-start(), calls=%async_computation.4 | async-start | bytes 8650752 | tf_op jit(solution)/shard_map/all_gather | solution.py:110
  7.9 171.2 %all-gather.12.cloned.1.call-start = ((), (), s32[]{:S(2)}) async-start(), calls=%async_computation.6 | async-start | bytes 8650752 | tf_op jit(solution)/shard_map/all_gather | solution.py:109
  8.7 300.2 %all-gather.10.cloned.1.call-start = ((), (), s32[]{:S(2)}) async-start(), calls=%async_computation.5 | async-start | bytes 8650752 | tf_op jit(solution)/shard_map/all_gather | solution.py:108
  9.4 441.9 %all-gather.14.cloned.1.call-start = ((), (), s32[]{:S(2)}) async-start(), calls=%async_computation.7 | async-start | bytes 8650752 | tf_op jit(solution)/shard_map/all_gather | solution.py:111
  10.0 603.9 %all-gather.16.cloned.1.call-start = ((), (), s32[]{:S(2)}) async-start(), calls=%async_computation.8 | async-start | bytes 34603008 | tf_op jit(solution)/shard_map/all_gather | solution.py:114
  10.6 799.0 %all-gather.18.cloned.1.call-start = ((), (), s32[]{:S(2)}) async-start(), calls=%async_computation.9 | async-start | bytes 34603008 | tf_op jit(solution)/shard_map/all_gather | solution.py:115
  11.1 994.3 %all-gather.20.cloned.1.call-start = ((), (), s32[]{:S(2)}) async-start(), calls=%async_computation.10 | async-start | bytes 34603008 | tf_op jit(solution)/shard_map/all_gather | solution.py:116
  11.9 1797.7 %reduce-scatter.13.cloned.1.call-start = ((), (), s32[]{:S(2)}) async-start(), calls=%async_computation.13 | async-start | bytes 6488064
  13.8 370.2 %copy-start.51 = (f32[256,64]{1,0:T(8,128)}, f32[256,64]{1,0:T(8,128)S(1)}, u32[]{:S(2)}) copy-start(f32[256,64]{1,0:T(8,128)S(1)} %get-tuple-element.30) | copy-start | bytes 196612
  15.5 81.8 %copy-start.58 = (f32[16,256]{1,0:T(8,128)}, f32[16,256]{1,0:T(8,128)S(1)}, u32[]{:S(2)}) copy-start(f32[16,256]{1,0:T(8,128)S(1)} %fusion.111) | copy-start | bytes 49156
  17.1 168.0 %copy-start.60 = (f32[16,256]{1,0:T(8,128)}, f32[16,256]{1,0:T(8,128)S(1)}, u32[]{:S(2)}) copy-start(f32[16,256]{1,0:T(8,128)S(1)} %fusion.103) | copy-start | bytes 49156
  100.2 101.3 %collective-permute-start = (bf16[256,2048]{1,0:T(8,128)(2,1)}, bf16[256,2048]{1,0:T(8,128)(2,1)}, u32[]{:S(2)}, u32[]{:S(2)}) collective-permute-start(bf16[256,2048]{1,0:T(8,128)(2,1)} %fusion.39), channel_id=1, source_target_pairs={{0,4},{4,8},{8,12},{12,16},{16,20},{20,24},{24,28},{1,5},{5,9},{9,... | collective-permute-start | bytes 3145736 | tf_op jit(solution)/shard_map/ppermute | solution.py:20
  196.3 34.6 %collective-permute-start.4 = (bf16[256,2048]{0,1:T(8,128)(2,1)}, bf16[256,2048]{0,1:T(8,128)(2,1)}, u32[]{:S(2)}, u32[]{:S(2)}) collective-permute-start(bf16[256,2048]{0,1:T(8,128)(2,1)} %bitcast.428), channel_id=1, source_target_pairs={{0,4},{4,8},{8,12},{12,16},{16,20},{20,24},{24,28},{1,5},{5,9},{9,... | collective-permute-start | bytes 3145736 | tf_op jit(solution)/shard_map/ppermute | solution.py:20
  201.5 66.8 %collective-permute-start.1 = (bf16[256,2048]{1,0:T(8,128)(2,1)}, bf16[256,2048]{1,0:T(8,128)(2,1)}, u32[]{:S(2)}, u32[]{:S(2)}) collective-permute-start(bf16[256,2048]{1,0:T(8,128)(2,1)} %collective-permute-done), channel_id=1, source_target_pairs={{0,4},{4,8},{8,12},{12,16},{16,20},{20,24},{24,28},{1,5},{5,9},{9,... | collective-permute-start | bytes 3145736 | tf_op jit(solution)/shard_map/ppermute | solution.py:20
  230.9 59.9 %collective-permute-start.5 = (bf16[256,2048]{0,1:T(8,128)(2,1)}, bf16[256,2048]{0,1:T(8,128)(2,1)}, u32[]{:S(2)}, u32[]{:S(2)}) collective-permute-start(bf16[256,2048]{0,1:T(8,128)(2,1)} %collective-permute-done.4), channel_id=1, source_target_pairs={{0,4},{4,8},{8,12},{12,16},{16,20},{20,24},{24,28},{1,5},{5,9},{9,... | collective-permute-start | bytes 3145736 | tf_op jit(solution)/shard_map/ppermute | solution.py:20
  241.3 73.7 %copy-start.62 = (f32[16,256]{1,0:T(8,128)}, f32[16,256]{1,0:T(8,128)S(1)}, u32[]{:S(2)}) copy-start(f32[16,256]{1,0:T(8,128)S(1)} %fusion.107) | copy-start | bytes 49156
  268.3 49.5 %collective-permute-start.2 = (bf16[256,2048]{1,0:T(8,128)(2,1)}, bf16[256,2048]{1,0:T(8,128)(2,1)}, u32[]{:S(2)}, u32[]{:S(2)}) collective-permute-start(bf16[256,2048]{1,0:T(8,128)(2,1)} %collective-permute-done.1), channel_id=1, source_target_pairs={{0,4},{4,8},{8,12},{12,16},{16,20},{20,24},{24,28},{1,5},{5,9},{9,... | collective-permute-start | bytes 3145736 | tf_op jit(solution)/shard_map/ppermute | solution.py:20
  290.8 54.3 %collective-permute-start.6 = (bf16[256,2048]{0,1:T(8,128)(2,1)}, bf16[256,2048]{0,1:T(8,128)(2,1)}, u32[]{:S(2)}, u32[]{:S(2)}) collective-permute-start(bf16[256,2048]{0,1:T(8,128)(2,1)} %collective-permute-done.5), channel_id=1, source_target_pairs={{0,4},{4,8},{8,12},{12,16},{16,20},{20,24},{24,28},{1,5},{5,9},{9,... | collective-permute-start | bytes 3145736 | tf_op jit(solution)/shard_map/ppermute | solution.py:20
  314.9 67.8 %copy-start.72 = (f32[2048]{0:T(1024)S(1)}, f32[2048]{0:T(1024)}, u32[]{:S(2)}) copy-start(f32[2048]{0:T(1024)} %param.30) | copy-start | bytes 24580
  317.1 65.8 %copy-start.7 = (f32[256,2048]{1,0:T(8,128)}, f32[256,2048]{1,0:T(8,128)S(1)}, u32[]{:S(2)}) copy-start(f32[256,2048]{1,0:T(8,128)S(1)} %get-tuple-element.40) | copy-start | bytes 6291460
  317.7 65.2 %copy-start.82 = (f32[256]{0:T(256)}, f32[256]{0:T(256)S(1)}, u32[]{:S(2)}) copy-start(f32[256]{0:T(256)S(1)} %get-tuple-element.34) | copy-start | bytes 3076
  317.8 88.8 %collective-permute-start.3 = (bf16[256,2048]{1,0:T(8,128)(2,1)}, bf16[256,2048]{1,0:T(8,128)(2,1)}, u32[]{:S(2)}, u32[]{:S(2)}) collective-permute-start(bf16[256,2048]{1,0:T(8,128)(2,1)} %collective-permute-done.2), channel_id=1, source_target_pairs={{0,4},{4,8},{8,12},{12,16},{16,20},{20,24},{24,28},{1,5},{5,9},{9,... | collective-permute-start | bytes 3145736 | tf_op jit(solution)/shard_map/ppermute | solution.py:20
  345.0 59.2 %collective-permute-start.7 = (bf16[256,2048]{0,1:T(8,128)(2,1)}, bf16[256,2048]{0,1:T(8,128)(2,1)}, u32[]{:S(2)}, u32[]{:S(2)}) collective-permute-start(bf16[256,2048]{0,1:T(8,128)(2,1)} %collective-permute-done.6), channel_id=1, source_target_pairs={{0,4},{4,8},{8,12},{12,16},{16,20},{20,24},{24,28},{1,5},{5,9},{9,... | collective-permute-start | bytes 3145736 | tf_op jit(solution)/shard_map/ppermute | solution.py:20
  413.8 6.3 copy-start.40
  430.0 10.7 copy-start.57
  451.3 6.1 copy-start.64
  461.4 366.8 %copy-start.76 = (f32[256,16]{0,1:T(8,128)}, f32[256,16]{0,1:T(8,128)S(1)}, u32[]{:S(2)}) copy-start(f32[256,16]{0,1:T(8,128)S(1)} %fusion.127) | copy-start | bytes 49156
  461.8 170.5 %copy-start.68 = (f32[256,16]{0,1:T(8,128)}, f32[256,16]{0,1:T(8,128)S(1)}, u32[]{:S(2)}) copy-start(f32[256,16]{0,1:T(8,128)S(1)} %fusion.126) | copy-start | bytes 49156
  843.5 178.8 %copy-start.66 = (f32[256,16]{0,1:T(8,128)}, f32[256,16]{0,1:T(8,128)S(1)}, u32[]{:S(2)}) copy-start(f32[256,16]{0,1:T(8,128)S(1)} %fusion.116) | copy-start | bytes 49156
  843.5 178.8 %copy-start.75 = (f32[2048]{0:T(1024)S(1)}, f32[2048]{0:T(1024)}, u32[]{:S(2)}) copy-start(f32[2048]{0:T(1024)} %param.33) | copy-start | bytes 24580
  1005.4 16.9 copy-start.35
  1028.3 18.5 copy-start.78
  1088.0 17.0 copy-start.36
  1105.0 4.7 copy-start.3
  1105.0 4.7 copy-start.10
  1105.0 4.7 copy-start.16
  1105.0 8.6 slice-start.6
  1153.5 61.6 %collective-permute-start.12 = (bf16[1,256,2048]{2,0,1:T(2,128)(2,1)}, bf16[1,256,2048]{2,0,1:T(2,128)(2,1)}, u32[]{:S(2)}, u32[]{:S(2)}) collective-permute-start(bf16[1,256,2048]{2,0,1:T(2,128)(2,1)} %convert_element_type.248), channel_id=1, source_target_pairs={{4,0},{8,4},{12,8},{16,12},{20,16},{24,20},{28,24},{5,1},{9,5},{13... | collective-permute-start | bytes 3145736 | tf_op jit(solution)/shard_map/ppermute | solution.py:20
  1170.7 18.5 copy-start.24
  1170.7 18.5 copy-start.26
  1207.1 102.7 %slice-start.3 = ((s8[10485760]{0:T(1024)(128)(4,1)}), s8[4194304]{0:T(1024)(128)(4,1)S(1)}, s32[]{:S(2)}) async-start(s8[10485760]{0:T(1024)(128)(4,1)} %bitcast.397), calls=%async_computation.18 | async-start | bytes 8388608
  1210.8 98.9 %slice-start.4 = ((s8[10485760]{0:T(1024)(128)(4,1)}), s8[4194304]{0:T(1024)(128)(4,1)S(1)}, s32[]{:S(2)}) async-start(s8[10485760]{0:T(1024)(128)(4,1)} %bitcast.397), calls=%async_computation.19 | async-start | bytes 8388608
  1213.5 96.3 %slice-start.5 = ((s8[10485760]{0:T(1024)(128)(4,1)}), s8[2097152]{0:T(1024)(128)(4,1)S(1)}, s32[]{:S(2)}) async-start(s8[10485760]{0:T(1024)(128)(4,1)} %bitcast.397), calls=%async_computation.20 | async-start | bytes 4194304
  1213.5 51.3 %collective-permute-start.8 = (bf16[1,256,2048]{2,0,1:T(2,128)(2,1)}, bf16[1,256,2048]{2,0,1:T(2,128)(2,1)S(1)}, u32[]{:S(2)}, u32[]{:S(2)}) collective-permute-start(bf16[1,256,2048]{2,0,1:T(2,128)(2,1)} %convert_element_type.238), channel_id=1, source_target_pairs={{4,0},{8,4},{12,8},{16,12},{20,16},{24,20},{28,24},{5,1},{9,5},{13... | collective-permute-start | bytes 3145736 | tf_op jit(solution)/shard_map/ppermute | solution.py:20
  1220.2 89.6 %collective-permute-start.13 = (bf16[1,256,2048]{2,0,1:T(2,128)(2,1)S(1)}, bf16[1,256,2048]{2,0,1:T(2,128)(2,1)S(1)}, u32[]{:S(2)}, u32[]{:S(2)}) collective-permute-start(bf16[1,256,2048]{2,0,1:T(2,128)(2,1)S(1)} %fusion.75), channel_id=1, source_target_pairs={{4,0},{8,4},{12,8},{16,12},{20,16},{24,20},{28,24},{5,1},{9,5},{13... | collective-permute-start | bytes 3145736 | tf_op jit(solution)/shard_map/ppermute | solution.py:20
  1269.2 85.5 %collective-permute-start.9 = (bf16[1,256,2048]{2,0,1:T(2,128)(2,1)S(1)}, bf16[1,256,2048]{2,0,1:T(2,128)(2,1)}, u32[]{:S(2)}, u32[]{:S(2)}) collective-permute-start(bf16[1,256,2048]{2,0,1:T(2,128)(2,1)S(1)} %fusion.82), channel_id=1, source_target_pairs={{4,0},{8,4},{12,8},{16,12},{20,16},{24,20},{28,24},{5,1},{9,5},{13... | collective-permute-start | bytes 3145736 | tf_op jit(solution)/shard_map/ppermute | solution.py:20
  1309.7 143.0 %slice-start = ((s8[10485760]{0:T(1024)(128)(4,1)}), s8[4194304]{0:T(1024)(128)(4,1)S(1)}, s32[]{:S(2)}) async-start(s8[10485760]{0:T(1024)(128)(4,1)} %bitcast.393), calls=%async_computation.15 | async-start | bytes 8388608
  1312.4 140.3 %slice-start.1 = ((s8[10485760]{0:T(1024)(128)(4,1)}), s8[4194304]{0:T(1024)(128)(4,1)S(1)}, s32[]{:S(2)}) async-start(s8[10485760]{0:T(1024)(128)(4,1)} %bitcast.393), calls=%async_computation.16 | async-start | bytes 8388608
  1312.5 87.2 %collective-permute-start.14 = (bf16[1,256,2048]{2,0,1:T(2,128)(2,1)S(1)}, bf16[1,256,2048]{2,0,1:T(2,128)(2,1)}, u32[]{:S(2)}, u32[]{:S(2)}) collective-permute-start(bf16[1,256,2048]{2,0,1:T(2,128)(2,1)S(1)} %fusion.73), channel_id=1, source_target_pairs={{4,0},{8,4},{12,8},{16,12},{20,16},{24,20},{28,24},{5,1},{9,5},{13... | collective-permute-start | bytes 3145736 | tf_op jit(solution)/shard_map/ppermute | solution.py:20
  1361.2 83.5 %collective-permute-start.10 = (bf16[1,256,2048]{2,0,1:T(2,128)(2,1)}, bf16[1,256,2048]{2,0,1:T(2,128)(2,1)}, u32[]{:S(2)}, u32[]{:S(2)}) collective-permute-start(bf16[1,256,2048]{2,0,1:T(2,128)(2,1)} %fusion.80), channel_id=1, source_target_pairs={{4,0},{8,4},{12,8},{16,12},{20,16},{24,20},{28,24},{5,1},{9,5},{13... | collective-permute-start | bytes 3145736 | tf_op jit(solution)/shard_map/ppermute | solution.py:20
  1362.5 90.3 %slice-start.2 = ((s8[10485760]{0:T(1024)(128)(4,1)}), s8[2097152]{0:T(1024)(128)(4,1)S(1)}, s32[]{:S(2)}) async-start(s8[10485760]{0:T(1024)(128)(4,1)} %bitcast.393), calls=%async_computation.17 | async-start | bytes 4194304
  1405.5 84.0 %collective-permute-start.15 = (bf16[1,256,2048]{2,0,1:T(2,128)(2,1)}, bf16[1,256,2048]{2,0,1:T(2,128)(2,1)}, u32[]{:S(2)}, u32[]{:S(2)}) collective-permute-start(bf16[1,256,2048]{2,0,1:T(2,128)(2,1)} %fusion.71), channel_id=1, source_target_pairs={{4,0},{8,4},{12,8},{16,12},{20,16},{24,20},{28,24},{5,1},{9,5},{13... | collective-permute-start | bytes 3145736 | tf_op jit(solution)/shard_map/ppermute | solution.py:20
  1451.1 82.8 %collective-permute-start.11 = (bf16[1,256,2048]{2,0,1:T(2,128)(2,1)}, bf16[1,256,2048]{2,0,1:T(2,128)(2,1)}, u32[]{:S(2)}, u32[]{:S(2)}) collective-permute-start(bf16[1,256,2048]{2,0,1:T(2,128)(2,1)} %fusion.78), channel_id=1, source_target_pairs={{4,0},{8,4},{12,8},{16,12},{20,16},{24,20},{28,24},{5,1},{9,5},{13... | collective-permute-start | bytes 3145736 | tf_op jit(solution)/shard_map/ppermute | solution.py:20
  1669.7 7.0 copy-start.65
  1669.7 7.5 copy-start.67
  1669.7 260.0 %reduce-scatter.15.cloned.1.call-start = ((), (), s32[]{:S(2)}) async-start(), calls=%async_computation.14 | async-start | bytes 5406720
  1670.4 6.3 copy-start.39
  1670.4 6.8 copy-start.32
  1770.9 298.8 %reduce-scatter.9.cloned.1.call-start = ((), (), s32[]{:S(2)}) async-start(), calls=%async_computation.11 | async-start | bytes 4325376 | tf_op jit(solution)/shard_map/reduce_scatter | solution.py:352
  1778.0 4.8 copy-start.69
  1778.0 439.5 %reduce-scatter.11.cloned.1.call-start = ((), (), s32[]{:S(2)}) async-start(), calls=%async_computation.12 | async-start | bytes 8650752 | tf_op jit(solution)/shard_map/reduce_scatter | solution.py:364
  1789.0 14.6 slice-start.8
  1796.6 7.1 slice-start.9
  (61 other events, 130.8 us)
Sparse Core Ops, SparseCore 0:
  10.9 80.2 all-gather.7
  94.0 85.0 all-gather.11
  182.0 100.3 all-gather.9
  285.1 108.5 all-gather.13
  396.4 217.3 all-gather.15
  616.6 192.9 all-gather.17
  812.4 192.9 all-gather.19
  1669.8 114.8 reduce-scatter.12
  1787.1 142.5 reduce-scatter.14
  1932.6 137.1 reduce-scatter.8
  2072.7 144.7 reduce-scatter.10
where the time goes:
time: 2240 us; the launch traced here: 2220 us
  waiting for transfers between devices  1350 us (60%)
  local copies, waits for them, and re-layouts  316 us (14%)
  matrix products  313 us (14%)
  starting transfers between devices  126 us (6%)
  other arithmetic  104 us (5%)
    ppermute x16, waiting for transfers between devices, shifted(): return lax.ppermute(value, axis, pairs)  331 us
    unnamed x222, local copies, waits for them, and re-layouts  239 us
    all_gather x1, waiting for transfers between devices, fetch_all(): lax.all_gather(up_weight, ('ctx', 'wt'), axis=0, tiled=True)  169 us
    all_gather x1, waiting for transfers between devices, fetch_all(): lax.all_gather(down_weight, ('ctx', 'wt'), axis=0, tiled=True)  162 us
    reduce_scatter x1, waiting for transfers between devices, on_device(): lax.psum_scatter(adapter_selector[:, None, None, None] * gb_hidden[None],...  148 us
    all_gather x1, waiting for transfers between devices, fetch_all(): lax.all_gather(gate_weight, ('ctx', 'wt'), axis=0, tiled=True)  140 us
    reduce_scatter x1, waiting for transfers between devices, on_device(): lax.psum_scatter(adapter_selector[:, None, None] * ga_down_part[None], ('...  134 us
    ppermute x16, starting transfers between devices, shifted(): return lax.ppermute(value, axis, pairs)  125 us
  transfers between devices with their start and end apart: 27, of which 20 were waited for; matrix products, arithmetic and copies ran while one was open for 19% of the time, Pallas kernels for 0%

commit v1 on v0

v1 whole, which is shorter than its diff:
```python
import functools

import jax
import jax.numpy as jnp
from jax import lax
from jax.experimental import pallas as pl
from jax.experimental.pallas import tpu as pltpu
from jax.sharding import Mesh
from jax.sharding import PartitionSpec as P

HD = 128
WINDOW = 1024
SCALE_ADAPT = 0.5
ROPE_BASE = 500000.0
EPS = 1e-06
BF = jnp.bfloat16
F32 = jnp.float32
VMEM_BYTES = 48 * 1024 * 1024


def cost(us):
    return pl.CostEstimate(flops=int(us * 1.1e9), bytes_accessed=int(us * 1e6), transcendentals=0)


def dot(a, b, dims=((1,), (0,))):
    return lax.dot_general(a, b, (dims, ((), ())), preferred_element_type=F32)


def dot_nt(a, b):
    return dot(a, b, ((1,), (1,)))


def dot_tn(a, b):
    return dot(a, b, ((0,), (0,)))


SWAP = [(0, 1), (1, 0)]


class Place:
    def __init__(self):
        self.np = lax.axis_size("p")
        self.p, self.x, self.y, self.c = (lax.axis_index(a) for a in ("p", "x", "y", "c"))
        self.quarter = 2 * self.x + self.c
        self.spot = jnp.stack([self.x, self.c, self.y]).astype(jnp.int32)

    def swap_core(self, value):
        return lax.ppermute(value, "c", SWAP)

    def swap_x(self, value):
        return lax.ppermute(value, "x", SWAP)

    def swap_both(self, value):
        return lax.ppermute(value, ("x", "c"), [(0, 3), (1, 2), (2, 1), (3, 0)])

    def swap_y(self, value):
        return lax.ppermute(value, "y", SWAP)

    def shift_p(self, value, by):
        return lax.ppermute(value, "p", [(p, p + by) for p in range(self.np) if 0 <= p + by < self.np])

    def turn_p(self, value, by):
        return lax.ppermute(value, "p", [(p, (p + by) % self.np) for p in range(self.np)])

    def gather4(self, own, work=None):
        across = self.swap_x(own)
        near = jnp.concatenate([own, self.swap_core(own)], axis=0)
        done = None
        if work is not None:
            done = work(near)
            across = after(across, done[0])
        far = jnp.concatenate([across, self.swap_core(across)], axis=0)
        return near, far, done

    def scatter4(self, far, near):
        rows = far.shape[0] // 2
        met = (far[:rows].astype(F32) + self.swap_core(far[rows:]).astype(F32)).astype(BF)
        across = self.swap_x(met)
        near = near(met)
        return near, self.swap_core(near[rows:]), across

    def sum4(self, value):
        def reordered(v, turn):
            v = v.reshape(v.shape[0], 2, 2, -1)
            return jnp.flip(v, turn).reshape(value.shape)

        value = value + reordered(self.swap_core(value), 2)
        return value + reordered(self.swap_x(value), 1)


def pick(v, axis, index):
    return lax.dynamic_index_in_dim(v, index, axis, keepdims=False)


def after(value, *others):
    return lax.optimization_barrier((value,) + others)[0]


def pack_kernel(count, width, offsets, spot_ref, *refs):
    x, c = spot_ref[0], spot_ref[1]
    outs = refs[-4:]
    for dx in range(2):
        for dc in range(2):
            places = offsets((x + dx) % 2, (c + dc) % 2)
            for w, ref in enumerate(refs[:count]):
                for k, place in enumerate(places):
                    at = (w * len(places) + k) * width
                    outs[2 * dx + dc][:, at : at + width] = ref[:, pl.ds(pl.multiple_of(place * width, HD), width)]


def pack(spot, weights, width, offsets):
    rows = weights[0].shape[0]
    size = len(weights) * len(offsets(0, 0)) * width
    if width % HD:
        outs = []
        for d in range(4):
            places = offsets((spot[0] + d // 2) % 2, (spot[1] + d % 2) % 2)
            cuts = [lax.dynamic_slice_in_dim(w, place * width, width, 1) for w in weights for place in places]
            outs.append(jnp.concatenate(cuts, axis=1))
        return outs
    whole = pl.BlockSpec(memory_space=pltpu.VMEM)
    return pl.pallas_call(
        functools.partial(pack_kernel, len(weights), width, offsets),
        in_specs=[pl.BlockSpec(memory_space=pltpu.SMEM)] + [whole] * len(weights),
        out_specs=[whole] * 4,
        out_shape=[jax.ShapeDtypeStruct((rows, size), BF)] * 4,
        compiler_params=pltpu.CompilerParams(vmem_limit_bytes=VMEM_BYTES),
        name="pack_columns",
        cost_estimate=cost(3),
    )(spot, *weights)


def join_kernel(spot_ref, *refs):
    x, c = spot_ref[0], spot_ref[1]
    rows = refs[0].shape[0]
    for dx in range(2):
        for dc in range(2):
            slot = 2 * ((x + dx) % 2) + (c + dc) % 2
            refs[4][pl.ds(pl.multiple_of(slot * rows, rows), rows), :] = refs[2 * dx + dc][...]


def join(spot, parts):
    rows, size = parts[0].shape
    whole = pl.BlockSpec(memory_space=pltpu.VMEM)
    return pl.pallas_call(
        join_kernel,
        in_specs=[pl.BlockSpec(memory_space=pltpu.SMEM)] + [whole] * 4,
        out_specs=whole,
        out_shape=jax.ShapeDtypeStruct((4 * rows, size), BF),
        compiler_params=pltpu.CompilerParams(vmem_limit_bytes=VMEM_BYTES),
        name="join_rows",
        cost_estimate=cost(2),
    )(spot, *parts)


def gate_up_kernel(spot_ref, x_ref, g0_ref, g1_ref, u0_ref, u1_ref, narrow_ref, maps_ref, gate_ref, up_ref, gated_ref):
    half, rank = g0_ref.shape[0], maps_ref.shape[1]
    y = spot_ref[2]
    x0 = x_ref[:, pl.ds(pl.multiple_of(y * half, HD), half)]
    x1 = x_ref[:, pl.ds(pl.multiple_of((1 - y) * half, HD), half)]
    gate = dot(x0, g0_ref[...]) + dot(x1, g1_ref[...])
    gate = gate + SCALE_ADAPT * dot(narrow_ref[:, :rank], maps_ref[0])
    up = dot(x0, u0_ref[...]) + dot(x1, u1_ref[...])
    up = up + SCALE_ADAPT * dot(narrow_ref[:, rank:], maps_ref[1])
    gate_ref[...] = gate.astype(BF)
    up_ref[...] = up.astype(BF)
    gated_ref[...] = (gate * jax.nn.sigmoid(gate) * up).astype(BF)


def gate_up(spot, x, gate_parts, up_parts, narrow, maps):
    rows, width = x.shape
    half, hidden = gate_parts[0].shape
    tile = 256
    steps = hidden // tile
    column = lambda s, spot: (0, (s + spot[2] * (steps // 2)) % steps)
    weight = pl.BlockSpec((half, tile), column)
    out = pl.BlockSpec((rows, tile), lambda s, spot: (0, s))
    return pl.pallas_call(
        gate_up_kernel,
        grid_spec=pltpu.PrefetchScalarGridSpec(
            num_scalar_prefetch=1,
            grid=(steps,),
            in_specs=[pl.BlockSpec((rows, width), lambda s, spot: (0, 0))]
            + [weight] * 4
            + [
                pl.BlockSpec(narrow.shape, lambda s, spot: (0, 0)),
                pl.BlockSpec(maps.shape[:2] + (tile,), lambda s, spot: (0, 0, s)),
            ],
            out_specs=[out] * 3,
        ),
        out_shape=[jax.ShapeDtypeStruct((rows, hidden), BF)] * 3,
        compiler_params=pltpu.CompilerParams(vmem_limit_bytes=VMEM_BYTES),
        name="gate_up",
        cost_estimate=cost(26),
    )(spot, x, *gate_parts, *up_parts, narrow, maps)


def down_kernel(gated_ref, *refs):
    d_refs = refs[:-4]
    in_maps_ref, out_maps_ref, feed_ref, narrow_ref = refs[-4:]
    depth = d_refs[0].shape[0]

    @pl.when(pl.program_id(0) == 0)
    def _():
        narrow_ref[...] = dot_nt(gated_ref[...], in_maps_ref[...]).astype(BF)

    feed = sum(dot(gated_ref[:, k * depth : (k + 1) * depth], ref[...]) for k, ref in enumerate(d_refs))
    feed_ref[...] = (feed + SCALE_ADAPT * dot(narrow_ref[...], out_maps_ref[...])).astype(BF)


def down(gated, part, parts, in_maps, out_maps):
    rows, hidden = gated.shape[0] // 2, gated.shape[1]
    depth, width = parts[0].shape
    rank = in_maps.shape[0]
    tile = 256
    weight = pl.BlockSpec((depth, tile), lambda s: (0, s))
    return pl.pallas_call(
        down_kernel,
        grid=(width // tile,),
        in_specs=[
            pl.BlockSpec((rows, hidden), lambda s: (part, 0)),
            *([weight] * len(parts)),
            pl.BlockSpec(in_maps.shape, lambda s: (0, 0)),
            pl.BlockSpec((rank, tile), lambda s: (0, s)),
        ],
        out_specs=[pl.BlockSpec((rows, tile), lambda s: (0, s)), pl.BlockSpec((rows, rank), lambda s: (0, 0))],
        out_shape=[jax.ShapeDtypeStruct((rows, width), BF), jax.ShapeDtypeStruct((rows, rank), BF)],
        compiler_params=pltpu.CompilerParams(vmem_limit_bytes=VMEM_BYTES),
        name="down",
        cost_estimate=cost(10),
    )(gated, *parts, in_maps, out_maps)


def feed_back_kernel(
    spot_ref,
    grad_ref,
    d0_ref,
    d1_ref,
    d2_ref,
    d3_ref,
    g0_ref,
    g1_ref,
    u0_ref,
    u1_ref,
    gate_ref,
    up_ref,
    gated_ref,
    narrow_ref,
    d_out_ref,
    d_in_ref,
    gu_out_ref,
    gu_in_ref,
    out_ref,
    back_gu_ref,
    maps_ref,
    total,
    grad_gated,
    back_d,
    back_gu,
):
    step, steps = pl.program_id(0), pl.num_programs(0)
    half, rank = g0_ref.shape[0], d_in_ref.shape[0]

    @pl.when(step == 0)
    def _():
        total[...] = jnp.zeros_like(total)
        back_gu[...] = jnp.zeros_like(back_gu)
        back_d[...] = dot_nt(grad_ref[...], d_out_ref[...]).astype(BF)

    for k, ref in enumerate((d0_ref, d1_ref, d2_ref, d3_ref)):

        @pl.when((step >= k * steps // 4) & (step < (k + 1) * steps // 4))
        def _(ref=ref):
            grad_gated[...] = dot_nt(grad_ref[...], ref[...])

    dm = grad_gated[...] + SCALE_ADAPT * dot(back_d[...], d_in_ref[...])
    gate, up = gate_ref[...].astype(F32), up_ref[...].astype(F32)
    sig = jax.nn.sigmoid(gate)
    silu = gate * sig
    du = (dm * silu).astype(BF)
    dg = (dm * up * (sig + silu * (1.0 - sig))).astype(BF)
    y = spot_ref[2]
    total[:, pl.ds(pl.multiple_of(y * half, HD), half)] += dot_nt(dg, g0_ref[...]) + dot_nt(du, u0_ref[...])
    total[:, pl.ds(pl.multiple_of((1 - y) * half, HD), half)] += dot_nt(dg, g1_ref[...]) + dot_nt(du, u1_ref[...])
    back_gu[:, :rank] += dot_nt(dg, gu_out_ref[0])
    back_gu[:, rank:] += dot_nt(du, gu_out_ref[1])
    maps_ref[0] = SCALE_ADAPT * dot_tn(back_d[...], gated_ref[...])
    maps_ref[1] = SCALE_ADAPT * dot_tn(narrow_ref[:, :rank], dg)
    maps_ref[2] = SCALE_ADAPT * dot_tn(narrow_ref[:, rank:], du)

    @pl.when(step == steps - 1)
    def _():
        low = back_gu[...].astype(BF)
        back_gu_ref[...] = low
        out_ref[...] = (total[...] + SCALE_ADAPT * dot(low, gu_in_ref[...])).astype(BF)


def feed_back(spot, part, grad, d_parts, g_parts, u_parts, gate, up, gated, narrow, d_out, d_in, gu_out, gu_in):
    rows, width = grad.shape
    half, hidden = g_parts[0].shape
    rank = d_in.shape[0]
    tile = 256
    steps = hidden // tile
    mid = steps // 2
    column = pl.BlockSpec((half, tile), lambda s, spot: (0, (s + spot[2] * mid) % steps))
    local = pl.BlockSpec((rows, tile), lambda s, spot: (part, s))
    fixed = lambda v: pl.BlockSpec(v.shape, lambda s, spot: (0,) * v.ndim)
    return pl.pallas_call(
        feed_back_kernel,
        grid_spec=pltpu.PrefetchScalarGridSpec(
            num_scalar_prefetch=1,
            grid=(steps,),
            in_specs=[
                fixed(grad),
            ]
            + [
                pl.BlockSpec((tile, width), lambda s, spot, k=k: (jnp.clip(s - k * mid // 2, 0, mid // 2 - 1), 0))
                for k in range(4)
            ]
            + [column] * 4
            + [local] * 3
            + [
                pl.BlockSpec((rows, 2 * rank), lambda s, spot: (part, 0)),
                fixed(d_out),
                pl.BlockSpec((rank, tile), lambda s, spot: (0, s)),
                pl.BlockSpec((2, rank, tile), lambda s, spot: (0, 0, s)),
                fixed(gu_in),
            ],
            out_specs=[
                pl.BlockSpec((rows, width), lambda s, spot: (0, 0)),
                pl.BlockSpec((rows, 2 * rank), lambda s, spot: (0, 0)),
                pl.BlockSpec((3, rank, tile), lambda s, spot: (0, 0, s)),
            ],
            scratch_shapes=[
                pltpu.VMEM((rows, width), F32),
                pltpu.VMEM((rows, tile), F32),
                pltpu.VMEM((rows, rank), BF),
                pltpu.VMEM((rows, 2 * rank), F32),
            ],
        ),
        out_shape=[
            jax.ShapeDtypeStruct((rows, width), BF),
            jax.ShapeDtypeStruct((rows, 2 * rank), BF),
            jax.ShapeDtypeStruct((3, rank, hidden), F32),
        ],
        compiler_params=pltpu.CompilerParams(vmem_limit_bytes=VMEM_BYTES),
        name="feed_backward",
        cost_estimate=cost(24),
    )(spot, grad, *d_parts, *g_parts, *u_parts, gate, up, gated, narrow, d_out, d_in, gu_out, gu_in)


def post_kernel(heads, pre_ref, inv_ref, gain_ref, cos_ref, sin_ref, q_ref, k_ref):
    width = heads * HD
    cos, sin = cos_ref[...], sin_ref[...]
    for part, out_ref in enumerate((q_ref, k_ref)):
        inv = inv_ref[:, part : part + 1]
        for h in range(heads):
            cols = slice(part * width + h * HD, part * width + (h + 1) * HD)
            v = pre_ref[:, cols] * inv * gain_ref[:, cols]
            out_ref[:, h * HD : (h + 1) * HD] = (v * cos + pltpu.roll(v, HD // 2, 1) * sin).astype(BF)


def post(pre, inv, gain, cos, sin, heads):
    rows, width = pre.shape[0], heads * HD
    tile = 256
    row = lambda n: pl.BlockSpec((tile, n), lambda r: (r, 0))
    return pl.pallas_call(
        functools.partial(post_kernel, heads),
        grid=(rows // tile,),
        in_specs=[row(2 * width), row(2), pl.BlockSpec((1, 2 * width), lambda r: (0, 0)), row(HD), row(HD)],
        out_specs=[row(width), row(width)],
        out_shape=[jax.ShapeDtypeStruct((rows, width), BF)] * 2,
        name="rope_forward",
        cost_estimate=cost(5),
    )(pre, inv, gain, cos, sin)


def unpost_kernel(heads, dq_ref, dk_ref, pre_ref, gain_ref, cos_ref, sin_ref, turn_ref, inner_ref):
    width = heads * HD
    cos, sin = cos_ref[...], sin_ref[...]
    for part, d_ref in enumerate((dq_ref, dk_ref)):
        total = None
        for h in range(heads):
            cols = slice(part * width + h * HD, part * width + (h + 1) * HD)
            v = d_ref[:, h * HD : (h + 1) * HD]
            turned = (v * cos - pltpu.roll(v, HD // 2, 1) * sin) * gain_ref[:, cols]
            turn_ref[:, cols] = turned
            inner = jnp.sum(turned * pre_ref[:, cols], axis=1, keepdims=True)
            total = inner if total is None else total + inner
        inner_ref[:, part : part + 1] = total


def unpost(dq, dk, pre, gain, cos, sin, heads):
    rows, width = pre.shape[0], heads * HD
    tile = 256
    row = lambda n: pl.BlockSpec((tile, n), lambda r: (r, 0))
    return pl.pallas_call(
        functools.partial(unpost_kernel, heads),
        grid=(rows // tile,),
        in_specs=[row(width), row(width), row(2 * width), pl.BlockSpec((1, 2 * width), lambda r: (0, 0)), row(HD), row(HD)],
        out_specs=[row(2 * width), row(2)],
        out_shape=[jax.ShapeDtypeStruct((rows, 2 * width), F32), jax.ShapeDtypeStruct((rows, 2), F32)],
        name="rope_backward",
        cost_estimate=cost(8),
    )(dq, dk, pre, gain, cos, sin)


NEG_FILL = -1e30


def attend_kernel(count, scale, q_ref, *refs):
    ks, vs = refs[:count], refs[count : 2 * count]
    lo_ref, pos_ref, key_ref, o_ref, log_ref = refs[2 * count :]
    rows = q_ref.shape[0] * q_ref.shape[2]
    q = q_ref[...].reshape(rows, HD)
    lo, pos = lo_ref[0], pos_ref[...]
    scores = []
    for t in range(count):
        s = dot_nt(q, ks[t][...].reshape(rows, HD)) * scale
        key = key_ref[t : t + 1, :]
        scores.append(jnp.where((key >= lo) & (key <= pos), s, NEG_FILL))
    top = functools.reduce(jnp.maximum, [jnp.max(s, axis=1, keepdims=True) for s in scores])
    powers = [jnp.exp(s - top) for s in scores]
    total = sum(jnp.sum(e, axis=1, keepdims=True) for e in powers)
    share = 1.0 / total
    out = sum(dot((e * share).astype(BF), vs[t][...].reshape(rows, HD)) for t, e in enumerate(powers))
    o_ref[...] = out.astype(BF).reshape(o_ref.shape)
    log_ref[0] = top + jnp.log(total)


def attend_back_kernel(count, first, scale, q_ref, do_ref, o_ref, *refs):
    ks, vs = refs[:count], refs[count : 2 * count]
    lo_ref, pos_ref, key_ref, log_ref = refs[2 * count : 2 * count + 4]
    refs = refs[2 * count + 4 :]
    dq = None
    rows = q_ref.shape[0] * q_ref.shape[2]
    if not first:
        dq = refs[0][...].reshape(rows, HD)
        refs = refs[1:]
    dq_ref, dks, dvs = refs[0], refs[1 : 1 + count], refs[1 + count :]
    q = q_ref[...].reshape(rows, HD)
    do = do_ref[...].reshape(rows, HD)
    inner = jnp.sum(do.astype(F32) * o_ref[...].reshape(rows, HD).astype(F32), axis=1, keepdims=True)
    lo, pos, log_total = lo_ref[0], pos_ref[...], log_ref[0]
    for t in range(count):
        k, v = ks[t][...].reshape(rows, HD), vs[t][...].reshape(rows, HD)
        key = key_ref[t : t + 1, :]
        s = dot_nt(q, k) * scale
        probs = jnp.where((key >= lo) & (key <= pos), jnp.exp(s - log_total), 0.0)
        ds = (probs * (dot_nt(do, v) - inner)).astype(BF)
        dvs[t][...] = dot_tn(probs.astype(BF), do).astype(dvs[t].dtype).reshape(dvs[t].shape)
        dks[t][...] = (dot_tn(ds, q) * scale).astype(dks[t].dtype).reshape(dks[t].shape)
        part = dot(ds, k) * scale
        dq = part if dq is None else dq + part
    dq_ref[...] = dq.reshape(dq_ref.shape)


class Attention:
    def __init__(self, rows, heads, count, lo, pos, key):
        self.rows, self.heads, self.count = rows, heads, count
        self.tables = (lo, pos, key)
        full = 2 * rows
        self.block = pl.BlockSpec((2, 1, rows, HD), lambda s, h: (0, s, 0, h))
        self.table_specs = lambda n: [
            pl.BlockSpec((1, full, 1), lambda s, h: (s, 0, 0)),
            pl.BlockSpec((full, 1), lambda s, h: (0, 0)),
            pl.BlockSpec((n, full), lambda s, h: (0, 0)),
        ]
        self.log_spec = pl.BlockSpec((1, full, 1), lambda s, h: (s * heads + h, 0, 0))
        self.params = pltpu.CompilerParams(vmem_limit_bytes=VMEM_BYTES)

    def shape(self, dtype):
        return jax.ShapeDtypeStruct((2, 2, self.rows, self.heads * HD), dtype)

    def view(self, v):
        return v.reshape(2, 2, self.rows, v.shape[-1])

    def forward(self, q, ks, vs):
        count = self.count
        out, log = pl.pallas_call(
            functools.partial(attend_kernel, count, HD**-0.5),
            grid=(2, self.heads),
            in_specs=[self.block] * (1 + 2 * count) + self.table_specs(count),
            out_specs=[self.block, self.log_spec],
            out_shape=[self.shape(BF), jax.ShapeDtypeStruct((2 * self.heads, 2 * self.rows, 1), F32)],
            compiler_params=self.params,
            name="attend_forward",
            cost_estimate=cost(23),
        )(*[self.view(v) for v in [q] + ks + vs], *self.tables)
        return out.reshape(q.shape), log

    def backward(self, q, do, o, ks, vs, log, blocks, dtypes, dq=None):
        lo, pos, key = self.tables
        count = len(blocks)
        grads = [self.shape(d) for d in dtypes]
        key = jnp.concatenate([key[t : t + 1] for t in blocks], axis=0)
        more = [] if dq is None else [self.view(dq)]
        outs = pl.pallas_call(
            functools.partial(attend_back_kernel, count, dq is None, HD**-0.5),
            grid=(2, self.heads),
            in_specs=[self.block] * (3 + 2 * count) + self.table_specs(count) + [self.log_spec] + [self.block] * len(more),
            out_specs=[self.block] * (1 + 2 * count),
            out_shape=[self.shape(F32)] + grads + grads,
            compiler_params=self.params,
            name="attend_backward",
            cost_estimate=cost(4 + 8 * count),
        )(*[self.view(v) for v in [q, do, o] + ks + vs], lo, pos, key, log, *more)
        flat = [v.reshape(q.shape) for v in outs]
        return flat[0], flat[1 : 1 + count], flat[1 + count :]


def rms_inverse(v):
    return lax.rsqrt(jnp.mean(v * v, axis=-1, keepdims=True) + EPS)


def rms_backward(v, gain, grad):
    inv = rms_inverse(v)
    turn = grad * gain
    inner = jnp.mean(v * turn, axis=-1, keepdims=True)
    return inv * turn - v * (inv * inv * inv) * inner


def fold(v, unit, groups):
    lead = v.shape[:-1]
    v = v.reshape(lead + (2 * groups, 2, unit))
    return jnp.swapaxes(v, -3, -2).reshape(lead + (-1,))


def unfold(v, unit, groups):
    lead = v.shape[:-1]
    v = v.reshape(lead + (2, 2 * groups, unit))
    return jnp.swapaxes(v, -3, -2).reshape(lead + (-1,))


def fold_blocks(v):
    blocks = v.shape[1] // HD
    return jnp.concatenate([v[:, k * HD : (k + 1) * HD] for y in range(2) for k in range(y, blocks, 2)], axis=1)


def unfold_blocks(v):
    half = v.shape[1] // HD // 2
    order = [y * half + k for k in range(half) for y in range(2)]
    return jnp.concatenate([v[:, k * HD : (k + 1) * HD] for k in order], axis=1)


def sum3(refs):
    return refs[0][...].astype(F32) + refs[1][...].astype(F32) + refs[2][...].astype(F32)


def fold_kernel(v_ref, out_ref):
    out_ref[...] = fold_blocks(v_ref[...])


def after_attention_kernel(folding, *refs):
    inputs_ref, gain_ref, attn_ref, middle_ref, low_ref = refs[3:]
    attn = sum3(refs)
    attn_ref[...] = attn
    middle = inputs_ref[...].astype(F32) + attn * rms_inverse(attn) * gain_ref[...]
    middle_ref[...] = middle
    low = middle.astype(BF)
    low_ref[...] = fold_blocks(low) if folding else low


def after_feed_kernel(*refs):
    middle_ref, gain_ref, cot_ref, result_ref, grad_ref = refs[3:]
    feed = sum3(refs)
    gain = gain_ref[...]
    result_ref[...] = (middle_ref[...] + feed * rms_inverse(feed) * gain).astype(BF)
    grad_ref[...] = rms_backward(feed, gain, cot_ref[...].astype(F32)).astype(BF)


def middle_kernel(folding, *refs):
    cot_ref, attn_ref, gain_ref, mid_ref, grad_ref = refs[3:]
    total = sum3(refs)
    mid = cot_ref[...].astype(F32) + (unfold_blocks(total) if folding else total)
    mid_ref[...] = mid
    grad_ref[...] = rms_backward(attn_ref[...], gain_ref[...], mid).astype(BF)


def end_kernel(folding, *refs):
    mid_ref, out_ref = refs[3:]
    total = sum3(refs)
    out_ref[...] = mid_ref[...] + (unfold_blocks(total) if folding else total)


def by_rows(kernel, name, rows, width, args, dtypes, us):
    tile = 64 if rows % 64 == 0 else rows
    spec = lambda v: pl.BlockSpec((1, width), lambda r: (0, 0)) if v.shape[0] == 1 else pl.BlockSpec((tile, width), lambda r: (r, 0))
    row = pl.BlockSpec((tile, width), lambda r: (r, 0))
    return pl.pallas_call(
        kernel,
        grid=(rows // tile,),
        in_specs=[spec(v) for v in args],
        out_specs=[row] * len(dtypes),
        out_shape=[jax.ShapeDtypeStruct((rows, width), d) for d in dtypes],
        compiler_params=pltpu.CompilerParams(vmem_limit_bytes=VMEM_BYTES),
        name=name,
        cost_estimate=cost(us),
    )(*args)


def on_device(
    layer_input,
    cotangent,
    document_length,
    adapter_choice_index,
    query_weight,
    key_weight,
    value_weight,
    output_weight,
    gate_weight,
    up_weight,
    down_weight,
    query_norm_gain,
    key_norm_gain,
    attention_norm_gain,
    feedforward_norm_gain,
    adapter_model_input_maps,
    adapter_down_input_maps,
    adapter_model_output_maps,
    adapter_hidden_output_maps,
):
    at = Place()
    rows = layer_input.shape[1]
    width = layer_input.shape[2]
    heads = width // HD // 4
    local = heads * HD
    rank = adapter_model_input_maps.shape[2]
    depth = query_weight.shape[0]
    hidden_rows = down_weight.shape[0]
    hidden = hidden_rows * at.np * 2
    reach = WINDOW // (2 * rows)
    count = reach + 1

    def head_cols(v, quarter):
        return pick(v.reshape(v.shape[:-1] + (heads, 4, HD)), v.ndim, quarter).reshape(v.shape[:-1] + (local,))

    def hidden_cols(v):
        lead = v.shape[:-1]
        n = len(lead)
        v = v.reshape(lead + (at.np, 2, 2, 2, 2, hidden_rows // 2))
        v = pick(v, n + 3, at.c)
        v = pick(v, n + 1, at.x)
        v = jnp.moveaxis(v, n, n + 2)
        first, second = (jnp.where(at.y == 0, v[..., k, :, :, :], v[..., 1 - k, :, :, :]) for k in range(2))
        return jnp.concatenate([first.reshape(lead + (-1,)), second.reshape(lead + (-1,))], axis=-1)

    def regroup(weights, size, offsets, *earlier):
        own, core, across, both = pack(at.spot, weights, size, offsets)
        core = after(core, *earlier)
        return join(at.spot, [own, at.swap_core(core), at.swap_x(across), at.swap_both(both)])

    def gather_p(v):
        return lax.all_gather(v, "p", axis=0, tiled=True)

    def in_order(own, other):
        size = own.shape[0]
        buf = jnp.zeros((2 * size,) + own.shape[1:], own.dtype)
        buf = lax.dynamic_update_slice(buf, own, (at.y * size, 0))
        return lax.dynamic_update_slice(buf, other, ((1 - at.y) * size, 0))

    own_inputs = layer_input[0]
    unit = 2 * depth
    folding = unit % HD == 0
    if folding:
        (folded_inputs,) = by_rows(fold_kernel, "fold", rows, width, [own_inputs], [BF], 2)
    else:
        folded_inputs = fold(own_inputs, unit, at.np)
    half_rows = hidden_rows // 2
    head_offsets = lambda x, c: [4 * k + 2 * x + c for k in range(heads)]
    feed_offsets = lambda x, c: [
        (((2 * p + x) * 2 + y) * 2 + c) * 2 + half for y in range(2) for half in range(2) for p in range(at.np)
    ]
    qkv_piece = regroup([query_weight, key_weight, value_weight], HD, head_offsets)
    gate_piece = regroup([gate_weight], half_rows, feed_offsets, qkv_piece)
    up_piece = regroup([up_weight], half_rows, feed_offsets, gate_piece)
    inputs = jnp.concatenate(at.gather4(folded_inputs)[:2])

    qkv_own = gather_p(qkv_piece)
    qkv_other = at.swap_y(qkv_own)
    w_qkv = in_order(qkv_own, qkv_other)
    gate_own = gather_p(gate_piece)
    up_own = gather_p(up_piece)
    if 2 * depth == HD:
        o_own = gather_p(after(output_weight, qkv_own))
        sent = lambda target: lax.ppermute(o_own, ("y", "c"), target)
        same = at.y == at.c
        mine_half = jnp.where(same, o_own, sent([(0, 2), (3, 1)]))
        other_half = jnp.where(same, sent([(1, 0), (2, 3)]), sent([(1, 2), (2, 1)]))
        halves = [jnp.where(at.c == 0, mine_half, other_half), jnp.where(at.c == 0, other_half, mine_half)]
        w_o = jnp.stack([v.reshape(at.np, depth, width) for v in halves], axis=1).reshape(local, width)
    else:
        o_own = qkv_own
        o_full = lax.all_gather(output_weight, ("p", "x", "y", "c"), axis=0, tiled=True)
        w_o = pick(o_full.reshape(heads, 4, HD, width), 1, at.quarter).reshape(local, width)
    down_own = [gather_p(after(down_weight[:half_rows], gate_own)), gather_p(after(down_weight[half_rows:], up_own))]
    w_g = (gate_own, at.swap_y(after(gate_own, qkv_other)))
    w_u = (up_own, at.swap_y(after(up_own, w_g[1])))
    down_other = [at.swap_y(after(down_own[0], w_u[1]))]
    down_other.append(at.swap_y(after(down_own[1], down_other[0])))
    w_d = (*down_own, *down_other)

    selected = adapter_choice_index[0]
    a_model = pick(adapter_model_input_maps, 0, selected)
    a_hidden = pick(adapter_down_input_maps, 0, selected)
    b_model = pick(adapter_model_output_maps, 0, selected)
    b_hidden = pick(adapter_hidden_output_maps, 0, selected)
    a_qkv = fold(a_model[:3].reshape(3 * rank, width), unit, at.np)
    a_gu = fold(a_model[4:6].reshape(2 * rank, width), unit, at.np)
    a_o = head_cols(a_model[3], at.quarter)
    a_d = hidden_cols(a_hidden)
    b_qkv = head_cols(b_model[:3], at.quarter)
    b_o, b_d = b_model[3], b_model[4]
    b_gu = hidden_cols(b_hidden)

    def diagonal(maps):
        k, r, n = maps.shape
        zero = jnp.zeros((r, n), BF)
        return jnp.concatenate(
            [jnp.concatenate([maps[a] if a == b else zero for b in range(k)], axis=1) for a in range(k)], axis=0
        )

    b_qkv_diag = diagonal(b_qkv)
    gain = jnp.concatenate(
        [head_cols(query_norm_gain[None], at.quarter), head_cols(key_norm_gain[None], at.quarter)], axis=1
    )

    step_rows = jnp.arange(rows, dtype=jnp.int32)
    spot = lambda xx: at.p * 2 * rows + xx * rows + step_rows
    pos = jnp.concatenate([spot(at.x), spot(1 - at.x)])
    lengths = lax.dynamic_slice_in_dim(document_length, 2 * at.y, 2, 0)
    bounds = jnp.cumsum(lengths, axis=1)
    bounds = jnp.where(at.c == 0, bounds, bounds[::-1])
    begin = jnp.max(jnp.where(bounds[:, None, :] <= pos[None, :, None], bounds[:, None, :], 0), axis=2)
    lo = jnp.maximum(begin, pos[None] - (WINDOW - 1))
    key = jnp.stack([pos - 2 * rows * t for t in range(count)])
    attention = Attention(rows, heads, count, lo[:, :, None], pos[:, None], key)

    half_dim = HD // 2
    inv_freq = ROPE_BASE ** (-(jnp.arange(half_dim, dtype=F32) * 2.0 / HD))
    angles = jnp.concatenate([spot(at.x), spot(at.x), spot(1 - at.x), spot(1 - at.x)]).astype(F32)[:, None] * inv_freq
    cos, sin = jnp.cos(angles), jnp.sin(angles)
    cos = jnp.concatenate([cos, cos], axis=1)
    sin = jnp.concatenate([-sin, sin], axis=1)

    narrow_qkv = dot_nt(inputs, a_qkv).astype(BF)
    pre = dot(inputs, w_qkv) + SCALE_ADAPT * dot(narrow_qkv, b_qkv_diag)
    value = pre[:, 2 * local :].astype(BF)
    squares = jnp.stack(
        [jnp.sum(jnp.square(pre[:, k * local : (k + 1) * local]), axis=1) for k in range(2)], axis=0
    )
    inv = lax.rsqrt(at.sum4(squares) / width + EPS).T
    query, key_own = post(pre, inv, gain, cos, sin, heads)
    keys, values = [key_own], [value]
    for _ in range(reach):
        values.append(at.shift_p(values[-1], 1))
        keys.append(at.shift_p(keys[-1], 1))
    o, log = attention.forward(query, keys, values)
    narrow_o = dot_nt(o, a_o).astype(BF)
    def attn_part(part, mark=None):
        ins, narrow = o[part], narrow_o[part]
        if mark is not None:
            ins = after(ins, mark)
        return (dot(ins, w_o) + SCALE_ADAPT * dot(narrow, b_o)).astype(BF)

    near_rows, far_rows = slice(0, 2 * rows), slice(2 * rows, 4 * rows)
    attn_parts = at.scatter4(attn_part(far_rows), lambda mark: attn_part(near_rows, mark))
    attn_gain, feed_gain = attention_norm_gain[None], feedforward_norm_gain[None]
    attn_out, middle, low = by_rows(
        functools.partial(after_attention_kernel, folding),
        "after_attention",
        rows,
        width,
        [*attn_parts, own_inputs, attn_gain],
        [F32, F32, BF],
        4,
    )
    middle_low = jnp.concatenate(at.gather4(low if folding else fold(low, unit, at.np))[:2])
    narrow_gu = dot_nt(middle_low, a_gu).astype(BF)
    gate, up, gated = gate_up(at.spot, middle_low, w_g, w_u, narrow_gu, b_gu)
    feed_far, narrow_d_far = down(gated, 1, w_d, a_d, b_d)
    narrow_d = []

    def feed_near(mark):
        part, narrow = down(after(gated, mark), 0, w_d, a_d, b_d)
        narrow_d.append(narrow)
        return part

    feed_parts = at.scatter4(feed_far, feed_near)
    narrow_d = jnp.concatenate([narrow_d[0], narrow_d_far])
    cot = cotangent[0]
    result, grad_feed_own = by_rows(
        after_feed_kernel,
        "after_feed",
        rows,
        width,
        [*feed_parts, middle, feed_gain, cot],
        [BF, BF],
        4,
    )

    feed_args = (w_d, w_g, w_u, gate, up, gated, narrow_gu, b_d, a_d, b_gu, a_gu)
    grad_near, grad_far, (mid_near, back_gu_near, maps_near) = at.gather4(
        grad_feed_own, lambda near: feed_back(at.spot, 0, near, *feed_args)
    )
    mid_far, back_gu_far, maps_far = feed_back(at.spot, 1, grad_far, *feed_args)
    grad_feed = jnp.concatenate([grad_near, grad_far])
    back_gu = jnp.concatenate([back_gu_near, back_gu_far])
    mid_parts = at.scatter4(mid_far, lambda mark: mid_near)
    if not folding:
        mid_parts = [unfold(v, unit, at.np) for v in mid_parts]
    grad_mid, grad_attn_own = by_rows(
        functools.partial(middle_kernel, folding),
        "middle",
        rows,
        width,
        [*mid_parts, cot, attn_out, attn_gain],
        [F32, BF],
        4,
    )
    grad_attn = jnp.concatenate(at.gather4(grad_attn_own)[:2])
    back_o = dot_nt(grad_attn, b_o).astype(BF)
    grad_o = (dot_nt(grad_attn, w_o) + SCALE_ADAPT * dot(back_o, a_o)).astype(BF)
    dq, dks, dvs = attention.backward(query, grad_o, o, keys[reach:], values[reach:], log, [reach], [BF])
    moved_k, moved_v = at.shift_p(dks[0], -1), at.shift_p(dvs[0], -1)
    dq, dks, dvs = attention.backward(
        query, grad_o, o, keys[:reach], values[:reach], log, range(reach), [F32] + [BF] * (reach - 1), dq
    )
    for t in range(reach - 1, 0, -1):
        moved_k = at.shift_p((dks[t].astype(F32) + moved_k.astype(F32)).astype(BF), -1)
        moved_v = at.shift_p((dvs[t].astype(F32) + moved_v.astype(F32)).astype(BF), -1)
    dk = dks[0] + moved_k.astype(F32)
    dv = dvs[0] + moved_v.astype(F32)
    turn, inner = unpost(dq, dk, pre, gain, cos, sin, heads)
    inner = at.sum4(inner.T).T / width

    def unnorm(part):
        cols = slice(part * local, (part + 1) * local)
        scale = inv[:, part : part + 1]
        return (scale * turn[:, cols] - pre[:, cols] * (scale * scale * scale * inner[:, part : part + 1])).astype(BF)

    grad_qkv = jnp.concatenate([unnorm(0), unnorm(1), dv.astype(BF)], axis=1)
    back_qkv = dot_nt(grad_qkv, b_qkv_diag).astype(BF)
    def end_part(part, mark=None):
        ins, back = grad_qkv[part], back_qkv[part]
        if mark is not None:
            ins = after(ins, mark)
        return (dot_nt(ins, w_qkv) + SCALE_ADAPT * dot(back, a_qkv)).astype(BF)

    end_parts = at.scatter4(end_part(far_rows), lambda mark: end_part(near_rows, mark))
    if not folding:
        end_parts = [unfold(v, unit, at.np) for v in end_parts]
    (grad_input,) = by_rows(
        functools.partial(end_kernel, folding), "end", rows, width, [*end_parts, grad_mid], [F32], 3
    )

    ga_qkv = SCALE_ADAPT * dot_tn(back_qkv, inputs)
    ga_gu = SCALE_ADAPT * dot_tn(back_gu, middle_low)
    ga_o = SCALE_ADAPT * dot_tn(back_o, o)
    gb_qkv = [
        SCALE_ADAPT * dot_tn(narrow_qkv[:, k * rank : (k + 1) * rank], grad_qkv[:, k * local : (k + 1) * local])
        for k in range(3)
    ]
    gb_o = SCALE_ADAPT * dot_tn(narrow_o, grad_attn)
    gb_d = SCALE_ADAPT * dot_tn(narrow_d, grad_feed)
    mine = (jnp.arange(4) == at.quarter).astype(F32)

    def spread(v):
        return (v.reshape(-1, heads, 1, HD) * mine[:, None]).reshape(-1, width)

    def share_y(mine, other):
        return mine + at.swap_y(other)

    def share_p(v):
        total = pick(v, 1, at.p)
        for by in range(1, at.np):
            total = total + at.turn_p(pick(v, 1, (at.p + by) % at.np), by)
        return total

    def sum_model(folded, plain):
        folded = folded.reshape(-1, 2, at.np, 2, 2 * depth)
        plain = plain.reshape(-1, at.np, 2, 2, 2 * depth)

        def cut(x):
            plain_part = jnp.swapaxes(pick(plain, 2, x), 1, 2)
            return jnp.concatenate([pick(folded, 3, x), plain_part], axis=0)

        v = cut(at.x) + at.swap_x(cut(1 - at.x))
        v = share_p(share_y(pick(v, 1, at.y), pick(v, 1, 1 - at.y)))
        v = v.reshape(v.shape[0], 2, depth)
        return (pick(v, 1, at.c) + at.swap_core(pick(v, 1, 1 - at.c))).reshape(-1, rank, depth)

    def sum_hidden(v):
        v = v.reshape(-1, 2, 2, at.np, half_rows)
        v = share_y(v[:, 0], v[:, 1])
        return share_p(jnp.swapaxes(v, 1, 2)).reshape(-1, rank, hidden_rows)

    wide = sum_hidden(maps_near + maps_far)
    early = sum_model(ga_gu, jnp.concatenate([spread(ga_o), gb_o, gb_d]))
    late = sum_model(ga_qkv, spread(jnp.concatenate(gb_qkv)))
    choose = (jnp.arange(adapter_model_input_maps.shape[0], dtype=jnp.int32) == selected).astype(F32)
    sum_a_model = choose[:, None, None, None] * jnp.concatenate([late[:3], early[2:3], early[:2]])[None]
    sum_a_hidden = choose[:, None, None] * wide[0][None]
    sum_b_model = choose[:, None, None, None] * jnp.concatenate([late[3:], early[3:]])[None]
    sum_b_hidden = choose[:, None, None, None] * wide[1:][None]
    return (result[None], grad_input[None], sum_a_model, sum_a_hidden, sum_b_model, sum_b_hidden)


def solution(mesh):
    grid = mesh.devices.reshape(mesh.shape["ctx"] // 2, 2, mesh.shape["wt"] // 2, 2)
    split = Mesh(grid, ("p", "x", "y", "c"))
    everyone = ("p", "x", "y", "c")
    rows = P(everyone, None)
    tokens = P(("y", "c"), ("p", "x"), None)
    placed = (tokens, tokens, P(), P()) + (rows,) * 7 + (P(),) * 8
    return jax.shard_map(
        on_device,
        mesh=split,
        in_specs=placed,
        out_specs=(
            tokens,
            tokens,
            P(None, None, None, everyone),
            P(None, None, everyone),
            P(None, None, None, everyone),
            P(None, None, None, everyone),
        ),
        check_vma=False,
    )
```

time: 2240 us -> 993 us (0.44)
  waiting for transfers between devices: 1350 us -> 446 us
  matrix products: 313 us -> 66.1 us
  local copies, waits for them, and re-layouts: 316 us -> 93.8 us
  Pallas kernels: 0 us -> 196 us
  other arithmetic: 104 us -> 50.1 us
    all_gather x7 -> x6, waiting for transfers between devices: 619 us -> 84.5 us  [gather_p(): return lax.all_gather(v, 'p', axis=0, tiled=True)]
    reduce_scatter x2 -> x0, waiting for transfers between devices: 282 us -> none  [the longest x1 148 us: on_device(): lax.psum_scatter(adapter_selector[:, None, None, None] * gb_hidden[None],...]
    dot_general x62 -> x25, matrix products: 313 us -> 66.1 us  [dot(): return lax.dot_general(a, b, (dims, ((), ())), preferred_element_type=F32)]
    unnamed x222 -> x204, local copies, waits for them, and re-layouts: 239 us -> 40.4 us
    pallas_call x0 -> x21, Pallas kernels: none -> 196 us  [the longest x2 52.7 us: feed_back(): pl.pallas_call(feed_back_kernel, grid_spec=pltpu.PrefetchScalarGridSpec(n...]
    unnamed x13 -> x6, waiting for transfers between devices: 118 us -> 0.1 us
    convert_element_type x15 -> x11, other arithmetic: 56.3 us -> 14.9 us  [the longest x4 6.26 us: scatter4(): (far[:rows].astype(F32) + self.swap_core(far[rows:]).astype(F32)).astype(BF)]
    ppermute x16 -> x69, waiting for transfers between devices: 331 us -> 361 us  [the longest x8 122 us: swap_y(): return lax.ppermute(value, 'y', SWAP)]
  transfers between devices with their start and end apart: 27 -> 75, of which waited for: 20 -> 33; matrix products, arithmetic and copies ran while one was open for 19% -> 14% of each run, Pallas kernels for 0% -> 15%
where the time goes in v1:
time: 993 us; the launch traced here: 981 us
  waiting for transfers between devices  446 us (45%)
  Pallas kernels  196 us (20%)
  starting transfers between devices  112 us (11%)
  local copies, waits for them, and re-layouts  93.8 us (9%)
  matrix products  66.1 us (7%)
  other arithmetic  50.1 us (5%)
  between operations  16.8 us (2%)
    ppermute x8, waiting for transfers between devices, swap_y(): return lax.ppermute(value, 'y', SWAP)  122 us
    ppermute x8, waiting for transfers between devices, shift_p(): lax.ppermute(value, 'p', [(p, p + by) for p in range(self.np) if 0 <= p +...  122 us
    all_gather x6, waiting for transfers between devices, gather_p(): return lax.all_gather(v, 'p', axis=0, tiled=True)  84.5 us
    ppermute x15, waiting for transfers between devices, swap_x(): return lax.ppermute(value, 'x', SWAP)  82.3 us
    dot_general x25, matrix products, dot(): return lax.dot_general(a, b, (dims, ((), ())), preferred_element_type=F32)  66.1 us
    pallas_call x2, Pallas kernels, feed_back(): pl.pallas_call(feed_back_kernel, grid_spec=pltpu.PrefetchScalarGridSpec(n...  52.7 us
    unnamed x204, local copies, waits for them, and re-layouts  40.4 us
    ppermute x9, starting transfers between devices, turn_p(): lax.ppermute(value, 'p', [(p, (p + by) % self.np) for p in range(self.np)])  38.5 us
  transfers between devices with their start and end apart: 75, of which 33 were waited for; matrix products, arithmetic and copies ran while one was open for 14% of the time, Pallas kernels for 15%

profile of v1, /device:TPU:0, one launch (start us, length us, event | category | flops | bytes accessed | tf_op | source)
XLA Modules:
  0.0 980.7 jit_solution(4750217346792666993)
XLA Ops:
  11.6 2.6 collective-permute-start.4
  14.2 5.7 collective-permute-done.4.refs_2_
  19.9 3.7 collective-permute-done.5.refs_3_
  29.5 60.6 %all-gather.7.cloned.1.call-done = bf16[1024,1536]{1,0:T(8,128)(2,1)} async-done(((bf16[256,1536]{1,0:T(8,128)(2,1)}), bf16[1024,1536]{1,0:T(8,128)(2,1)}) %all-gather.7.cloned.1.call-update) | async-done | bytes 3145744 | tf_op jit(solution)/shard_map/all_gather | solution.py:654
  103.9 3.2 fusion.31
  118.0 3.6 convolution_convert_fusion.2
  126.1 34.2 %collective-permute-done.6 = bf16[1024,1536]{1,0:T(8,128)(2,1)} collective-permute-done((bf16[1024,1536]{1,0:T(8,128)(2,1)}, bf16[1024,1536]{1,0:T(8,128)(2,1)}, u32[]{:S(2)}, u32[]{:S(2)}) %collective-permute-start.6) | collective-permute-done | bytes 3145760 | tf_op jit(solution)/shard_map/ppermute | solution.py:57
  162.6 12.7 %multiply_add_fusion.pre_ref = f32[1024,1536]{1,0:T(8,128)} fusion(f32[1024,1536]{1,0:T(8,128)S(1)} %fusion.67, bf16[2048,1536]{1,0:T(8,128)(2,1)S(1)} %constant_dynamic-update-slice_fusion.12, bf16[256,2048]{1,0:T(8,128)(2,1)} %collective-permute-done.2, bf16[256,2048]{1,0:T(8,128)(2,1)} %collective-permute-done.1, ...), kind=kOutput, calls=%fused_computation | convolution fusion | flops 6462373888 | bytes 23068672 | tf_op jit(solution)/shard_map/dot_general | solution.py:26
  175.3 2.6 multiply_reduce_fusion.1
  186.5 2.7 slice.350
  189.2 2.7 collective-permute-start.11
  192.0 7.3 collective-permute-done.8
  203.2 5.3 rope_forward.1
  213.8 5.7 collective-permute-start.13
  225.7 4.2 collective-permute-start.12
  229.8 22.0 %collective-permute-done.9 = bf16[1024,512]{1,0:T(8,128)(2,1)} collective-permute-done((bf16[1024,512]{1,0:T(8,128)(2,1)}, bf16[1024,512]{1,0:T(8,128)(2,1)}, u32[]{:S(2)}, u32[]{:S(2)}) %collective-permute-start.9) | collective-permute-done | bytes 1048608 | tf_op jit(solution)/shard_map/ppermute | solution.py:60
  251.8 11.2 %collective-permute-start.10 = (bf16[1024,512]{1,0:T(8,128)(2,1)}, bf16[1024,512]{1,0:T(8,128)(2,1)}, u32[]{:S(2)}, u32[]{:S(2)}) collective-permute-start(bf16[1024,512]{1,0:T(8,128)(2,1)} %collective-permute-done.9), channel_id=1, source_target_pairs={{0,8},{8,16},{16,24},{1,9},{9,17},{17,25},{2,10},{10,18},{18,26},{... | collective-permute-start | bytes 3145736 | tf_op jit(solution)/shard_map/ppermute | solution.py:60
  268.7 28.1 %collective-permute-done.12 = bf16[1024,512]{1,0:T(8,128)(2,1)} collective-permute-done((bf16[1024,512]{1,0:T(8,128)(2,1)}, bf16[1024,512]{1,0:T(8,128)(2,1)}, u32[]{:S(2)}, u32[]{:S(2)}) %collective-permute-start.12) | collective-permute-done | bytes 1048608 | tf_op jit(solution)/shard_map/ppermute | solution.py:60
  296.8 44.8 %collective-permute-done.10 = bf16[1024,512]{1,0:T(8,128)(2,1)} collective-permute-done((bf16[1024,512]{1,0:T(8,128)(2,1)}, bf16[1024,512]{1,0:T(8,128)(2,1)}, u32[]{:S(2)}, u32[]{:S(2)}) %collective-permute-start.10) | collective-permute-done | bytes 1048608 | tf_op jit(solution)/shard_map/ppermute | solution.py:60
  344.0 23.2 %attend_forward.1 = (bf16[2,2,256,512]{3,2,1,0:T(8,128)(2,1)S(1)}, f32[8,512,1]{2,1,0:T(8,128)}) custom-call(bf16[2,2,256,512]{3,2,1,0:T(8,128)(2,1)S(1)} %bitcast.276, bf16[2,2,256,512]{3,2,1,0:T(8,128)(2,1)S(1)} %bitcast.272, bf16[2,2,256,512]{3,2,1,0:T(8,128)(2,1)} %bitcast.19.refs_1_, bf16[2,2,256,512]{3,2,1,0:T(8,128)(2,1)} %bitcast.20.refs_2_.refs_0_, ...), custom_call_target="tpu_custom_call" | custom-call | flops 25300000768 | bytes 23000000 | tf_op jit(solution)/shard_map/attend_forward/pallas_call | solution.py:480
  376.2 2.9 add_convert_fusion.8
  380.6 2.8 fusion.74
  389.9 14.7 %collective-permute-done.18.refs_2_ = bf16[256,2048]{1,0:T(8,128)(2,1)} collective-permute-done((bf16[256,2048]{1,0:T(8,128)(2,1)}, bf16[256,2048]{1,0:T(8,128)(2,1)}, u32[]{:S(2)}, u32[]{:S(2)}) %collective-permute-start.18) | collective-permute-done | bytes 1048608 | tf_op jit(solution)/shard_map/ppermute | solution.py:51
  405.9 4.6 after_attention.1
  413.9 20.6 %all-gather.15.cloned.1.call-done.refs_0_.d0_ref = bf16[512,2048]{1,0:T(8,128)(2,1)} async-done(((bf16[128,2048]{1,0:T(8,128)(2,1)}), bf16[512,2048]{1,0:T(8,128)(2,1)}) %all-gather.15.cloned.1.call-update) | async-done | bytes 2097168 | tf_op jit(solution)/shard_map/all_gather | solution.py:654
  434.5 33.2 %collective-permute-done.29.u1_ref = bf16[1024,2048]{1,0:T(8,128)(2,1)} collective-permute-done((bf16[1024,2048]{1,0:T(8,128)(2,1)}, bf16[1024,2048]{1,0:T(8,128)(2,1)}, u32[]{:S(2)}, u32[]{:S(2)}) %collective-permute-start.29) | collective-permute-done | bytes 4194336 | tf_op jit(solution)/shard_map/ppermute | solution.py:57
  477.3 3.3 all-gather.17.cloned.1.call-done.refs_1_.d1_ref
  480.6 34.7 %collective-permute-done.30.refs_2_.d2_ref = bf16[512,2048]{1,0:T(8,128)(2,1)} collective-permute-done((bf16[512,2048]{1,0:T(8,128)(2,1)}, bf16[512,2048]{1,0:T(8,128)(2,1)}, u32[]{:S(2)}, u32[]{:S(2)}) %collective-permute-start.30) | collective-permute-done | bytes 2097184 | tf_op jit(solution)/shard_map/ppermute | solution.py:57
  517.0 26.3 %gate_up.1 = (bf16[1024,2048]{1,0:T(8,128)(2,1)S(1)}, bf16[1024,2048]{1,0:T(8,128)(2,1)}, bf16[1024,2048]{1,0:T(8,128)(2,1)}) custom-call(s32[3]{0:T(128)S(1)} %pad_add_fusion.4.spot_ref, bf16[1024,2048]{1,0:T(8,128)(2,1)} %copy-done.51, bf16[1024,2048]{1,0:T(8,128)(2,1)} %all-gather.11.cloned.1.call-done.g0_ref, ...), custom_call_target="tpu_custom_call" | custom-call | flops 28600000512 | bytes 26000000 | tf_op jit(solution)/shard_map/gate_up/pallas_call | solution.py:178
  545.3 16.6 %collective-permute-done.31.refs_3_.d3_ref = bf16[512,2048]{1,0:T(8,128)(2,1)S(1)} collective-permute-done((bf16[512,2048]{1,0:T(8,128)(2,1)}, bf16[512,2048]{1,0:T(8,128)(2,1)S(1)}, u32[]{:S(2)}, u32[]{:S(2)}) %collective-permute-start.31) | collective-permute-done | bytes 2097184 | tf_op jit(solution)/shard_map/ppermute | solution.py:57
  563.3 10.3 %down.2 = (bf16[512,2048]{1,0:T(8,128)(2,1)S(1)}, bf16[512,16]{1,0:T(8,128)(2,1)S(1)}) custom-call(bf16[1024,2048]{1,0:T(8,128)(2,1)} %get-tuple-element.93.gated_ref, bf16[512,2048]{1,0:T(8,128)(2,1)S(1)} %copy-done.14, bf16[512,2048]{1,0:T(8,128)(2,1)} %all-gather.17.cloned.1.call-done.refs_1_.d1_ref, ...), custom_call_target="tpu_custom_call" | custom-call | flops 11000000512 | bytes 10000000 | tf_op jit(solution)/shard_map/down/pallas_call | solution.py:217
  573.8 2.6 collective-permute-done.32
  578.6 10.3 %down.3 = (bf16[512,2048]{1,0:T(8,128)(2,1)S(1)}, bf16[512,16]{1,0:T(8,128)(2,1)S(1)}) custom-call(bf16[1024,2048]{1,0:T(8,128)(2,1)} %get-tuple-element.93.gated_ref, bf16[512,2048]{1,0:T(8,128)(2,1)S(1)} %copy-done.14, bf16[512,2048]{1,0:T(8,128)(2,1)} %all-gather.17.cloned.1.call-done.refs_1_.d1_ref, ...), custom_call_target="tpu_custom_call" | custom-call | flops 11000000512 | bytes 10000000 | tf_op jit(solution)/shard_map/down/pallas_call | solution.py:217
  589.2 13.0 %collective-permute-done.34.refs_2_ = bf16[256,2048]{1,0:T(8,128)(2,1)S(1)} collective-permute-done((bf16[256,2048]{1,0:T(8,128)(2,1)S(1)}, bf16[256,2048]{1,0:T(8,128)(2,1)S(1)}, u32[]{:S(2)}, u32[]{:S(2)}) %collective-permute-start.34) | collective-permute-done | bytes 1048608 | tf_op jit(solution)/shard_map/ppermute | solution.py:51
  602.1 4.4 after_feed.1
  609.4 26.2 %feed_backward.2 = (bf16[512,2048]{1,0:T(8,128)(2,1)S(1)}, bf16[512,32]{1,0:T(8,128)(2,1)S(1)}, f32[3,16,2048]{2,1,0:T(8,128)S(1)}) custom-call(s32[3]{0:T(128)S(1)} %pad_add_fusion.4.spot_ref, bf16[512,2048]{1,0:T(8,128)(2,1)S(1)} %pad_maximum_fusion.3.grad_ref, bf16[512,2048]{1,0:T(8,128)(2,1)} %all-gather.15.cloned.1.call-done.refs_0_.d0_ref, ...), custom_call_target="tpu_custom_call" | custom-call | flops 26400000000 | bytes 24000000 | tf_op jit(solution)/shard_map/feed_backward/pallas_call | solution.py:308
  635.9 2.5 collective-permute-done.38
  638.6 26.5 %feed_backward.3 = (bf16[512,2048]{1,0:T(8,128)(2,1)S(1)}, bf16[512,32]{1,0:T(8,128)(2,1)S(1)}, f32[3,16,2048]{2,1,0:T(8,128)S(1)}) custom-call(s32[3]{0:T(128)S(1)} %pad_add_fusion.4.spot_ref, bf16[512,2048]{1,0:T(8,128)(2,1)S(1)} %pad_maximum_fusion.4.grad_ref, bf16[512,2048]{1,0:T(8,128)(2,1)} %all-gather.15.cloned.1.call-done.refs_0_.d0_ref, ...), custom_call_target="tpu_custom_call" | custom-call | flops 26400000000 | bytes 24000000 | tf_op jit(solution)/shard_map/feed_backward/pallas_call | solution.py:308
  671.5 3.0 convolution_multiply_fusion.1
  677.5 17.4 %collective-permute-done.40.refs_2_ = bf16[256,2048]{1,0:T(8,128)(2,1)} collective-permute-done((bf16[256,2048]{1,0:T(8,128)(2,1)}, bf16[256,2048]{1,0:T(8,128)(2,1)}, u32[]{:S(2)}, u32[]{:S(2)}) %collective-permute-start.40) | collective-permute-done | bytes 1048608 | tf_op jit(solution)/shard_map/ppermute | solution.py:51
  696.1 5.0 middle.1
  705.1 3.7 collective-permute-done.65
  709.7 15.9 %collective-permute-start.68 = (f32[48,2,128]{2,1,0:T(2,128)}, f32[48,2,128]{2,1,0:T(2,128)}, u32[]{:S(2)}, u32[]{:S(2)}) collective-permute-start(f32[48,2,128]{2,1,0:T(2,128)} %bitcast.101), channel_id=1, source_target_pairs={{0,24},{8,0},{16,8},{24,16},{1,25},{9,1},{17,9},{25,17},{2,26},{10... | collective-permute-start | bytes 147464 | tf_op jit(solution)/shard_map/ppermute | solution.py:63
  728.2 3.6 collective-permute-done.66
  743.1 5.8 add_convert_fusion.5
  749.0 12.4 %attend_backward.2 = (f32[2,2,256,512]{3,2,1,0:T(8,128)}, bf16[2,2,256,512]{3,2,1,0:T(8,128)(2,1)}, bf16[2,2,256,512]{3,2,1,0:T(8,128)(2,1)}) custom-call(bf16[2,2,256,512]{3,2,1,0:T(8,128)(2,1)S(1)} %bitcast.277, bf16[2,2,256,512]{3,2,1,0:T(8,128)(2,1)S(1)} %bitcast.279, bf16[2,2,256,512]{3,2,1,0:T(8,128)(2,1)S(1)} %copy-done.3, ...), custom_call_target="tpu_custom_call" | custom-call | flops 13200000000 | bytes 12000000 | tf_op jit(solution)/shard_map/attend_backward/pallas_call | solution.py:498
  771.3 19.9 %attend_backward.3 = (f32[2,2,256,512]{3,2,1,0:T(8,128)}, f32[2,2,256,512]{3,2,1,0:T(8,128)}, bf16[2,2,256,512]{3,2,1,0:T(8,128)(2,1)S(1)}, f32[2,2,256,512]{3,2,1,0:T(8,128)}, bf16[2,2,256,512]{3,2,1,0:T(8,128)(2,1)S(1)}) custom-call(bf16[2,2,256,512]{3,2,1,0:T(8,128)(2,1)S(1)} %bitcast.278, bf16[2,2,256,512]{3,2,1,0:T(8,128)(2,1)S(1)} %bitcast.280, ...), custom_call_target="tpu_custom_call" | custom-call | flops 22000001024 | bytes 20000000 | tf_op jit(solution)/shard_map/attend_backward/pallas_call | solution.py:498
  792.5 9.9 %collective-permute-start.61 = (f32[80,128]{0,1:T(8,128)S(1)}, f32[80,128]{0,1:T(8,128)S(1)}, u32[]{:S(2)}, u32[]{:S(2)}) collective-permute-start(f32[80,128]{0,1:T(8,128)S(1)} %get-tuple-element.154), channel_id=1, source_target_pairs={{0,8},{8,16},{16,24},{24,0},{1,9},{9,17},{17,25},{25,1},{2,10},{10... | collective-permute-start | bytes 122888 | tf_op jit(solution)/shard_map/ppermute | solution.py:63
  802.4 4.8 collective-permute-start.63
  810.5 12.9 %collective-permute-done.61 = f32[80,128]{0,1:T(8,128)S(1)} collective-permute-done((f32[80,128]{0,1:T(8,128)S(1)}, f32[80,128]{0,1:T(8,128)S(1)}, u32[]{:S(2)}, u32[]{:S(2)}) %collective-permute-start.61) | collective-permute-done | bytes 40992 | tf_op jit(solution)/shard_map/ppermute | solution.py:63
  823.4 2.5 collective-permute-done.62
  830.7 14.5 %collective-permute-done.45 = bf16[1024,512]{1,0:T(8,128)(2,1)S(1)} collective-permute-done((bf16[1024,512]{1,0:T(8,128)(2,1)S(1)}, bf16[1024,512]{1,0:T(8,128)(2,1)S(1)}, u32[]{:S(2)}, u32[]{:S(2)}) %collective-permute-start.45) | collective-permute-done | bytes 1048608 | tf_op jit(solution)/shard_map/ppermute | solution.py:60
  846.8 7.9 rope_backward.1
  854.8 12.6 %collective-permute-done.49 = bf16[1024,512]{1,0:T(8,128)(2,1)} collective-permute-done((bf16[1024,512]{1,0:T(8,128)(2,1)S(1)}, bf16[1024,512]{1,0:T(8,128)(2,1)}, u32[]{:S(2)}, u32[]{:S(2)}) %collective-permute-start.49) | collective-permute-done | bytes 1048608 | tf_op jit(solution)/shard_map/ppermute | solution.py:60
  872.8 12.9 %collective-permute-done.47 = f32[2,1024]{0,1:T(8,128)S(1)} collective-permute-done((f32[2,1024]{0,1:T(8,128)S(1)}, f32[2,1024]{0,1:T(8,128)S(1)}, u32[]{:S(2)}, u32[]{:S(2)}) %collective-permute-start.47) | collective-permute-done | bytes 8224 | tf_op jit(solution)/shard_map/ppermute | solution.py:51
  886.8 3.9 subtract_convert_fusion.1
  893.0 2.9 convolution_convert_fusion.1
  896.0 2.8 fusion.27
  898.8 3.9 convolution_multiply_fusion
  907.0 7.2 add_convert_fusion.1
  929.5 3.9 collective-permute-start.55
  942.8 6.4 add_convert_fusion.refs_0_
  955.4 11.4 %collective-permute-done.52.refs_2_ = bf16[256,2048]{1,0:T(8,128)(2,1)S(1)} collective-permute-done((bf16[256,2048]{1,0:T(8,128)(2,1)S(1)}, bf16[256,2048]{1,0:T(8,128)(2,1)S(1)}, u32[]{:S(2)}, u32[]{:S(2)}) %collective-permute-start.52) | collective-permute-done | bytes 1048608 | tf_op jit(solution)/shard_map/ppermute | solution.py:51
  969.8 3.9 end.1
  (506 shorter events, 211.2 us)
Async XLA Ops:
  7.2 82.9 %all-gather.7.cloned.1.call-start = ((), (), s32[]{:S(2)}) async-start(), calls=%async_computation | async-start | bytes 3932160 | tf_op jit(solution)/shard_map/all_gather | solution.py:654
  11.6 8.3 collective-permute-start.4
  14.1 9.4 collective-permute-start.5
  25.1 185.7 %all-gather.9.cloned.1.call-start = ((), (), s32[]{:S(2)}) async-start(), calls=%async_computation.1 | async-start | bytes 1310720 | tf_op jit(solution)/shard_map/all_gather | solution.py:654
  27.9 70.1 %collective-permute-start.1 = (bf16[256,2048]{1,0:T(8,128)(2,1)}, bf16[256,2048]{1,0:T(8,128)(2,1)}, u32[]{:S(2)}, u32[]{:S(2)}) collective-permute-start(bf16[256,2048]{1,0:T(8,128)(2,1)} %fold.1), channel_id=1, source_target_pairs={{0,4},{4,0},{1,5},{5,1},{2,6},{6,2},{3,7},{7,3},{8,12},{12,8},{9,1... | collective-permute-start | bytes 3145736 | tf_op jit(solution)/shard_map/ppermute | solution.py:51
  29.5 88.5 %collective-permute-start = (bf16[256,2048]{1,0:T(8,128)(2,1)}, bf16[256,2048]{1,0:T(8,128)(2,1)}, u32[]{:S(2)}, u32[]{:S(2)}) collective-permute-start(bf16[256,2048]{1,0:T(8,128)(2,1)} %fold.1), channel_id=1, source_target_pairs={{0,1},{1,0},{2,3},{3,2},{4,5},{5,4},{6,7},{7,6},{8,9},{9,8},{10,11... | collective-permute-start | bytes 3145736 | tf_op jit(solution)/shard_map/ppermute | solution.py:48
  90.1 176.7 %all-gather.11.cloned.1.call-start = ((), (), s32[]{:S(2)}) async-start(), calls=%async_computation.2 | async-start | bytes 5242880 | tf_op jit(solution)/shard_map/all_gather | solution.py:654
  90.1 70.2 %collective-permute-start.6 = (bf16[1024,1536]{1,0:T(8,128)(2,1)}, bf16[1024,1536]{1,0:T(8,128)(2,1)}, u32[]{:S(2)}, u32[]{:S(2)}) collective-permute-start(bf16[1024,1536]{1,0:T(8,128)(2,1)} %all-gather.7.cloned.1.call-done), channel_id=1, source_target_pairs={{0,2},{2,0},{1,3},{3,1},{4,6},{6,4},{5,7},{7,5},{8,10},{10,8},{9,1... | collective-permute-start | bytes 9437192 | tf_op jit(solution)/shard_map/ppermute | solution.py:57
  94.0 9.7 collective-permute-start.23
  95.5 11.6 %collective-permute-start.24 = (bf16[64,2048]{1,0:T(8,128)(2,1)}, bf16[64,2048]{1,0:T(8,128)(2,1)S(1)}, u32[]{:S(2)}, u32[]{:S(2)}) collective-permute-start(bf16[64,2048]{1,0:T(8,128)(2,1)} %get-tuple-element.79), channel_id=1, source_target_pairs={{0,5},{1,4},{4,1},{5,0},{2,7},{3,6},{6,3},{7,2},{8,13},{9,12},{12,... | collective-permute-start | bytes 786440 | tf_op jit(solution)/shard_map/ppermute | solution.py:54
  98.0 20.0 %collective-permute-start.2 = (bf16[256,2048]{1,0:T(8,128)(2,1)}, bf16[256,2048]{1,0:T(8,128)(2,1)}, u32[]{:S(2)}, u32[]{:S(2)}) collective-permute-start(bf16[256,2048]{1,0:T(8,128)(2,1)} %collective-permute-done.1), channel_id=1, source_target_pairs={{0,1},{1,0},{2,3},{3,2},{4,5},{5,4},{6,7},{7,6},{8,9},{9,8},{10,11... | collective-permute-start | bytes 3145736 | tf_op jit(solution)/shard_map/ppermute | solution.py:48
  103.9 5.4 collective-permute-start.22
  107.8 103.1 %collective-permute-start.27 = (bf16[64,2048]{1,0:T(8,128)(2,1)S(1)}, bf16[64,2048]{1,0:T(8,128)(2,1)S(1)}, u32[]{:S(2)}, u32[]{:S(2)}) collective-permute-start(bf16[64,2048]{1,0:T(8,128)(2,1)S(1)} %get-tuple-element.84), channel_id=1, source_target_pairs={{0,4},{4,0},{1,5},{5,1},{2,6},{6,2},{3,7},{7,3},{8,12},{12,8},{9,1... | collective-permute-start | bytes 786440 | tf_op jit(solution)/shard_map/ppermute | solution.py:51
  109.2 103.2 %collective-permute-start.28 = (bf16[64,2048]{1,0:T(8,128)(2,1)S(1)}, bf16[64,2048]{1,0:T(8,128)(2,1)S(1)}, u32[]{:S(2)}, u32[]{:S(2)}) collective-permute-start(bf16[64,2048]{1,0:T(8,128)(2,1)S(1)} %get-tuple-element.85), channel_id=1, source_target_pairs={{0,5},{1,4},{4,1},{5,0},{2,7},{3,6},{6,3},{7,2},{8,13},{9,12},{12,... | collective-permute-start | bytes 786440 | tf_op jit(solution)/shard_map/ppermute | solution.py:54
  113.4 261.0 %all-gather.13.cloned.1.call-start = ((), (), s32[]{:S(2)}) async-start(), calls=%async_computation.3 | async-start | bytes 5242880 | tf_op jit(solution)/shard_map/all_gather | solution.py:654
  184.6 14.6 %collective-permute-start.8 = (f32[2,1024]{0,1:T(8,128)}, f32[2,1024]{0,1:T(8,128)}, u32[]{:S(2)}, u32[]{:S(2)}) collective-permute-start(f32[2,1024]{0,1:T(8,128)} %bitcast_add_fusion.5), channel_id=1, source_target_pairs={{0,4},{4,0},{1,5},{5,1},{2,6},{6,2},{3,7},{7,3},{8,12},{12,8},{9,1... | collective-permute-start | bytes 24584 | tf_op jit(solution)/shard_map/ppermute | solution.py:51
  186.3 27.5 %collective-permute-start.26 = (bf16[64,2048]{1,0:T(8,128)(2,1)S(1)}, bf16[64,2048]{1,0:T(8,128)(2,1)}, u32[]{:S(2)}, u32[]{:S(2)}) collective-permute-start(bf16[64,2048]{1,0:T(8,128)(2,1)S(1)} %get-tuple-element.83), channel_id=1, source_target_pairs={{0,1},{1,0},{2,3},{3,2},{4,5},{5,4},{6,7},{7,6},{8,9},{9,8},{10,11... | collective-permute-start | bytes 786440 | tf_op jit(solution)/shard_map/ppermute | solution.py:48
  189.2 36.4 %collective-permute-start.11 = (bf16[1024,512]{1,0:T(8,128)(2,1)}, bf16[1024,512]{1,0:T(8,128)(2,1)}, u32[]{:S(2)}, u32[]{:S(2)}) collective-permute-start(bf16[1024,512]{1,0:T(8,128)(2,1)} %slice.350), channel_id=1, source_target_pairs={{0,8},{8,16},{16,24},{1,9},{9,17},{17,25},{2,10},{10,18},{18,26},{... | collective-permute-start | bytes 3145736 | tf_op jit(solution)/shard_map/ppermute | solution.py:60
  208.5 43.3 %collective-permute-start.9 = (bf16[1024,512]{1,0:T(8,128)(2,1)}, bf16[1024,512]{1,0:T(8,128)(2,1)}, u32[]{:S(2)}, u32[]{:S(2)}) collective-permute-start(bf16[1024,512]{1,0:T(8,128)(2,1)} %get-tuple-element.70), channel_id=1, source_target_pairs={{0,8},{8,16},{16,24},{1,9},{9,17},{17,25},{2,10},{10,18},{18,26},{... | collective-permute-start | bytes 3145736 | tf_op jit(solution)/shard_map/ppermute | solution.py:60
  210.8 52.6 %collective-permute-start.15 = (bf16[256,2048]{1,0:T(8,128)(2,1)}, bf16[256,2048]{1,0:T(8,128)(2,1)}, u32[]{:S(2)}, u32[]{:S(2)}) collective-permute-start(bf16[256,2048]{1,0:T(8,128)(2,1)} %all-gather.9.cloned.1.call-done), channel_id=1, source_target_pairs={{1,2},{2,1},{5,6},{6,5},{9,10},{10,9},{13,14},{14,13},{17,18},{18,... | collective-permute-start | bytes 3145736 | tf_op jit(solution)/shard_map/ppermute | solution.py:686
  212.5 51.0 %collective-permute-start.14 = (bf16[256,2048]{1,0:T(8,128)(2,1)}, bf16[256,2048]{1,0:T(8,128)(2,1)}, u32[]{:S(2)}, u32[]{:S(2)}) collective-permute-start(bf16[256,2048]{1,0:T(8,128)(2,1)} %all-gather.9.cloned.1.call-done), channel_id=1, source_target_pairs={{1,0},{2,3},{5,4},{6,7},{9,8},{10,11},{13,12},{14,15},{17,16},{18,... | collective-permute-start | bytes 3145736 | tf_op jit(solution)/shard_map/ppermute | solution.py:686
  213.8 49.7 %collective-permute-start.13 = (bf16[256,2048]{1,0:T(8,128)(2,1)}, bf16[256,2048]{1,0:T(8,128)(2,1)}, u32[]{:S(2)}, u32[]{:S(2)}) collective-permute-start(bf16[256,2048]{1,0:T(8,128)(2,1)} %all-gather.9.cloned.1.call-done), channel_id=1, source_target_pairs={{0,2},{3,1},{4,6},{7,5},{8,10},{11,9},{12,14},{15,13},{16,18},{19,... | collective-permute-start | bytes 3145736 | tf_op jit(solution)/shard_map/ppermute | solution.py:686
  223.6 210.9 %all-gather.15.cloned.1.call-start = ((), (), s32[]{:S(2)}) async-start(), calls=%async_computation.4 | async-start | bytes 2621440 | tf_op jit(solution)/shard_map/all_gather | solution.py:654
  225.7 71.1 %collective-permute-start.12 = (bf16[1024,512]{1,0:T(8,128)(2,1)}, bf16[1024,512]{1,0:T(8,128)(2,1)}, u32[]{:S(2)}, u32[]{:S(2)}) collective-permute-start(bf16[1024,512]{1,0:T(8,128)(2,1)} %collective-permute-done.11), channel_id=1, source_target_pairs={{0,8},{8,16},{16,24},{1,9},{9,17},{17,25},{2,10},{10,18},{18,26},{... | collective-permute-start | bytes 3145736 | tf_op jit(solution)/shard_map/ppermute | solution.py:60
  251.8 89.8 %collective-permute-start.10 = (bf16[1024,512]{1,0:T(8,128)(2,1)}, bf16[1024,512]{1,0:T(8,128)(2,1)}, u32[]{:S(2)}, u32[]{:S(2)}) collective-permute-start(bf16[1024,512]{1,0:T(8,128)(2,1)} %collective-permute-done.9), channel_id=1, source_target_pairs={{0,8},{8,16},{16,24},{1,9},{9,17},{17,25},{2,10},{10,18},{18,26},{... | collective-permute-start | bytes 3145736 | tf_op jit(solution)/shard_map/ppermute | solution.py:60
  266.8 107.6 %collective-permute-start.25 = (bf16[1024,2048]{1,0:T(8,128)(2,1)}, bf16[1024,2048]{1,0:T(8,128)(2,1)}, u32[]{:S(2)}, u32[]{:S(2)}) collective-permute-start(bf16[1024,2048]{1,0:T(8,128)(2,1)} %all-gather.11.cloned.1.call-done.g0_ref), channel_id=1, source_target_pairs={{0,2},{2,0},{1,3},{3,1},{4,6},{6,4},{5,7},{7,5},{8,10},{10,8},{9,1... | collective-permute-start | bytes 12582920 | tf_op jit(solution)/shard_map/ppermute | solution.py:57
  374.1 106.5 %all-gather.17.cloned.1.call-start = ((), (), s32[]{:S(2)}) async-start(), calls=%async_computation.5 | async-start | bytes 2621440 | tf_op jit(solution)/shard_map/all_gather | solution.py:654
  374.4 93.4 %collective-permute-start.29 = (bf16[1024,2048]{1,0:T(8,128)(2,1)}, bf16[1024,2048]{1,0:T(8,128)(2,1)}, u32[]{:S(2)}, u32[]{:S(2)}) collective-permute-start(bf16[1024,2048]{1,0:T(8,128)(2,1)} %all-gather.13.cloned.1.call-done.u0_ref), channel_id=1, source_target_pairs={{0,2},{2,0},{1,3},{3,1},{4,6},{6,4},{5,7},{7,5},{8,10},{10,8},{9,1... | collective-permute-start | bytes 12582920 | tf_op jit(solution)/shard_map/ppermute | solution.py:57
  379.1 25.6 %collective-permute-start.18 = (bf16[256,2048]{1,0:T(8,128)(2,1)}, bf16[256,2048]{1,0:T(8,128)(2,1)}, u32[]{:S(2)}, u32[]{:S(2)}) collective-permute-start(bf16[256,2048]{1,0:T(8,128)(2,1)} %add_convert_fusion.8), channel_id=1, source_target_pairs={{0,4},{4,0},{1,5},{5,1},{2,6},{6,2},{3,7},{7,3},{8,12},{12,8},{9,1... | collective-permute-start | bytes 3145736 | tf_op jit(solution)/shard_map/ppermute | solution.py:51
  387.4 17.2 %collective-permute-start.17 = (bf16[256,2048]{1,0:T(8,128)(2,1)}, bf16[256,2048]{1,0:T(8,128)(2,1)}, u32[]{:S(2)}, u32[]{:S(2)}) collective-permute-start(bf16[256,2048]{1,0:T(8,128)(2,1)} %slice.277), channel_id=1, source_target_pairs={{0,1},{1,0},{2,3},{3,2},{4,5},{5,4},{6,7},{7,6},{8,9},{9,8},{10,11... | collective-permute-start | bytes 3145736 | tf_op jit(solution)/shard_map/ppermute | solution.py:48
  410.5 60.8 %collective-permute-start.20 = (bf16[256,2048]{1,0:T(8,128)(2,1)S(1)}, bf16[256,2048]{1,0:T(8,128)(2,1)S(1)}, u32[]{:S(2)}, u32[]{:S(2)}) collective-permute-start(bf16[256,2048]{1,0:T(8,128)(2,1)S(1)} %get-tuple-element.74), channel_id=1, source_target_pairs={{0,4},{4,0},{1,5},{5,1},{2,6},{6,2},{3,7},{7,3},{8,12},{12,8},{9,1... | collective-permute-start | bytes 3145736 | tf_op jit(solution)/shard_map/ppermute | solution.py:51
  413.9 58.4 %collective-permute-start.19 = (bf16[256,2048]{1,0:T(8,128)(2,1)S(1)}, bf16[256,2048]{1,0:T(8,128)(2,1)}, u32[]{:S(2)}, u32[]{:S(2)}) collective-permute-start(bf16[256,2048]{1,0:T(8,128)(2,1)S(1)} %get-tuple-element.74), channel_id=1, source_target_pairs={{0,1},{1,0},{2,3},{3,2},{4,5},{5,4},{6,7},{7,6},{8,9},{9,8},{10,11... | collective-permute-start | bytes 3145736 | tf_op jit(solution)/shard_map/ppermute | solution.py:48
  467.7 47.6 %collective-permute-start.30 = (bf16[512,2048]{1,0:T(8,128)(2,1)}, bf16[512,2048]{1,0:T(8,128)(2,1)}, u32[]{:S(2)}, u32[]{:S(2)}) collective-permute-start(bf16[512,2048]{1,0:T(8,128)(2,1)} %all-gather.15.cloned.1.call-done.refs_0_.d0_ref), channel_id=1, source_target_pairs={{0,2},{2,0},{1,3},{3,1},{4,6},{6,4},{5,7},{7,5},{8,10},{10,8},{9,1... | collective-permute-start | bytes 6291464 | tf_op jit(solution)/shard_map/ppermute | solution.py:57
  515.3 46.6 %collective-permute-start.31 = (bf16[512,2048]{1,0:T(8,128)(2,1)}, bf16[512,2048]{1,0:T(8,128)(2,1)S(1)}, u32[]{:S(2)}, u32[]{:S(2)}) collective-permute-start(bf16[512,2048]{1,0:T(8,128)(2,1)} %all-gather.17.cloned.1.call-done.refs_1_.d1_ref), channel_id=1, source_target_pairs={{0,2},{2,0},{1,3},{3,1},{4,6},{6,4},{5,7},{7,5},{8,10},{10,8},{9,1... | collective-permute-start | bytes 6291464 | tf_op jit(solution)/shard_map/ppermute | solution.py:57
  576.9 25.3 %collective-permute-start.34 = (bf16[256,2048]{1,0:T(8,128)(2,1)S(1)}, bf16[256,2048]{1,0:T(8,128)(2,1)S(1)}, u32[]{:S(2)}, u32[]{:S(2)}) collective-permute-start(bf16[256,2048]{1,0:T(8,128)(2,1)S(1)} %add_convert_fusion.7), channel_id=1, source_target_pairs={{0,4},{4,0},{1,5},{5,1},{2,6},{6,2},{3,7},{7,3},{8,12},{12,8},{9,1... | collective-permute-start | bytes 3145736 | tf_op jit(solution)/shard_map/ppermute | solution.py:51
  589.1 13.0 %collective-permute-start.33 = (bf16[256,2048]{1,0:T(8,128)(2,1)S(1)}, bf16[256,2048]{1,0:T(8,128)(2,1)S(1)}, u32[]{:S(2)}, u32[]{:S(2)}) collective-permute-start(bf16[256,2048]{1,0:T(8,128)(2,1)S(1)} %slice.236), channel_id=1, source_target_pairs={{0,1},{1,0},{2,3},{3,2},{4,5},{5,4},{6,7},{7,6},{8,9},{9,8},{10,11... | collective-permute-start | bytes 3145736 | tf_op jit(solution)/shard_map/ppermute | solution.py:48
  606.6 29.1 %collective-permute-start.37 = (bf16[256,2048]{1,0:T(8,128)(2,1)S(1)}, bf16[256,2048]{1,0:T(8,128)(2,1)S(1)}, u32[]{:S(2)}, u32[]{:S(2)}) collective-permute-start(bf16[256,2048]{1,0:T(8,128)(2,1)S(1)} %get-tuple-element.97), channel_id=1, source_target_pairs={{0,4},{4,0},{1,5},{5,1},{2,6},{6,2},{3,7},{7,3},{8,12},{12,8},{9,1... | collective-permute-start | bytes 3145736 | tf_op jit(solution)/shard_map/ppermute | solution.py:51
  666.6 11.0 %collective-permute-start.36 = (bf16[256,2048]{1,0:T(8,128)(2,1)}, bf16[256,2048]{1,0:T(8,128)(2,1)}, u32[]{:S(2)}, u32[]{:S(2)}) collective-permute-start(bf16[256,2048]{1,0:T(8,128)(2,1)} %slice.238), channel_id=1, source_target_pairs={{0,1},{1,0},{2,3},{3,2},{4,5},{5,4},{6,7},{7,6},{8,9},{9,8},{10,11... | collective-permute-start | bytes 3145736 | tf_op jit(solution)/shard_map/ppermute | solution.py:48
  669.3 25.5 %collective-permute-start.40 = (bf16[256,2048]{1,0:T(8,128)(2,1)}, bf16[256,2048]{1,0:T(8,128)(2,1)}, u32[]{:S(2)}, u32[]{:S(2)}) collective-permute-start(bf16[256,2048]{1,0:T(8,128)(2,1)} %add_convert_fusion.6), channel_id=1, source_target_pairs={{0,4},{4,0},{1,5},{5,1},{2,6},{6,2},{3,7},{7,3},{8,12},{12,8},{9,1... | collective-permute-start | bytes 3145736 | tf_op jit(solution)/shard_map/ppermute | solution.py:51
  701.1 27.0 %collective-permute-start.42 = (bf16[256,2048]{1,0:T(8,128)(2,1)S(1)}, bf16[256,2048]{1,0:T(8,128)(2,1)}, u32[]{:S(2)}, u32[]{:S(2)}) collective-permute-start(bf16[256,2048]{1,0:T(8,128)(2,1)S(1)} %get-tuple-element.104), channel_id=1, source_target_pairs={{0,4},{4,0},{1,5},{5,1},{2,6},{6,2},{3,7},{7,3},{8,12},{12,8},{9,1... | collective-permute-start | bytes 3145736 | tf_op jit(solution)/shard_map/ppermute | solution.py:51
  702.9 5.9 collective-permute-start.65
  705.1 28.6 %collective-permute-start.41 = (bf16[256,2048]{1,0:T(8,128)(2,1)S(1)}, bf16[256,2048]{1,0:T(8,128)(2,1)S(1)}, u32[]{:S(2)}, u32[]{:S(2)}) collective-permute-start(bf16[256,2048]{1,0:T(8,128)(2,1)S(1)} %get-tuple-element.104), channel_id=1, source_target_pairs={{0,1},{1,0},{2,3},{3,2},{4,5},{5,4},{6,7},{7,6},{8,9},{9,8},{10,11... | collective-permute-start | bytes 3145736 | tf_op jit(solution)/shard_map/ppermute | solution.py:48
  709.7 18.5 %collective-permute-start.68 = (f32[48,2,128]{2,1,0:T(2,128)}, f32[48,2,128]{2,1,0:T(2,128)}, u32[]{:S(2)}, u32[]{:S(2)}) collective-permute-start(f32[48,2,128]{2,1,0:T(2,128)} %bitcast.101), channel_id=1, source_target_pairs={{0,24},{8,0},{16,8},{24,16},{1,25},{9,1},{17,9},{25,17},{2,26},{10... | collective-permute-start | bytes 147464 | tf_op jit(solution)/shard_map/ppermute | solution.py:63
  725.6 6.2 collective-permute-start.66
  725.6 6.2 collective-permute-start.67
  728.1 7.0 collective-permute-start.43
  742.1 21.9 %collective-permute-start.59 = (f32[80,2,4,128]{3,1,2,0:T(2,128)S(1)}, f32[80,2,4,128]{3,1,2,0:T(2,128)S(1)}, u32[]{:S(2)}, u32[]{:S(2)}) collective-permute-start(f32[80,2,4,128]{3,1,2,0:T(2,128)S(1)} %pad_maximum_fusion.9), channel_id=1, source_target_pairs={{0,4},{4,0},{1,5},{5,1},{2,6},{6,2},{3,7},{7,3},{8,12},{12,8},{9,1... | collective-permute-start | bytes 983048 | tf_op jit(solution)/shard_map/ppermute | solution.py:51
  761.4 46.3 %collective-permute-start.44 = (bf16[1024,512]{1,0:T(8,128)(2,1)}, bf16[1024,512]{1,0:T(8,128)(2,1)}, u32[]{:S(2)}, u32[]{:S(2)}) collective-permute-start(bf16[1024,512]{1,0:T(8,128)(2,1)} %bitcast.52), channel_id=1, source_target_pairs={{8,0},{16,8},{24,16},{9,1},{17,9},{25,17},{10,2},{18,10},{26,18},{... | collective-permute-start | bytes 3145736 | tf_op jit(solution)/shard_map/ppermute | solution.py:60
  762.7 65.1 %collective-permute-start.48 = (bf16[1024,512]{1,0:T(8,128)(2,1)}, bf16[1024,512]{1,0:T(8,128)(2,1)}, u32[]{:S(2)}, u32[]{:S(2)}) collective-permute-start(bf16[1024,512]{1,0:T(8,128)(2,1)} %bitcast.61), channel_id=1, source_target_pairs={{8,0},{16,8},{24,16},{9,1},{17,9},{25,17},{10,2},{18,10},{26,18},{... | collective-permute-start | bytes 3145736 | tf_op jit(solution)/shard_map/ppermute | solution.py:60
  765.4 26.0 %collective-permute-start.60 = (f32[80,4,128]{0,2,1:T(8,128)}, f32[80,4,128]{0,2,1:T(8,128)}, u32[]{:S(2)}, u32[]{:S(2)}) collective-permute-start(f32[80,4,128]{0,2,1:T(8,128)} %bitcast.86), channel_id=1, source_target_pairs={{0,2},{2,0},{1,3},{3,1},{4,6},{6,4},{5,7},{7,5},{8,10},{10,8},{9,1... | collective-permute-start | bytes 491528 | tf_op jit(solution)/shard_map/ppermute | solution.py:57
  792.5 30.9 %collective-permute-start.61 = (f32[80,128]{0,1:T(8,128)S(1)}, f32[80,128]{0,1:T(8,128)S(1)}, u32[]{:S(2)}, u32[]{:S(2)}) collective-permute-start(f32[80,128]{0,1:T(8,128)S(1)} %get-tuple-element.154), channel_id=1, source_target_pairs={{0,8},{8,16},{16,24},{24,0},{1,9},{9,17},{17,25},{25,1},{2,10},{10... | collective-permute-start | bytes 122888 | tf_op jit(solution)/shard_map/ppermute | solution.py:63
  802.4 21.0 %collective-permute-start.63 = (f32[80,128]{0,1:T(8,128)S(1)}, f32[80,128]{0,1:T(8,128)S(1)}, u32[]{:S(2)}, u32[]{:S(2)}) collective-permute-start(f32[80,128]{0,1:T(8,128)S(1)} %get-tuple-element.155), channel_id=1, source_target_pairs={{0,24},{8,0},{16,8},{24,16},{1,25},{9,1},{17,9},{25,17},{2,26},{10... | collective-permute-start | bytes 122888 | tf_op jit(solution)/shard_map/ppermute | solution.py:63
  807.2 18.7 %collective-permute-start.62 = (f32[80,128]{0,1:T(8,128)S(1)}, f32[80,128]{0,1:T(8,128)S(1)}, u32[]{:S(2)}, u32[]{:S(2)}) collective-permute-start(f32[80,128]{0,1:T(8,128)S(1)} %get-tuple-element.156), channel_id=1, source_target_pairs={{0,16},{8,24},{16,0},{24,8},{1,17},{9,25},{17,1},{25,9},{2,18},{10... | collective-permute-start | bytes 122888 | tf_op jit(solution)/shard_map/ppermute | solution.py:63
  809.2 36.0 %collective-permute-start.45 = (bf16[1024,512]{1,0:T(8,128)(2,1)S(1)}, bf16[1024,512]{1,0:T(8,128)(2,1)S(1)}, u32[]{:S(2)}, u32[]{:S(2)}) collective-permute-start(bf16[1024,512]{1,0:T(8,128)(2,1)S(1)} %fusion.12), channel_id=1, source_target_pairs={{8,0},{16,8},{24,16},{9,1},{17,9},{25,17},{10,2},{18,10},{26,18},{... | collective-permute-start | bytes 3145736 | tf_op jit(solution)/shard_map/ppermute | solution.py:60
  829.4 38.0 %collective-permute-start.49 = (bf16[1024,512]{1,0:T(8,128)(2,1)S(1)}, bf16[1024,512]{1,0:T(8,128)(2,1)}, u32[]{:S(2)}, u32[]{:S(2)}) collective-permute-start(bf16[1024,512]{1,0:T(8,128)(2,1)S(1)} %fusion.11), channel_id=1, source_target_pairs={{8,0},{16,8},{24,16},{9,1},{17,9},{25,17},{10,2},{18,10},{26,18},{... | collective-permute-start | bytes 3145736 | tf_op jit(solution)/shard_map/ppermute | solution.py:60
  854.7 14.4 %collective-permute-start.46 = (f32[2,1024]{0,1:T(8,128)}, f32[2,1024]{0,1:T(8,128)S(1)}, u32[]{:S(2)}, u32[]{:S(2)}) collective-permute-start(f32[2,1024]{0,1:T(8,128)} %bitcast.297), channel_id=1, source_target_pairs={{0,1},{1,0},{2,3},{3,2},{4,5},{5,4},{6,7},{7,6},{8,9},{9,8},{10,11... | collective-permute-start | bytes 24584 | tf_op jit(solution)/shard_map/ppermute | solution.py:48
  872.1 13.6 %collective-permute-start.47 = (f32[2,1024]{0,1:T(8,128)S(1)}, f32[2,1024]{0,1:T(8,128)S(1)}, u32[]{:S(2)}, u32[]{:S(2)}) collective-permute-start(f32[2,1024]{0,1:T(8,128)S(1)} %bitcast_add_fusion.3), channel_id=1, source_target_pairs={{0,4},{4,0},{1,5},{5,1},{2,6},{6,2},{3,7},{7,3},{8,12},{12,8},{9,1... | collective-permute-start | bytes 24584 | tf_op jit(solution)/shard_map/ppermute | solution.py:51
  906.5 10.1 %collective-permute-start.53 = (f32[96,2,4,128]{3,2,1,0:T(4,128)S(1)}, f32[96,2,4,128]{3,2,1,0:T(4,128)S(1)}, u32[]{:S(2)}, u32[]{:S(2)}) collective-permute-start(f32[96,2,4,128]{3,2,1,0:T(4,128)S(1)} %pad_maximum_fusion.7), channel_id=1, source_target_pairs={{0,4},{4,0},{1,5},{5,1},{2,6},{6,2},{3,7},{7,3},{8,12},{12,8},{9,1... | collective-permute-start | bytes 1179656 | tf_op jit(solution)/shard_map/ppermute | solution.py:51
  916.6 22.9 %collective-permute-start.50 = (bf16[256,2048]{1,0:T(8,128)(2,1)}, bf16[256,2048]{1,0:T(8,128)(2,1)}, u32[]{:S(2)}, u32[]{:S(2)}) collective-permute-start(bf16[256,2048]{1,0:T(8,128)(2,1)} %slice.290), channel_id=1, source_target_pairs={{0,1},{1,0},{2,3},{3,2},{4,5},{5,4},{6,7},{7,6},{8,9},{9,8},{10,11... | collective-permute-start | bytes 3145736 | tf_op jit(solution)/shard_map/ppermute | solution.py:48
  919.3 9.1 collective-permute-start.54
  929.5 7.0 collective-permute-start.55
  933.4 6.0 collective-permute-start.56
  939.4 12.4 %collective-permute-start.58 = (f32[96,64]{0,1:T(8,128)S(1)}, f32[96,64]{0,1:T(8,128)S(1)}, u32[]{:S(2)}, u32[]{:S(2)}) collective-permute-start(f32[96,64]{0,1:T(8,128)S(1)} %dynamic-slice_bitcast_fusion.16), channel_id=1, source_target_pairs={{0,1},{1,0},{2,3},{3,2},{4,5},{5,4},{6,7},{7,6},{8,9},{9,8},{10,11... | collective-permute-start | bytes 73736 | tf_op jit(solution)/shard_map/ppermute | solution.py:48
  941.2 25.6 %collective-permute-start.52 = (bf16[256,2048]{1,0:T(8,128)(2,1)S(1)}, bf16[256,2048]{1,0:T(8,128)(2,1)S(1)}, u32[]{:S(2)}, u32[]{:S(2)}) collective-permute-start(bf16[256,2048]{1,0:T(8,128)(2,1)S(1)} %add_convert_fusion.4), channel_id=1, source_target_pairs={{0,4},{4,0},{1,5},{5,1},{2,6},{6,2},{3,7},{7,3},{8,12},{12,8},{9,1... | collective-permute-start | bytes 3145736 | tf_op jit(solution)/shard_map/ppermute | solution.py:51
  (107 other events, 2582.0 us)
Sparse Core Ops, SparseCore 0:
  25.2 64.8 all-gather.6
  91.6 26.5 all-gather.8
  120.4 81.5 all-gather.10
  223.7 130.4 all-gather.12
  374.2 60.2 all-gather.14
  435.9 44.6 all-gather.16

commit v2 on v1

v2 whole, which is shorter than its diff:
```python
import functools

import jax
import jax.numpy as jnp
from jax import lax
from jax.experimental import pallas as pl
from jax.experimental.pallas import tpu as pltpu
from jax.sharding import Mesh
from jax.sharding import PartitionSpec as P

HD = 128
WINDOW = 1024
SCALE_ADAPT = 0.5
ROPE_BASE = 500000.0
EPS = 1e-06
BF = jnp.bfloat16
F32 = jnp.float32
VMEM_BYTES = 56 * 1024 * 1024


def cost(us):
    return pl.CostEstimate(flops=int(us * 1.1e9), bytes_accessed=int(us * 1e6), transcendentals=0)


def dot(a, b, dims=((1,), (0,))):
    return lax.dot_general(a, b, (dims, ((), ())), preferred_element_type=F32)


def dot_nt(a, b):
    return dot(a, b, ((1,), (1,)))


def dot_tn(a, b):
    return dot(a, b, ((0,), (0,)))


SWAP = [(0, 1), (1, 0)]


class Place:
    def __init__(self):
        self.np = lax.axis_size("p")
        self.p, self.x, self.y, self.c = (lax.axis_index(a) for a in ("p", "x", "y", "c"))
        self.quarter = 2 * self.x + self.c
        self.spot = jnp.stack([self.x, self.y, self.c]).astype(jnp.int32)

    def swap_core(self, value):
        return lax.ppermute(value, "c", SWAP)

    def swap_x(self, value):
        return lax.ppermute(value, "x", SWAP)

    def swap_both(self, value):
        return lax.ppermute(value, ("x", "c"), [(0, 3), (1, 2), (2, 1), (3, 0)])

    def swap_y(self, value):
        return lax.ppermute(value, "y", SWAP)

    def shift_p(self, value, by):
        return lax.ppermute(value, "p", [(p, p + by) for p in range(self.np) if 0 <= p + by < self.np])

    def turn_p(self, value, by):
        return lax.ppermute(value, "p", [(p, (p + by) % self.np) for p in range(self.np)])

    def gather4(self, own):
        across = self.swap_x(own)
        return self.paired(own), self.paired(across)

    def paired(self, block):
        return jnp.concatenate([block, self.swap_core(block)], axis=0)

    def gather8(self, own, work=None):
        half = own.shape[0] // 2
        across, over = self.swap_x(own), self.swap_y(own)
        first = self.paired(own)
        done = None
        if work is not None:
            done = work(first)
            across, over = after(across, done[0]), after(over, done[0])
        far = jnp.concatenate([self.swap_y(across[:half]), self.swap_x(over[half:])])
        return (first, self.paired(across), self.paired(over), self.paired(far)), done

    def met(self, pair):
        rows = pair.shape[0] // 2
        return (pair[:rows].astype(F32) + self.swap_core(pair[rows:]).astype(F32)).astype(BF)

    def scatter4(self, second, first):
        met = self.met(second)
        across = self.swap_x(met)
        first = first(met)
        return first, self.swap_core(first[first.shape[0] // 2 :]), across

    def scatter8(self, second, third, fourth, first):
        far = self.met(fourth)
        half = far.shape[0] // 2
        by_x, by_y = self.swap_x(far[:half]), self.swap_y(far[half:])
        second, third = self.met(second), self.met(third)
        add = lambda u, v: (u.astype(F32) + v.astype(F32)).astype(BF)
        across = [self.swap_x(second[:half]), self.swap_x(add(second[half:], by_y))]
        over = [self.swap_y(add(third[:half], by_x)), self.swap_y(third[half:])]
        first = first(far)
        core = self.swap_core(first[first.shape[0] // 2 :])
        return first, core, jnp.concatenate(across), jnp.concatenate(over)

    def sum4(self, value, parts):
        def reordered(v, x, c):
            v = v.reshape(v.shape[0], parts, 2, 2, -1)
            if x:
                v = jnp.concatenate([v[:, :, 1:], v[:, :, :1]], axis=2)
            if c:
                v = jnp.concatenate([v[:, :, :, 1:], v[:, :, :, :1]], axis=3)
            return v.reshape(value.shape)

        core, across, both = self.swap_core(value), self.swap_x(value), self.swap_both(value)
        return value + reordered(core, 0, 1) + reordered(across, 1, 0) + reordered(both, 1, 1)


def pick(v, axis, index):
    return lax.dynamic_index_in_dim(v, index, axis, keepdims=False)


def after(value, *others):
    return lax.optimization_barrier((value,) + others)[0]


def pack_kernel(count, width, offsets, turns, spot_ref, *refs):
    spot = [spot_ref[k] for k in range(3)]
    for out, turn in zip(refs[count:], turns):
        places = offsets(*[(s + t) % 2 for s, t in zip(spot, turn)])
        for w, ref in enumerate(refs[:count]):
            for k, place in enumerate(places):
                at = (w * len(places) + k) * width
                out[:, at : at + width] = ref[:, pl.ds(pl.multiple_of(place * width, HD), width)]


def pack(spot, weights, width, offsets, turns):
    rows = weights[0].shape[0]
    size = len(weights) * len(offsets(0, 0, 0)) * width
    if width % HD:
        outs = []
        for turn in turns:
            places = offsets(*[(spot[k] + turn[k]) % 2 for k in range(3)])
            cuts = [lax.dynamic_slice_in_dim(w, place * width, width, 1) for w in weights for place in places]
            outs.append(jnp.concatenate(cuts, axis=1))
        return outs
    whole = pl.BlockSpec(memory_space=pltpu.VMEM)
    return pl.pallas_call(
        functools.partial(pack_kernel, len(weights), width, offsets, turns),
        in_specs=[pl.BlockSpec(memory_space=pltpu.SMEM)] + [whole] * len(weights),
        out_specs=[whole] * len(turns),
        out_shape=[jax.ShapeDtypeStruct((rows, size), BF)] * len(turns),
        compiler_params=pltpu.CompilerParams(vmem_limit_bytes=VMEM_BYTES),
        name="pack_columns",
        cost_estimate=cost(3),
    )(spot, *weights)


TURNS8 = [(dx, dy, dc) for dy in range(2) for dx in range(2) for dc in range(2)]
TURNS4 = TURNS8[:4]


def start_kernel(groups, reach, *refs):
    qkv_pack, feed_packs, x_ref = refs[0:4], (refs[4:12], refs[12:20]), refs[20]
    w_ref, gate_ref, up_ref, all_ref, local_sem, send_sem, recv_sem = refs[21:]
    p, x, y, c = (lax.axis_index(a) for a in ("p", "x", "y", "c"))
    turned = lambda u, t: 1 - u if t else u
    group = [(p, turned(x, dx), turned(y, dy), turned(c, dc)) for dx, dy, dc in TURNS8]
    core, across, over = group[1], group[2], group[4]
    right, left = (lax.rem(p + 1, groups), x, y, c), (lax.rem(p + groups - 1, groups), x, y, c)
    rows, depth = x_ref.shape[0], qkv_pack[0].shape[0]
    used = [0]

    def remote(src, dst, device):
        k = used[0]
        used[0] += 1
        copy = pltpu.make_async_remote_copy(
            src_ref=src,
            dst_ref=dst,
            send_sem=send_sem.at[k],
            recv_sem=recv_sem.at[k],
            device_id=device,
            device_id_type=pl.DeviceIdType.MESH,
        )
        copy.start()
        return copy

    def local(k, src, dst):
        copy = pltpu.make_async_copy(src, dst, local_sem.at[k])
        copy.start()
        return copy

    barrier = pltpu.get_barrier_semaphore()
    for device in group[1:] + [right, left]:
        pl.semaphore_signal(barrier, inc=1, device_id=device, device_id_type=pl.DeviceIdType.MESH)
    pl.semaphore_wait(barrier, 9)

    def at(ref, start, size):
        return ref.at[pl.ds(pl.multiple_of(start, 16), size)]

    def tokens(t, block):
        return all_ref.at[pl.ds((4 * t + block) * rows, rows)]

    def owned(q):
        return w_ref.at[lax.rem(p + 2 * groups - q, groups), :, y]

    slot = (4 * x + 2 * y + c) * depth
    mine = [
        w_ref.at[p, x, y, pl.ds(pl.multiple_of(c * depth, 16), depth)],
        at(gate_ref, slot, depth),
        at(up_ref, slot, depth),
    ]
    firsts = (qkv_pack[0], feed_packs[0][0], feed_packs[1][0])
    kept = [local(k, firsts[k], mine[k]) for k in range(3)] + [local(3, x_ref, tokens(0, 0))]
    regrouped = [remote(qkv_pack[d], mine[0], group[d]) for d in (1, 2, 3)]
    moves = [remote(x_ref, tokens(1, 0), right)]
    sent = list(regrouped) + moves
    kept[0].wait()
    for copy in regrouped:
        copy.wait_recv()
    along = remote(owned(0), owned(0), right)
    later = [remote(owned(0), owned(0), over)]
    spread = [(remote(x_ref, tokens(0, 1), core), remote(x_ref, tokens(0, 2), across))]
    for k in (1, 2):
        later += [remote(feed_packs[k - 1][d], mine[k], group[d]) for d in range(1, 8)]
    sent.append(along)
    step = 1
    ready = 0

    def pass_on(t):
        spread[t][1].wait_recv()
        later.append(remote(tokens(t, 2), tokens(t, 3), core))

    while step < groups or ready <= reach:
        if ready < reach:
            moves[ready].wait_recv()
            if ready + 1 < reach:
                moves.append(remote(tokens(ready + 1, 0), tokens(ready + 2, 0), right))
                sent.append(moves[-1])
            spread.append(
                (
                    remote(tokens(ready + 1, 0), tokens(ready + 1, 1), core),
                    remote(tokens(ready + 1, 0), tokens(ready + 1, 2), across),
                )
            )
        if step < groups:
            along.wait_recv()
            if step < groups - 1:
                along = remote(owned(step), owned(step), right)
                sent.append(along)
            later.append(remote(owned(step), owned(step), over))
            step += 1
        if ready <= reach:
            pass_on(ready)
            ready += 1
    for near, far in spread:
        near.wait_recv()
        sent += [near, far]
    for copy in later:
        copy.wait_recv()
    for copy in sent + later:
        copy.wait_send()
    for copy in kept[1:]:
        copy.wait()


def start(groups, reach, qkv_pack, gate_pack, up_pack, own_inputs):
    depth, size = qkv_pack[0].shape
    rows, width = own_inputs.shape
    hidden = gate_pack[0].shape[1]
    copies = 3 + 1 + 1 + 1 + 14 + (groups - 2) + (groups - 1) + (reach - 1) + 2 * (reach + 1) + (reach + 1)
    anywhere = pl.BlockSpec(memory_space=pl.ANY)
    weight, gate, up, inputs = pl.pallas_call(
        functools.partial(start_kernel, groups, reach),
        in_specs=[anywhere] * 21,
        out_specs=[anywhere] * 4,
        out_shape=[
            jax.ShapeDtypeStruct((groups, 2, 2, 2 * depth, size), BF),
            jax.ShapeDtypeStruct((8 * depth, hidden), BF),
            jax.ShapeDtypeStruct((8 * depth, hidden), BF),
            jax.ShapeDtypeStruct((4 * (reach + 1) * rows, width), BF),
        ],
        scratch_shapes=[
            pltpu.SemaphoreType.DMA((4,)),
            pltpu.SemaphoreType.DMA((copies,)),
            pltpu.SemaphoreType.DMA((copies,)),
        ],
        compiler_params=pltpu.CompilerParams(collective_id=0, has_side_effects=True),
        name="start",
        cost_estimate=cost(120),
    )(*qkv_pack, *gate_pack, *up_pack, own_inputs)
    return weight.reshape(-1, size), gate, up, inputs


def gate_up_kernel(x_ref, gate_w_ref, up_w_ref, narrow_ref, maps_ref, gate_ref, up_ref, gated_ref):
    rank = maps_ref.shape[1]
    gate = dot(x_ref[...], gate_w_ref[...]) + SCALE_ADAPT * dot(narrow_ref[:, :rank], maps_ref[0])
    up = dot(x_ref[...], up_w_ref[...]) + SCALE_ADAPT * dot(narrow_ref[:, rank:], maps_ref[1])
    gate_ref[...] = gate.astype(BF)
    up_ref[...] = up.astype(BF)
    gated_ref[...] = (gate * jax.nn.sigmoid(gate) * up).astype(BF)


def gate_up(x, gate_w, up_w, narrow, maps):
    rows, width = x.shape
    hidden = gate_w.shape[1]
    tile = 256
    weight = pl.BlockSpec((width, tile), lambda s: (0, s))
    out = pl.BlockSpec((rows, tile), lambda s: (0, s))
    return pl.pallas_call(
        gate_up_kernel,
        grid=(hidden // tile,),
        in_specs=[
            pl.BlockSpec((rows, width), lambda s: (0, 0)),
            weight,
            weight,
            pl.BlockSpec(narrow.shape, lambda s: (0, 0)),
            pl.BlockSpec(maps.shape[:2] + (tile,), lambda s: (0, 0, s)),
        ],
        out_specs=[out] * 3,
        out_shape=[jax.ShapeDtypeStruct((rows, hidden), BF)] * 3,
        compiler_params=pltpu.CompilerParams(vmem_limit_bytes=VMEM_BYTES),
        name="gate_up",
        cost_estimate=cost(26),
    )(x, gate_w, up_w, narrow, maps)


def down_kernel(gated_ref, weight_ref, in_maps_ref, out_maps_ref, feed_ref, narrow_ref):
    @pl.when(pl.program_id(0) == 0)
    def _():
        narrow_ref[...] = dot_nt(gated_ref[...], in_maps_ref[...]).astype(BF)

    feed = dot(gated_ref[...], weight_ref[...]) + SCALE_ADAPT * dot(narrow_ref[...], out_maps_ref[...])
    feed_ref[...] = feed.astype(BF)


def down(gated, weight, in_maps, out_maps):
    rows, hidden = gated.shape
    width = weight.shape[1]
    rank = in_maps.shape[0]
    tile = 512
    return pl.pallas_call(
        down_kernel,
        grid=(width // tile,),
        in_specs=[
            pl.BlockSpec((rows, hidden), lambda s: (0, 0)),
            pl.BlockSpec((hidden, tile), lambda s: (0, s)),
            pl.BlockSpec(in_maps.shape, lambda s: (0, 0)),
            pl.BlockSpec((rank, tile), lambda s: (0, s)),
        ],
        out_specs=[pl.BlockSpec((rows, tile), lambda s: (0, s)), pl.BlockSpec((rows, rank), lambda s: (0, 0))],
        out_shape=[jax.ShapeDtypeStruct((rows, width), BF), jax.ShapeDtypeStruct((rows, rank), BF)],
        compiler_params=pltpu.CompilerParams(vmem_limit_bytes=VMEM_BYTES),
        name="down",
        cost_estimate=cost(15),
    )(gated, weight, in_maps, out_maps)


def feed_back_kernel(
    grad_ref,
    down_ref,
    gate_w_ref,
    up_w_ref,
    gate_ref,
    up_ref,
    gated_ref,
    narrow_ref,
    d_out_ref,
    d_in_ref,
    gu_out_ref,
    gu_in_ref,
    out_ref,
    back_gu_ref,
    maps_ref,
):
    rank = d_in_ref.shape[0]
    grad = grad_ref[...]
    back_d = dot_nt(grad, d_out_ref[...]).astype(BF)
    dm = dot_nt(grad, down_ref[...]) + SCALE_ADAPT * dot(back_d, d_in_ref[...])
    gate, up = gate_ref[...].astype(F32), up_ref[...].astype(F32)
    sig = jax.nn.sigmoid(gate)
    silu = gate * sig
    du = (dm * silu).astype(BF)
    dg = (dm * up * (sig + silu * (1.0 - sig))).astype(BF)
    back_g = dot_nt(dg, gu_out_ref[0]).astype(BF)
    back_u = dot_nt(du, gu_out_ref[1]).astype(BF)
    back_gu_ref[:, :rank] = back_g
    back_gu_ref[:, rank:] = back_u
    into = dot_nt(dg, gate_w_ref[...]) + dot_nt(du, up_w_ref[...])
    into = into + SCALE_ADAPT * (dot(back_g, gu_in_ref[:rank, :]) + dot(back_u, gu_in_ref[rank:, :]))
    out_ref[...] = into.astype(BF)

    @pl.when(pl.program_id(0) == 0)
    def _():
        maps_ref[...] = jnp.zeros_like(maps_ref)

    maps_ref[0] += SCALE_ADAPT * dot_tn(back_d, gated_ref[...])
    maps_ref[1] += SCALE_ADAPT * dot_tn(narrow_ref[:, :rank], dg)
    maps_ref[2] += SCALE_ADAPT * dot_tn(narrow_ref[:, rank:], du)


def feed_back(first, grad, down_w, gate_w, up_w, gate, up, gated, narrow, d_out, d_in, gu_out, gu_in):
    rows, width = grad.shape
    hidden = gate_w.shape[1]
    rank = d_in.shape[0]
    tile = 256
    row = lambda n: pl.BlockSpec((tile, n), lambda r: (r, 0))
    local = lambda n: pl.BlockSpec((tile, n), lambda r: (r + first, 0))
    fixed = lambda v: pl.BlockSpec(v.shape, lambda r: (0,) * v.ndim, pipeline_mode=pl.Buffered(1))
    return pl.pallas_call(
        feed_back_kernel,
        grid=(rows // tile,),
        in_specs=[
            row(width),
            fixed(down_w),
            fixed(gate_w),
            fixed(up_w),
            local(hidden),
            local(hidden),
            local(hidden),
            local(2 * rank),
            fixed(d_out),
            fixed(d_in),
            fixed(gu_out),
            fixed(gu_in),
        ],
        out_specs=[row(width), row(2 * rank), pl.BlockSpec((3, rank, hidden), lambda r: (0, 0, 0))],
        out_shape=[
            jax.ShapeDtypeStruct((rows, width), BF),
            jax.ShapeDtypeStruct((rows, 2 * rank), BF),
            jax.ShapeDtypeStruct((3, rank, hidden), F32),
        ],
        compiler_params=pltpu.CompilerParams(vmem_limit_bytes=VMEM_BYTES),
        name="feed_backward",
        cost_estimate=cost(2 + rows // 50),
    )(grad, down_w, gate_w, up_w, gate, up, gated, narrow, d_out, d_in, gu_out, gu_in)


def project_kernel(heads, own_tiles, x_ref, w_ref, in_maps_ref, out_maps_ref, *out_refs):
    pre_q_ref, pre_k_ref, value_ref, narrow_ref, square_q_ref, square_k_ref = out_refs
    width = heads * HD
    rank = out_maps_ref.shape[1]
    narrow_ref[...] = dot_nt(x_ref[...], in_maps_ref[...]).astype(BF)

    def part(k):
        cols = slice(k * width, (k + 1) * width)
        return dot(x_ref[...], w_ref[:, cols]) + SCALE_ADAPT * dot(narrow_ref[:, k * rank : (k + 1) * rank], out_maps_ref[k])

    ones = jnp.ones((8, width), BF)
    key = part(1)
    pre_k_ref[...] = key
    square_k_ref[...] = dot_nt(ones, (key * key).astype(BF))
    value_ref[...] = part(2).astype(BF)

    @pl.when(pl.program_id(0) < own_tiles)
    def _():
        query = part(0)
        pre_q_ref[...] = query
        square_q_ref[...] = dot_nt(ones, (query * query).astype(BF))


def project(x, own_rows, weight, in_maps, out_maps, heads):
    rows, width = x.shape
    local = heads * HD
    tile = 512
    own_tiles = own_rows // tile
    fixed = lambda v: pl.BlockSpec(v.shape, lambda t: (0,) * v.ndim)
    row = lambda n: pl.BlockSpec((tile, n), lambda t: (t, 0))
    return pl.pallas_call(
        functools.partial(project_kernel, heads, own_tiles),
        grid=(rows // tile,),
        in_specs=[row(width), fixed(weight), fixed(in_maps), fixed(out_maps)],
        out_specs=[
            pl.BlockSpec((tile, local), lambda t: (jnp.minimum(t, own_tiles - 1), 0)),
            row(local),
            row(local),
            row(in_maps.shape[0]),
            pl.BlockSpec((8, tile), lambda t: (0, jnp.minimum(t, own_tiles - 1))),
            pl.BlockSpec((8, tile), lambda t: (0, t)),
        ],
        out_shape=[
            jax.ShapeDtypeStruct((own_rows, local), F32),
            jax.ShapeDtypeStruct((rows, local), F32),
            jax.ShapeDtypeStruct((rows, local), BF),
            jax.ShapeDtypeStruct((rows, in_maps.shape[0]), BF),
            jax.ShapeDtypeStruct((8, own_rows), F32),
            jax.ShapeDtypeStruct((8, rows), F32),
        ],
        compiler_params=pltpu.CompilerParams(vmem_limit_bytes=VMEM_BYTES),
        name="project",
        cost_estimate=cost(30),
    )(x, weight, in_maps, out_maps)


def post_kernel(heads, own_tiles, q_ref, k_ref, inv_q_ref, inv_k_ref, gain_ref, cos_ref, sin_ref, q_out, k_out):
    width = heads * HD
    cos, sin = cos_ref[...], sin_ref[...]

    def turn(pre_ref, inv, part, out_ref):
        for h in range(heads):
            cols = slice(h * HD, (h + 1) * HD)
            v = pre_ref[:, cols] * inv * gain_ref[:, part * width + h * HD : part * width + (h + 1) * HD]
            out_ref[:, cols] = (v * cos + pltpu.roll(v, HD // 2, 1) * sin).astype(BF)

    turn(k_ref, inv_k_ref[...], 1, k_out)

    @pl.when(pl.program_id(0) < own_tiles)
    def _():
        turn(q_ref, inv_q_ref[...], 0, q_out)


def post(pre_q, pre_k, inv_q, inv_k, gain, cos, sin, heads):
    rows, width = pre_k.shape
    tile = 256
    own_tiles = pre_q.shape[0] // tile
    row = lambda n: pl.BlockSpec((tile, n), lambda r: (r, 0))
    own = lambda n: pl.BlockSpec((tile, n), lambda r: (jnp.minimum(r, own_tiles - 1), 0))
    return pl.pallas_call(
        functools.partial(post_kernel, heads, own_tiles),
        grid=(rows // tile,),
        in_specs=[
            own(width),
            row(width),
            own(1),
            row(1),
            pl.BlockSpec((1, 2 * width), lambda r: (0, 0)),
            row(HD),
            row(HD),
        ],
        out_specs=[own(width), row(width)],
        out_shape=[jax.ShapeDtypeStruct(pre_q.shape, BF), jax.ShapeDtypeStruct(pre_k.shape, BF)],
        name="rope_forward",
        cost_estimate=cost(10),
    )(pre_q, pre_k, inv_q, inv_k, gain, cos, sin)


def unpost_kernel(heads, dq_ref, dk_ref, pre_q_ref, pre_k_ref, gain_ref, cos_ref, sin_ref, turn_ref, inner_ref):
    width = heads * HD
    cos, sin = cos_ref[...], sin_ref[...]
    for part, (d_ref, pre_ref) in enumerate(((dq_ref, pre_q_ref), (dk_ref, pre_k_ref))):
        total = None
        for h in range(heads):
            cols = slice(part * width + h * HD, part * width + (h + 1) * HD)
            v = d_ref[:, h * HD : (h + 1) * HD]
            turned = (v * cos - pltpu.roll(v, HD // 2, 1) * sin) * gain_ref[:, cols]
            turn_ref[:, cols] = turned
            inner = jnp.sum(turned * pre_ref[:, h * HD : (h + 1) * HD], axis=1, keepdims=True)
            total = inner if total is None else total + inner
        inner_ref[:, part : part + 1] = total


def unpost(dq, dk, pre_q, pre_k, gain, cos, sin, heads):
    rows, width = dq.shape
    tile = 256
    row = lambda n: pl.BlockSpec((tile, n), lambda r: (r, 0))
    return pl.pallas_call(
        functools.partial(unpost_kernel, heads),
        grid=(rows // tile,),
        in_specs=[row(width)] * 4 + [pl.BlockSpec((1, 2 * width), lambda r: (0, 0)), row(HD), row(HD)],
        out_specs=[row(2 * width), row(2)],
        out_shape=[jax.ShapeDtypeStruct((rows, 2 * width), F32), jax.ShapeDtypeStruct((rows, 2), F32)],
        name="rope_backward",
        cost_estimate=cost(8),
    )(dq, dk, pre_q, pre_k, gain, cos, sin)


NEG_FILL = -1e30


def attend_kernel(count, scale, q_ref, *refs):
    ks, vs = refs[:count], refs[count : 2 * count]
    lo_ref, pos_ref, key_ref, o_ref, log_ref = refs[2 * count :]
    rows = q_ref.shape[0] * q_ref.shape[2]
    q = q_ref[...].reshape(rows, HD)
    lo, pos = lo_ref[0], pos_ref[...]
    scores = []
    for t in range(count):
        s = dot_nt(q, ks[t][...].reshape(rows, HD)) * scale
        key = key_ref[t : t + 1, :]
        scores.append(jnp.where((key >= lo) & (key <= pos), s, NEG_FILL))
    top = functools.reduce(jnp.maximum, [jnp.max(s, axis=1, keepdims=True) for s in scores])
    powers = [jnp.exp(s - top) for s in scores]
    total = sum(jnp.sum(e, axis=1, keepdims=True) for e in powers)
    share = 1.0 / total
    out = sum(dot((e * share).astype(BF), vs[t][...].reshape(rows, HD)) for t, e in enumerate(powers))
    o_ref[...] = out.astype(BF).reshape(o_ref.shape)
    log_ref[0] = top + jnp.log(total)


def attend_back_kernel(count, first, scale, q_ref, do_ref, o_ref, *refs):
    ks, vs = refs[:count], refs[count : 2 * count]
    lo_ref, pos_ref, key_ref, log_ref = refs[2 * count : 2 * count + 4]
    refs = refs[2 * count + 4 :]
    dq = None
    rows = q_ref.shape[0] * q_ref.shape[2]
    if not first:
        dq = refs[0][...].reshape(rows, HD)
        refs = refs[1:]
    dq_ref, dks, dvs = refs[0], refs[1 : 1 + count], refs[1 + count :]
    q = q_ref[...].reshape(rows, HD)
    do = do_ref[...].reshape(rows, HD)
    inner = jnp.sum(do.astype(F32) * o_ref[...].reshape(rows, HD).astype(F32), axis=1, keepdims=True)
    lo, pos, log_total = lo_ref[0], pos_ref[...], log_ref[0]
    for t in range(count):
        k, v = ks[t][...].reshape(rows, HD), vs[t][...].reshape(rows, HD)
        key = key_ref[t : t + 1, :]
        s = dot_nt(q, k) * scale
        probs = jnp.where((key >= lo) & (key <= pos), jnp.exp(s - log_total), 0.0)
        ds = (probs * (dot_nt(do, v) - inner)).astype(BF)
        dvs[t][...] = dot_tn(probs.astype(BF), do).astype(dvs[t].dtype).reshape(dvs[t].shape)
        dks[t][...] = (dot_tn(ds, q) * scale).astype(dks[t].dtype).reshape(dks[t].shape)
        part = dot(ds, k) * scale
        dq = part if dq is None else dq + part
    dq_ref[...] = dq.reshape(dq_ref.shape)


class Attention:
    def __init__(self, rows, heads, count, lo, pos, key):
        self.rows, self.heads, self.count = rows, heads, count
        self.tables = (lo, pos, key)
        full = 2 * rows
        self.block = pl.BlockSpec((2, 1, rows, HD), lambda s, h: (0, s, 0, h))
        self.part = lambda t: pl.BlockSpec((2, 1, rows, HD), lambda s, h: (t, s, 0, h))
        self.table_specs = lambda n: [
            pl.BlockSpec((1, full, 1), lambda s, h: (s, 0, 0)),
            pl.BlockSpec((full, 1), lambda s, h: (0, 0)),
            pl.BlockSpec((n, full), lambda s, h: (0, 0)),
        ]
        self.log_spec = pl.BlockSpec((1, full, 1), lambda s, h: (s * heads + h, 0, 0))
        self.params = pltpu.CompilerParams(vmem_limit_bytes=VMEM_BYTES)

    def shape(self, dtype):
        return jax.ShapeDtypeStruct((2, 2, self.rows, self.heads * HD), dtype)

    def view(self, v):
        return v.reshape(-1, 2, self.rows, v.shape[-1])

    def forward(self, q, key, value):
        count = self.count
        parts = [self.part(t) for t in range(count)]
        out, log = pl.pallas_call(
            functools.partial(attend_kernel, count, HD**-0.5),
            grid=(2, self.heads),
            in_specs=[self.block] + parts * 2 + self.table_specs(count),
            out_specs=[self.block, self.log_spec],
            out_shape=[self.shape(BF), jax.ShapeDtypeStruct((2 * self.heads, 2 * self.rows, 1), F32)],
            compiler_params=self.params,
            name="attend_forward",
            cost_estimate=cost(23),
        )(self.view(q), *[self.view(key)] * count, *[self.view(value)] * count, *self.tables)
        return out.reshape(q.shape), log

    def backward(self, q, do, o, key, value, log, blocks, dtypes, dq=None):
        lo, pos, key_pos = self.tables
        count = len(blocks)
        grads = [self.shape(d) for d in dtypes]
        key_pos = jnp.concatenate([key_pos[t : t + 1] for t in blocks], axis=0)
        more = [] if dq is None else [self.view(dq)]
        parts = [self.part(t) for t in blocks]
        outs = pl.pallas_call(
            functools.partial(attend_back_kernel, count, dq is None, HD**-0.5),
            grid=(2, self.heads),
            in_specs=[self.block] * 3 + parts * 2 + self.table_specs(count) + [self.log_spec] + [self.block] * len(more),
            out_specs=[self.block] * (1 + 2 * count),
            out_shape=[self.shape(F32)] + grads + grads,
            compiler_params=self.params,
            name="attend_backward",
            cost_estimate=cost(4 + 8 * count),
        )(
            *[self.view(v) for v in [q, do, o]],
            *[self.view(key)] * count,
            *[self.view(value)] * count,
            lo,
            pos,
            key_pos,
            log,
            *more,
        )
        flat = [v.reshape(q.shape) for v in outs]
        return flat[0], flat[1 : 1 + count], flat[1 + count :]


def rms_inverse(v):
    return lax.rsqrt(jnp.mean(v * v, axis=-1, keepdims=True) + EPS)


def rms_backward(v, gain, grad):
    inv = rms_inverse(v)
    turn = grad * gain
    inner = jnp.mean(v * turn, axis=-1, keepdims=True)
    return inv * turn - v * (inv * inv * inv) * inner


def total(refs):
    return sum(ref[...].astype(F32) for ref in refs)


def after_attention_kernel(*refs):
    inputs_ref, gain_ref, attn_ref, middle_ref, low_ref = refs[3:]
    attn = total(refs[:3])
    attn_ref[...] = attn
    middle = inputs_ref[...].astype(F32) + attn * rms_inverse(attn) * gain_ref[...]
    middle_ref[...] = middle
    low_ref[...] = middle.astype(BF)


def after_feed_kernel(*refs):
    middle_ref, gain_ref, cot_ref, result_ref, grad_ref = refs[4:]
    feed = total(refs[:4])
    gain = gain_ref[...]
    result_ref[...] = (middle_ref[...] + feed * rms_inverse(feed) * gain).astype(BF)
    grad_ref[...] = rms_backward(feed, gain, cot_ref[...].astype(F32)).astype(BF)


def middle_kernel(*refs):
    cot_ref, attn_ref, gain_ref, mid_ref, grad_ref = refs[4:]
    mid = cot_ref[...].astype(F32) + total(refs[:4])
    mid_ref[...] = mid
    grad_ref[...] = rms_backward(attn_ref[...], gain_ref[...], mid).astype(BF)


def end_kernel(*refs):
    mid_ref, out_ref = refs[3:]
    out_ref[...] = mid_ref[...] + total(refs[:3])


def by_rows(kernel, name, rows, width, args, dtypes, us):
    tile = 64 if rows % 64 == 0 else rows
    spec = lambda v: pl.BlockSpec((1, width), lambda r: (0, 0)) if v.shape[0] == 1 else pl.BlockSpec((tile, width), lambda r: (r, 0))
    row = pl.BlockSpec((tile, width), lambda r: (r, 0))
    return pl.pallas_call(
        kernel,
        grid=(rows // tile,),
        in_specs=[spec(v) for v in args],
        out_specs=[row] * len(dtypes),
        out_shape=[jax.ShapeDtypeStruct((rows, width), d) for d in dtypes],
        compiler_params=pltpu.CompilerParams(vmem_limit_bytes=VMEM_BYTES),
        name=name,
        cost_estimate=cost(us),
    )(*args)


def on_device(
    layer_input,
    cotangent,
    document_length,
    adapter_choice_index,
    query_weight,
    key_weight,
    value_weight,
    output_weight,
    gate_weight,
    up_weight,
    down_weight,
    query_norm_gain,
    key_norm_gain,
    attention_norm_gain,
    feedforward_norm_gain,
    adapter_model_input_maps,
    adapter_down_input_maps,
    adapter_model_output_maps,
    adapter_hidden_output_maps,
):
    at = Place()
    rows = layer_input.shape[1]
    width = layer_input.shape[2]
    heads = width // HD // 4
    local = heads * HD
    rank = adapter_model_input_maps.shape[2]
    depth = query_weight.shape[0]
    hidden_rows = down_weight.shape[0]
    hidden = hidden_rows * at.np
    reach = WINDOW // (2 * rows)
    count = reach + 1

    def head_cols(v, quarter):
        return pick(v.reshape(v.shape[:-1] + (heads, 4, HD)), v.ndim, quarter).reshape(v.shape[:-1] + (local,))

    def hidden_cols(v):
        lead = v.shape[:-1]
        n = len(lead)
        v = v.reshape(lead + (at.np, 2, 2, 2, hidden_rows))
        v = pick(v, n + 3, at.c)
        v = pick(v, n + 2, at.y)
        return pick(v, n + 1, at.x).reshape(lead + (-1,))

    def gather_p(v):
        return lax.all_gather(v, "p", axis=0, tiled=True)

    own_inputs = layer_input[0]
    head_offsets = lambda x, y, c: [4 * k + 2 * x + c for k in range(heads)]
    feed_offsets = lambda x, y, c: [((2 * p + x) * 2 + y) * 2 + c for p in range(at.np)]
    w_qkv, gate_piece, up_piece, inputs = start(
        at.np,
        reach,
        pack(at.spot, [query_weight, key_weight, value_weight], HD, head_offsets, TURNS4),
        pack(at.spot, [gate_weight], hidden_rows, feed_offsets, TURNS8),
        pack(at.spot, [up_weight], hidden_rows, feed_offsets, TURNS8),
        own_inputs,
    )
    w_g = gather_p(gate_piece)
    w_u = gather_p(up_piece)
    w_d = gather_p(after(down_weight, w_g))
    if 2 * depth == HD:
        o_own = gather_p(output_weight)
        o_sent = after(o_own, w_qkv)
        sent = lambda target: lax.ppermute(o_sent, ("y", "c"), target)
        same = at.y == at.c
        mine_half = jnp.where(same, o_own, sent([(0, 2), (3, 1)]))
        other_half = jnp.where(same, sent([(1, 0), (2, 3)]), sent([(1, 2), (2, 1)]))
        halves = [jnp.where(at.c == 0, mine_half, other_half), jnp.where(at.c == 0, other_half, mine_half)]
        w_o = jnp.stack([v.reshape(at.np, depth, width) for v in halves], axis=1).reshape(local, width)
    else:
        o_full = lax.all_gather(output_weight, ("p", "x", "y", "c"), axis=0, tiled=True)
        w_o = pick(o_full.reshape(heads, 4, HD, width), 1, at.quarter).reshape(local, width)
    selected = adapter_choice_index[0]
    a_model = pick(adapter_model_input_maps, 0, selected)
    a_hidden = pick(adapter_down_input_maps, 0, selected)
    b_model = pick(adapter_model_output_maps, 0, selected)
    b_hidden = pick(adapter_hidden_output_maps, 0, selected)
    a_qkv = a_model[:3].reshape(3 * rank, width)
    a_gu = a_model[4:6].reshape(2 * rank, width)
    a_o = head_cols(a_model[3], at.quarter)
    a_d = hidden_cols(a_hidden)
    b_qkv = head_cols(b_model[:3], at.quarter)
    b_o, b_d = b_model[3], b_model[4]
    b_gu = hidden_cols(b_hidden)

    def diagonal(maps):
        k, r, n = maps.shape
        zero = jnp.zeros((r, n), BF)
        return jnp.concatenate(
            [jnp.concatenate([maps[a] if a == b else zero for b in range(k)], axis=1) for a in range(k)], axis=0
        )

    b_qkv_diag = diagonal(b_qkv)
    gain = jnp.concatenate(
        [head_cols(query_norm_gain[None], at.quarter), head_cols(key_norm_gain[None], at.quarter)], axis=1
    )

    step_rows = jnp.arange(rows, dtype=jnp.int32)
    spot = lambda xx: at.p * 2 * rows + xx * rows + step_rows
    pos = jnp.concatenate([spot(at.x), spot(1 - at.x)])
    lengths = lax.dynamic_slice_in_dim(document_length, 2 * at.y, 2, 0)
    bounds = jnp.cumsum(lengths, axis=1)
    bounds = jnp.where(at.c == 0, bounds, bounds[::-1])
    begin = jnp.max(jnp.where(bounds[:, None, :] <= pos[None, :, None], bounds[:, None, :], 0), axis=2)
    lo = jnp.maximum(begin, pos[None] - (WINDOW - 1))
    key = jnp.stack([pos - 2 * rows * t for t in range(count)])
    attention = Attention(rows, heads, count, lo[:, :, None], pos[:, None], key)

    half_dim = HD // 2
    inv_freq = ROPE_BASE ** (-(jnp.arange(half_dim, dtype=F32) * 2.0 / HD))
    spots = jnp.concatenate([spot(at.x), spot(at.x), spot(1 - at.x), spot(1 - at.x)])
    angles = jnp.concatenate([spots - 2 * rows * t for t in range(count)]).astype(F32)[:, None] * inv_freq
    cos, sin = jnp.cos(angles), jnp.sin(angles)
    cos = jnp.concatenate([cos, cos], axis=1)
    sin = jnp.concatenate([-sin, sin], axis=1)

    own = 4 * rows
    pre_q, pre_k, value_all, narrow_qkv, square_q, square_k = project(
        inputs, own, w_qkv, a_qkv, b_qkv, heads
    )
    inputs = inputs[:own]
    narrow_qkv = narrow_qkv[:own]
    squares = jnp.concatenate([square_q[:1], square_k[:1]], axis=1)
    inv = lax.rsqrt(at.sum4(squares, 2 + reach) / width + EPS).reshape(-1, 1)
    inv_q, inv_k = inv[:own], inv[own:]
    query, key_all = post(pre_q, pre_k, inv_q, inv_k, gain, cos, sin, heads)
    cos, sin = cos[:own], sin[:own]
    inv_k = inv_k[:own]
    o, log = attention.forward(query, key_all, value_all)
    narrow_o = dot_nt(o, a_o).astype(BF)
    def attn_part(part, mark=None):
        ins, narrow = o[part], narrow_o[part]
        if mark is not None:
            ins = after(ins, mark)
        return (dot(ins, w_o) + SCALE_ADAPT * dot(narrow, b_o)).astype(BF)

    near_rows, far_rows = slice(0, 2 * rows), slice(2 * rows, 4 * rows)
    attn_parts = at.scatter4(attn_part(far_rows), lambda mark: attn_part(near_rows, mark))
    attn_gain, feed_gain = attention_norm_gain[None], feedforward_norm_gain[None]
    attn_out, middle, low = by_rows(
        after_attention_kernel,
        "after_attention",
        rows,
        width,
        [*attn_parts, own_inputs, attn_gain],
        [F32, F32, BF],
        4,
    )
    middle_low = jnp.concatenate(at.gather8(low)[0])
    narrow_gu = dot_nt(middle_low, a_gu).astype(BF)
    gate, up, gated = gate_up(middle_low, w_g, w_u, narrow_gu, b_gu)
    feed, narrow_d = down(gated, w_d, a_d, b_d)
    pairs = [feed[2 * rows * k : 2 * rows * (k + 1)] for k in range(4)]
    feed_parts = at.scatter8(*pairs[1:], lambda mark: pairs[0])
    cot = cotangent[0]
    result, grad_feed_own = by_rows(
        after_feed_kernel,
        "after_feed",
        rows,
        width,
        [*feed_parts, middle, feed_gain, cot],
        [BF, BF],
        4,
    )

    feed_args = (w_d, w_g, w_u, gate, up, gated, narrow_gu, b_d, a_d, b_gu, a_gu)
    grad_feed, first = at.gather8(grad_feed_own, lambda pair: feed_back(0, pair, *feed_args))
    tiles = 2 * rows // 256
    backs = [first, feed_back(tiles, grad_feed[1], *feed_args)]
    backs.append(feed_back(2 * tiles, jnp.concatenate(grad_feed[2:]), *feed_args))
    mids = [backs[1][0], backs[2][0][: 2 * rows], backs[2][0][2 * rows :]]
    back_gu = jnp.concatenate([back[1] for back in backs])
    mid_parts = at.scatter8(*mids, lambda mark: backs[0][0])
    grad_mid, grad_attn_own = by_rows(
        middle_kernel, "middle", rows, width, [*mid_parts, cot, attn_out, attn_gain], [F32, BF], 4
    )
    grad_attn = jnp.concatenate(at.gather4(grad_attn_own))
    back_o = dot_nt(grad_attn, b_o).astype(BF)
    grad_o = (dot_nt(grad_attn, w_o) + SCALE_ADAPT * dot(back_o, a_o)).astype(BF)
    dq, dks, dvs = attention.backward(query, grad_o, o, key_all, value_all, log, [reach], [BF])
    moved_k, moved_v = at.shift_p(dks[0], -1), at.shift_p(dvs[0], -1)
    dq, dks, dvs = attention.backward(
        query, grad_o, o, key_all, value_all, log, range(reach), [F32] + [BF] * (reach - 1), dq
    )
    for t in range(reach - 1, 0, -1):
        moved_k = at.shift_p((dks[t].astype(F32) + moved_k.astype(F32)).astype(BF), -1)
        moved_v = at.shift_p((dvs[t].astype(F32) + moved_v.astype(F32)).astype(BF), -1)
    dk = dks[0] + moved_k.astype(F32)
    dv = dvs[0] + moved_v.astype(F32)
    def share_y(mine, other):
        return mine + at.swap_y(other)

    def share_p(v):
        total = pick(v, 1, at.p)
        for by in range(1, at.np):
            total = total + at.turn_p(pick(v, 1, (at.p + by) % at.np), by)
        return total

    def sum_model(v):
        v = v.reshape(-1, at.np, 2, 2, 2 * depth)
        v = pick(v, 2, at.x) + at.swap_x(pick(v, 2, 1 - at.x))
        return share_y(pick(v, 2, at.y), pick(v, 2, 1 - at.y))

    mine = (jnp.arange(4) == at.quarter).astype(F32)

    def spread(v):
        return (v.reshape(-1, heads, 1, HD) * mine[:, None]).reshape(-1, width)

    ga_gu = SCALE_ADAPT * dot_tn(back_gu, middle_low)
    ga_o = SCALE_ADAPT * dot_tn(back_o, o)
    gb_o = SCALE_ADAPT * dot_tn(narrow_o, grad_attn)
    gb_d = SCALE_ADAPT * sum(
        dot_tn(narrow_d[2 * rows * k : 2 * rows * (k + 1)], grad_feed[k]) for k in range(4)
    )
    early = sum_model(after(jnp.concatenate([ga_gu, spread(ga_o), gb_o, gb_d]), dq))
    wide = sum(back[2] for back in backs).reshape(-1, at.np, hidden_rows)
    dk = after(dk, early)
    turn, inner = unpost(dq, dk, pre_q, pre_k, gain, cos, sin, heads)
    inner = at.sum4(inner.T, 1).T / width

    def unnorm(part, pre, scale):
        cols = slice(part * local, (part + 1) * local)
        return (scale * turn[:, cols] - pre * (scale * scale * scale * inner[:, part : part + 1])).astype(BF)

    grad_qkv = jnp.concatenate(
        [unnorm(0, pre_q, inv_q), unnorm(1, pre_k[:own], inv_k), dv.astype(BF)], axis=1
    )
    back_qkv = dot_nt(grad_qkv, b_qkv_diag).astype(BF)

    def late_adapters(mark):
        back = after(back_qkv, mark)
        ga_qkv = SCALE_ADAPT * dot_tn(back, inputs)
        gb_qkv = [
            SCALE_ADAPT * dot_tn(narrow_qkv[:, k * rank : (k + 1) * rank], grad_qkv[:, k * local : (k + 1) * local])
            for k in range(3)
        ]
        return sum_model(jnp.concatenate([ga_qkv, spread(jnp.concatenate(gb_qkv))]))

    def end_part(part, mark=None):
        ins, back = grad_qkv[part], back_qkv[part]
        if mark is not None:
            ins = after(ins, mark)
        return (dot_nt(ins, w_qkv) + SCALE_ADAPT * dot(back, a_qkv)).astype(BF)

    marks = []

    def end_near(mark):
        marks.append(mark)
        return end_part(near_rows, mark)

    end_parts = at.scatter4(end_part(far_rows), end_near)
    (grad_input,) = by_rows(end_kernel, "end", rows, width, [*end_parts, grad_mid], [F32], 3)
    late = late_adapters(marks[0])
    narrow_sums = share_p(jnp.concatenate([late, early], axis=0))
    narrow_sums = narrow_sums.reshape(narrow_sums.shape[0], 2, depth)
    sums = pick(narrow_sums, 1, at.c) + at.swap_core(pick(narrow_sums, 1, 1 - at.c))
    sums = sums.reshape(-1, rank, depth)
    late, early = sums[:6], sums[6:]
    wide = share_p(after(wide, marks[0])).reshape(-1, rank, hidden_rows)
    choose = (jnp.arange(adapter_model_input_maps.shape[0], dtype=jnp.int32) == selected).astype(F32)
    sum_a_model = choose[:, None, None, None] * jnp.concatenate([late[:3], early[2:3], early[:2]])[None]
    sum_a_hidden = choose[:, None, None] * wide[0][None]
    sum_b_model = choose[:, None, None, None] * jnp.concatenate([late[3:], early[3:]])[None]
    sum_b_hidden = choose[:, None, None, None] * wide[1:][None]
    return (result[None], grad_input[None], sum_a_model, sum_a_hidden, sum_b_model, sum_b_hidden)


def solution(mesh):
    grid = mesh.devices.reshape(mesh.shape["ctx"] // 2, 2, mesh.shape["wt"] // 2, 2)
    split = Mesh(grid, ("p", "x", "y", "c"))
    everyone = ("p", "x", "y", "c")
    rows = P(everyone, None)
    tokens = P(("y", "c"), ("p", "x"), None)
    placed = (tokens, tokens, P(), P()) + (rows,) * 7 + (P(),) * 8
    return jax.shard_map(
        on_device,
        mesh=split,
        in_specs=placed,
        out_specs=(
            tokens,
            tokens,
            P(None, None, None, everyone),
            P(None, None, everyone),
            P(None, None, None, everyone),
            P(None, None, None, everyone),
        ),
        check_vma=False,
    )
```

time: 993 us -> 889 us (0.90)
  waiting for transfers between devices: 446 us -> 246 us
  Pallas kernels: 196 us -> 388 us
  starting transfers between devices: 112 us -> 57.3 us
  local copies, waits for them, and re-layouts: 93.8 us -> 71.6 us
  matrix products: 66.1 us -> 46.5 us
    pallas_call x7, Pallas kernels: 89.4 us -> 279 us  [the longest x1 141 us: start(): pl.pallas_call(functools.partial(start_kernel, groups, reach), in_specs=[...]
    ppermute x8 -> x4, waiting for transfers between devices: 122 us -> 40.6 us  [shift_p(): lax.ppermute(value, 'p', [(p, p + by) for p in range(self.np) if 0 <= p +...]
    all_gather x6 -> x4, waiting for transfers between devices: 84.5 us -> 10.1 us  [gather_p(): return lax.all_gather(v, 'p', axis=0, tiled=True)]
    ppermute x8 -> x12, waiting for transfers between devices: 122 us -> 53.7 us  [swap_y(): return lax.ppermute(value, 'y', SWAP)]
    ppermute x15 -> x17, waiting for transfers between devices: 82.3 us -> 115 us  [swap_x(): return lax.ppermute(value, 'x', SWAP)]
    ppermute x9 -> x6, starting transfers between devices: 38.5 us -> 8.12 us  [turn_p(): lax.ppermute(value, 'p', [(p, (p + by) % self.np) for p in range(self.np)])]
    ppermute x8 -> x4, starting transfers between devices: 25.6 us -> 5.37 us  [shift_p(): lax.ppermute(value, 'p', [(p, p + by) for p in range(self.np) if 0 <= p +...]
    dot_general x25, matrix products: 66.1 us -> 46.5 us  [dot(): return lax.dot_general(a, b, (dims, ((), ())), preferred_element_type=F32)]
  transfers between devices with their start and end apart: 75 -> 73, of which waited for: 33 -> 34; matrix products, arithmetic and copies ran while one was open for 14% -> 15% of each run, Pallas kernels for 15% -> 39%
where the time goes in v2:
time: 889 us; the launch traced here: 881 us
  Pallas kernels  388 us (44%)
  waiting for transfers between devices  246 us (28%)
  local copies, waits for them, and re-layouts  71.6 us (8%)
  starting transfers between devices  57.3 us (6%)
  other arithmetic  54.6 us (6%)
  matrix products  46.5 us (5%)
  between operations  17 us (2%)
    pallas_call x1, Pallas kernels, start(): pl.pallas_call(functools.partial(start_kernel, groups, reach), in_specs=[...  141 us
    ppermute x17, waiting for transfers between devices, swap_x(): return lax.ppermute(value, 'x', SWAP)  115 us
    pallas_call x3, Pallas kernels, feed_back(): pl.pallas_call(feed_back_kernel, grid=(rows // tile,), in_specs=[row(widt...  66 us
    ppermute x12, waiting for transfers between devices, swap_y(): return lax.ppermute(value, 'y', SWAP)  53.7 us
    dot_general x25, matrix products, dot(): return lax.dot_general(a, b, (dims, ((), ())), preferred_element_type=F32)  46.5 us
    ppermute x4, waiting for transfers between devices, shift_p(): lax.ppermute(value, 'p', [(p, p + by) for p in range(self.np) if 0 <= p +...  40.6 us
    pallas_call x1, Pallas kernels, project(): pl.pallas_call(functools.partial(project_kernel, heads, own_tiles), grid=...  33.5 us
    pallas_call x2, Pallas kernels, backward(): pl.pallas_call(functools.partial(attend_back_kernel, count, dq is None, H...  32.4 us
  transfers between devices with their start and end apart: 73, of which 34 were waited for; matrix products, arithmetic and copies ran while one was open for 15% of the time, Pallas kernels for 39%

profile of v2, /device:TPU:0, one launch (start us, length us, event | category | flops | bytes accessed | tf_op | source)
XLA Modules:
  0.0 880.8 jit_solution(17207584625480766743)
XLA Ops:
  8.6 2.4 pack_columns.4
  10.9 2.4 pack_columns.5
  15.5 140.6 %start.1 = (bf16[4,2,2,128,1536]{4,3,2,1,0:T(8,128)(2,1)}, bf16[512,1024]{1,0:T(8,128)(2,1)}, bf16[512,1024]{1,0:T(8,128)(2,1)}, bf16[3072,2048]{1,0:T(8,128)(2,1)}) custom-call(bf16[64,1536]{1,0:T(8,128)(2,1)} %get-tuple-element.81.refs_0_, bf16[64,1536]{1,0:T(8,128)(2,1)} %get-tuple-element.82.refs_1_, bf16[64,1536]{1,0:T(8,128)(2,1)} %get-tuple-element.83.refs_2_, ...), custom_call_target="tpu_custom_call" | custom-call | flops 131999997952 | bytes 120000000 | tf_op jit(solution)/shard_map/start/pallas_call | solution.py:272
  159.5 33.5 %project.1 = (f32[1024,512]{1,0:T(8,128)}, f32[3072,512]{1,0:T(8,128)}, bf16[3072,512]{1,0:T(8,128)(2,1)}, bf16[3072,48]{1,0:T(8,128)(2,1)}, f32[8,1024]{1,0:T(8,128)}, /*index=5*/f32[8,3072]{1,0:T(8,128)}) custom-call(bf16[3072,2048]{1,0:T(8,128)(2,1)} %get-tuple-element.101.x_ref, bf16[2048,1536]{1,0:T(8,128)(2,1)} %bitcast.276, ...), custom_call_target="tpu_custom_call" | custom-call | flops 32999999488 | bytes 30000000 | tf_op jit(solution)/shard_map/project/pallas_call | solution.py:468
  198.8 5.8 fusion.28
  219.3 12.1 %rope_forward.1 = (bf16[1024,512]{1,0:T(8,128)(2,1)}, bf16[3072,512]{1,0:T(8,128)(2,1)}) custom-call(f32[1024,512]{1,0:T(8,128)} %get-tuple-element.103.q_ref.pre_q_ref, f32[3072,512]{1,0:T(8,128)} %get-tuple-element.104.k_ref.pre_k_ref, f32[1024,1]{1,0:T(8,128)} %copy.161.inv_q_ref, f32[3072,1]{1,0:T(8,128)} %copy.162.inv_k_ref, ...), custom_call_target="tpu_custom_call" | custom-call | flops 11000000512 | bytes 10000000 | tf_op jit(solution)/shard_map/rope_forward/pallas_call | solution.py:517
  233.4 6.1 collective-permute-start.3
  239.5 23.3 %attend_forward.1 = (bf16[2,2,256,512]{3,2,1,0:T(8,128)(2,1)}, f32[8,512,1]{2,1,0:T(8,128)}) custom-call(bf16[2,2,256,512]{3,2,1,0:T(8,128)(2,1)} %bitcast.294, bf16[6,2,256,512]{3,2,1,0:T(8,128)(2,1)} %bitcast.285, bf16[6,2,256,512]{3,2,1,0:T(8,128)(2,1)} %bitcast.286, bf16[6,2,256,512]{3,2,1,0:T(8,128)(2,1)} %bitcast.287, ...), custom_call_target="tpu_custom_call" | custom-call | flops 25300000768 | bytes 23000000 | tf_op jit(solution)/shard_map/attend_forward/pallas_call | solution.py:640
  269.4 2.6 collective-permute-done.6
  275.7 2.3 constant_dynamic-slice_fusion.12
  277.9 19.8 %collective-permute-done.8.refs_2_ = bf16[256,2048]{1,0:T(8,128)(2,1)S(1)} collective-permute-done((bf16[256,2048]{1,0:T(8,128)(2,1)S(1)}, bf16[256,2048]{1,0:T(8,128)(2,1)S(1)}, u32[]{:S(2)}, u32[]{:S(2)}) %collective-permute-start.8) | collective-permute-done | bytes 1048608 | tf_op jit(solution)/shard_map/ppermute | solution.py:51
  299.0 5.3 after_attention.1
  307.4 23.5 %collective-permute-done.10 = bf16[256,2048]{1,0:T(8,128)(2,1)} collective-permute-done((bf16[256,2048]{1,0:T(8,128)(2,1)}, bf16[256,2048]{1,0:T(8,128)(2,1)}, u32[]{:S(2)}, u32[]{:S(2)}) %collective-permute-start.10) | collective-permute-done | bytes 1048608 | tf_op jit(solution)/shard_map/ppermute | solution.py:51
  340.7 9.6 %collective-permute-done.15 = bf16[128,2048]{1,0:T(8,128)(2,1)S(1)} collective-permute-done((bf16[128,2048]{1,0:T(8,128)(2,1)S(1)}, bf16[128,2048]{1,0:T(8,128)(2,1)S(1)}, u32[]{:S(2)}, u32[]{:S(2)}) %collective-permute-start.15) | collective-permute-done | bytes 524320 | tf_op jit(solution)/shard_map/ppermute | solution.py:51
  354.6 3.3 copy-done.2
  357.9 3.2 convolution_convert_fusion.narrow_ref
  361.0 26.7 %gate_up.1 = (bf16[2048,1024]{1,0:T(8,128)(2,1)}, bf16[2048,1024]{1,0:T(8,128)(2,1)}, bf16[2048,1024]{1,0:T(8,128)(2,1)}) custom-call(bf16[2048,2048]{1,0:T(8,128)(2,1)} %copy-done.2, bf16[2048,1024]{1,0:T(8,128)(2,1)} %all-gather.7.cloned.1.call-done.gate_w_ref, bf16[2048,1024]{1,0:T(8,128)(2,1)} %all-gather.9.cloned.1.call-done.up_w_ref, ...), custom_call_target="tpu_custom_call" | custom-call | flops 28600000512 | bytes 26000000 | tf_op jit(solution)/shard_map/gate_up/pallas_call | solution.py:309
  387.7 10.1 %all-gather.11.cloned.1.call-done.weight_ref.down_ref = bf16[1024,2048]{1,0:T(8,128)(2,1)} async-done(((bf16[256,2048]{1,0:T(8,128)(2,1)}), bf16[1024,2048]{1,0:T(8,128)(2,1)}) %all-gather.11.cloned.1.call-update) | async-done | bytes 4194320 | tf_op jit(solution)/shard_map/all_gather | solution.py:787
  397.8 16.9 %down.1 = (bf16[2048,2048]{1,0:T(8,128)(2,1)}, bf16[2048,16]{1,0:T(8,128)(2,1)}) custom-call(bf16[2048,1024]{1,0:T(8,128)(2,1)} %get-tuple-element.116.gated_ref, bf16[1024,2048]{1,0:T(8,128)(2,1)} %all-gather.11.cloned.1.call-done.weight_ref.down_ref, bf16[16,1024]{1,0:T(8,128)(2,1)} %bitcast.253, ...), custom_call_target="tpu_custom_call" | custom-call | flops 16499999744 | bytes 15000000 | tf_op jit(solution)/shard_map/down/pallas_call | solution.py:341
  414.7 2.9 fusion.101
  429.1 10.6 %collective-permute-done.24 = bf16[128,2048]{1,0:T(8,128)(2,1)S(1)} collective-permute-done((bf16[128,2048]{1,0:T(8,128)(2,1)S(1)}, bf16[128,2048]{1,0:T(8,128)(2,1)S(1)}, u32[]{:S(2)}, u32[]{:S(2)}) %collective-permute-start.24) | collective-permute-done | bytes 524320 | tf_op jit(solution)/shard_map/ppermute | solution.py:51
  444.7 7.8 collective-permute-done.26
  452.4 10.1 %collective-permute-done.25 = bf16[128,2048]{1,0:T(8,128)(2,1)S(1)} collective-permute-done((bf16[128,2048]{1,0:T(8,128)(2,1)S(1)}, bf16[128,2048]{1,0:T(8,128)(2,1)S(1)}, u32[]{:S(2)}, u32[]{:S(2)}) %collective-permute-start.25) | collective-permute-done | bytes 524320 | tf_op jit(solution)/shard_map/ppermute | solution.py:57
  465.7 5.6 after_feed.1
  476.8 18.4 %feed_backward.3 = (bf16[512,2048]{1,0:T(8,128)(2,1)}, bf16[512,32]{1,0:T(8,128)(2,1)}, f32[3,16,1024]{2,1,0:T(8,128)}) custom-call(bf16[512,2048]{1,0:T(8,128)(2,1)} %copy-done.19, bf16[1024,2048]{1,0:T(8,128)(2,1)} %all-gather.11.cloned.1.call-done.weight_ref.down_ref, bf16[2048,1024]{1,0:T(8,128)(2,1)} %all-gather.7.cloned.1.call-done.gate_w_ref, ...), custom_call_target="tpu_custom_call" | custom-call | flops 13200000000 | bytes 12000000 | tf_op jit(solution)/shard_map/feed_backward/pallas_call | solution.py:409
  495.2 2.5 collective-permute-done.33
  502.8 9.4 %collective-permute-done.36 = bf16[128,2048]{1,0:T(8,128)(2,1)S(1)} collective-permute-done((bf16[128,2048]{1,0:T(8,128)(2,1)S(1)}, bf16[128,2048]{1,0:T(8,128)(2,1)S(1)}, u32[]{:S(2)}, u32[]{:S(2)}) %collective-permute-start.36) | collective-permute-done | bytes 524320 | tf_op jit(solution)/shard_map/ppermute | solution.py:51
  520.5 29.4 %feed_backward.5 = (bf16[1024,2048]{1,0:T(8,128)(2,1)}, bf16[1024,32]{1,0:T(8,128)(2,1)}, f32[3,16,1024]{2,1,0:T(8,128)}) custom-call(bf16[1024,2048]{1,0:T(8,128)(2,1)} %constant_dynamic-update-slice_fusion.14.grad_ref, bf16[1024,2048]{1,0:T(8,128)(2,1)} %all-gather.11.cloned.1.call-done.weight_ref.down_ref, ...), custom_call_target="tpu_custom_call" | custom-call | flops 24199999488 | bytes 22000000 | tf_op jit(solution)/shard_map/feed_backward/pallas_call | solution.py:409
  549.9 2.8 fusion.102
  553.2 18.2 %feed_backward.4 = (bf16[512,2048]{1,0:T(8,128)(2,1)}, bf16[512,32]{1,0:T(8,128)(2,1)}, f32[3,16,1024]{2,1,0:T(8,128)}) custom-call(bf16[512,2048]{1,0:T(8,128)(2,1)} %copy-done.16, bf16[1024,2048]{1,0:T(8,128)(2,1)} %all-gather.11.cloned.1.call-done.weight_ref.down_ref, bf16[2048,1024]{1,0:T(8,128)(2,1)} %all-gather.7.cloned.1.call-done.gate_w_ref, ...), custom_call_target="tpu_custom_call" | custom-call | flops 13200000000 | bytes 12000000 | tf_op jit(solution)/shard_map/feed_backward/pallas_call | solution.py:409
  573.8 2.4 add_convert_fusion.6
  581.5 9.7 %collective-permute-done.42 = bf16[128,2048]{1,0:T(8,128)(2,1)S(1)} collective-permute-done((bf16[128,2048]{1,0:T(8,128)(2,1)S(1)}, bf16[128,2048]{1,0:T(8,128)(2,1)S(1)}, u32[]{:S(2)}, u32[]{:S(2)}) %collective-permute-start.42) | collective-permute-done | bytes 524320 | tf_op jit(solution)/shard_map/ppermute | solution.py:51
  595.1 8.9 %collective-permute-done.44 = bf16[128,2048]{1,0:T(8,128)(2,1)S(1)} collective-permute-done((bf16[128,2048]{1,0:T(8,128)(2,1)S(1)}, bf16[128,2048]{1,0:T(8,128)(2,1)S(1)}, u32[]{:S(2)}, u32[]{:S(2)}) %collective-permute-start.44) | collective-permute-done | bytes 524320 | tf_op jit(solution)/shard_map/ppermute | solution.py:57
  603.9 10.5 %collective-permute-done.43 = bf16[128,2048]{1,0:T(8,128)(2,1)S(1)} collective-permute-done((bf16[128,2048]{1,0:T(8,128)(2,1)S(1)}, bf16[128,2048]{1,0:T(8,128)(2,1)S(1)}, u32[]{:S(2)}, u32[]{:S(2)}) %collective-permute-start.43) | collective-permute-done | bytes 524320 | tf_op jit(solution)/shard_map/ppermute | solution.py:57
  616.6 5.9 middle.1
  626.3 2.4 fusion.8
  630.3 5.1 convolution_multiply_fusion
  635.4 11.9 %collective-permute-done.46 = bf16[256,2048]{1,0:T(8,128)(2,1)} collective-permute-done((bf16[256,2048]{1,0:T(8,128)(2,1)}, bf16[256,2048]{1,0:T(8,128)(2,1)}, u32[]{:S(2)}, u32[]{:S(2)}) %collective-permute-start.46) | collective-permute-done | bytes 1048608 | tf_op jit(solution)/shard_map/ppermute | solution.py:51
  654.8 3.3 add_convert_fusion.5
  658.1 12.6 %attend_backward.2 = (f32[2,2,256,512]{3,2,1,0:T(8,128)}, bf16[2,2,256,512]{3,2,1,0:T(8,128)(2,1)}, bf16[2,2,256,512]{3,2,1,0:T(8,128)(2,1)}) custom-call(bf16[2,2,256,512]{3,2,1,0:T(8,128)(2,1)} %bitcast.295, bf16[2,2,256,512]{3,2,1,0:T(8,128)(2,1)} %bitcast.297, bf16[2,2,256,512]{3,2,1,0:T(8,128)(2,1)} %get-tuple-element.110.o_ref, ...), custom_call_target="tpu_custom_call" | custom-call | flops 13200000000 | bytes 12000000 | tf_op jit(solution)/shard_map/attend_backward/pallas_call | solution.py:659
  672.1 19.8 %attend_backward.3 = (f32[2,2,256,512]{3,2,1,0:T(8,128)}, f32[2,2,256,512]{3,2,1,0:T(8,128)}, bf16[2,2,256,512]{3,2,1,0:T(8,128)(2,1)}, f32[2,2,256,512]{3,2,1,0:T(8,128)}, bf16[2,2,256,512]{3,2,1,0:T(8,128)(2,1)}) custom-call(bf16[2,2,256,512]{3,2,1,0:T(8,128)(2,1)} %bitcast.296, bf16[2,2,256,512]{3,2,1,0:T(8,128)(2,1)} %bitcast.298, ...), custom_call_target="tpu_custom_call" | custom-call | flops 22000001024 | bytes 20000000 | tf_op jit(solution)/shard_map/attend_backward/pallas_call | solution.py:659
  698.5 2.5 fusion.19
  705.7 6.1 collective-permute-done.51
  711.9 13.8 %collective-permute-done.55 = bf16[1024,512]{1,0:T(8,128)(2,1)} collective-permute-done((bf16[1024,512]{1,0:T(8,128)(2,1)}, bf16[1024,512]{1,0:T(8,128)(2,1)}, u32[]{:S(2)}, u32[]{:S(2)}) %collective-permute-start.55) | collective-permute-done | bytes 1048608 | tf_op jit(solution)/shard_map/ppermute | solution.py:60
  725.7 2.8 fusion.18
  729.8 18.4 %collective-permute-done.49 = bf16[1024,512]{1,0:T(8,128)(2,1)} collective-permute-done((bf16[1024,512]{1,0:T(8,128)(2,1)}, bf16[1024,512]{1,0:T(8,128)(2,1)}, u32[]{:S(2)}, u32[]{:S(2)}) %collective-permute-start.49) | collective-permute-done | bytes 1048608 | tf_op jit(solution)/shard_map/ppermute | solution.py:60
  748.2 3.0 bitcast_add_fusion.1.dk_ref
  751.2 8.1 rope_backward.1
  761.5 8.4 collective-permute-done.56
  769.9 2.2 fusion.20
  772.1 2.3 collective-permute-done.53
  774.7 7.7 collective-permute-done.54
  790.0 2.7 subtract_convert_fusion.1
  793.0 6.7 fusion.21
  806.0 2.9 add_convert_fusion.4
  810.4 3.0 fusion.2
  813.8 5.6 fusion.118
  822.5 2.7 collective-permute-start.68
  827.2 15.8 %collective-permute-done.60 = f32[96,4,2,128]{3,2,1,0:T(2,128)S(1)} collective-permute-done((f32[96,4,2,128]{3,2,1,0:T(2,128)S(1)}, f32[96,4,2,128]{3,2,1,0:T(2,128)S(1)}, u32[]{:S(2)}, u32[]{:S(2)}) %collective-permute-start.60) | collective-permute-done | bytes 393248 | tf_op jit(solution)/shard_map/ppermute | solution.py:51
  846.4 6.2 collective-permute-done.61
  854.2 2.5 collective-permute-start.64
  857.5 3.6 collective-permute-done.62
  861.1 4.3 collective-permute-done.63
  869.2 4.6 end.1
  (501 shorter events, 168.5 us)
Async XLA Ops:
  7.2 224.2 %all-gather.5.cloned.1.call-start = ((), (), s32[]{:S(2)}) async-start(), calls=%async_computation | async-start | bytes 1310720 | tf_op jit(solution)/shard_map/all_gather | solution.py:787
  7.9 298.5 %all-gather.7.cloned.1.call-start = ((), (), s32[]{:S(2)}) async-start(), calls=%async_computation.1 | async-start | bytes 5242880 | tf_op jit(solution)/shard_map/all_gather | solution.py:787
  156.1 204.9 %all-gather.9.cloned.1.call-start = ((), (), s32[]{:S(2)}) async-start(), calls=%async_computation.2 | async-start | bytes 5242880 | tf_op jit(solution)/shard_map/all_gather | solution.py:787
  194.6 17.7 %collective-permute-start.1 = (f32[1,4096]{1,0:T(1,128)S(1)}, f32[1,4096]{1,0:T(1,128)S(1)}, u32[]{:S(2)}, u32[]{:S(2)}) collective-permute-start(f32[1,4096]{1,0:T(1,128)S(1)} %pad_maximum_fusion.15), channel_id=1, source_target_pairs={{0,4},{4,0},{1,5},{5,1},{2,6},{6,2},{3,7},{7,3},{8,12},{12,8},{9,1... | collective-permute-start | bytes 49160 | tf_op jit(solution)/shard_map/ppermute | solution.py:51
  194.7 18.8 %collective-permute-start.2 = (f32[1,4096]{1,0:T(1,128)S(1)}, f32[1,4096]{1,0:T(1,128)S(1)}, u32[]{:S(2)}, u32[]{:S(2)}) collective-permute-start(f32[1,4096]{1,0:T(1,128)S(1)} %pad_maximum_fusion.15), channel_id=1, source_target_pairs={{0,5},{1,4},{4,1},{5,0},{2,7},{3,6},{6,3},{7,2},{8,13},{9,12},{12,... | collective-permute-start | bytes 49160 | tf_op jit(solution)/shard_map/ppermute | solution.py:54
  194.8 19.6 %collective-permute-start = (f32[1,4096]{1,0:T(1,128)S(1)}, f32[1,4096]{1,0:T(1,128)S(1)}, u32[]{:S(2)}, u32[]{:S(2)}) collective-permute-start(f32[1,4096]{1,0:T(1,128)S(1)} %pad_maximum_fusion.15), channel_id=1, source_target_pairs={{0,1},{1,0},{2,3},{3,2},{4,5},{5,4},{6,7},{7,6},{8,9},{9,8},{10,11... | collective-permute-start | bytes 49160 | tf_op jit(solution)/shard_map/ppermute | solution.py:48
  196.9 201.0 %all-gather.11.cloned.1.call-start = ((), (), s32[]{:S(2)}) async-start(), calls=%async_computation.3 | async-start | bytes 5242880 | tf_op jit(solution)/shard_map/all_gather | solution.py:787
  231.4 34.4 %collective-permute-start.5 = (bf16[256,2048]{1,0:T(8,128)(2,1)}, bf16[256,2048]{1,0:T(8,128)(2,1)S(1)}, u32[]{:S(2)}, u32[]{:S(2)}) collective-permute-start(bf16[256,2048]{1,0:T(8,128)(2,1)} %all-gather.5.cloned.1.call-done), channel_id=1, source_target_pairs={{1,2},{2,1},{5,6},{6,5},{9,10},{10,9},{13,14},{14,13},{17,18},{18,... | collective-permute-start | bytes 3145736 | tf_op jit(solution)/shard_map/ppermute | solution.py:806
  232.1 33.7 %collective-permute-start.4 = (bf16[256,2048]{1,0:T(8,128)(2,1)}, bf16[256,2048]{1,0:T(8,128)(2,1)S(1)}, u32[]{:S(2)}, u32[]{:S(2)}) collective-permute-start(bf16[256,2048]{1,0:T(8,128)(2,1)} %all-gather.5.cloned.1.call-done), channel_id=1, source_target_pairs={{1,0},{2,3},{5,4},{6,7},{9,8},{10,11},{13,12},{14,15},{17,16},{18,... | collective-permute-start | bytes 3145736 | tf_op jit(solution)/shard_map/ppermute | solution.py:806
  233.4 32.4 %collective-permute-start.3 = (bf16[256,2048]{1,0:T(8,128)(2,1)}, bf16[256,2048]{1,0:T(8,128)(2,1)S(1)}, u32[]{:S(2)}, u32[]{:S(2)}) collective-permute-start(bf16[256,2048]{1,0:T(8,128)(2,1)} %all-gather.5.cloned.1.call-done), channel_id=1, source_target_pairs={{0,2},{3,1},{4,6},{7,5},{8,10},{11,9},{12,14},{15,13},{16,18},{19,... | collective-permute-start | bytes 3145736 | tf_op jit(solution)/shard_map/ppermute | solution.py:806
  272.4 25.3 %collective-permute-start.8 = (bf16[256,2048]{1,0:T(8,128)(2,1)S(1)}, bf16[256,2048]{1,0:T(8,128)(2,1)S(1)}, u32[]{:S(2)}, u32[]{:S(2)}) collective-permute-start(bf16[256,2048]{1,0:T(8,128)(2,1)S(1)} %add_convert_fusion.12), channel_id=1, source_target_pairs={{0,4},{4,0},{1,5},{5,1},{2,6},{6,2},{3,7},{7,3},{8,12},{12,8},{9,1... | collective-permute-start | bytes 3145736 | tf_op jit(solution)/shard_map/ppermute | solution.py:51
  275.6 22.1 %collective-permute-start.7 = (bf16[256,2048]{1,0:T(8,128)(2,1)S(1)}, bf16[256,2048]{1,0:T(8,128)(2,1)S(1)}, u32[]{:S(2)}, u32[]{:S(2)}) collective-permute-start(bf16[256,2048]{1,0:T(8,128)(2,1)S(1)} %slice.483), channel_id=1, source_target_pairs={{0,1},{1,0},{2,3},{3,2},{4,5},{5,4},{6,7},{7,6},{8,9},{9,8},{10,11... | collective-permute-start | bytes 3145736 | tf_op jit(solution)/shard_map/ppermute | solution.py:48
  304.3 31.5 %collective-permute-start.12 = (bf16[256,2048]{1,0:T(8,128)(2,1)}, bf16[256,2048]{1,0:T(8,128)(2,1)S(1)}, u32[]{:S(2)}, u32[]{:S(2)}) collective-permute-start(bf16[256,2048]{1,0:T(8,128)(2,1)} %get-tuple-element.113), channel_id=1, source_target_pairs={{0,2},{2,0},{1,3},{3,1},{4,6},{6,4},{5,7},{7,5},{8,10},{10,8},{9,1... | collective-permute-start | bytes 3145736 | tf_op jit(solution)/shard_map/ppermute | solution.py:57
  306.1 24.8 %collective-permute-start.10 = (bf16[256,2048]{1,0:T(8,128)(2,1)}, bf16[256,2048]{1,0:T(8,128)(2,1)}, u32[]{:S(2)}, u32[]{:S(2)}) collective-permute-start(bf16[256,2048]{1,0:T(8,128)(2,1)} %get-tuple-element.113), channel_id=1, source_target_pairs={{0,4},{4,0},{1,5},{5,1},{2,6},{6,2},{3,7},{7,3},{8,12},{12,8},{9,1... | collective-permute-start | bytes 3145736 | tf_op jit(solution)/shard_map/ppermute | solution.py:51
  306.4 31.7 %collective-permute-start.9 = (bf16[256,2048]{1,0:T(8,128)(2,1)}, bf16[256,2048]{1,0:T(8,128)(2,1)}, u32[]{:S(2)}, u32[]{:S(2)}) collective-permute-start(bf16[256,2048]{1,0:T(8,128)(2,1)} %get-tuple-element.113), channel_id=1, source_target_pairs={{0,1},{1,0},{2,3},{3,2},{4,5},{5,4},{6,7},{7,6},{8,9},{9,8},{10,11... | collective-permute-start | bytes 3145736 | tf_op jit(solution)/shard_map/ppermute | solution.py:48
  330.9 21.0 %collective-permute-start.11 = (bf16[256,2048]{1,0:T(8,128)(2,1)}, bf16[256,2048]{1,0:T(8,128)(2,1)}, u32[]{:S(2)}, u32[]{:S(2)}) collective-permute-start(bf16[256,2048]{1,0:T(8,128)(2,1)} %collective-permute-done.10), channel_id=1, source_target_pairs={{0,1},{1,0},{2,3},{3,2},{4,5},{5,4},{6,7},{7,6},{8,9},{9,8},{10,11... | collective-permute-start | bytes 3145736 | tf_op jit(solution)/shard_map/ppermute | solution.py:48
  335.9 14.4 %collective-permute-start.15 = (bf16[128,2048]{1,0:T(8,128)(2,1)S(1)}, bf16[128,2048]{1,0:T(8,128)(2,1)S(1)}, u32[]{:S(2)}, u32[]{:S(2)}) collective-permute-start(bf16[128,2048]{1,0:T(8,128)(2,1)S(1)} %slice.485), channel_id=1, source_target_pairs={{0,4},{4,0},{1,5},{5,1},{2,6},{6,2},{3,7},{7,3},{8,12},{12,8},{9,1... | collective-permute-start | bytes 1572872 | tf_op jit(solution)/shard_map/ppermute | solution.py:51
  337.5 14.1 %collective-permute-start.14 = (bf16[128,2048]{1,0:T(8,128)(2,1)S(1)}, bf16[128,2048]{1,0:T(8,128)(2,1)S(1)}, u32[]{:S(2)}, u32[]{:S(2)}) collective-permute-start(bf16[128,2048]{1,0:T(8,128)(2,1)S(1)} %slice.484), channel_id=1, source_target_pairs={{0,2},{2,0},{1,3},{3,1},{4,6},{6,4},{5,7},{7,5},{8,10},{10,8},{9,1... | collective-permute-start | bytes 1572872 | tf_op jit(solution)/shard_map/ppermute | solution.py:57
  338.0 15.2 %collective-permute-start.13 = (bf16[256,2048]{1,0:T(8,128)(2,1)S(1)}, bf16[256,2048]{1,0:T(8,128)(2,1)S(1)}, u32[]{:S(2)}, u32[]{:S(2)}) collective-permute-start(bf16[256,2048]{1,0:T(8,128)(2,1)S(1)} %collective-permute-done.12), channel_id=1, source_target_pairs={{0,1},{1,0},{2,3},{3,2},{4,5},{5,4},{6,7},{7,6},{8,9},{9,8},{10,11... | collective-permute-start | bytes 3145736 | tf_op jit(solution)/shard_map/ppermute | solution.py:48
  424.8 14.8 %collective-permute-start.24 = (bf16[128,2048]{1,0:T(8,128)(2,1)S(1)}, bf16[128,2048]{1,0:T(8,128)(2,1)S(1)}, u32[]{:S(2)}, u32[]{:S(2)}) collective-permute-start(bf16[128,2048]{1,0:T(8,128)(2,1)S(1)} %get-tuple-element.175), channel_id=1, source_target_pairs={{0,4},{4,0},{1,5},{5,1},{2,6},{6,2},{3,7},{7,3},{8,12},{12,8},{9,1... | collective-permute-start | bytes 1572872 | tf_op jit(solution)/shard_map/ppermute | solution.py:51
  426.4 15.0 %collective-permute-start.21 = (bf16[128,2048]{1,0:T(8,128)(2,1)S(1)}, bf16[128,2048]{1,0:T(8,128)(2,1)S(1)}, u32[]{:S(2)}, u32[]{:S(2)}) collective-permute-start(bf16[128,2048]{1,0:T(8,128)(2,1)S(1)} %get-tuple-element.176), channel_id=1, source_target_pairs={{0,2},{2,0},{1,3},{3,1},{4,6},{6,4},{5,7},{7,5},{8,10},{10,8},{9,1... | collective-permute-start | bytes 1572872 | tf_op jit(solution)/shard_map/ppermute | solution.py:57
  427.9 36.8 %collective-permute-start.17 = (bf16[256,2048]{1,0:T(8,128)(2,1)S(1)}, bf16[256,2048]{1,0:T(8,128)(2,1)S(1)}, u32[]{:S(2)}, u32[]{:S(2)}) collective-permute-start(bf16[256,2048]{1,0:T(8,128)(2,1)S(1)} %get-tuple-element.164), channel_id=1, source_target_pairs={{0,1},{1,0},{2,3},{3,2},{4,5},{5,4},{6,7},{7,6},{8,9},{9,8},{10,11... | collective-permute-start | bytes 3145736 | tf_op jit(solution)/shard_map/ppermute | solution.py:48
  428.0 35.7 %collective-permute-start.19 = (bf16[128,2048]{1,0:T(8,128)(2,1)S(1)}, bf16[128,2048]{1,0:T(8,128)(2,1)S(1)}, u32[]{:S(2)}, u32[]{:S(2)}) collective-permute-start(bf16[128,2048]{1,0:T(8,128)(2,1)S(1)} %slice.486), channel_id=1, source_target_pairs={{0,4},{4,0},{1,5},{5,1},{2,6},{6,2},{3,7},{7,3},{8,12},{12,8},{9,1... | collective-permute-start | bytes 1572872 | tf_op jit(solution)/shard_map/ppermute | solution.py:51
  428.6 23.9 %collective-permute-start.26 = (bf16[128,2048]{1,0:T(8,128)(2,1)S(1)}, bf16[128,2048]{1,0:T(8,128)(2,1)S(1)}, u32[]{:S(2)}, u32[]{:S(2)}) collective-permute-start(bf16[128,2048]{1,0:T(8,128)(2,1)S(1)} %slice.491), channel_id=1, source_target_pairs={{0,2},{2,0},{1,3},{3,1},{4,6},{6,4},{5,7},{7,5},{8,10},{10,8},{9,1... | collective-permute-start | bytes 1572872 | tf_op jit(solution)/shard_map/ppermute | solution.py:57
  439.8 22.8 %collective-permute-start.25 = (bf16[128,2048]{1,0:T(8,128)(2,1)S(1)}, bf16[128,2048]{1,0:T(8,128)(2,1)S(1)}, u32[]{:S(2)}, u32[]{:S(2)}) collective-permute-start(bf16[128,2048]{1,0:T(8,128)(2,1)S(1)} %add_convert_fusion.15), channel_id=1, source_target_pairs={{0,2},{2,0},{1,3},{3,1},{4,6},{6,4},{5,7},{7,5},{8,10},{10,8},{9,1... | collective-permute-start | bytes 1572872 | tf_op jit(solution)/shard_map/ppermute | solution.py:57
  441.5 22.1 %collective-permute-start.22 = (bf16[128,2048]{1,0:T(8,128)(2,1)S(1)}, bf16[128,2048]{1,0:T(8,128)(2,1)S(1)}, u32[]{:S(2)}, u32[]{:S(2)}) collective-permute-start(bf16[128,2048]{1,0:T(8,128)(2,1)S(1)} %add_convert_fusion.16), channel_id=1, source_target_pairs={{0,4},{4,0},{1,5},{5,1},{2,6},{6,2},{3,7},{7,3},{8,12},{12,8},{9,1... | collective-permute-start | bytes 1572872 | tf_op jit(solution)/shard_map/ppermute | solution.py:51
  471.9 25.8 %collective-permute-start.33 = (bf16[256,2048]{1,0:T(8,128)(2,1)}, bf16[256,2048]{1,0:T(8,128)(2,1)S(1)}, u32[]{:S(2)}, u32[]{:S(2)}) collective-permute-start(bf16[256,2048]{1,0:T(8,128)(2,1)} %get-tuple-element.121), channel_id=1, source_target_pairs={{0,2},{2,0},{1,3},{3,1},{4,6},{6,4},{5,7},{7,5},{8,10},{10,8},{9,1... | collective-permute-start | bytes 3145736 | tf_op jit(solution)/shard_map/ppermute | solution.py:57
  473.4 25.5 %collective-permute-start.29 = (bf16[256,2048]{1,0:T(8,128)(2,1)}, bf16[256,2048]{1,0:T(8,128)(2,1)S(1)}, u32[]{:S(2)}, u32[]{:S(2)}) collective-permute-start(bf16[256,2048]{1,0:T(8,128)(2,1)} %get-tuple-element.121), channel_id=1, source_target_pairs={{0,4},{4,0},{1,5},{5,1},{2,6},{6,2},{3,7},{7,3},{8,12},{12,8},{9,1... | collective-permute-start | bytes 3145736 | tf_op jit(solution)/shard_map/ppermute | solution.py:51
  497.7 17.6 %collective-permute-start.34 = (bf16[256,2048]{1,0:T(8,128)(2,1)S(1)}, bf16[256,2048]{1,0:T(8,128)(2,1)S(1)}, u32[]{:S(2)}, u32[]{:S(2)}) collective-permute-start(bf16[256,2048]{1,0:T(8,128)(2,1)S(1)} %collective-permute-done.33), channel_id=1, source_target_pairs={{0,1},{1,0},{2,3},{3,2},{4,5},{5,4},{6,7},{7,6},{8,9},{9,8},{10,11... | collective-permute-start | bytes 3145736 | tf_op jit(solution)/shard_map/ppermute | solution.py:48
  498.9 13.3 %collective-permute-start.36 = (bf16[128,2048]{1,0:T(8,128)(2,1)S(1)}, bf16[128,2048]{1,0:T(8,128)(2,1)S(1)}, u32[]{:S(2)}, u32[]{:S(2)}) collective-permute-start(bf16[128,2048]{1,0:T(8,128)(2,1)S(1)} %slice.413), channel_id=1, source_target_pairs={{0,4},{4,0},{1,5},{5,1},{2,6},{6,2},{3,7},{7,3},{8,12},{12,8},{9,1... | collective-permute-start | bytes 1572872 | tf_op jit(solution)/shard_map/ppermute | solution.py:51
  499.6 13.0 %collective-permute-start.35 = (bf16[128,2048]{1,0:T(8,128)(2,1)S(1)}, bf16[128,2048]{1,0:T(8,128)(2,1)S(1)}, u32[]{:S(2)}, u32[]{:S(2)}) collective-permute-start(bf16[128,2048]{1,0:T(8,128)(2,1)S(1)} %slice.412), channel_id=1, source_target_pairs={{0,2},{2,0},{1,3},{3,1},{4,6},{6,4},{5,7},{7,5},{8,10},{10,8},{9,1... | collective-permute-start | bytes 1572872 | tf_op jit(solution)/shard_map/ppermute | solution.py:57
  502.7 15.6 %collective-permute-start.30 = (bf16[256,2048]{1,0:T(8,128)(2,1)S(1)}, bf16[256,2048]{1,0:T(8,128)(2,1)S(1)}, u32[]{:S(2)}, u32[]{:S(2)}) collective-permute-start(bf16[256,2048]{1,0:T(8,128)(2,1)S(1)} %collective-permute-done.29), channel_id=1, source_target_pairs={{0,1},{1,0},{2,3},{3,2},{4,5},{5,4},{6,7},{7,6},{8,9},{9,8},{10,11... | collective-permute-start | bytes 3145736 | tf_op jit(solution)/shard_map/ppermute | solution.py:48
  512.6 5.8 collective-permute-start.37
  514.8 101.8 %collective-permute-start.28 = (bf16[256,2048]{1,0:T(8,128)(2,1)}, bf16[256,2048]{1,0:T(8,128)(2,1)}, u32[]{:S(2)}, u32[]{:S(2)}) collective-permute-start(bf16[256,2048]{1,0:T(8,128)(2,1)} %slice.407), channel_id=1, source_target_pairs={{0,1},{1,0},{2,3},{3,2},{4,5},{5,4},{6,7},{7,6},{8,9},{9,8},{10,11... | collective-permute-start | bytes 3145736 | tf_op jit(solution)/shard_map/ppermute | solution.py:48
  552.7 20.2 %collective-permute-start.41 = (bf16[256,2048]{1,0:T(8,128)(2,1)}, bf16[256,2048]{1,0:T(8,128)(2,1)S(1)}, u32[]{:S(2)}, u32[]{:S(2)}) collective-permute-start(bf16[256,2048]{1,0:T(8,128)(2,1)} %get-tuple-element.169), channel_id=1, source_target_pairs={{0,1},{1,0},{2,3},{3,2},{4,5},{5,4},{6,7},{7,6},{8,9},{9,8},{10,11... | collective-permute-start | bytes 3145736 | tf_op jit(solution)/shard_map/ppermute | solution.py:48
  552.7 21.1 %collective-permute-start.38 = (bf16[256,2048]{1,0:T(8,128)(2,1)S(1)}, bf16[256,2048]{1,0:T(8,128)(2,1)}, u32[]{:S(2)}, u32[]{:S(2)}) collective-permute-start(bf16[256,2048]{1,0:T(8,128)(2,1)S(1)} %get-tuple-element.170), channel_id=1, source_target_pairs={{0,1},{1,0},{2,3},{3,2},{4,5},{5,4},{6,7},{7,6},{8,9},{9,8},{10,11... | collective-permute-start | bytes 3145736 | tf_op jit(solution)/shard_map/ppermute | solution.py:48
  572.8 6.6 collective-permute-start.31
  576.4 14.8 %collective-permute-start.42 = (bf16[128,2048]{1,0:T(8,128)(2,1)S(1)}, bf16[128,2048]{1,0:T(8,128)(2,1)S(1)}, u32[]{:S(2)}, u32[]{:S(2)}) collective-permute-start(bf16[128,2048]{1,0:T(8,128)(2,1)S(1)} %get-tuple-element.173), channel_id=1, source_target_pairs={{0,4},{4,0},{1,5},{5,1},{2,6},{6,2},{3,7},{7,3},{8,12},{12,8},{9,1... | collective-permute-start | bytes 1572872 | tf_op jit(solution)/shard_map/ppermute | solution.py:51
  577.9 14.9 %collective-permute-start.39 = (bf16[128,2048]{1,0:T(8,128)(2,1)S(1)}, bf16[128,2048]{1,0:T(8,128)(2,1)S(1)}, u32[]{:S(2)}, u32[]{:S(2)}) collective-permute-start(bf16[128,2048]{1,0:T(8,128)(2,1)S(1)} %get-tuple-element.174), channel_id=1, source_target_pairs={{0,2},{2,0},{1,3},{3,1},{4,6},{6,4},{5,7},{7,5},{8,10},{10,8},{9,1... | collective-permute-start | bytes 1572872 | tf_op jit(solution)/shard_map/ppermute | solution.py:57
  579.9 35.7 %collective-permute-start.32 = (bf16[128,2048]{1,0:T(8,128)(2,1)S(1)}, bf16[128,2048]{1,0:T(8,128)(2,1)S(1)}, u32[]{:S(2)}, u32[]{:S(2)}) collective-permute-start(bf16[128,2048]{1,0:T(8,128)(2,1)S(1)} %slice.492), channel_id=1, source_target_pairs={{0,4},{4,0},{1,5},{5,1},{2,6},{6,2},{3,7},{7,3},{8,12},{12,8},{9,1... | collective-permute-start | bytes 1572872 | tf_op jit(solution)/shard_map/ppermute | solution.py:51
  580.5 23.4 %collective-permute-start.44 = (bf16[128,2048]{1,0:T(8,128)(2,1)S(1)}, bf16[128,2048]{1,0:T(8,128)(2,1)S(1)}, u32[]{:S(2)}, u32[]{:S(2)}) collective-permute-start(bf16[128,2048]{1,0:T(8,128)(2,1)S(1)} %slice.497), channel_id=1, source_target_pairs={{0,2},{2,0},{1,3},{3,1},{4,6},{6,4},{5,7},{7,5},{8,10},{10,8},{9,1... | collective-permute-start | bytes 1572872 | tf_op jit(solution)/shard_map/ppermute | solution.py:57
  591.3 23.2 %collective-permute-start.43 = (bf16[128,2048]{1,0:T(8,128)(2,1)S(1)}, bf16[128,2048]{1,0:T(8,128)(2,1)S(1)}, u32[]{:S(2)}, u32[]{:S(2)}) collective-permute-start(bf16[128,2048]{1,0:T(8,128)(2,1)S(1)} %add_convert_fusion.13), channel_id=1, source_target_pairs={{0,2},{2,0},{1,3},{3,1},{4,6},{6,4},{5,7},{7,5},{8,10},{10,8},{9,1... | collective-permute-start | bytes 1572872 | tf_op jit(solution)/shard_map/ppermute | solution.py:57
  593.0 22.5 %collective-permute-start.40 = (bf16[128,2048]{1,0:T(8,128)(2,1)S(1)}, bf16[128,2048]{1,0:T(8,128)(2,1)S(1)}, u32[]{:S(2)}, u32[]{:S(2)}) collective-permute-start(bf16[128,2048]{1,0:T(8,128)(2,1)S(1)} %add_convert_fusion.14), channel_id=1, source_target_pairs={{0,4},{4,0},{1,5},{5,1},{2,6},{6,2},{3,7},{7,3},{8,12},{12,8},{9,1... | collective-permute-start | bytes 1572872 | tf_op jit(solution)/shard_map/ppermute | solution.py:51
  622.5 24.8 %collective-permute-start.46 = (bf16[256,2048]{1,0:T(8,128)(2,1)}, bf16[256,2048]{1,0:T(8,128)(2,1)}, u32[]{:S(2)}, u32[]{:S(2)}) collective-permute-start(bf16[256,2048]{1,0:T(8,128)(2,1)} %get-tuple-element.130), channel_id=1, source_target_pairs={{0,4},{4,0},{1,5},{5,1},{2,6},{6,2},{3,7},{7,3},{8,12},{12,8},{9,1... | collective-permute-start | bytes 3145736 | tf_op jit(solution)/shard_map/ppermute | solution.py:51
  630.2 18.8 %collective-permute-start.45 = (bf16[256,2048]{1,0:T(8,128)(2,1)S(1)}, bf16[256,2048]{1,0:T(8,128)(2,1)S(1)}, u32[]{:S(2)}, u32[]{:S(2)}) collective-permute-start(bf16[256,2048]{1,0:T(8,128)(2,1)S(1)} %copy-done.33), channel_id=1, source_target_pairs={{0,1},{1,0},{2,3},{3,2},{4,5},{5,4},{6,7},{7,6},{8,9},{9,8},{10,11... | collective-permute-start | bytes 3145736 | tf_op jit(solution)/shard_map/ppermute | solution.py:48
  670.8 27.6 %collective-permute-start.48 = (bf16[1024,512]{1,0:T(8,128)(2,1)}, bf16[1024,512]{1,0:T(8,128)(2,1)S(1)}, u32[]{:S(2)}, u32[]{:S(2)}) collective-permute-start(bf16[1024,512]{1,0:T(8,128)(2,1)} %bitcast.272), channel_id=1, source_target_pairs={{8,0},{16,8},{24,16},{9,1},{17,9},{25,17},{10,2},{18,10},{26,18},{... | collective-permute-start | bytes 3145736 | tf_op jit(solution)/shard_map/ppermute | solution.py:60
  693.1 10.2 %collective-permute-start.50 = (f32[80,4,2,128]{3,2,1,0:T(2,128)S(1)}, f32[80,4,2,128]{3,2,1,0:T(2,128)S(1)}, u32[]{:S(2)}, u32[]{:S(2)}) collective-permute-start(f32[80,4,2,128]{3,2,1,0:T(2,128)S(1)} %dynamic-slice_bitcast_fusion), channel_id=1, source_target_pairs={{0,4},{4,0},{1,5},{5,1},{2,6},{6,2},{3,7},{7,3},{8,12},{12,8},{9,1... | collective-permute-start | bytes 983048 | tf_op jit(solution)/shard_map/ppermute | solution.py:51
  696.9 28.8 %collective-permute-start.55 = (bf16[1024,512]{1,0:T(8,128)(2,1)}, bf16[1024,512]{1,0:T(8,128)(2,1)}, u32[]{:S(2)}, u32[]{:S(2)}) collective-permute-start(bf16[1024,512]{1,0:T(8,128)(2,1)} %bitcast.271), channel_id=1, source_target_pairs={{8,0},{16,8},{24,16},{9,1},{17,9},{25,17},{10,2},{18,10},{26,18},{... | collective-permute-start | bytes 3145736 | tf_op jit(solution)/shard_map/ppermute | solution.py:60
  701.0 47.2 %collective-permute-start.49 = (bf16[1024,512]{1,0:T(8,128)(2,1)}, bf16[1024,512]{1,0:T(8,128)(2,1)}, u32[]{:S(2)}, u32[]{:S(2)}) collective-permute-start(bf16[1024,512]{1,0:T(8,128)(2,1)} %fusion.19), channel_id=1, source_target_pairs={{8,0},{16,8},{24,16},{9,1},{17,9},{25,17},{10,2},{18,10},{26,18},{... | collective-permute-start | bytes 3145736 | tf_op jit(solution)/shard_map/ppermute | solution.py:60
  703.9 8.0 collective-permute-start.51
  728.5 41.4 %collective-permute-start.56 = (bf16[1024,512]{1,0:T(8,128)(2,1)}, bf16[1024,512]{1,0:T(8,128)(2,1)}, u32[]{:S(2)}, u32[]{:S(2)}) collective-permute-start(bf16[1024,512]{1,0:T(8,128)(2,1)} %fusion.18), channel_id=1, source_target_pairs={{8,0},{16,8},{24,16},{9,1},{17,9},{25,17},{10,2},{18,10},{26,18},{... | collective-permute-start | bytes 3145736 | tf_op jit(solution)/shard_map/ppermute | solution.py:60
  759.4 15.1 %collective-permute-start.53 = (f32[2,1024]{0,1:T(8,128)}, f32[2,1024]{0,1:T(8,128)S(1)}, u32[]{:S(2)}, u32[]{:S(2)}) collective-permute-start(f32[2,1024]{0,1:T(8,128)} %bitcast.220), channel_id=1, source_target_pairs={{0,4},{4,0},{1,5},{5,1},{2,6},{6,2},{3,7},{7,3},{8,12},{12,8},{9,1... | collective-permute-start | bytes 24584 | tf_op jit(solution)/shard_map/ppermute | solution.py:51
  760.9 21.5 %collective-permute-start.54 = (f32[2,1024]{0,1:T(8,128)}, f32[2,1024]{0,1:T(8,128)S(1)}, u32[]{:S(2)}, u32[]{:S(2)}) collective-permute-start(f32[2,1024]{0,1:T(8,128)} %bitcast.221), channel_id=1, source_target_pairs={{0,5},{1,4},{4,1},{5,0},{2,7},{3,6},{6,3},{7,2},{8,13},{9,12},{12,... | collective-permute-start | bytes 24584 | tf_op jit(solution)/shard_map/ppermute | solution.py:54
  760.9 22.3 %collective-permute-start.52 = (f32[2,1024]{0,1:T(8,128)}, f32[2,1024]{0,1:T(8,128)S(1)}, u32[]{:S(2)}, u32[]{:S(2)}) collective-permute-start(f32[2,1024]{0,1:T(8,128)} %bitcast.222), channel_id=1, source_target_pairs={{0,1},{1,0},{2,3},{3,2},{4,5},{5,4},{6,7},{7,6},{8,9},{9,8},{10,11... | collective-permute-start | bytes 24584 | tf_op jit(solution)/shard_map/ppermute | solution.py:48
  808.9 60.3 %collective-permute-start.59 = (bf16[256,2048]{1,0:T(8,128)(2,1)}, bf16[256,2048]{1,0:T(8,128)(2,1)}, u32[]{:S(2)}, u32[]{:S(2)}) collective-permute-start(bf16[256,2048]{1,0:T(8,128)(2,1)} %add_convert_fusion.4), channel_id=1, source_target_pairs={{0,4},{4,0},{1,5},{5,1},{2,6},{6,2},{3,7},{7,3},{8,12},{12,8},{9,1... | collective-permute-start | bytes 3145736 | tf_op jit(solution)/shard_map/ppermute | solution.py:51
  819.6 23.4 %collective-permute-start.60 = (f32[96,4,2,128]{3,2,1,0:T(2,128)S(1)}, f32[96,4,2,128]{3,2,1,0:T(2,128)S(1)}, u32[]{:S(2)}, u32[]{:S(2)}) collective-permute-start(f32[96,4,2,128]{3,2,1,0:T(2,128)S(1)} %fusion.30), channel_id=1, source_target_pairs={{0,4},{4,0},{1,5},{5,1},{2,6},{6,2},{3,7},{7,3},{8,12},{12,8},{9,1... | collective-permute-start | bytes 1179656 | tf_op jit(solution)/shard_map/ppermute | solution.py:51
  821.0 22.8 %collective-permute-start.66 = (f32[48,256]{1,0:T(8,128)S(1)}, f32[48,256]{1,0:T(8,128)S(1)}, u32[]{:S(2)}, u32[]{:S(2)}) collective-permute-start(f32[48,256]{1,0:T(8,128)S(1)} %bitcast.250), channel_id=1, source_target_pairs={{0,8},{8,16},{16,24},{24,0},{1,9},{9,17},{17,25},{25,1},{2,10},{10... | collective-permute-start | bytes 147464 | tf_op jit(solution)/shard_map/ppermute | solution.py:63
  822.5 22.9 %collective-permute-start.67 = (f32[48,256]{1,0:T(8,128)S(1)}, f32[48,256]{1,0:T(8,128)}, u32[]{:S(2)}, u32[]{:S(2)}) collective-permute-start(f32[48,256]{1,0:T(8,128)S(1)} %bitcast.249), channel_id=1, source_target_pairs={{0,16},{8,24},{16,0},{24,8},{1,17},{9,25},{17,1},{25,9},{2,18},{10... | collective-permute-start | bytes 147464 | tf_op jit(solution)/shard_map/ppermute | solution.py:63
  822.5 22.9 %collective-permute-start.68 = (f32[48,256]{1,0:T(8,128)S(1)}, f32[48,256]{1,0:T(8,128)}, u32[]{:S(2)}, u32[]{:S(2)}) collective-permute-start(f32[48,256]{1,0:T(8,128)S(1)} %bitcast.248), channel_id=1, source_target_pairs={{0,24},{8,0},{16,8},{24,16},{1,25},{9,1},{17,9},{25,17},{2,26},{10... | collective-permute-start | bytes 147464 | tf_op jit(solution)/shard_map/ppermute | solution.py:63
  843.0 26.2 %collective-permute-start.58 = (bf16[256,2048]{1,0:T(8,128)(2,1)}, bf16[256,2048]{1,0:T(8,128)(2,1)}, u32[]{:S(2)}, u32[]{:S(2)}) collective-permute-start(bf16[256,2048]{1,0:T(8,128)(2,1)} %slice.522), channel_id=1, source_target_pairs={{0,1},{1,0},{2,3},{3,2},{4,5},{5,4},{6,7},{7,6},{8,9},{9,8},{10,11... | collective-permute-start | bytes 3145736 | tf_op jit(solution)/shard_map/ppermute | solution.py:48
  843.8 8.8 collective-permute-start.61
  852.8 8.3 collective-permute-start.62
  854.2 11.2 %collective-permute-start.63 = (f32[176,128]{0,1:T(8,128)S(1)}, f32[176,128]{0,1:T(8,128)S(1)}, u32[]{:S(2)}, u32[]{:S(2)}) collective-permute-start(f32[176,128]{0,1:T(8,128)S(1)} %get-tuple-element.180), channel_id=1, source_target_pairs={{0,16},{8,24},{16,0},{24,8},{1,17},{9,25},{17,1},{25,9},{2,18},{10... | collective-permute-start | bytes 270344 | tf_op jit(solution)/shard_map/ppermute | solution.py:63
  854.2 11.2 %collective-permute-start.64 = (f32[176,128]{0,1:T(8,128)S(1)}, f32[176,128]{0,1:T(8,128)S(1)}, u32[]{:S(2)}, u32[]{:S(2)}) collective-permute-start(f32[176,128]{0,1:T(8,128)S(1)} %get-tuple-element.181), channel_id=1, source_target_pairs={{0,24},{8,0},{16,8},{24,16},{1,25},{9,1},{17,9},{25,17},{2,26},{10... | collective-permute-start | bytes 270344 | tf_op jit(solution)/shard_map/ppermute | solution.py:63
  (84 other events, 1076.6 us)
Sparse Core Ops, SparseCore 0:
  9.6 47.5 all-gather.4
  156.2 79.9 all-gather.6
  237.8 79.2 all-gather.8
  318.5 79.2 all-gather.10

commit v3 on v2

--- a/solution.py
+++ b/solution.py
@@ -121,6 +121,30 @@
 
 def after(value, *others):
     return lax.optimization_barrier((value,) + others)[0]
+
+
+class Copies:
+    def __init__(self, send_sem, recv_sem):
+        self.sems, self.used, self.all = (send_sem, recv_sem), 0, []
+
+    def remote(self, src, dst, device):
+        k = self.used
+        self.used += 1
+        copy = pltpu.make_async_remote_copy(
+            src_ref=src,
+            dst_ref=dst,
+            send_sem=self.sems[0].at[k],
+            recv_sem=self.sems[1].at[k],
+            device_id=device,
+            device_id_type=pl.DeviceIdType.MESH,
+        )
+        copy.start()
+        self.all.append(copy)
+        return copy
+
+    def finish(self):
+        for copy in self.all:
+            copy.wait_send()
 
 
 def pack_kernel(count, width, offsets, turns, spot_ref, *refs):
@@ -324,117 +348,6 @@
     )(x, gate_w, up_w, narrow, maps)
 
 
-def down_kernel(gated_ref, weight_ref, in_maps_ref, out_maps_ref, feed_ref, narrow_ref):
-    @pl.when(pl.program_id(0) == 0)
-    def _():
-        narrow_ref[...] = dot_nt(gated_ref[...], in_maps_ref[...]).astype(BF)
-
-    feed = dot(gated_ref[...], weight_ref[...]) + SCALE_ADAPT * dot(narrow_ref[...], out_maps_ref[...])
-    feed_ref[...] = feed.astype(BF)
-
-
-def down(gated, weight, in_maps, out_maps):
-    rows, hidden = gated.shape
-    width = weight.shape[1]
-    rank = in_maps.shape[0]
-    tile = 512
-    return pl.pallas_call(
-        down_kernel,
-        grid=(width // tile,),
-        in_specs=[
-            pl.BlockSpec((rows, hidden), lambda s: (0, 0)),
-            pl.BlockSpec((hidden, tile), lambda s: (0, s)),
-            pl.BlockSpec(in_maps.shape, lambda s: (0, 0)),
-            pl.BlockSpec((rank, tile), lambda s: (0, s)),
-        ],
-        out_specs=[pl.BlockSpec((rows, tile), lambda s: (0, s)), pl.BlockSpec((rows, rank), lambda s: (0, 0))],
-        out_shape=[jax.ShapeDtypeStruct((rows, width), BF), jax.ShapeDtypeStruct((rows, rank), BF)],
-        compiler_params=pltpu.CompilerParams(vmem_limit_bytes=VMEM_BYTES),
-        name="down",
-        cost_estimate=cost(15),
-    )(gated, weight, in_maps, out_maps)
-
-
-def feed_back_kernel(
-    grad_ref,
-    down_ref,
-    gate_w_ref,
-    up_w_ref,
-    gate_ref,
-    up_ref,
-    gated_ref,
-    narrow_ref,
-    d_out_ref,
-    d_in_ref,
-    gu_out_ref,
-    gu_in_ref,
-    out_ref,
-    back_gu_ref,
-    maps_ref,
-):
-    rank = d_in_ref.shape[0]
-    grad = grad_ref[...]
-    back_d = dot_nt(grad, d_out_ref[...]).astype(BF)
-    dm = dot_nt(grad, down_ref[...]) + SCALE_ADAPT * dot(back_d, d_in_ref[...])
-    gate, up = gate_ref[...].astype(F32), up_ref[...].astype(F32)
-    sig = jax.nn.sigmoid(gate)
-    silu = gate * sig
-    du = (dm * silu).astype(BF)
-    dg = (dm * up * (sig + silu * (1.0 - sig))).astype(BF)
-    back_g = dot_nt(dg, gu_out_ref[0]).astype(BF)
-    back_u = dot_nt(du, gu_out_ref[1]).astype(BF)
-    back_gu_ref[:, :rank] = back_g
-    back_gu_ref[:, rank:] = back_u
-    into = dot_nt(dg, gate_w_ref[...]) + dot_nt(du, up_w_ref[...])
-    into = into + SCALE_ADAPT * (dot(back_g, gu_in_ref[:rank, :]) + dot(back_u, gu_in_ref[rank:, :]))
-    out_ref[...] = into.astype(BF)
-
-    @pl.when(pl.program_id(0) == 0)
-    def _():
-        maps_ref[...] = jnp.zeros_like(maps_ref)
-
-    maps_ref[0] += SCALE_ADAPT * dot_tn(back_d, gated_ref[...])
-    maps_ref[1] += SCALE_ADAPT * dot_tn(narrow_ref[:, :rank], dg)
-    maps_ref[2] += SCALE_ADAPT * dot_tn(narrow_ref[:, rank:], du)
-
-
-def feed_back(first, grad, down_w, gate_w, up_w, gate, up, gated, narrow, d_out, d_in, gu_out, gu_in):
-    rows, width = grad.shape
-    hidden = gate_w.shape[1]
-    rank = d_in.shape[0]
-    tile = 256
-    row = lambda n: pl.BlockSpec((tile, n), lambda r: (r, 0))
-    local = lambda n: pl.BlockSpec((tile, n), lambda r: (r + first, 0))
-    fixed = lambda v: pl.BlockSpec(v.shape, lambda r: (0,) * v.ndim, pipeline_mode=pl.Buffered(1))
-    return pl.pallas_call(
-        feed_back_kernel,
-        grid=(rows // tile,),
-        in_specs=[
-            row(width),
-            fixed(down_w),
-            fixed(gate_w),
-            fixed(up_w),
-            local(hidden),
-            local(hidden),
-            local(hidden),
-            local(2 * rank),
-            fixed(d_out),
-            fixed(d_in),
-            fixed(gu_out),
-            fixed(gu_in),
-        ],
-        out_specs=[row(width), row(2 * rank), pl.BlockSpec((3, rank, hidden), lambda r: (0, 0, 0))],
-        out_shape=[
-            jax.ShapeDtypeStruct((rows, width), BF),
-            jax.ShapeDtypeStruct((rows, 2 * rank), BF),
-            jax.ShapeDtypeStruct((3, rank, hidden), F32),
-        ],
-        compiler_params=pltpu.CompilerParams(vmem_limit_bytes=VMEM_BYTES),
-        name="feed_backward",
-        cost_estimate=cost(2 + rows // 50),
-    )(grad, down_w, gate_w, up_w, gate, up, gated, narrow, d_out, d_in, gu_out, gu_in)
-
-
 def project_kernel(heads, own_tiles, x_ref, w_ref, in_maps_ref, out_maps_ref, *out_refs):
     pre_q_ref, pre_k_ref, value_ref, narrow_ref, square_q_ref, square_k_ref = out_refs
     width = heads * HD
@@ -563,6 +476,259 @@
     )(dq, dk, pre_q, pre_k, gain, cos, sin)
 
 
+def finish_kernel(groups, heads, early_rows, *refs):
+    (
+        dq_ref,
+        dk_ref,
+        dv_ref,
+        more_k_ref,
+        more_v_ref,
+        pre_q_ref,
+        pre_k_ref,
+        inv_q_ref,
+        inv_k_ref,
+        gain_ref,
+        cos_ref,
+        sin_ref,
+        in_maps_ref,
+        out_maps_ref,
+        narrow_ref,
+        early_ref,
+        wide_ref,
+        weight_any,
+        inputs_any,
+        mid_any,
+    ) = refs[:20]
+    out_ref, sums_ref, wide_out_ref = refs[20:23]
+    (
+        weight,
+        inputs,
+        mid,
+        turn,
+        grad,
+        back,
+        stat,
+        stat_in,
+        far,
+        near,
+        core_in,
+        met,
+        across_in,
+        near_in,
+        maps,
+        maps_in,
+        by_x,
+        by_y,
+        by_y_in,
+        by_p_in,
+        own_sum,
+        own_sum_in,
+        wide_in,
+        local_sem,
+        send_sem,
+        recv_sem,
+    ) = refs[23:]
+    p, x, y, c = (lax.axis_index(a) for a in ("p", "x", "y", "c"))
+    core, across, both, over = (p, x, y, 1 - c), (p, 1 - x, y, c), (p, 1 - x, y, 1 - c), (p, x, 1 - y, c)
+    others = [lax.rem(p + s, groups) for s in range(1, groups)]
+    width = heads * HD
+    rows = out_ref.shape[0]
+    model = out_ref.shape[1]
+    rank = out_maps_ref.shape[1]
+    copies = Copies(send_sem, recv_sem)
+    loads = []
+    for k, (src, dst) in enumerate(((weight_any, weight), (inputs_any, inputs), (mid_any, mid))):
+        loads.append(pltpu.make_async_copy(src, dst, local_sem.at[k]))
+        loads[-1].start()
+
+    barrier = pltpu.get_barrier_semaphore()
+    for device in [core, across, both, over] + [(q, x, y, c) for q in others]:
+        pl.semaphore_signal(barrier, inc=1, device_id=device, device_id_type=pl.DeviceIdType.MESH)
+
+    ones = jnp.ones((8, HD), BF)
+
+    def unturn(b, carry):
+        here = pl.ds(pl.multiple_of(b * rows, rows), rows)
+        cos, sin = cos_ref[here, :], sin_ref[here, :]
+        for part, pre_ref in enumerate((pre_q_ref, pre_k_ref)):
+            product = None
+            for h in range(heads):
+                cols = slice(h * HD, (h + 1) * HD)
+                wide_cols = slice(part * width + h * HD, part * width + (h + 1) * HD)
+                v = dq_ref[here, cols] if part == 0 else dk_ref[here, cols] + more_k_ref[here, cols].astype(F32)
+                turned = (v * cos - pltpu.roll(v, HD // 2, 1) * sin) * gain_ref[:, wide_cols]
+                turn[here, wide_cols] = turned
+                term = turned * pre_ref[here, cols]
+                product = term if product is None else product + term
+            high = product.astype(BF)
+            low = (product - high.astype(F32)).astype(BF)
+            summed = dot_nt(ones, high) + dot_nt(ones, low)
+            stat[part : part + 1, here] = summed[:1, :]
+        grad[here, 2 * width :] = (dv_ref[here, :] + more_v_ref[here, :].astype(F32)).astype(BF)
+        return carry
+
+    stat[...] = jnp.zeros_like(stat)
+    lax.fori_loop(0, 4, unturn, 0)
+    for b in range(2 * groups):
+        maps[b, :early_rows, :] = early_ref[:, b * 256 : (b + 1) * 256]
+    pl.semaphore_wait(barrier, 3 + groups)
+    stats = [copies.remote(stat, stat_in.at[k], device) for k, device in enumerate((core, across, both))]
+    early = pl.ds(0, early_rows)
+    exchanged = [copies.remote(maps.at[2 * q + 1 - x, early], maps_in.at[q, early], across) for q in range(groups)]
+    wides = [
+        copies.remote(wide_ref.at[:, pl.ds(pl.multiple_of(q * 256, 256), 256)], wide_in.at[k], (q, x, y, c))
+        for k, q in enumerate(others)
+    ]
+    for copy in stats:
+        copy.wait_recv()
+
+    for b in range(4):
+        here = slice(b * rows, (b + 1) * rows)
+        total_row = stat[:, here]
+        for k in range(3):
+            d = b ^ (k + 1)
+            total_row = total_row + stat_in[k, :, d * rows : (d + 1) * rows]
+        inner = total_row.T / model
+        for part, (pre_ref, inv_ref) in enumerate(((pre_q_ref, inv_q_ref), (pre_k_ref, inv_k_ref))):
+            cols = slice(part * width, (part + 1) * width)
+            inv = inv_ref[here, :]
+            scale = inv * inv * inv * inner[:, part : part + 1]
+            grad[here, cols] = (inv * turn[here, cols] - pre_ref[here, :] * scale).astype(BF)
+
+    loads[0].wait()
+
+    def into(start, dst):
+        here = slice(start, start + 2 * rows)
+        for k in range(3):
+            part = dot_nt(grad[here, k * width : (k + 1) * width], out_maps_ref[k])
+            back[here, k * rank : (k + 1) * rank] = part.astype(BF)
+
+        def columns(n, carry):
+            cols = pl.ds(pl.multiple_of(n * 512, 512), 512)
+            full = dot_nt(grad[here, :], weight[cols, :]) + SCALE_ADAPT * dot(back[here, :], in_maps_ref[:, cols])
+            dst[:, cols] = full.astype(BF)
+            return carry
+
+        lax.fori_loop(0, model // 512, columns, 0)
+
+    into(2 * rows, far)
+    far_copy = copies.remote(far.at[pl.ds(rows, rows)], core_in, core)
+    far_copy.wait_recv()
+    met[...] = (far[:rows, :].astype(F32) + core_in[...].astype(F32)).astype(BF)
+    across_copy = copies.remote(met, across_in, across)
+    into(0, near)
+    near_copy = copies.remote(near.at[pl.ds(rows, rows)], near_in, core)
+
+    loads[1].wait()
+    late = early_rows + 3 * rank
+    for b in range(2 * groups):
+        cols = slice(b * 256, (b + 1) * 256)
+        maps[b, early_rows:late, :] = SCALE_ADAPT * dot_tn(back[...], inputs[:, cols])
+    send_late = pl.ds(early_rows, 3 * rank)
+    exchanged += [
+        copies.remote(maps.at[2 * q + 1 - x, send_late], maps_in.at[q, send_late], across) for q in range(groups)
+    ]
+    for q in range(groups):
+        by_x[q, late:, :] = jnp.zeros_like(by_x[q, late:, :])
+    for k in range(3):
+        own = SCALE_ADAPT * dot_tn(narrow_ref[:, k * rank : (k + 1) * rank], grad[:, k * width : (k + 1) * width])
+        here = slice(late + k * rank, late + (k + 1) * rank)
+        for q in range(groups):
+            by_x[q, here, pl.ds(pl.multiple_of(c * HD, HD), HD)] = own[:, q * HD : (q + 1) * HD]
+    for copy in exchanged:
+        copy.wait_recv()
+    for q in range(groups):
+        by_x[q, :late, :] = maps[2 * q + x, :late, :] + maps_in[q]
+    halves = lambda ref, q, side: ref.at[q, :, pl.ds(pl.multiple_of(side * HD, HD), HD)]
+    exchanged = [copies.remote(halves(by_x, q, 1 - y), by_y_in.at[q], over) for q in range(groups)]
+    for q, copy in enumerate(exchanged):
+        copy.wait_recv()
+        by_y[q] = by_x[q, :, pl.ds(pl.multiple_of(y * HD, HD), HD)] + by_y_in[q]
+    exchanged = [copies.remote(by_y.at[q], by_p_in.at[k], (q, x, y, c)) for k, q in enumerate(others)]
+    summed = by_y[p]
+    wide_sum = wide_ref[:, pl.ds(pl.multiple_of(p * 256, 256), 256)]
+    for k, copy in enumerate(exchanged):
+        copy.wait_recv()
+        summed = summed + by_p_in[k]
+    own_sum[...] = summed
+    last = copies.remote(own_sum, own_sum_in, core)
+    for k, copy in enumerate(wides):
+        copy.wait_recv()
+        wide_sum = wide_sum + wide_in[k]
+    wide_out_ref[...] = wide_sum
+    last.wait_recv()
+    summed = summed + own_sum_in[...]
+    sums_ref[...] = jnp.where(c == 0, summed[:, : HD // 2], summed[:, HD // 2 :])
+
+    loads[2].wait()
+    near_copy.wait_recv()
+    across_copy.wait_recv()
+    out_ref[...] = (
+        mid[...]
+        + near[:rows, :].astype(F32)
+        + near_in[...].astype(F32)
+        + across_in[...].astype(F32)
+    )
+    copies.finish()
+
+
+def finish(groups, heads, args, weight, inputs, mid):
+    own, width = args[0].shape
+    rows, model = mid.shape
+    rank = args[13].shape[1]
+    early_rows, wide_rows = args[15].shape[0], args[16].shape[0]
+    total_rows = early_rows + 6 * rank
+    late = early_rows + 3 * rank
+    vm = pl.BlockSpec(memory_space=pltpu.VMEM)
+    anywhere = pl.BlockSpec(memory_space=pl.ANY)
+    count = 3 + groups + (groups - 1) + 3 + 2 * groups + (groups - 1) + 1
+    block = lambda *shape: pltpu.VMEM(shape, BF)
+    full = lambda *shape: pltpu.VMEM(shape, F32)
+    return pl.pallas_call(
+        functools.partial(finish_kernel, groups, heads, early_rows),
+        in_specs=[vm] * 17 + [anywhere] * 3,
+        out_specs=[vm] * 3,
+        out_shape=[
+            jax.ShapeDtypeStruct((rows, model), F32),
+            jax.ShapeDtypeStruct((total_rows, HD // 2), F32),
+            jax.ShapeDtypeStruct((wide_rows, 256), F32),
+        ],
+        scratch_shapes=[
+            pltpu.VMEM(weight.shape, BF),
+            pltpu.VMEM(inputs.shape, BF),
+            pltpu.VMEM(mid.shape, F32),
+            full(own, 2 * width),
+            block(own, 3 * width),
+            block(own, 3 * rank),
+            full(8, own),
+            full(3, 8, own),
+            block(2 * rows, model),
+            block(2 * rows, model),
+            block(rows, model),
+            block(rows, model),
+            block(rows, model),
+            block(rows, model),
+            full(2 * groups, late, 256),
+            full(groups, late, 256),
+            full(groups, total_rows, 256),
+            full(groups, total_rows, HD),
+            full(groups, total_rows, HD),
+            full(groups - 1, total_rows, HD),
+            full(total_rows, HD),
+            full(total_rows, HD),
+            full(groups - 1, wide_rows, 256),
+            pltpu.SemaphoreType.DMA((3,)),
+            pltpu.SemaphoreType.DMA((count,)),
+            pltpu.SemaphoreType.DMA((count,)),
+        ],
+        compiler_params=pltpu.CompilerParams(
+            collective_id=1, has_side_effects=True, vmem_limit_bytes=VMEM_BYTES
+        ),
+        name="finish",
+        cost_estimate=cost(60),
+    )(*args, weight, inputs, mid)
+
+
 NEG_FILL = -1e30
 
 
@@ -703,24 +869,330 @@
     low_ref[...] = middle.astype(BF)
 
 
-def after_feed_kernel(*refs):
-    middle_ref, gain_ref, cot_ref, result_ref, grad_ref = refs[4:]
-    feed = total(refs[:4])
-    gain = gain_ref[...]
-    result_ref[...] = (middle_ref[...] + feed * rms_inverse(feed) * gain).astype(BF)
-    grad_ref[...] = rms_backward(feed, gain, cot_ref[...].astype(F32)).astype(BF)
-
-
-def middle_kernel(*refs):
-    cot_ref, attn_ref, gain_ref, mid_ref, grad_ref = refs[4:]
-    mid = cot_ref[...].astype(F32) + total(refs[:4])
-    mid_ref[...] = mid
-    grad_ref[...] = rms_backward(attn_ref[...], gain_ref[...], mid).astype(BF)
-
-
 def end_kernel(*refs):
     mid_ref, out_ref = refs[3:]
     out_ref[...] = mid_ref[...] + total(refs[:3])
+
+
+def feed_kernel(*refs):
+    (
+        d_in_ref,
+        d_out_ref,
+        gu_out_ref,
+        gu_in_ref,
+        feed_gain_ref,
+        attn_gain_ref,
+        narrow_gu_ref,
+        gated_any,
+        gate_any,
+        up_any,
+        down_any,
+        gate_w_any,
+        up_w_any,
+        middle_any,
+        cot_any,
+        attn_any,
+    ) = refs[:16]
+    result_ref, mid_ref, grad_attn_ref, back_gu_ref, maps_ref, gb_d_ref = refs[16:22]
+    (
+        down_w,
+        gate_w,
+        up_w,
+        acts,
+        blocks,
+        own_pair,
+        core_in,
+        by_x,
+        by_y,
+        across_in,
+        over_in,
+        tokens,
+        cot,
+        dgu,
+        narrow_d,
+        load_sem,
+        act_sem,
+        free_sem,
+        send_sem,
+        recv_sem,
+    ) = refs[22:]
+    p, x, y, c = (lax.axis_index(a) for a in ("p", "x", "y", "c"))
+    core, across, over = (p, x, y, 1 - c), (p, 1 - x, y, c), (p, x, 1 - y, c)
+    rows, model = result_ref.shape
+    pair = 2 * rows
+    half = rows // 2
+    hidden = down_w.shape[0]
+    rank = d_in_ref.shape[0]
+    copies = Copies(send_sem, recv_sem)
+
+    def load(k, src, dst):
+        copy = pltpu.make_async_copy(src, dst, load_sem.at[k])
+        copy.start()
+        return copy
+
+    def load_acts(turn, kind, k):
+        src = (gated_any, gate_any, up_any)[kind].at[pl.ds(k * pair, pair)]
+        copy = pltpu.make_async_copy(src, acts.at[turn % 2, kind], act_sem.at[turn % 2, kind])
+        copy.start()
+        return copy
+
+    first_order, back_order = (3, 1, 2, 0), (0, 1, 3, 2)
+    loaded = load(0, down_any, down_w)
+    gated_loads = [load_acts(0, 0, first_order[0]), load_acts(1, 0, first_order[1])]
+    middle_load, cot_load = load(1, middle_any, tokens), load(2, cot_any, cot)
+    gate_load, up_load = load(3, gate_w_any, gate_w), load(4, up_w_any, up_w)
+    barrier = pltpu.get_barrier_semaphore()
+    for device in (core, across, over):
+        pl.semaphore_signal(barrier, inc=1, device_id=device, device_id_type=pl.DeviceIdType.MESH)
+    pl.semaphore_wait(barrier, 3)
+    maps_ref[...] = jnp.zeros_like(maps_ref)
+    gb_d_ref[...] = jnp.zeros_like(gb_d_ref)
+
+    def part(k):
+        return own_pair if k == 0 else blocks.at[pl.ds(2 * k, 2)]
+
+    def store(k, cols, value):
+        dst = part(k)
+        dst[0, :, cols] = value[:rows].astype(BF)
+        dst[1, :, cols] = value[rows:].astype(BF)
+
+    def columns(n):
+        return pl.ds(pl.multiple_of(n * 512, 512), 512)
+
+    def forward(k, slot):
+        here = slice(k * pair, (k + 1) * pair)
+        narrow_d[here, :] = dot_nt(acts[slot, 0], d_in_ref[...]).astype(BF)
+
+        def body(n, carry):
+            cols = columns(n)
+            value = dot(acts[slot, 0], down_w[:, cols])
+            store(k, cols, value + SCALE_ADAPT * dot(narrow_d[here, :], d_out_ref[:, cols]))
+            return carry
+
+        lax.fori_loop(0, model // 512, body, 0)
+
+    def backward(k, slot):
+        here = slice(k * pair, (k + 1) * pair)
+        grad = blocks[2 * k : 2 * k + 2].reshape(pair, model)
+        back_d = dot_nt(grad, d_out_ref[...]).astype(BF)
+        gb_d_ref[...] += SCALE_ADAPT * dot_tn(narrow_d[here, :], grad)
+
+        def tile(t, carry):
+            cols = pl.ds(pl.multiple_of(t * 256, 256), 256)
+            grad = blocks[2 * k : 2 * k + 2].reshape(pair, model)
+            dm = dot_nt(grad, down_w[cols, :]) + SCALE_ADAPT * dot(back_d, d_in_ref[:, cols])
+            gate, up = acts[slot, 1, :, cols].astype(F32), acts[slot, 2, :, cols].astype(F32)
+            sig = jax.nn.sigmoid(gate)
+            silu = gate * sig
+            du = (dm * silu).astype(BF)
+            dg = (dm * up * (sig + silu * (1.0 - sig))).astype(BF)
+            dgu[0, :, cols] = dg
+            dgu[1, :, cols] = du
+            narrow = narrow_gu_ref[here, :]
+            maps_ref[0, :, cols] += SCALE_ADAPT * dot_tn(back_d, acts[slot, 0, :, cols])
+            maps_ref[1, :, cols] += SCALE_ADAPT * dot_tn(narrow[:, :rank], dg)
+            maps_ref[2, :, cols] += SCALE_ADAPT * dot_tn(narrow[:, rank:], du)
+            return carry
+
+        lax.fori_loop(0, hidden // 256, tile, 0)
+        back_g = dot_nt(dgu[0], gu_out_ref[0]).astype(BF)
+        back_u = dot_nt(dgu[1], gu_out_ref[1]).astype(BF)
+        back_gu_ref[here, :rank] = back_g
+        back_gu_ref[here, rank:] = back_u
+
+        def body(n, carry):
+            cols = columns(n)
+            value = dot_nt(dgu[0], gate_w[cols, :]) + dot_nt(dgu[1], up_w[cols, :])
+            value = value + SCALE_ADAPT * (dot(back_g, gu_in_ref[:rank, cols]) + dot(back_u, gu_in_ref[rank:, cols]))
+            store(k, cols, value)
+            return carry
+
+        lax.fori_loop(0, model // 512, body, 0)
+
+    def to_core(k):
+        return copies.remote(part(k).at[1], core_in.at[k], core)
+
+    def meet(k, copy):
+        copy.wait_recv()
+        blocks[2 * k] = (blocks[2 * k].astype(F32) + core_in[k].astype(F32)).astype(BF)
+
+    top, low = pl.ds(0, half), pl.ds(half, half)
+
+    def add(block, here, more):
+        blocks[block, here, :] = (blocks[block, here, :].astype(F32) + more[...].astype(F32)).astype(BF)
+
+    def far_halves():
+        return (
+            copies.remote(blocks.at[6, top], by_x, across),
+            copies.remote(blocks.at[6, low], by_y, over),
+        )
+
+    def send_top_across():
+        return copies.remote(blocks.at[2, top], across_in.at[top], across)
+
+    def finish_sum(far, own, parts):
+        far_x, far_y = far
+        parts.append(copies.remote(blocks.at[4, low], over_in.at[low], over))
+        far_y.wait_recv()
+        add(2, low, by_y)
+        parts.append(copies.remote(blocks.at[2, low], across_in.at[low], across))
+        far_x.wait_recv()
+        add(4, top, by_x)
+        parts.append(copies.remote(blocks.at[4, top], over_in.at[top], over))
+        own.wait_recv()
+        for copy in parts:
+            copy.wait_recv()
+        return (
+            own_pair[0].astype(F32) + core_in[0].astype(F32) + across_in[...].astype(F32) + over_in[...].astype(F32)
+        )
+
+    loaded.wait()
+    gated_loads[0].wait()
+    forward(3, 0)
+    sent = to_core(3)
+    gated_loads.append(load_acts(2, 0, first_order[2]))
+    gated_loads[1].wait()
+    forward(1, 1)
+    sent1 = to_core(1)
+    meet(3, sent)
+    far = far_halves()
+    gated_loads.append(load_acts(3, 0, first_order[3]))
+    gated_loads[2].wait()
+    forward(2, 0)
+    sent2 = to_core(2)
+    meet(1, sent1)
+    parts = [send_top_across()]
+    gated_loads[3].wait()
+    forward(0, 1)
+    own = to_core(0)
+    meet(2, sent2)
+    act_loads = [[load_acts(0, kind, 0) for kind in range(3)], [load_acts(1, kind, 1) for kind in range(3)]]
+    feed = finish_sum(far, own, parts)
+    copies.finish()
+    for device in (core, across, over):
+        pl.semaphore_signal(free_sem, inc=1, device_id=device, device_id_type=pl.DeviceIdType.MESH)
+    gain = feed_gain_ref[...]
+    middle_load.wait()
+    cot_load.wait()
+    result_ref[...] = (tokens[...] + feed * rms_inverse(feed) * gain).astype(BF)
+    blocks[0] = rms_backward(feed, gain, cot[...].astype(F32)).astype(BF)
+
+    pl.semaphore_wait(free_sem, 3)
+    copies.all = []
+    to_x = copies.remote(blocks.at[0], blocks.at[2], across)
+    to_y = copies.remote(blocks.at[0], blocks.at[4], over)
+    to_c = copies.remote(blocks.at[0], blocks.at[1], core)
+    attn_load = load(5, attn_any, tokens)
+    gate_load.wait()
+    up_load.wait()
+    to_c.wait_recv()
+    for copy in act_loads[0]:
+        copy.wait()
+    backward(0, 0)
+    own = to_core(0)
+    act_loads.append([load_acts(2, kind, 3) for kind in range(3)])
+    to_x.wait_recv()
+    x_on = [copies.remote(blocks.at[2], blocks.at[3], core), copies.remote(blocks.at[2, top], blocks.at[6, top], over)]
+    to_y.wait_recv()
+    y_on = [copies.remote(blocks.at[4], blocks.at[5], core), copies.remote(blocks.at[4, low], blocks.at[6, low], across)]
+    x_on[0].wait_recv()
+    for copy in act_loads[1]:
+        copy.wait()
+    for copy in x_on:
+        copy.wait_send()
+    backward(1, 1)
+    sent1 = to_core(1)
+    act_loads.append([load_acts(3, kind, 2) for kind in range(3)])
+    x_on[1].wait_recv()
+    y_on[1].wait_recv()
+    far_on = copies.remote(blocks.at[6], blocks.at[7], core)
+    meet(1, sent1)
+    parts = [send_top_across()]
+    far_on.wait_recv()
+    for copy in act_loads[2]:
+        copy.wait()
+    far_on.wait_send()
+    backward(3, 0)
+    sent = to_core(3)
+    meet(3, sent)
+    far = far_halves()
+    y_on[0].wait_recv()
+    for copy in act_loads[3]:
+        copy.wait()
+    for copy in y_on:
+        copy.wait_send()
+    backward(2, 1)
+    sent2 = to_core(2)
+    meet(2, sent2)
+    total_grad = finish_sum(far, own, parts)
+    mid = cot[...].astype(F32) + total_grad
+    mid_ref[...] = mid
+    attn_load.wait()
+    grad_attn_ref[:rows, :] = rms_backward(tokens[...], attn_gain_ref[...], mid).astype(BF)
+
+    def block(k):
+        return grad_attn_ref.at[pl.ds(k * rows, rows)]
+
+    to_x = copies.remote(block(0), block(2), across)
+    to_c = copies.remote(block(0), block(1), core)
+    to_x.wait_recv()
+    on = copies.remote(block(2), block(3), core)
+    to_c.wait_recv()
+    on.wait_recv()
+    done = (*x_on, far_on, *y_on)
+    for copy in copies.all:
+        if not any(copy is other for other in done):
+            copy.wait_send()
+
+
+def feed_layer(maps, narrow_gu, acts, weights, middle, cot, attn_out):
+    rows, model = cot.shape
+    hidden = weights[0].shape[0]
+    rank = maps[0].shape[0]
+    vm = pl.BlockSpec(memory_space=pltpu.VMEM)
+    anywhere = pl.BlockSpec(memory_space=pl.ANY)
+    block = lambda *shape: pltpu.VMEM(shape, BF)
+    count = 48
+    return pl.pallas_call(
+        feed_kernel,
+        in_specs=[vm] * 7 + [anywhere] * 9,
+        out_specs=[vm] * 6,
+        out_shape=[
+            jax.ShapeDtypeStruct((rows, model), BF),
+            jax.ShapeDtypeStruct((rows, model), F32),
+            jax.ShapeDtypeStruct((4 * rows, model), BF),
+            jax.ShapeDtypeStruct((8 * rows, 2 * rank), BF),
+            jax.ShapeDtypeStruct((3, rank, hidden), F32),
+            jax.ShapeDtypeStruct((rank, model), F32),
+        ],
+        scratch_shapes=[
+            block(hidden, model),
+            block(model, hidden),
+            block(model, hidden),
+            block(2, 3, 2 * rows, hidden),
+            block(8, rows, model),
+            block(2, rows, model),
+            block(4, rows, model),
+            block(rows // 2, model),
+            block(rows // 2, model),
+            block(rows, model),
+            block(rows, model),
+            pltpu.VMEM((rows, model), F32),
+            block(rows, model),
+            block(2, 2 * rows, hidden),
+            block(8 * rows, rank),
+            pltpu.SemaphoreType.DMA((6,)),
+            pltpu.SemaphoreType.DMA((2, 3)),
+            pltpu.SemaphoreType.REGULAR,
+            pltpu.SemaphoreType.DMA((count,)),
+            pltpu.SemaphoreType.DMA((count,)),
+        ],
+        compiler_params=pltpu.CompilerParams(
+            collective_id=2, has_side_effects=True, vmem_limit_bytes=60 * 1024 * 1024
+        ),
+        name="feed_layer",
+        cost_estimate=cost(170),
+    )(*maps, narrow_gu, *acts, *weights, middle, cot, attn_out)
 
 
 def by_rows(kernel, name, rows, width, args, dtypes, us):
@@ -891,32 +1363,15 @@
     middle_low = jnp.concatenate(at.gather8(low)[0])
     narrow_gu = dot_nt(middle_low, a_gu).astype(BF)
     gate, up, gated = gate_up(middle_low, w_g, w_u, narrow_gu, b_gu)
-    feed, narrow_d = down(gated, w_d, a_d, b_d)
-    pairs = [feed[2 * rows * k : 2 * rows * (k + 1)] for k in range(4)]
-    feed_parts = at.scatter8(*pairs[1:], lambda mark: pairs[0])
-    cot = cotangent[0]
-    result, grad_feed_own = by_rows(
-        after_feed_kernel,
-        "after_feed",
-        rows,
-        width,
-        [*feed_parts, middle, feed_gain, cot],
-        [BF, BF],
-        4,
+    result, grad_mid, grad_attn, back_gu, wide, gb_d = feed_layer(
+        (a_d, b_d, b_gu, a_gu, feed_gain, attn_gain),
+        narrow_gu,
+        (gated, gate, up),
+        (w_d, w_g, w_u),
+        middle,
+        cotangent[0],
+        attn_out,
     )
-
-    feed_args = (w_d, w_g, w_u, gate, up, gated, narrow_gu, b_d, a_d, b_gu, a_gu)
-    grad_feed, first = at.gather8(grad_feed_own, lambda pair: feed_back(0, pair, *feed_args))
-    tiles = 2 * rows // 256
-    backs = [first, feed_back(tiles, grad_feed[1], *feed_args)]
-    backs.append(feed_back(2 * tiles, jnp.concatenate(grad_feed[2:]), *feed_args))
-    mids = [backs[1][0], backs[2][0][: 2 * rows], backs[2][0][2 * rows :]]
-    back_gu = jnp.concatenate([back[1] for back in backs])
-    mid_parts = at.scatter8(*mids, lambda mark: backs[0][0])
-    grad_mid, grad_attn_own = by_rows(
-        middle_kernel, "middle", rows, width, [*mid_parts, cot, attn_out, attn_gain], [F32, BF], 4
-    )
-    grad_attn = jnp.concatenate(at.gather4(grad_attn_own))
     back_o = dot_nt(grad_attn, b_o).astype(BF)
     grad_o = (dot_nt(grad_attn, w_o) + SCALE_ADAPT * dot(back_o, a_o)).astype(BF)
     dq, dks, dvs = attention.backward(query, grad_o, o, key_all, value_all, log, [reach], [BF])
@@ -927,8 +1382,6 @@
     for t in range(reach - 1, 0, -1):
         moved_k = at.shift_p((dks[t].astype(F32) + moved_k.astype(F32)).astype(BF), -1)
         moved_v = at.shift_p((dvs[t].astype(F32) + moved_v.astype(F32)).astype(BF), -1)
-    dk = dks[0] + moved_k.astype(F32)
-    dv = dvs[0] + moved_v.astype(F32)
     def share_y(mine, other):
         return mine + at.swap_y(other)
 
@@ -951,54 +1404,84 @@
     ga_gu = SCALE_ADAPT * dot_tn(back_gu, middle_low)
     ga_o = SCALE_ADAPT * dot_tn(back_o, o)
     gb_o = SCALE_ADAPT * dot_tn(narrow_o, grad_attn)
-    gb_d = SCALE_ADAPT * sum(
-        dot_tn(narrow_d[2 * rows * k : 2 * rows * (k + 1)], grad_feed[k]) for k in range(4)
-    )
-    early = sum_model(after(jnp.concatenate([ga_gu, spread(ga_o), gb_o, gb_d]), dq))
-    wide = sum(back[2] for back in backs).reshape(-1, at.np, hidden_rows)
-    dk = after(dk, early)
-    turn, inner = unpost(dq, dk, pre_q, pre_k, gain, cos, sin, heads)
-    inner = at.sum4(inner.T, 1).T / width
-
-    def unnorm(part, pre, scale):
-        cols = slice(part * local, (part + 1) * local)
-        return (scale * turn[:, cols] - pre * (scale * scale * scale * inner[:, part : part + 1])).astype(BF)
-
-    grad_qkv = jnp.concatenate(
-        [unnorm(0, pre_q, inv_q), unnorm(1, pre_k[:own], inv_k), dv.astype(BF)], axis=1
-    )
-    back_qkv = dot_nt(grad_qkv, b_qkv_diag).astype(BF)
-
-    def late_adapters(mark):
-        back = after(back_qkv, mark)
-        ga_qkv = SCALE_ADAPT * dot_tn(back, inputs)
-        gb_qkv = [
-            SCALE_ADAPT * dot_tn(narrow_qkv[:, k * rank : (k + 1) * rank], grad_qkv[:, k * local : (k + 1) * local])
-            for k in range(3)
-        ]
-        return sum_model(jnp.concatenate([ga_qkv, spread(jnp.concatenate(gb_qkv))]))
-
-    def end_part(part, mark=None):
-        ins, back = grad_qkv[part], back_qkv[part]
-        if mark is not None:
-            ins = after(ins, mark)
-        return (dot_nt(ins, w_qkv) + SCALE_ADAPT * dot(back, a_qkv)).astype(BF)
-
-    marks = []
-
-    def end_near(mark):
-        marks.append(mark)
-        return end_part(near_rows, mark)
-
-    end_parts = at.scatter4(end_part(far_rows), end_near)
-    (grad_input,) = by_rows(end_kernel, "end", rows, width, [*end_parts, grad_mid], [F32], 3)
-    late = late_adapters(marks[0])
-    narrow_sums = share_p(jnp.concatenate([late, early], axis=0))
-    narrow_sums = narrow_sums.reshape(narrow_sums.shape[0], 2, depth)
-    sums = pick(narrow_sums, 1, at.c) + at.swap_core(pick(narrow_sums, 1, 1 - at.c))
-    sums = sums.reshape(-1, rank, depth)
-    late, early = sums[:6], sums[6:]
-    wide = share_p(after(wide, marks[0])).reshape(-1, rank, hidden_rows)
+    early = jnp.concatenate([ga_gu, spread(ga_o), gb_o, gb_d])
+    wide = wide.reshape(3 * rank, -1)
+    if 2 * depth == HD and hidden_rows == 2 * HD:
+        grad_input, sums, wide = finish(
+            at.np,
+            heads,
+            [
+                dq,
+                dks[0],
+                dvs[0],
+                moved_k,
+                moved_v,
+                pre_q,
+                pre_k[:own],
+                inv_q,
+                inv_k,
+                gain,
+                cos,
+                sin,
+                a_qkv,
+                b_qkv,
+                narrow_qkv,
+                early,
+                wide,
+            ],
+            w_qkv,
+            inputs,
+            grad_mid,
+        )
+        sums, wide = sums.reshape(-1, rank, depth), wide.reshape(-1, rank, hidden_rows)
+        early, late = sums[:5], sums[5:]
+    else:
+        early = sum_model(after(early, dq))
+        wide = wide.reshape(-1, at.np, hidden_rows)
+        dk = after(dks[0] + moved_k.astype(F32), early)
+        dv = dvs[0] + moved_v.astype(F32)
+        turn, inner = unpost(dq, dk, pre_q, pre_k, gain, cos, sin, heads)
+        inner = at.sum4(inner.T, 1).T / width
+
+        def unnorm(part, pre, scale):
+            cols = slice(part * local, (part + 1) * local)
+            return (scale * turn[:, cols] - pre * (scale * scale * scale * inner[:, part : part + 1])).astype(BF)
+
+        grad_qkv = jnp.concatenate(
+            [unnorm(0, pre_q, inv_q), unnorm(1, pre_k[:own], inv_k), dv.astype(BF)], axis=1
+        )
+        back_qkv = dot_nt(grad_qkv, b_qkv_diag).astype(BF)
+
+        def late_adapters(mark):
+            back = after(back_qkv, mark)
+            ga_qkv = SCALE_ADAPT * dot_tn(back, inputs)
+            gb_qkv = [
+                SCALE_ADAPT * dot_tn(narrow_qkv[:, k * rank : (k + 1) * rank], grad_qkv[:, k * local : (k + 1) * local])
+                for k in range(3)
+            ]
+            return sum_model(jnp.concatenate([ga_qkv, spread(jnp.concatenate(gb_qkv))]))
+
+        def end_part(part, mark=None):
+            ins, back = grad_qkv[part], back_qkv[part]
+            if mark is not None:
+                ins = after(ins, mark)
+            return (dot_nt(ins, w_qkv) + SCALE_ADAPT * dot(back, a_qkv)).astype(BF)
+
+        marks = []
+
+        def end_near(mark):
+            marks.append(mark)
+            return end_part(near_rows, mark)
+
+        end_parts = at.scatter4(end_part(far_rows), end_near)
+        (grad_input,) = by_rows(end_kernel, "end", rows, width, [*end_parts, grad_mid], [F32], 3)
+        late = late_adapters(marks[0])
+        narrow_sums = share_p(jnp.concatenate([late, early], axis=0))
+        narrow_sums = narrow_sums.reshape(narrow_sums.shape[0], 2, depth)
+        sums = pick(narrow_sums, 1, at.c) + at.swap_core(pick(narrow_sums, 1, 1 - at.c))
+        sums = sums.reshape(-1, rank, depth)
+        late, early = sums[:6], sums[6:]
+        wide = share_p(after(wide, marks[0])).reshape(-1, rank, hidden_rows)
     choose = (jnp.arange(adapter_model_input_maps.shape[0], dtype=jnp.int32) == selected).astype(F32)
     sum_a_model = choose[:, None, None, None] * jnp.concatenate([late[:3], early[2:3], early[:2]])[None]
     sum_a_hidden = choose[:, None, None] * wide[0][None]

time: 889 us -> 795 us (0.89)
  Pallas kernels: 388 us -> 537 us
  waiting for transfers between devices: 246 us -> 112 us
  starting transfers between devices: 57.3 us -> 21.6 us
  other arithmetic: 54.6 us -> 26.7 us
  matrix products: 46.5 us -> 24.5 us
  local copies, waits for them, and re-layouts: 71.6 us -> 50.3 us
    pallas_call x5 -> x2, Pallas kernels: 91 us -> 256 us  [the longest x1 189 us: feed_layer(): pl.pallas_call(feed_kernel, in_specs=[vm] * 7 + [anywhere] * 9, out_specs...]
    ppermute x17 -> x4, waiting for transfers between devices: 115 us -> 42.3 us  [swap_x(): return lax.ppermute(value, 'x', SWAP)]
    ppermute x12 -> x2, waiting for transfers between devices: 53.7 us -> 1.64 us  [swap_y(): return lax.ppermute(value, 'y', SWAP)]
    dot_general x25 -> x12, matrix products: 46.5 us -> 24.5 us  [dot(): return lax.dot_general(a, b, (dims, ((), ())), preferred_element_type=F32)]
    ppermute x4, waiting for transfers between devices: 40.6 us -> 60.1 us  [shift_p(): lax.ppermute(value, 'p', [(p, p + by) for p in range(self.np) if 0 <= p +...]
    pallas_call x4 -> x1, Pallas kernels: 21.3 us -> 5.4 us  [by_rows(): pl.pallas_call(kernel, grid=(rows // tile,), in_specs=[spec(v) for v in a...]
    ppermute x17 -> x4, starting transfers between devices: 14.5 us -> 1.28 us  [swap_x(): return lax.ppermute(value, 'x', SWAP)]
    ppermute x12 -> x2, starting transfers between devices: 14.9 us -> 3.73 us  [swap_y(): return lax.ppermute(value, 'y', SWAP)]
  transfers between devices with their start and end apart: 73 -> 25, of which waited for: 34 -> 11; matrix products, arithmetic and copies ran while one was open for 15% -> 10% of each run, Pallas kernels for 39% -> 34%
where the time goes in v3:
time: 795 us; the launch traced here: 788 us
  Pallas kernels  537 us (68%)
  waiting for transfers between devices  112 us (14%)
  local copies, waits for them, and re-layouts  50.3 us (6%)
  other arithmetic  26.7 us (3%)
  matrix products  24.5 us (3%)
  starting transfers between devices  21.6 us (3%)
  between operations  15.7 us (2%)
    pallas_call x1, Pallas kernels, feed_layer(): pl.pallas_call(feed_kernel, in_specs=[vm] * 7 + [anywhere] * 9, out_specs...  189 us
    pallas_call x1, Pallas kernels, start(): pl.pallas_call(functools.partial(start_kernel, groups, reach), in_specs=[...  141 us
    pallas_call x1, Pallas kernels, finish(): pl.pallas_call(functools.partial(finish_kernel, groups, heads, early_rows...  67.1 us
    ppermute x4, waiting for transfers between devices, shift_p(): lax.ppermute(value, 'p', [(p, p + by) for p in range(self.np) if 0 <= p +...  60.1 us
    ppermute x4, waiting for transfers between devices, swap_x(): return lax.ppermute(value, 'x', SWAP)  42.3 us
    pallas_call x1, Pallas kernels, project(): pl.pallas_call(functools.partial(project_kernel, heads, own_tiles), grid=...  33.5 us
    pallas_call x2, Pallas kernels, backward(): pl.pallas_call(functools.partial(attend_back_kernel, count, dq is None, H...  32.5 us
    pallas_call x1, Pallas kernels, gate_up(): pl.pallas_call(gate_up_kernel, grid=(hidden // tile,), in_specs=[pl.Block...  26.8 us
  transfers between devices with their start and end apart: 25, of which 11 were waited for; matrix products, arithmetic and copies ran while one was open for 10% of the time, Pallas kernels for 34%

profile of v3, /device:TPU:0, one launch (start us, length us, event | category | flops | bytes accessed | tf_op | source)
XLA Modules:
  0.0 787.7 jit_solution(2644590284731044731)
XLA Ops:
  8.6 2.4 pack_columns.5
  11.0 2.3 pack_columns.4
  13.4 2.2 pack_columns.3
  15.6 140.6 %start.1 = (bf16[4,2,2,128,1536]{4,3,2,1,0:T(8,128)(2,1)}, bf16[512,1024]{1,0:T(8,128)(2,1)}, bf16[512,1024]{1,0:T(8,128)(2,1)}, bf16[3072,2048]{1,0:T(8,128)(2,1)}) custom-call(bf16[64,1536]{1,0:T(8,128)(2,1)} %get-tuple-element.66.refs_0_, bf16[64,1536]{1,0:T(8,128)(2,1)} %get-tuple-element.67.refs_1_, bf16[64,1536]{1,0:T(8,128)(2,1)} %get-tuple-element.68.refs_2_, ...), custom_call_target="tpu_custom_call" | custom-call | flops 131999997952 | bytes 120000000 | tf_op jit(solution)/shard_map/start/pallas_call | solution.py:296
  159.6 33.5 %project.1 = (f32[1024,512]{1,0:T(8,128)}, f32[3072,512]{1,0:T(8,128)}, bf16[3072,512]{1,0:T(8,128)(2,1)}, bf16[3072,48]{1,0:T(8,128)(2,1)}, f32[8,1024]{1,0:T(8,128)}, /*index=5*/f32[8,3072]{1,0:T(8,128)}) custom-call(bf16[3072,2048]{1,0:T(8,128)(2,1)} %get-tuple-element.86.x_ref, bf16[2048,1536]{1,0:T(8,128)(2,1)} %bitcast.143, ...), custom_call_target="tpu_custom_call" | custom-call | flops 32999999488 | bytes 30000000 | tf_op jit(solution)/shard_map/project/pallas_call | solution.py:381
  194.9 2.0 collective-permute-start
  199.1 5.8 fusion.4
  204.9 1.6 pad_maximum_fusion.1.cos_ref
  208.3 1.6 pad_maximum_fusion.2.sin_ref
  216.2 1.7 copy.51.inv_k_ref
  217.9 12.0 %rope_forward.1 = (bf16[1024,512]{1,0:T(8,128)(2,1)}, bf16[3072,512]{1,0:T(8,128)(2,1)}) custom-call(f32[1024,512]{1,0:T(8,128)} %get-tuple-element.88.q_ref.refs_5_, f32[3072,512]{1,0:T(8,128)} %get-tuple-element.89.k_ref, f32[1024,1]{1,0:T(8,128)} %copy.50.inv_q_ref.refs_7_, f32[3072,1]{1,0:T(8,128)} %copy.51.inv_k_ref, ...), custom_call_target="tpu_custom_call" | custom-call | flops 11000000512 | bytes 10000000 | tf_op jit(solution)/shard_map/rope_forward/pallas_call | solution.py:430
  230.6 1.3 collective-permute-start.4
  231.9 5.8 collective-permute-start.3
  237.8 23.3 %attend_forward.1 = (bf16[2,2,256,512]{3,2,1,0:T(8,128)(2,1)}, f32[8,512,1]{2,1,0:T(8,128)}) custom-call(bf16[2,2,256,512]{3,2,1,0:T(8,128)(2,1)} %bitcast.160, bf16[6,2,256,512]{3,2,1,0:T(8,128)(2,1)} %bitcast.151, bf16[6,2,256,512]{3,2,1,0:T(8,128)(2,1)} %bitcast.152, bf16[6,2,256,512]{3,2,1,0:T(8,128)(2,1)} %bitcast.153, ...), custom_call_target="tpu_custom_call" | custom-call | flops 25300000768 | bytes 23000000 | tf_op jit(solution)/shard_map/attend_forward/pallas_call | solution.py:806
  261.0 1.7 convolution_convert_fusion.2
  262.7 1.3 fusion.19
  264.6 1.3 fusion.25
  265.9 1.6 add_convert_fusion.1
  267.6 2.6 collective-permute-done.6
  270.8 1.3 fusion.26
  272.1 1.6 add_convert_fusion.refs_0_
  273.9 2.3 constant_dynamic-slice_fusion.7
  276.2 19.8 %collective-permute-done.8.refs_2_ = bf16[256,2048]{1,0:T(8,128)(2,1)S(1)} collective-permute-done((bf16[256,2048]{1,0:T(8,128)(2,1)S(1)}, bf16[256,2048]{1,0:T(8,128)(2,1)S(1)}, u32[]{:S(2)}, u32[]{:S(2)}) %collective-permute-start.8) | collective-permute-done | bytes 1048608 | tf_op jit(solution)/shard_map/ppermute | solution.py:51
  297.3 5.4 after_attention.1
  304.0 1.8 collective-permute-start.12
  306.4 2.2 fusion.2.refs_11_
  310.2 1.5 dynamic-slice_bitcast_fusion.1.refs_1_
  311.7 15.9 %collective-permute-done.10 = bf16[256,2048]{1,0:T(8,128)(2,1)} collective-permute-done((bf16[256,2048]{1,0:T(8,128)(2,1)}, bf16[256,2048]{1,0:T(8,128)(2,1)}, u32[]{:S(2)}, u32[]{:S(2)}) %collective-permute-start.10) | collective-permute-done | bytes 1048608 | tf_op jit(solution)/shard_map/ppermute | solution.py:51
  328.1 4.8 slice.205.refs_18_
  333.0 3.2 slice.199.refs_6_
  338.6 1.7 slice.204.refs_14_
  340.3 1.0 copy.59.refs_8_
  341.3 1.1 slice.234
  343.1 1.1 slice.233
  344.2 1.9 collective-permute-start.14
  346.1 1.3 constant_dynamic-update-slice_fusion.9
  347.5 1.3 constant_dynamic-update-slice_fusion.8
  348.8 1.3 constant_dynamic-update-slice_fusion.7
  350.1 6.6 collective-permute-done.15
  356.8 1.6 collective-permute-done.14
  358.7 1.3 constant_dynamic-update-slice_fusion.5
  360.2 1.1 collective-permute-done.16
  361.3 3.3 copy-done.2
  364.6 3.2 convolution_convert_fusion.narrow_ref.refs_6_
  367.8 26.8 %gate_up.1 = (bf16[2048,1024]{1,0:T(8,128)(2,1)}, bf16[2048,1024]{1,0:T(8,128)(2,1)}, bf16[2048,1024]{1,0:T(8,128)(2,1)}) custom-call(bf16[2048,2048]{1,0:T(8,128)(2,1)} %copy-done.2, bf16[2048,1024]{1,0:T(8,128)(2,1)} %all-gather.7.cloned.1.call-done.gate_w_ref.refs_11_, bf16[2048,1024]{1,0:T(8,128)(2,1)} %all-gather.9.cloned.1.call-done.up_w_ref.refs_12_, ...), custom_call_target="tpu_custom_call" | custom-call | flops 28600000512 | bytes 26000000 | tf_op jit(solution)/shard_map/gate_up/pallas_call | solution.py:333
  394.6 3.4 all-gather.11.cloned.1.call-done.refs_10_
  398.0 189.0 %feed_layer.1 = (bf16[256,2048]{1,0:T(8,128)(2,1)}, f32[256,2048]{1,0:T(8,128)}, bf16[1024,2048]{1,0:T(8,128)(2,1)}, bf16[2048,32]{1,0:T(8,128)(2,1)}, f32[3,16,1024]{2,1,0:T(8,128)}, /*index=5*/f32[16,2048]{1,0:T(8,128)}) custom-call(bf16[16,1024]{1,0:T(8,128)(2,1)} %bitcast.129, bf16[16,2048]{1,0:T(8,128)(2,1)} %dynamic-slice_bitcast_fusion.1.refs_1_, ...), custom_call_target="tpu_custom_call" | custom-call | flops 186999996416 | bytes 170000000 | tf_op jit(solution)/shard_map/feed_layer/pallas_call | solution.py:1156
  587.0 3.5 convolution_convert_fusion.1
  590.5 1.2 fusion.5
  591.7 3.4 add_convert_fusion.2
  595.1 12.7 %attend_backward.2 = (f32[2,2,256,512]{3,2,1,0:T(8,128)}, bf16[2,2,256,512]{3,2,1,0:T(8,128)(2,1)}, bf16[2,2,256,512]{3,2,1,0:T(8,128)(2,1)}) custom-call(bf16[2,2,256,512]{3,2,1,0:T(8,128)(2,1)} %bitcast.161, bf16[2,2,256,512]{3,2,1,0:T(8,128)(2,1)} %bitcast.163, bf16[2,2,256,512]{3,2,1,0:T(8,128)(2,1)} %get-tuple-element.95.o_ref, ...), custom_call_target="tpu_custom_call" | custom-call | flops 13200000000 | bytes 12000000 | tf_op jit(solution)/shard_map/attend_backward/pallas_call | solution.py:825
  607.8 1.3 collective-permute-start.17
  609.1 1.3 collective-permute-start.19
  610.4 19.8 %attend_backward.3 = (f32[2,2,256,512]{3,2,1,0:T(8,128)}, f32[2,2,256,512]{3,2,1,0:T(8,128)}, bf16[2,2,256,512]{3,2,1,0:T(8,128)(2,1)}, f32[2,2,256,512]{3,2,1,0:T(8,128)}, bf16[2,2,256,512]{3,2,1,0:T(8,128)(2,1)}) custom-call(bf16[2,2,256,512]{3,2,1,0:T(8,128)(2,1)} %bitcast.162, bf16[2,2,256,512]{3,2,1,0:T(8,128)(2,1)} %bitcast.164, ...), custom_call_target="tpu_custom_call" | custom-call | flops 22000001024 | bytes 20000000 | tf_op jit(solution)/shard_map/attend_backward/pallas_call | solution.py:825
  630.7 5.3 collective-permute-done.17
  635.9 2.0 fusion.1
  637.9 1.3 collective-permute-start.18
  639.2 19.1 %collective-permute-done.19 = bf16[1024,512]{1,0:T(8,128)(2,1)S(1)} collective-permute-done((bf16[1024,512]{1,0:T(8,128)(2,1)}, bf16[1024,512]{1,0:T(8,128)(2,1)S(1)}, u32[]{:S(2)}, u32[]{:S(2)}) %collective-permute-start.19) | collective-permute-done | bytes 1048608 | tf_op jit(solution)/shard_map/ppermute | solution.py:60
  658.7 1.7 collective-permute-start.20
  661.0 5.0 convolution_multiply_fusion
  667.0 13.8 %collective-permute-done.18.refs_3_ = bf16[1024,512]{1,0:T(8,128)(2,1)S(1)} collective-permute-done((bf16[1024,512]{1,0:T(8,128)(2,1)S(1)}, bf16[1024,512]{1,0:T(8,128)(2,1)S(1)}, u32[]{:S(2)}, u32[]{:S(2)}) %collective-permute-start.18) | collective-permute-done | bytes 1048608 | tf_op jit(solution)/shard_map/ppermute | solution.py:60
  680.8 22.0 %collective-permute-done.20.refs_4_ = bf16[1024,512]{1,0:T(8,128)(2,1)S(1)} collective-permute-done((bf16[1024,512]{1,0:T(8,128)(2,1)S(1)}, bf16[1024,512]{1,0:T(8,128)(2,1)S(1)}, u32[]{:S(2)}, u32[]{:S(2)}) %collective-permute-start.20) | collective-permute-done | bytes 1048608 | tf_op jit(solution)/shard_map/ppermute | solution.py:60
  703.7 67.1 %finish.1 = (f32[256,2048]{1,0:T(8,128)}, f32[176,64]{1,0:T(8,128)}, f32[48,256]{1,0:T(8,128)}) custom-call(f32[1024,512]{1,0:T(8,128)} %bitcast.157, f32[1024,512]{1,0:T(8,128)} %bitcast.158, f32[1024,512]{1,0:T(8,128)} %bitcast.159, bf16[1024,512]{1,0:T(8,128)(2,1)} %copy-done.29, bf16[1024,512]{1,0:T(8,128)(2,1)} %copy-done.30, ...), custom_call_target="tpu_custom_call" | custom-call | flops 65999998976 | bytes 60000000 | tf_op jit(solution)/shard_map/finish/pallas_call | solution.py:687
  778.8 1.3 copy.91
  (199 shorter events, 39.3 us)
Async XLA Ops:
  7.2 151.7 %copy-start = (bf16[8,6,16,2048]{3,2,1,0:T(8,128)(2,1)S(1)}, bf16[8,6,16,2048]{3,2,1,0:T(8,128)(2,1)}, u32[]{:S(2)}) copy-start(bf16[8,6,16,2048]{3,2,1,0:T(8,128)(2,1)} %param.34) | copy-start | bytes 9437188
  7.2 222.7 %all-gather.5.cloned.1.call-start = ((), (), s32[]{:S(2)}) async-start(), calls=%async_computation | async-start | bytes 1310720 | tf_op jit(solution)/shard_map/all_gather | solution.py:1259
  7.9 302.2 %all-gather.7.cloned.1.call-start = ((), (), s32[]{:S(2)}) async-start(), calls=%async_computation.1 | async-start | bytes 5242880 | tf_op jit(solution)/shard_map/all_gather | solution.py:1259
  156.2 211.6 %all-gather.9.cloned.1.call-start = ((), (), s32[]{:S(2)}) async-start(), calls=%async_computation.2 | async-start | bytes 5242880 | tf_op jit(solution)/shard_map/all_gather | solution.py:1259
  159.6 38.0 %copy-start.28 = (s32[4,8]{1,0:T(4,128)S(1)}, s32[4,8]{1,0:T(4,128)}, u32[]{:S(2)}) copy-start(s32[4,8]{1,0:T(4,128)} %param.21) | copy-start | bytes 388
  194.7 17.4 %collective-permute-start.1 = (f32[1,4096]{1,0:T(1,128)S(1)}, f32[1,4096]{1,0:T(1,128)S(1)}, u32[]{:S(2)}, u32[]{:S(2)}) collective-permute-start(f32[1,4096]{1,0:T(1,128)S(1)} %pad_maximum_fusion.8), channel_id=1, source_target_pairs={{0,4},{4,0},{1,5},{5,1},{2,6},{6,2},{3,7},{7,3},{8,12},{12,8},{9,1... | collective-permute-start | bytes 49160 | tf_op jit(solution)/shard_map/ppermute | solution.py:51
  194.8 18.6 %collective-permute-start.2 = (f32[1,4096]{1,0:T(1,128)S(1)}, f32[1,4096]{1,0:T(1,128)S(1)}, u32[]{:S(2)}, u32[]{:S(2)}) collective-permute-start(f32[1,4096]{1,0:T(1,128)S(1)} %pad_maximum_fusion.8), channel_id=1, source_target_pairs={{0,5},{1,4},{4,1},{5,0},{2,7},{3,6},{6,3},{7,2},{8,13},{9,12},{12,... | collective-permute-start | bytes 49160 | tf_op jit(solution)/shard_map/ppermute | solution.py:54
  194.9 19.4 %collective-permute-start = (f32[1,4096]{1,0:T(1,128)S(1)}, f32[1,4096]{1,0:T(1,128)S(1)}, u32[]{:S(2)}, u32[]{:S(2)}) collective-permute-start(f32[1,4096]{1,0:T(1,128)S(1)} %pad_maximum_fusion.8), channel_id=1, source_target_pairs={{0,1},{1,0},{2,3},{3,2},{4,5},{5,4},{6,7},{7,6},{8,9},{9,8},{10,11... | collective-permute-start | bytes 49160 | tf_op jit(solution)/shard_map/ppermute | solution.py:48
  197.0 201.0 %all-gather.11.cloned.1.call-start = ((), (), s32[]{:S(2)}) async-start(), calls=%async_computation.3 | async-start | bytes 5242880 | tf_op jit(solution)/shard_map/all_gather | solution.py:1259
  204.9 5.1 copy-start.7
  204.9 5.1 copy-start.9
  204.9 5.1 copy-start.10
  204.9 2.5 copy-start.15
  207.4 2.6 copy-start.25
  212.2 48.8 %copy-start.22 = (bf16[16,4,128]{2,1,0:T(4,128)(2,1)}, bf16[16,4,128]{2,1,0:T(4,128)(2,1)S(1)}, u32[]{:S(2)}) copy-start(bf16[16,4,128]{2,1,0:T(4,128)(2,1)S(1)} %dynamic-slice_reduce_fusion.3) | copy-start | bytes 49156
  229.9 34.2 %collective-permute-start.5 = (bf16[256,2048]{1,0:T(8,128)(2,1)}, bf16[256,2048]{1,0:T(8,128)(2,1)S(1)}, u32[]{:S(2)}, u32[]{:S(2)}) collective-permute-start(bf16[256,2048]{1,0:T(8,128)(2,1)} %all-gather.5.cloned.1.call-done), channel_id=1, source_target_pairs={{1,2},{2,1},{5,6},{6,5},{9,10},{10,9},{13,14},{14,13},{17,18},{18,... | collective-permute-start | bytes 3145736 | tf_op jit(solution)/shard_map/ppermute | solution.py:1278
  230.6 33.4 %collective-permute-start.4 = (bf16[256,2048]{1,0:T(8,128)(2,1)}, bf16[256,2048]{1,0:T(8,128)(2,1)S(1)}, u32[]{:S(2)}, u32[]{:S(2)}) collective-permute-start(bf16[256,2048]{1,0:T(8,128)(2,1)} %all-gather.5.cloned.1.call-done), channel_id=1, source_target_pairs={{1,0},{2,3},{5,4},{6,7},{9,8},{10,11},{13,12},{14,15},{17,16},{18,... | collective-permute-start | bytes 3145736 | tf_op jit(solution)/shard_map/ppermute | solution.py:1278
  231.9 32.2 %collective-permute-start.3 = (bf16[256,2048]{1,0:T(8,128)(2,1)}, bf16[256,2048]{1,0:T(8,128)(2,1)S(1)}, u32[]{:S(2)}, u32[]{:S(2)}) collective-permute-start(bf16[256,2048]{1,0:T(8,128)(2,1)} %all-gather.5.cloned.1.call-done), channel_id=1, source_target_pairs={{0,2},{3,1},{4,6},{7,5},{8,10},{11,9},{12,14},{15,13},{16,18},{19,... | collective-permute-start | bytes 3145736 | tf_op jit(solution)/shard_map/ppermute | solution.py:1278
  261.0 3.1 copy-start.19
  262.7 9.4 %copy-start.20 = (bf16[1024,16]{0,1:T(8,128)(2,1)}, bf16[1024,16]{0,1:T(8,128)(2,1)S(1)}, u32[]{:S(2)}) copy-start(bf16[1024,16]{0,1:T(8,128)(2,1)S(1)} %convolution_convert_fusion.2) | copy-start | bytes 98308
  264.6 6.2 copy-start.5
  267.6 2.7 collective-permute-start.6
  270.7 25.3 %collective-permute-start.8 = (bf16[256,2048]{1,0:T(8,128)(2,1)S(1)}, bf16[256,2048]{1,0:T(8,128)(2,1)S(1)}, u32[]{:S(2)}, u32[]{:S(2)}) collective-permute-start(bf16[256,2048]{1,0:T(8,128)(2,1)S(1)} %add_convert_fusion.3), channel_id=1, source_target_pairs={{0,4},{4,0},{1,5},{5,1},{2,6},{6,2},{3,7},{7,3},{8,12},{12,8},{9,1... | collective-permute-start | bytes 3145736 | tf_op jit(solution)/shard_map/ppermute | solution.py:51
  273.7 22.3 %copy-start.12 = (bf16[512,2048]{1,0:T(8,128)(2,1)}, bf16[512,2048]{1,0:T(8,128)(2,1)S(1)}, u32[]{:S(2)}) copy-start(bf16[512,2048]{1,0:T(8,128)(2,1)S(1)} %add_convert_fusion.refs_0_) | copy-start | bytes 6291460
  273.8 22.2 %collective-permute-start.7 = (bf16[256,2048]{1,0:T(8,128)(2,1)S(1)}, bf16[256,2048]{1,0:T(8,128)(2,1)S(1)}, u32[]{:S(2)}, u32[]{:S(2)}) collective-permute-start(bf16[256,2048]{1,0:T(8,128)(2,1)S(1)} %slice.232), channel_id=1, source_target_pairs={{0,1},{1,0},{2,3},{3,2},{4,5},{5,4},{6,7},{7,6},{8,9},{9,8},{10,11... | collective-permute-start | bytes 3145736 | tf_op jit(solution)/shard_map/ppermute | solution.py:48
  295.9 1.0 copy-start.31
  296.0 1.3 copy-start.32
  302.7 24.9 %collective-permute-start.10 = (bf16[256,2048]{1,0:T(8,128)(2,1)}, bf16[256,2048]{1,0:T(8,128)(2,1)}, u32[]{:S(2)}, u32[]{:S(2)}) collective-permute-start(bf16[256,2048]{1,0:T(8,128)(2,1)} %get-tuple-element.98), channel_id=1, source_target_pairs={{0,4},{4,0},{1,5},{5,1},{2,6},{6,2},{3,7},{7,3},{8,12},{12,8},{9,1... | collective-permute-start | bytes 3145736 | tf_op jit(solution)/shard_map/ppermute | solution.py:51
  304.0 5.2 copy-start.8
  304.0 37.3 %collective-permute-start.12 = (bf16[256,2048]{1,0:T(8,128)(2,1)}, bf16[256,2048]{1,0:T(8,128)(2,1)}, u32[]{:S(2)}, u32[]{:S(2)}) collective-permute-start(bf16[256,2048]{1,0:T(8,128)(2,1)} %get-tuple-element.98), channel_id=1, source_target_pairs={{0,2},{2,0},{1,3},{3,1},{4,6},{6,4},{5,7},{7,5},{8,10},{10,8},{9,1... | collective-permute-start | bytes 3145736 | tf_op jit(solution)/shard_map/ppermute | solution.py:57
  308.6 38.9 %collective-permute-start.9 = (bf16[256,2048]{1,0:T(8,128)(2,1)}, bf16[256,2048]{1,0:T(8,128)(2,1)}, u32[]{:S(2)}, u32[]{:S(2)}) collective-permute-start(bf16[256,2048]{1,0:T(8,128)(2,1)} %get-tuple-element.98), channel_id=1, source_target_pairs={{0,1},{1,0},{2,3},{3,2},{4,5},{5,4},{6,7},{7,6},{8,9},{9,8},{10,11... | collective-permute-start | bytes 3145736 | tf_op jit(solution)/shard_map/ppermute | solution.py:48
  311.7 49.7 %copy-start.24 = (bf16[1,2,16,2048]{3,2,1,0:T(8,128)(2,1)}, bf16[1,2,16,2048]{3,2,1,0:T(8,128)(2,1)S(1)}, u32[]{:S(2)}) copy-start(bf16[1,2,16,2048]{3,2,1,0:T(8,128)(2,1)S(1)} %constant_dynamic-slice_fusion.2) | copy-start | bytes 393220
  327.6 31.1 %collective-permute-start.11 = (bf16[256,2048]{1,0:T(8,128)(2,1)}, bf16[256,2048]{1,0:T(8,128)(2,1)S(1)}, u32[]{:S(2)}, u32[]{:S(2)}) collective-permute-start(bf16[256,2048]{1,0:T(8,128)(2,1)} %collective-permute-done.10), channel_id=1, source_target_pairs={{0,1},{1,0},{2,3},{3,2},{4,5},{5,4},{6,7},{7,6},{8,9},{9,8},{10,11... | collective-permute-start | bytes 3145736 | tf_op jit(solution)/shard_map/ppermute | solution.py:48
  333.0 4.2 copy-start.14
  342.4 14.4 %collective-permute-start.15 = (bf16[128,2048]{1,0:T(8,128)(2,1)S(1)}, bf16[128,2048]{1,0:T(8,128)(2,1)S(1)}, u32[]{:S(2)}, u32[]{:S(2)}) collective-permute-start(bf16[128,2048]{1,0:T(8,128)(2,1)S(1)} %slice.234), channel_id=1, source_target_pairs={{0,4},{4,0},{1,5},{5,1},{2,6},{6,2},{3,7},{7,3},{8,12},{12,8},{9,1... | collective-permute-start | bytes 1572872 | tf_op jit(solution)/shard_map/ppermute | solution.py:51
  344.2 14.2 %collective-permute-start.14 = (bf16[128,2048]{1,0:T(8,128)(2,1)S(1)}, bf16[128,2048]{1,0:T(8,128)(2,1)S(1)}, u32[]{:S(2)}, u32[]{:S(2)}) collective-permute-start(bf16[128,2048]{1,0:T(8,128)(2,1)S(1)} %slice.233), channel_id=1, source_target_pairs={{0,2},{2,0},{1,3},{3,1},{4,6},{6,4},{5,7},{7,5},{8,10},{10,8},{9,1... | collective-permute-start | bytes 1572872 | tf_op jit(solution)/shard_map/ppermute | solution.py:57
  347.4 12.6 %collective-permute-start.13 = (bf16[256,2048]{1,0:T(8,128)(2,1)}, bf16[256,2048]{1,0:T(8,128)(2,1)S(1)}, u32[]{:S(2)}, u32[]{:S(2)}) collective-permute-start(bf16[256,2048]{1,0:T(8,128)(2,1)} %collective-permute-done.12), channel_id=1, source_target_pairs={{0,1},{1,0},{2,3},{3,2},{4,5},{5,4},{6,7},{7,6},{8,9},{9,8},{10,11... | collective-permute-start | bytes 3145736 | tf_op jit(solution)/shard_map/ppermute | solution.py:48
  358.5 2.7 collective-permute-start.16
  361.3 3.3 copy-start.2
  587.0 4.7 copy-start.3
  587.0 4.7 copy-start.6
  607.8 28.2 %collective-permute-start.17 = (bf16[1024,512]{1,0:T(8,128)(2,1)}, bf16[1024,512]{1,0:T(8,128)(2,1)}, u32[]{:S(2)}, u32[]{:S(2)}) collective-permute-start(bf16[1024,512]{1,0:T(8,128)(2,1)} %bitcast.139), channel_id=1, source_target_pairs={{8,0},{16,8},{24,16},{9,1},{17,9},{25,17},{10,2},{18,10},{26,18},{... | collective-permute-start | bytes 3145736 | tf_op jit(solution)/shard_map/ppermute | solution.py:60
  609.1 49.2 %collective-permute-start.19 = (bf16[1024,512]{1,0:T(8,128)(2,1)}, bf16[1024,512]{1,0:T(8,128)(2,1)S(1)}, u32[]{:S(2)}, u32[]{:S(2)}) collective-permute-start(bf16[1024,512]{1,0:T(8,128)(2,1)} %bitcast.138), channel_id=1, source_target_pairs={{8,0},{16,8},{24,16},{9,1},{17,9},{25,17},{10,2},{18,10},{26,18},{... | collective-permute-start | bytes 3145736 | tf_op jit(solution)/shard_map/ppermute | solution.py:60
  610.4 19.8 %copy-start.11 = (bf16[2,2,256,512]{3,2,1,0:T(8,128)(2,1)S(1)}, bf16[2,2,256,512]{3,2,1,0:T(8,128)(2,1)}, u32[]{:S(2)}) copy-start(bf16[2,2,256,512]{3,2,1,0:T(8,128)(2,1)} %get-tuple-element.95.o_ref) | copy-start | bytes 3145732
  610.4 20.2 %copy-start.27 = (f32[4]{0:T(128)S(1)}, f32[4]{0:T(128)}, u32[]{:S(2)}) copy-start(f32[4]{0:T(128)} %compare_convert_fusion.1) | copy-start | bytes 52
  630.2 28.1 %copy-start.17 = (bf16[2,2,256,512]{3,2,1,0:T(8,128)(2,1)S(1)}, bf16[2,2,256,512]{3,2,1,0:T(8,128)(2,1)}, u32[]{:S(2)}) copy-start(bf16[2,2,256,512]{3,2,1,0:T(8,128)(2,1)} %get-tuple-element.116) | copy-start | bytes 3145732
  635.9 24.4 %copy-start.4 = (bf16[1024,2048]{1,0:T(8,128)(2,1)S(1)}, bf16[1024,2048]{1,0:T(8,128)(2,1)}, u32[]{:S(2)}) copy-start(bf16[1024,2048]{1,0:T(8,128)(2,1)} %get-tuple-element.108) | copy-start | bytes 12582916
  635.9 24.4 %copy-start.21 = (bf16[1024,16]{0,1:T(8,128)(2,1)S(1)}, bf16[1024,16]{0,1:T(8,128)(2,1)}, u32[]{:S(2)}) copy-start(bf16[1024,16]{0,1:T(8,128)(2,1)} %copy-done.20) | copy-start | bytes 98308
  637.9 42.8 %collective-permute-start.18 = (bf16[1024,512]{1,0:T(8,128)(2,1)S(1)}, bf16[1024,512]{1,0:T(8,128)(2,1)S(1)}, u32[]{:S(2)}, u32[]{:S(2)}) collective-permute-start(bf16[1024,512]{1,0:T(8,128)(2,1)S(1)} %fusion.1), channel_id=1, source_target_pairs={{8,0},{16,8},{24,16},{9,1},{17,9},{25,17},{10,2},{18,10},{26,18},{... | collective-permute-start | bytes 3145736 | tf_op jit(solution)/shard_map/ppermute | solution.py:60
  658.7 2.4 copy-start.16
  658.7 44.1 %collective-permute-start.20 = (bf16[1024,512]{1,0:T(8,128)(2,1)S(1)}, bf16[1024,512]{1,0:T(8,128)(2,1)S(1)}, u32[]{:S(2)}, u32[]{:S(2)}) collective-permute-start(bf16[1024,512]{1,0:T(8,128)(2,1)S(1)} %fusion), channel_id=1, source_target_pairs={{8,0},{16,8},{24,16},{9,1},{17,9},{25,17},{10,2},{18,10},{26,18},{... | collective-permute-start | bytes 3145736 | tf_op jit(solution)/shard_map/ppermute | solution.py:60
  661.0 5.0 copy-start.23
  680.8 22.0 %copy-start.29 = (bf16[1024,512]{1,0:T(8,128)(2,1)}, bf16[1024,512]{1,0:T(8,128)(2,1)S(1)}, u32[]{:S(2)}) copy-start(bf16[1024,512]{1,0:T(8,128)(2,1)S(1)} %collective-permute-done.18.refs_3_) | copy-start | bytes 3145732
  702.8 1.0 copy-start.30
  703.7 70.9 %copy-start.26 = (f32[8]{0:T(128)S(1)}, f32[8]{0:T(128)}, u32[]{:S(2)}) copy-start(f32[8]{0:T(128)} %compare_convert_fusion) | copy-start | bytes 100
  703.7 74.1 %copy-start.18 = (bf16[256,2048]{1,0:T(8,128)(2,1)S(1)}, bf16[256,2048]{1,0:T(8,128)(2,1)}, u32[]{:S(2)}) copy-start(bf16[256,2048]{1,0:T(8,128)(2,1)} %get-tuple-element.107) | copy-start | bytes 3145732
  770.8 8.0 %copy-start.13 = (f32[256,2048]{1,0:T(8,128)S(1)}, f32[256,2048]{1,0:T(8,128)}, u32[]{:S(2)}) copy-start(f32[256,2048]{1,0:T(8,128)} %get-tuple-element.123) | copy-start | bytes 6291460
  777.9 3.0 copy-start.1
Sparse Core Ops, SparseCore 0:
  9.6 45.9 all-gather.4
  156.3 80.0 all-gather.6
  237.9 79.2 all-gather.8
  318.7 79.2 all-gather.10

commit v4 on v3

--- a/solution.py
+++ b/solution.py
@@ -184,14 +184,14 @@
 
 
 def start_kernel(groups, reach, *refs):
-    qkv_pack, feed_packs, x_ref = refs[0:4], (refs[4:12], refs[12:20]), refs[20]
-    w_ref, gate_ref, up_ref, all_ref, local_sem, send_sem, recv_sem = refs[21:]
+    qkv_pack, feed_packs, x_ref, o_ref = refs[0:4], (refs[4:12], refs[12:20]), refs[20], refs[21]
+    w_ref, feed_ref, all_ref, o_all_ref, local_sem, send_sem, recv_sem = refs[22:]
     p, x, y, c = (lax.axis_index(a) for a in ("p", "x", "y", "c"))
     turned = lambda u, t: 1 - u if t else u
     group = [(p, turned(x, dx), turned(y, dy), turned(c, dc)) for dx, dy, dc in TURNS8]
     core, across, over = group[1], group[2], group[4]
     right, left = (lax.rem(p + 1, groups), x, y, c), (lax.rem(p + groups - 1, groups), x, y, c)
-    rows, depth = x_ref.shape[0], qkv_pack[0].shape[0]
+    rows, depth, hidden = x_ref.shape[0], qkv_pack[0].shape[0], feed_packs[0][0].shape[1]
     used = [0]
 
     def remote(src, dst, device):
@@ -230,11 +230,13 @@
     slot = (4 * x + 2 * y + c) * depth
     mine = [
         w_ref.at[p, x, y, pl.ds(pl.multiple_of(c * depth, 16), depth)],
-        at(gate_ref, slot, depth),
-        at(up_ref, slot, depth),
+        feed_ref.at[pl.ds(pl.multiple_of(slot, 16), depth), pl.ds(0, hidden)],
+        feed_ref.at[pl.ds(pl.multiple_of(slot, 16), depth), pl.ds(hidden, hidden)],
     ]
     firsts = (qkv_pack[0], feed_packs[0][0], feed_packs[1][0])
     kept = [local(k, firsts[k], mine[k]) for k in range(3)] + [local(3, x_ref, tokens(0, 0))]
+    kept.append(local(4, o_ref, o_all_ref.at[p]))
+    o_of = lambda q: o_all_ref.at[lax.rem(p + 2 * groups - q, groups)]
     regrouped = [remote(qkv_pack[d], mine[0], group[d]) for d in (1, 2, 3)]
     moves = [remote(x_ref, tokens(1, 0), right)]
     sent = list(regrouped) + moves
@@ -242,6 +244,8 @@
     for copy in regrouped:
         copy.wait_recv()
     along = remote(owned(0), owned(0), right)
+    o_along = remote(o_ref, o_of(0), right)
+    sent.append(o_along)
     later = [remote(owned(0), owned(0), over)]
     spread = [(remote(x_ref, tokens(0, 1), core), remote(x_ref, tokens(0, 2), across))]
     for k in (1, 2):
@@ -272,6 +276,10 @@
                 along = remote(owned(step), owned(step), right)
                 sent.append(along)
             later.append(remote(owned(step), owned(step), over))
+            o_along.wait_recv()
+            if step < groups - 1:
+                o_along = remote(o_of(step), o_of(step), right)
+                sent.append(o_along)
             step += 1
         if ready <= reach:
             pass_on(ready)
@@ -287,56 +295,58 @@
         copy.wait()
 
 
-def start(groups, reach, qkv_pack, gate_pack, up_pack, own_inputs):
+def start(groups, reach, qkv_pack, gate_pack, up_pack, own_inputs, own_o):
     depth, size = qkv_pack[0].shape
     rows, width = own_inputs.shape
     hidden = gate_pack[0].shape[1]
-    copies = 3 + 1 + 1 + 1 + 14 + (groups - 2) + (groups - 1) + (reach - 1) + 2 * (reach + 1) + (reach + 1)
+    copies = 3 + 1 + 1 + 1 + 14 + (groups - 1) + (groups - 2) + (groups - 1) + (reach - 1) + 2 * (reach + 1) + (reach + 1)
     anywhere = pl.BlockSpec(memory_space=pl.ANY)
-    weight, gate, up, inputs = pl.pallas_call(
+    weight, feed, inputs, o_all = pl.pallas_call(
         functools.partial(start_kernel, groups, reach),
-        in_specs=[anywhere] * 21,
+        in_specs=[anywhere] * 22,
         out_specs=[anywhere] * 4,
         out_shape=[
             jax.ShapeDtypeStruct((groups, 2, 2, 2 * depth, size), BF),
-            jax.ShapeDtypeStruct((8 * depth, hidden), BF),
-            jax.ShapeDtypeStruct((8 * depth, hidden), BF),
+            jax.ShapeDtypeStruct((8 * depth, 2 * hidden), BF),
             jax.ShapeDtypeStruct((4 * (reach + 1) * rows, width), BF),
+            jax.ShapeDtypeStruct((groups,) + own_o.shape, BF),
         ],
         scratch_shapes=[
-            pltpu.SemaphoreType.DMA((4,)),
+            pltpu.SemaphoreType.DMA((5,)),
             pltpu.SemaphoreType.DMA((copies,)),
             pltpu.SemaphoreType.DMA((copies,)),
         ],
         compiler_params=pltpu.CompilerParams(collective_id=0, has_side_effects=True),
         name="start",
         cost_estimate=cost(120),
-    )(*qkv_pack, *gate_pack, *up_pack, own_inputs)
-    return weight.reshape(-1, size), gate, up, inputs
+    )(*qkv_pack, *gate_pack, *up_pack, own_inputs, own_o)
+    return weight.reshape(-1, size), feed, inputs, o_all.reshape(-1, width)
 
 
 def gate_up_kernel(x_ref, gate_w_ref, up_w_ref, narrow_ref, maps_ref, gate_ref, up_ref, gated_ref):
-    rank = maps_ref.shape[1]
-    gate = dot(x_ref[...], gate_w_ref[...]) + SCALE_ADAPT * dot(narrow_ref[:, :rank], maps_ref[0])
-    up = dot(x_ref[...], up_w_ref[...]) + SCALE_ADAPT * dot(narrow_ref[:, rank:], maps_ref[1])
+    rank, tile = maps_ref.shape[1:]
+    gate_w, up_w = gate_w_ref[...].reshape(-1, tile), up_w_ref[...].reshape(-1, tile)
+    gate = dot(x_ref[...], gate_w) + SCALE_ADAPT * dot(narrow_ref[:, :rank], maps_ref[0])
+    up = dot(x_ref[...], up_w) + SCALE_ADAPT * dot(narrow_ref[:, rank:], maps_ref[1])
     gate_ref[...] = gate.astype(BF)
     up_ref[...] = up.astype(BF)
     gated_ref[...] = (gate * jax.nn.sigmoid(gate) * up).astype(BF)
 
 
-def gate_up(x, gate_w, up_w, narrow, maps):
+def gate_up(x, weight, narrow, maps):
     rows, width = x.shape
-    hidden = gate_w.shape[1]
+    groups = weight.shape[0]
+    hidden = weight.shape[2] // 2
     tile = 256
-    weight = pl.BlockSpec((width, tile), lambda s: (0, s))
+    steps = hidden // tile
     out = pl.BlockSpec((rows, tile), lambda s: (0, s))
     return pl.pallas_call(
         gate_up_kernel,
-        grid=(hidden // tile,),
+        grid=(steps,),
         in_specs=[
             pl.BlockSpec((rows, width), lambda s: (0, 0)),
-            weight,
-            weight,
+            pl.BlockSpec((groups, width // groups, tile), lambda s: (0, 0, s)),
+            pl.BlockSpec((groups, width // groups, tile), lambda s: (0, 0, s + steps)),
             pl.BlockSpec(narrow.shape, lambda s: (0, 0)),
             pl.BlockSpec(maps.shape[:2] + (tile,), lambda s: (0, 0, s)),
         ],
@@ -344,8 +354,8 @@
         out_shape=[jax.ShapeDtypeStruct((rows, hidden), BF)] * 3,
         compiler_params=pltpu.CompilerParams(vmem_limit_bytes=VMEM_BYTES),
         name="gate_up",
-        cost_estimate=cost(26),
-    )(x, gate_w, up_w, narrow, maps)
+        cost_estimate=cost(1),
+    )(x, weight, weight, narrow, maps)
 
 
 def project_kernel(heads, own_tiles, x_ref, w_ref, in_maps_ref, out_maps_ref, *out_refs):
@@ -400,7 +410,7 @@
         ],
         compiler_params=pltpu.CompilerParams(vmem_limit_bytes=VMEM_BYTES),
         name="project",
-        cost_estimate=cost(30),
+        cost_estimate=cost(1),
     )(x, weight, in_maps, out_maps)
 
 
@@ -442,7 +452,7 @@
         out_specs=[own(width), row(width)],
         out_shape=[jax.ShapeDtypeStruct(pre_q.shape, BF), jax.ShapeDtypeStruct(pre_k.shape, BF)],
         name="rope_forward",
-        cost_estimate=cost(10),
+        cost_estimate=cost(1),
     )(pre_q, pre_k, inv_q, inv_k, gain, cos, sin)
 
 
@@ -481,8 +491,6 @@
         dq_ref,
         dk_ref,
         dv_ref,
-        more_k_ref,
-        more_v_ref,
         pre_q_ref,
         pre_k_ref,
         inv_q_ref,
@@ -498,8 +506,8 @@
         weight_any,
         inputs_any,
         mid_any,
-    ) = refs[:20]
-    out_ref, sums_ref, wide_out_ref = refs[20:23]
+    ) = refs[:18]
+    out_ref, sums_ref, wide_out_ref = refs[18:21]
     (
         weight,
         inputs,
@@ -527,7 +535,7 @@
         local_sem,
         send_sem,
         recv_sem,
-    ) = refs[23:]
+    ) = refs[21:]
     p, x, y, c = (lax.axis_index(a) for a in ("p", "x", "y", "c"))
     core, across, both, over = (p, x, y, 1 - c), (p, 1 - x, y, c), (p, 1 - x, y, 1 - c), (p, x, 1 - y, c)
     others = [lax.rem(p + s, groups) for s in range(1, groups)]
@@ -537,7 +545,7 @@
     rank = out_maps_ref.shape[1]
     copies = Copies(send_sem, recv_sem)
     loads = []
-    for k, (src, dst) in enumerate(((weight_any, weight), (inputs_any, inputs), (mid_any, mid))):
+    for k, (src, dst) in enumerate(((weight_any, weight), (inputs_any.at[pl.ds(0, 4 * mid.shape[0])], inputs), (mid_any, mid))):
         loads.append(pltpu.make_async_copy(src, dst, local_sem.at[k]))
         loads[-1].start()
 
@@ -555,7 +563,7 @@
             for h in range(heads):
                 cols = slice(h * HD, (h + 1) * HD)
                 wide_cols = slice(part * width + h * HD, part * width + (h + 1) * HD)
-                v = dq_ref[here, cols] if part == 0 else dk_ref[here, cols] + more_k_ref[here, cols].astype(F32)
+                v = dq_ref[here, cols] if part == 0 else dk_ref[here, cols]
                 turned = (v * cos - pltpu.roll(v, HD // 2, 1) * sin) * gain_ref[:, wide_cols]
                 turn[here, wide_cols] = turned
                 term = turned * pre_ref[here, cols]
@@ -564,7 +572,7 @@
             low = (product - high.astype(F32)).astype(BF)
             summed = dot_nt(ones, high) + dot_nt(ones, low)
             stat[part : part + 1, here] = summed[:1, :]
-        grad[here, 2 * width :] = (dv_ref[here, :] + more_v_ref[here, :].astype(F32)).astype(BF)
+        grad[here, 2 * width :] = dv_ref[here, :].astype(BF)
         return carry
 
     stat[...] = jnp.zeros_like(stat)
@@ -675,8 +683,8 @@
 def finish(groups, heads, args, weight, inputs, mid):
     own, width = args[0].shape
     rows, model = mid.shape
-    rank = args[13].shape[1]
-    early_rows, wide_rows = args[15].shape[0], args[16].shape[0]
+    rank = args[11].shape[1]
+    early_rows, wide_rows = args[13].shape[0], args[14].shape[0]
     total_rows = early_rows + 6 * rank
     late = early_rows + 3 * rank
     vm = pl.BlockSpec(memory_space=pltpu.VMEM)
@@ -684,9 +692,13 @@
     count = 3 + groups + (groups - 1) + 3 + 2 * groups + (groups - 1) + 1
     block = lambda *shape: pltpu.VMEM(shape, BF)
     full = lambda *shape: pltpu.VMEM(shape, F32)
+    first_rows = lambda v: vm if v.shape[0] <= own else pl.BlockSpec(
+        (own, v.shape[1]), lambda k: (0, 0), pipeline_mode=pl.Buffered(1)
+    )
     return pl.pallas_call(
         functools.partial(finish_kernel, groups, heads, early_rows),
-        in_specs=[vm] * 17 + [anywhere] * 3,
+        grid=(1,),
+        in_specs=[first_rows(v) for v in args] + [anywhere] * 3,
         out_specs=[vm] * 3,
         out_shape=[
             jax.ShapeDtypeStruct((rows, model), F32),
@@ -695,7 +707,7 @@
         ],
         scratch_shapes=[
             pltpu.VMEM(weight.shape, BF),
-            pltpu.VMEM(inputs.shape, BF),
+            pltpu.VMEM((own, model), BF),
             pltpu.VMEM(mid.shape, F32),
             full(own, 2 * width),
             block(own, 3 * width),
@@ -752,31 +764,166 @@
     log_ref[0] = top + jnp.log(total)
 
 
-def attend_back_kernel(count, first, scale, q_ref, do_ref, o_ref, *refs):
-    ks, vs = refs[:count], refs[count : 2 * count]
-    lo_ref, pos_ref, key_ref, log_ref = refs[2 * count : 2 * count + 4]
-    refs = refs[2 * count + 4 :]
-    dq = None
-    rows = q_ref.shape[0] * q_ref.shape[2]
-    if not first:
-        dq = refs[0][...].reshape(rows, HD)
-        refs = refs[1:]
-    dq_ref, dks, dvs = refs[0], refs[1 : 1 + count], refs[1 + count :]
-    q = q_ref[...].reshape(rows, HD)
-    do = do_ref[...].reshape(rows, HD)
-    inner = jnp.sum(do.astype(F32) * o_ref[...].reshape(rows, HD).astype(F32), axis=1, keepdims=True)
-    lo, pos, log_total = lo_ref[0], pos_ref[...], log_ref[0]
-    for t in range(count):
-        k, v = ks[t][...].reshape(rows, HD), vs[t][...].reshape(rows, HD)
-        key = key_ref[t : t + 1, :]
-        s = dot_nt(q, k) * scale
-        probs = jnp.where((key >= lo) & (key <= pos), jnp.exp(s - log_total), 0.0)
-        ds = (probs * (dot_nt(do, v) - inner)).astype(BF)
-        dvs[t][...] = dot_tn(probs.astype(BF), do).astype(dvs[t].dtype).reshape(dvs[t].shape)
-        dks[t][...] = (dot_tn(ds, q) * scale).astype(dks[t].dtype).reshape(dks[t].shape)
-        part = dot(ds, k) * scale
-        dq = part if dq is None else dq + part
-    dq_ref[...] = dq.reshape(dq_ref.shape)
+def attend_back_kernel(groups, reach, heads, scale, *refs):
+    (
+        grad_ref,
+        weight_ref,
+        in_maps_ref,
+        out_maps_ref,
+        lo_ref,
+        pos_ref,
+        key_ref,
+        lo_rows_ref,
+        query_rows_ref,
+        log_ref,
+        log_rows_ref,
+        q_any,
+        k_any,
+        v_any,
+        o_any,
+    ) = refs[:15]
+    later_any = refs[15]
+    dq_ref, dk_ref, dv_ref, back_ref = refs[16:20]
+    (
+        q_buf,
+        k_buf,
+        v_buf,
+        o_buf,
+        later_buf,
+        do_buf,
+        do_in,
+        inner,
+        inner_in,
+        load_sem,
+        send_sem,
+        recv_sem,
+    ) = refs[20:]
+    p, x, y, c = (lax.axis_index(a) for a in ("p", "x", "y", "c"))
+    right, left = (lax.rem(p + 1, groups), x, y, c), (lax.rem(p + groups - 1, groups), x, y, c)
+    rows = q_buf.shape[2]
+    full = 2 * rows
+    copies = Copies(send_sem, recv_sem)
+    sources = [(q_any, q_buf), (k_any, k_buf), (v_any, v_buf), (o_any, o_buf)]
+    sources.append((later_any, later_buf))
+    loads = []
+    for n, (src, dst) in enumerate(sources):
+        loads.append(pltpu.make_async_copy(src, dst, load_sem.at[n]))
+        loads[-1].start()
+    barrier = pltpu.get_barrier_semaphore()
+    for device in (left, right):
+        pl.semaphore_signal(barrier, inc=1, device_id=device, device_id_type=pl.DeviceIdType.MESH)
+
+    for b in range(2):
+        here = slice(b * full, (b + 1) * full)
+        low = dot_nt(grad_ref[here, :], out_maps_ref[...]).astype(BF)
+        back_ref[here, :] = low
+        value = dot_nt(grad_ref[here, :], weight_ref[...]) + SCALE_ADAPT * dot(low, in_maps_ref[...])
+        do_buf[b] = value.astype(BF).reshape(2, rows, heads * HD)
+    pl.semaphore_wait(barrier, 2)
+    moves = [copies.remote(do_buf, do_in.at[0], left)]
+    for load in loads:
+        load.wait()
+
+    def piece(ref, s, cols, first=0):
+        return ref[first : first + 2, s, :, cols].reshape(full, HD)
+
+    def put(ref, s, cols, value):
+        ref[:, s, :, cols] = value.reshape(2, rows, HD)
+
+    ones = jnp.ones((8, HD), BF)
+
+    def sums(n, carry):
+        s, cols = n // heads, pl.ds(pl.multiple_of(n % heads * HD, HD), HD)
+        product = piece(do_buf, s, cols).astype(F32) * piece(o_buf, s, cols).astype(F32)
+        high = product.astype(BF)
+        low = (product - high.astype(F32)).astype(BF)
+        inner[pl.ds(n, 1), :] = (dot_nt(ones, high) + dot_nt(ones, low))[:1, :]
+        return carry
+
+    lax.fori_loop(0, 2 * heads, sums, 0)
+    inner_moves = [copies.remote(inner, inner_in.at[0], left)]
+
+    def own(n, carry):
+        s, cols = n // heads, pl.ds(pl.multiple_of(n % heads * HD, HD), HD)
+        q, do = piece(q_buf, s, cols), piece(do_buf, s, cols)
+        delta = jnp.sum(do.astype(F32) * piece(o_buf, s, cols).astype(F32), axis=1, keepdims=True)
+        lo, pos, log_total = lo_ref[s], pos_ref[...], log_ref[n]
+        dq = None
+        for t in range(reach + 1):
+            k, v = piece(k_buf, s, cols, 2 * t), piece(v_buf, s, cols, 2 * t)
+            key = key_ref[t : t + 1, :]
+            score = dot_nt(q, k) * scale
+            probs = jnp.where((key >= lo) & (key <= pos), jnp.exp(score - log_total), 0.0)
+            ds = (probs * (dot_nt(do, v) - delta)).astype(BF)
+            part = dot(ds, k)
+            dq = part if dq is None else dq + part
+            if t == 0:
+                put(dv_ref, s, cols, dot_tn(probs.astype(BF), do))
+                put(dk_ref, s, cols, dot_tn(ds, q) * scale)
+        put(dq_ref, s, cols, dq * scale)
+        return carry
+
+    lax.fori_loop(0, 2 * heads, own, 0)
+
+    for t in range(1, reach + 1):
+        moves[-1].wait_recv()
+        inner_moves[-1].wait_recv()
+        if t < reach:
+            moves.append(copies.remote(do_in.at[t - 1], do_in.at[t], left))
+            inner_moves.append(copies.remote(inner_in.at[t - 1], inner_in.at[t], left))
+
+        def from_later(n, carry, t=t):
+            s, cols = n // heads, pl.ds(pl.multiple_of(n % heads * HD, HD), HD)
+            k, v = piece(k_buf, s, cols), piece(v_buf, s, cols)
+            q, do = piece(later_buf.at[t - 1], s, cols), piece(do_in.at[t - 1], s, cols)
+            score = dot_nt(k, q) * scale
+            key = pos_ref[...]
+            lo, pos = lo_rows_ref[t, pl.ds(s, 1), :], query_rows_ref[t : t + 1, :]
+            probs = jnp.where((key >= lo) & (key <= pos), jnp.exp(score - log_rows_ref[t - 1, pl.ds(n, 1), :]), 0.0)
+            ds = (probs * (dot_nt(v, do) - inner_in[t - 1, pl.ds(n, 1), :])).astype(BF)
+            put(dv_ref, s, cols, piece(dv_ref, s, cols) + dot(probs.astype(BF), do))
+            put(dk_ref, s, cols, piece(dk_ref, s, cols) + dot(ds, q) * scale)
+            return carry
+
+        lax.fori_loop(0, 2 * heads, from_later, 0)
+    copies.finish()
+
+
+def attend_back(groups, reach, heads, rows, args, later):
+    own = 4 * rows
+    local = heads * HD
+    vm = pl.BlockSpec(memory_space=pltpu.VMEM)
+    anywhere = pl.BlockSpec(memory_space=pl.ANY)
+    block = lambda n: pltpu.VMEM((2 * n, 2, rows, local), BF)
+    view = lambda v: v.reshape(-1, 2, rows, local)
+    count = 2 * reach
+    dq, dk, dv, back = pl.pallas_call(
+        functools.partial(attend_back_kernel, groups, reach, heads, HD**-0.5),
+        in_specs=[vm] * 11 + [anywhere] * 5,
+        out_specs=[vm] * 4,
+        out_shape=[jax.ShapeDtypeStruct((2, 2, rows, local), F32)] * 3
+        + [jax.ShapeDtypeStruct((own, args[2].shape[0]), BF)],
+        scratch_shapes=[
+            block(1),
+            block(reach + 1),
+            block(reach + 1),
+            block(1),
+            pltpu.VMEM((reach, 2, 2, rows, local), BF),
+            block(1),
+            pltpu.VMEM((reach, 2, 2, rows, local), BF),
+            pltpu.VMEM((2 * heads, 2 * rows), F32),
+            pltpu.VMEM((reach, 2 * heads, 2 * rows), F32),
+            pltpu.SemaphoreType.DMA((5,)),
+            pltpu.SemaphoreType.DMA((count,)),
+            pltpu.SemaphoreType.DMA((count,)),
+        ],
+        compiler_params=pltpu.CompilerParams(
+            collective_id=3, has_side_effects=True, vmem_limit_bytes=VMEM_BYTES
+        ),
+        name="attend_backward",
+        cost_estimate=cost(70),
+    )(*args[:11], *[view(v) for v in args[11:]], later.reshape(reach, 2, 2, rows, local))
+    return [v.reshape(own, local) for v in (dq, dk, dv)], back
 
 
 class Attention:
@@ -811,38 +958,9 @@
             out_shape=[self.shape(BF), jax.ShapeDtypeStruct((2 * self.heads, 2 * self.rows, 1), F32)],
             compiler_params=self.params,
             name="attend_forward",
-            cost_estimate=cost(23),
+            cost_estimate=cost(1),
         )(self.view(q), *[self.view(key)] * count, *[self.view(value)] * count, *self.tables)
         return out.reshape(q.shape), log
-
-    def backward(self, q, do, o, key, value, log, blocks, dtypes, dq=None):
-        lo, pos, key_pos = self.tables
-        count = len(blocks)
-        grads = [self.shape(d) for d in dtypes]
-        key_pos = jnp.concatenate([key_pos[t : t + 1] for t in blocks], axis=0)
-        more = [] if dq is None else [self.view(dq)]
-        parts = [self.part(t) for t in blocks]
-        outs = pl.pallas_call(
-            functools.partial(attend_back_kernel, count, dq is None, HD**-0.5),
-            grid=(2, self.heads),
-            in_specs=[self.block] * 3 + parts * 2 + self.table_specs(count) + [self.log_spec] + [self.block] * len(more),
-            out_specs=[self.block] * (1 + 2 * count),
-            out_shape=[self.shape(F32)] + grads + grads,
-            compiler_params=self.params,
-            name="attend_backward",
-            cost_estimate=cost(4 + 8 * count),
-        )(
-            *[self.view(v) for v in [q, do, o]],
-            *[self.view(key)] * count,
-            *[self.view(value)] * count,
-            lo,
-            pos,
-            key_pos,
-            log,
-            *more,
-        )
-        flat = [v.reshape(q.shape) for v in outs]
-        return flat[0], flat[1 : 1 + count], flat[1 + count :]
 
 
 def rms_inverse(v):
@@ -886,14 +1004,15 @@
         gated_any,
         gate_any,
         up_any,
+        feed_any,
         down_any,
-        gate_w_any,
-        up_w_any,
         middle_any,
         cot_any,
         attn_any,
-    ) = refs[:16]
-    result_ref, mid_ref, grad_attn_ref, back_gu_ref, maps_ref, gb_d_ref = refs[16:22]
+        query_any,
+        log_any,
+    ) = refs[:17]
+    result_ref, mid_ref, grad_attn_ref, back_gu_ref, maps_ref, gb_d_ref, later_any, later_log_any = refs[17:25]
     (
         down_w,
         gate_w,
@@ -910,12 +1029,13 @@
         cot,
         dgu,
         narrow_d,
+        back_d,
         load_sem,
         act_sem,
         free_sem,
         send_sem,
         recv_sem,
-    ) = refs[22:]
+    ) = refs[25:]
     p, x, y, c = (lax.axis_index(a) for a in ("p", "x", "y", "c"))
     core, across, over = (p, x, y, 1 - c), (p, 1 - x, y, c), (p, x, 1 - y, c)
     rows, model = result_ref.shape
@@ -937,14 +1057,29 @@
         return copy
 
     first_order, back_order = (3, 1, 2, 0), (0, 1, 3, 2)
+    groups = feed_any.shape[0]
+    depth = model // groups
+    reach = later_any.shape[0]
     loaded = load(0, down_any, down_w)
     gated_loads = [load_acts(0, 0, first_order[0]), load_acts(1, 0, first_order[1])]
     middle_load, cot_load = load(1, middle_any, tokens), load(2, cot_any, cot)
-    gate_load, up_load = load(3, gate_w_any, gate_w), load(4, up_w_any, up_w)
+    feed_loads = []
+    for k in range(groups):
+        for n, dst in enumerate((gate_w, up_w)):
+            src = feed_any.at[k, :, pl.ds(n * hidden, hidden)]
+            feed_loads.append(load(4 + 2 * k + n, src, dst.at[pl.ds(k * depth, depth)]))
+    ring = lax.axis_size("p")
+    right, left = (lax.rem(p + 1, ring), x, y, c), (lax.rem(p + ring - 1, ring), x, y, c)
     barrier = pltpu.get_barrier_semaphore()
-    for device in (core, across, over):
+    for device in (core, across, over, right, left):
         pl.semaphore_signal(barrier, inc=1, device_id=device, device_id_type=pl.DeviceIdType.MESH)
-    pl.semaphore_wait(barrier, 3)
+    pl.semaphore_wait(barrier, 5)
+
+    def pull(t):
+        src = (query_any, log_any) if t == 0 else (later_any.at[t - 1], later_log_any.at[t - 1])
+        return [copies.remote(src[0], later_any.at[t], left), copies.remote(src[1], later_log_any.at[t], left)]
+
+    pulls = pull(0)
     maps_ref[...] = jnp.zeros_like(maps_ref)
     gb_d_ref[...] = jnp.zeros_like(gb_d_ref)
 
@@ -974,52 +1109,71 @@
     def backward(k, slot):
         here = slice(k * pair, (k + 1) * pair)
         grad = blocks[2 * k : 2 * k + 2].reshape(pair, model)
-        back_d = dot_nt(grad, d_out_ref[...]).astype(BF)
+        low_d = dot_nt(grad, d_out_ref[...]).astype(BF)
+        back_d[here, :] = low_d
         gb_d_ref[...] += SCALE_ADAPT * dot_tn(narrow_d[here, :], grad)
 
         def tile(t, carry):
             cols = pl.ds(pl.multiple_of(t * 256, 256), 256)
             grad = blocks[2 * k : 2 * k + 2].reshape(pair, model)
-            dm = dot_nt(grad, down_w[cols, :]) + SCALE_ADAPT * dot(back_d, d_in_ref[:, cols])
+            dm = dot_nt(grad, down_w[cols, :]) + SCALE_ADAPT * dot(low_d, d_in_ref[:, cols])
             gate, up = acts[slot, 1, :, cols].astype(F32), acts[slot, 2, :, cols].astype(F32)
             sig = jax.nn.sigmoid(gate)
             silu = gate * sig
-            du = (dm * silu).astype(BF)
-            dg = (dm * up * (sig + silu * (1.0 - sig))).astype(BF)
-            dgu[0, :, cols] = dg
-            dgu[1, :, cols] = du
-            narrow = narrow_gu_ref[here, :]
-            maps_ref[0, :, cols] += SCALE_ADAPT * dot_tn(back_d, acts[slot, 0, :, cols])
-            maps_ref[1, :, cols] += SCALE_ADAPT * dot_tn(narrow[:, :rank], dg)
-            maps_ref[2, :, cols] += SCALE_ADAPT * dot_tn(narrow[:, rank:], du)
+            dgu[k, 0, :, cols] = (dm * up * (sig + silu * (1.0 - sig))).astype(BF)
+            dgu[k, 1, :, cols] = (dm * silu).astype(BF)
             return carry
 
         lax.fori_loop(0, hidden // 256, tile, 0)
-        back_g = dot_nt(dgu[0], gu_out_ref[0]).astype(BF)
-        back_u = dot_nt(dgu[1], gu_out_ref[1]).astype(BF)
-        back_gu_ref[here, :rank] = back_g
-        back_gu_ref[here, rank:] = back_u
+        back_gu_ref[here, :rank] = dot_nt(dgu[k, 0], gu_out_ref[0]).astype(BF)
+        back_gu_ref[here, rank:] = dot_nt(dgu[k, 1], gu_out_ref[1]).astype(BF)
 
         def body(n, carry):
             cols = columns(n)
-            value = dot_nt(dgu[0], gate_w[cols, :]) + dot_nt(dgu[1], up_w[cols, :])
-            value = value + SCALE_ADAPT * (dot(back_g, gu_in_ref[:rank, cols]) + dot(back_u, gu_in_ref[rank:, cols]))
-            store(k, cols, value)
+            value = dot_nt(dgu[k, 0], gate_w[cols, :]) + dot_nt(dgu[k, 1], up_w[cols, :])
+            store(k, cols, value + SCALE_ADAPT * dot(back_gu_ref[here, :], gu_in_ref[:, cols]))
             return carry
 
         lax.fori_loop(0, model // 512, body, 0)
+
+    def adapter_maps():
+        turns = [load_acts(k, 0, k) for k in range(2)]
+        for k in range(4):
+            here = slice(k * pair, (k + 1) * pair)
+            turns[k].wait()
+            maps_ref[0] += SCALE_ADAPT * dot_tn(back_d[here, :], acts[k % 2, 0])
+            if k < 2:
+                turns.append(load_acts(k + 2, 0, k + 2))
+            for n in range(2):
+                narrow = narrow_gu_ref[here, n * rank : (n + 1) * rank]
+                maps_ref[1 + n] += SCALE_ADAPT * dot_tn(narrow, dgu[k, n])
 
     def to_core(k):
         return copies.remote(part(k).at[1], core_in.at[k], core)
 
+    def by_tiles(size, work):
+        def body(n, carry):
+            work(pl.ds(pl.multiple_of(n * 64, 64), 64))
+            return carry
+
+        lax.fori_loop(0, size // 64, body, 0)
+
     def meet(k, copy):
         copy.wait_recv()
-        blocks[2 * k] = (blocks[2 * k].astype(F32) + core_in[k].astype(F32)).astype(BF)
+
+        def work(tile):
+            blocks[2 * k, tile, :] = (blocks[2 * k, tile, :].astype(F32) + core_in[k, tile, :].astype(F32)).astype(BF)
+
+        by_tiles(rows, work)
 
     top, low = pl.ds(0, half), pl.ds(half, half)
 
-    def add(block, here, more):
-        blocks[block, here, :] = (blocks[block, here, :].astype(F32) + more[...].astype(F32)).astype(BF)
+    def add(block, start, more):
+        def work(tile):
+            here = pl.ds(tile.start + start, tile.size)
+            blocks[block, here, :] = (blocks[block, here, :].astype(F32) + more[tile, :].astype(F32)).astype(BF)
+
+        by_tiles(half, work)
 
     def far_halves():
         return (
@@ -1034,17 +1188,18 @@
         far_x, far_y = far
         parts.append(copies.remote(blocks.at[4, low], over_in.at[low], over))
         far_y.wait_recv()
-        add(2, low, by_y)
+        add(2, half, by_y)
         parts.append(copies.remote(blocks.at[2, low], across_in.at[low], across))
         far_x.wait_recv()
-        add(4, top, by_x)
+        add(4, 0, by_x)
         parts.append(copies.remote(blocks.at[4, top], over_in.at[top], over))
         own.wait_recv()
         for copy in parts:
             copy.wait_recv()
-        return (
-            own_pair[0].astype(F32) + core_in[0].astype(F32) + across_in[...].astype(F32) + over_in[...].astype(F32)
-        )
+
+    def summed(tile):
+        total = own_pair[0, tile, :].astype(F32) + core_in[0, tile, :].astype(F32)
+        return total + across_in[tile, :].astype(F32) + over_in[tile, :].astype(F32)
 
     loaded.wait()
     gated_loads[0].wait()
@@ -1067,30 +1222,38 @@
     own = to_core(0)
     meet(2, sent2)
     act_loads = [[load_acts(0, kind, 0) for kind in range(3)], [load_acts(1, kind, 1) for kind in range(3)]]
-    feed = finish_sum(far, own, parts)
+    finish_sum(far, own, parts)
     copies.finish()
     for device in (core, across, over):
         pl.semaphore_signal(free_sem, inc=1, device_id=device, device_id_type=pl.DeviceIdType.MESH)
-    gain = feed_gain_ref[...]
     middle_load.wait()
     cot_load.wait()
-    result_ref[...] = (tokens[...] + feed * rms_inverse(feed) * gain).astype(BF)
-    blocks[0] = rms_backward(feed, gain, cot[...].astype(F32)).astype(BF)
+
+    def close(tile):
+        feed, gain = summed(tile), feed_gain_ref[...]
+        result_ref[tile, :] = (tokens[tile, :] + feed * rms_inverse(feed) * gain).astype(BF)
+        blocks[0, tile, :] = rms_backward(feed, gain, cot[tile, :].astype(F32)).astype(BF)
+
+    by_tiles(rows, close)
 
     pl.semaphore_wait(free_sem, 3)
     copies.all = []
     to_x = copies.remote(blocks.at[0], blocks.at[2], across)
     to_y = copies.remote(blocks.at[0], blocks.at[4], over)
     to_c = copies.remote(blocks.at[0], blocks.at[1], core)
-    attn_load = load(5, attn_any, tokens)
-    gate_load.wait()
-    up_load.wait()
+    attn_load = load(3, attn_any, tokens)
+    for copy in feed_loads:
+        copy.wait()
     to_c.wait_recv()
     for copy in act_loads[0]:
         copy.wait()
     backward(0, 0)
     own = to_core(0)
     act_loads.append([load_acts(2, kind, 3) for kind in range(3)])
+    for t in range(1, reach):
+        for copy in pulls:
+            copy.wait_recv()
+        pulls = pull(t)
     to_x.wait_recv()
     x_on = [copies.remote(blocks.at[2], blocks.at[3], core), copies.remote(blocks.at[2, top], blocks.at[6, top], over)]
     to_y.wait_recv()
@@ -1124,11 +1287,15 @@
     backward(2, 1)
     sent2 = to_core(2)
     meet(2, sent2)
-    total_grad = finish_sum(far, own, parts)
-    mid = cot[...].astype(F32) + total_grad
-    mid_ref[...] = mid
+    finish_sum(far, own, parts)
     attn_load.wait()
-    grad_attn_ref[:rows, :] = rms_backward(tokens[...], attn_gain_ref[...], mid).astype(BF)
+
+    def open_attention(tile):
+        mid = cot[tile, :].astype(F32) + summed(tile)
+        mid_ref[tile, :] = mid
+        grad_attn_ref[tile, :] = rms_backward(tokens[tile, :], attn_gain_ref[...], mid).astype(BF)
+
+    by_tiles(rows, open_attention)
 
     def block(k):
         return grad_attn_ref.at[pl.ds(k * rows, rows)]
@@ -1137,26 +1304,29 @@
     to_c = copies.remote(block(0), block(1), core)
     to_x.wait_recv()
     on = copies.remote(block(2), block(3), core)
+    adapter_maps()
     to_c.wait_recv()
     on.wait_recv()
+    for copy in pulls:
+        copy.wait_recv()
     done = (*x_on, far_on, *y_on)
     for copy in copies.all:
         if not any(copy is other for other in done):
             copy.wait_send()
 
 
-def feed_layer(maps, narrow_gu, acts, weights, middle, cot, attn_out):
+def feed_layer(maps, narrow_gu, acts, weights, middle, cot, attn_out, query, log, reach):
     rows, model = cot.shape
-    hidden = weights[0].shape[0]
+    groups, hidden = weights[0].shape[0], weights[1].shape[0]
     rank = maps[0].shape[0]
     vm = pl.BlockSpec(memory_space=pltpu.VMEM)
     anywhere = pl.BlockSpec(memory_space=pl.ANY)
     block = lambda *shape: pltpu.VMEM(shape, BF)
-    count = 48
+    count = 48 + 2 * reach
     return pl.pallas_call(
         feed_kernel,
-        in_specs=[vm] * 7 + [anywhere] * 9,
-        out_specs=[vm] * 6,
+        in_specs=[vm] * 7 + [anywhere] * 10,
+        out_specs=[vm] * 6 + [anywhere] * 2,
         out_shape=[
             jax.ShapeDtypeStruct((rows, model), BF),
             jax.ShapeDtypeStruct((rows, model), F32),
@@ -1164,6 +1334,8 @@
             jax.ShapeDtypeStruct((8 * rows, 2 * rank), BF),
             jax.ShapeDtypeStruct((3, rank, hidden), F32),
             jax.ShapeDtypeStruct((rank, model), F32),
+            jax.ShapeDtypeStruct((reach,) + query.shape, BF),
+            jax.ShapeDtypeStruct((reach,) + log.shape, F32),
         ],
         scratch_shapes=[
             block(hidden, model),
@@ -1179,9 +1351,10 @@
             block(rows, model),
             pltpu.VMEM((rows, model), F32),
             block(rows, model),
-            block(2, 2 * rows, hidden),
+            block(4, 2, 2 * rows, hidden),
             block(8 * rows, rank),
-            pltpu.SemaphoreType.DMA((6,)),
+            block(8 * rows, rank),
+            pltpu.SemaphoreType.DMA((2 * groups + 4,)),
             pltpu.SemaphoreType.DMA((2, 3)),
             pltpu.SemaphoreType.REGULAR,
             pltpu.SemaphoreType.DMA((count,)),
@@ -1192,7 +1365,7 @@
         ),
         name="feed_layer",
         cost_estimate=cost(170),
-    )(*maps, narrow_gu, *acts, *weights, middle, cot, attn_out)
+    )(*maps, narrow_gu, *acts, *weights, middle, cot, attn_out, query, log)
 
 
 def by_rows(kernel, name, rows, width, args, dtypes, us):
@@ -1255,27 +1428,21 @@
         v = pick(v, n + 2, at.y)
         return pick(v, n + 1, at.x).reshape(lead + (-1,))
 
-    def gather_p(v):
-        return lax.all_gather(v, "p", axis=0, tiled=True)
-
     own_inputs = layer_input[0]
     head_offsets = lambda x, y, c: [4 * k + 2 * x + c for k in range(heads)]
     feed_offsets = lambda x, y, c: [((2 * p + x) * 2 + y) * 2 + c for p in range(at.np)]
-    w_qkv, gate_piece, up_piece, inputs = start(
+    w_qkv, feed_piece, inputs, o_own = start(
         at.np,
         reach,
         pack(at.spot, [query_weight, key_weight, value_weight], HD, head_offsets, TURNS4),
         pack(at.spot, [gate_weight], hidden_rows, feed_offsets, TURNS8),
         pack(at.spot, [up_weight], hidden_rows, feed_offsets, TURNS8),
         own_inputs,
+        output_weight,
     )
-    w_g = gather_p(gate_piece)
-    w_u = gather_p(up_piece)
-    w_d = gather_p(after(down_weight, w_g))
+    w_gu = lax.all_gather(feed_piece, "p", axis=0)
     if 2 * depth == HD:
-        o_own = gather_p(output_weight)
-        o_sent = after(o_own, w_qkv)
-        sent = lambda target: lax.ppermute(o_sent, ("y", "c"), target)
+        sent = lambda target: lax.ppermute(o_own, ("y", "c"), target)
         same = at.y == at.c
         mine_half = jnp.where(same, o_own, sent([(0, 2), (3, 1)]))
         other_half = jnp.where(same, sent([(1, 0), (2, 3)]), sent([(1, 2), (2, 1)]))
@@ -1315,8 +1482,12 @@
     lengths = lax.dynamic_slice_in_dim(document_length, 2 * at.y, 2, 0)
     bounds = jnp.cumsum(lengths, axis=1)
     bounds = jnp.where(at.c == 0, bounds, bounds[::-1])
-    begin = jnp.max(jnp.where(bounds[:, None, :] <= pos[None, :, None], bounds[:, None, :], 0), axis=2)
-    lo = jnp.maximum(begin, pos[None] - (WINDOW - 1))
+
+    def lo_of(pos):
+        begin = jnp.max(jnp.where(bounds[:, None, :] <= pos[None, :, None], bounds[:, None, :], 0), axis=2)
+        return jnp.maximum(begin, pos[None] - (WINDOW - 1))
+
+    lo = lo_of(pos)
     key = jnp.stack([pos - 2 * rows * t for t in range(count)])
     attention = Attention(rows, heads, count, lo[:, :, None], pos[:, None], key)
 
@@ -1332,14 +1503,11 @@
     pre_q, pre_k, value_all, narrow_qkv, square_q, square_k = project(
         inputs, own, w_qkv, a_qkv, b_qkv, heads
     )
-    inputs = inputs[:own]
-    narrow_qkv = narrow_qkv[:own]
+    w_d = lax.all_gather(after(down_weight, square_q), "p", axis=0, tiled=True)
     squares = jnp.concatenate([square_q[:1], square_k[:1]], axis=1)
     inv = lax.rsqrt(at.sum4(squares, 2 + reach) / width + EPS).reshape(-1, 1)
     inv_q, inv_k = inv[:own], inv[own:]
     query, key_all = post(pre_q, pre_k, inv_q, inv_k, gain, cos, sin, heads)
-    cos, sin = cos[:own], sin[:own]
-    inv_k = inv_k[:own]
     o, log = attention.forward(query, key_all, value_all)
     narrow_o = dot_nt(o, a_o).astype(BF)
     def attn_part(part, mark=None):
@@ -1362,26 +1530,43 @@
     )
     middle_low = jnp.concatenate(at.gather8(low)[0])
     narrow_gu = dot_nt(middle_low, a_gu).astype(BF)
-    gate, up, gated = gate_up(middle_low, w_g, w_u, narrow_gu, b_gu)
-    result, grad_mid, grad_attn, back_gu, wide, gb_d = feed_layer(
+    gate, up, gated = gate_up(middle_low, w_gu, narrow_gu, b_gu)
+    result, grad_mid, grad_attn, back_gu, wide, gb_d, later, later_logs = feed_layer(
         (a_d, b_d, b_gu, a_gu, feed_gain, attn_gain),
         narrow_gu,
         (gated, gate, up),
-        (w_d, w_g, w_u),
+        (w_gu, w_d),
         middle,
         cotangent[0],
         attn_out,
+        query,
+        log[:, :, 0],
+        reach,
     )
-    back_o = dot_nt(grad_attn, b_o).astype(BF)
-    grad_o = (dot_nt(grad_attn, w_o) + SCALE_ADAPT * dot(back_o, a_o)).astype(BF)
-    dq, dks, dvs = attention.backward(query, grad_o, o, key_all, value_all, log, [reach], [BF])
-    moved_k, moved_v = at.shift_p(dks[0], -1), at.shift_p(dvs[0], -1)
-    dq, dks, dvs = attention.backward(
-        query, grad_o, o, key_all, value_all, log, range(reach), [F32] + [BF] * (reach - 1), dq
+    lo_rows = jnp.stack([lo_of(pos + 2 * rows * t) for t in range(count)])
+    query_rows = jnp.stack([pos + 2 * rows * t for t in range(count)])
+    (dq, dk, dv), back_o = attend_back(
+        at.np,
+        reach,
+        heads,
+        rows,
+        [
+            grad_attn,
+            w_o,
+            a_o,
+            b_o,
+            *attention.tables,
+            lo_rows,
+            query_rows,
+            log,
+            later_logs,
+            query,
+            key_all,
+            value_all,
+            o,
+        ],
+        later,
     )
-    for t in range(reach - 1, 0, -1):
-        moved_k = at.shift_p((dks[t].astype(F32) + moved_k.astype(F32)).astype(BF), -1)
-        moved_v = at.shift_p((dvs[t].astype(F32) + moved_v.astype(F32)).astype(BF), -1)
     def share_y(mine, other):
         return mine + at.swap_y(other)
 
@@ -1412,12 +1597,10 @@
             heads,
             [
                 dq,
-                dks[0],
-                dvs[0],
-                moved_k,
-                moved_v,
+                dk,
+                dv,
                 pre_q,
-                pre_k[:own],
+                pre_k,
                 inv_q,
                 inv_k,
                 gain,
@@ -1437,9 +1620,9 @@
         early, late = sums[:5], sums[5:]
     else:
         early = sum_model(after(early, dq))
+        inputs, narrow_qkv, pre_k, inv_k, cos, sin = (v[:own] for v in (inputs, narrow_qkv, pre_k, inv_k, cos, sin))
         wide = wide.reshape(-1, at.np, hidden_rows)
-        dk = after(dks[0] + moved_k.astype(F32), early)
-        dv = dvs[0] + moved_v.astype(F32)
+        dk = after(dk, early)
         turn, inner = unpost(dq, dk, pre_q, pre_k, gain, cos, sin, heads)
         inner = at.sum4(inner.T, 1).T / width
 
@@ -1448,7 +1631,7 @@
             return (scale * turn[:, cols] - pre * (scale * scale * scale * inner[:, part : part + 1])).astype(BF)
 
         grad_qkv = jnp.concatenate(
-            [unnorm(0, pre_q, inv_q), unnorm(1, pre_k[:own], inv_k), dv.astype(BF)], axis=1
+            [unnorm(0, pre_q, inv_q), unnorm(1, pre_k, inv_k), dv.astype(BF)], axis=1
         )
         back_qkv = dot_nt(grad_qkv, b_qkv_diag).astype(BF)
 

time: 795 us -> 748 us (0.941)
  waiting for transfers between devices: 112 us -> 53.9 us
  Pallas kernels: 537 us -> 564 us
  local copies, waits for them, and re-layouts: 50.3 us -> 39.8 us
  matrix products: 24.5 us -> 16 us
    ppermute x7 -> x3, waiting for transfers between devices: 60.2 us -> 0.01 us  [on_device(): sent = lambda target: lax.ppermute(o_own, ('y', 'c'), target)]
    pallas_call x4 -> x3, Pallas kernels: 248 us -> 278 us  [the longest x1 188 us: feed_layer(): pl.pallas_call(feed_kernel, in_specs=[vm] * 7 + [anywhere] * 10, out_spec...]
    slice x5 -> x0, local copies, waits for them, and re-layouts: 10.7 us -> none  [the longest x1 4.84 us: on_device(): inputs = inputs[:own]]
    dot_general x12 -> x9, matrix products: 24.5 us -> 16 us  [dot(): return lax.dot_general(a, b, (dims, ((), ())), preferred_element_type=F32)]
  transfers between devices with their start and end apart: 25 -> 19, of which waited for: 11 -> 8; matrix products, arithmetic and copies ran while one was open for 10% -> 8% of each run, Pallas kernels for 34% -> 14%
where the time goes in v4:
time: 748 us; the launch traced here: 737 us
  Pallas kernels  564 us (75%)
  waiting for transfers between devices  53.9 us (7%)
  local copies, waits for them, and re-layouts  39.8 us (5%)
  other arithmetic  27.8 us (4%)
  starting transfers between devices  19.5 us (3%)
  matrix products  16 us (2%)
  between operations  15.9 us (2%)
    pallas_call x1, Pallas kernels, feed_layer(): pl.pallas_call(feed_kernel, in_specs=[vm] * 7 + [anywhere] * 10, out_spec...  188 us
    pallas_call x1, Pallas kernels, start(): pl.pallas_call(functools.partial(start_kernel, groups, reach), in_specs=[...  135 us
    pallas_call x1, Pallas kernels, finish(): pl.pallas_call(functools.partial(finish_kernel, groups, heads, early_rows...  70.1 us
    pallas_call x1, Pallas kernels, attend_back(): pl.pallas_call(functools.partial(attend_back_kernel, groups, reach, heads...  63.5 us
    ppermute x4, waiting for transfers between devices, swap_x(): return lax.ppermute(value, 'x', SWAP)  40.1 us
    pallas_call x1, Pallas kernels, project(): pl.pallas_call(functools.partial(project_kernel, heads, own_tiles), grid=...  33.1 us
    pallas_call x1, Pallas kernels, gate_up(): pl.pallas_call(gate_up_kernel, grid=(steps,), in_specs=[pl.BlockSpec((row...  26.9 us
    pallas_call x1, Pallas kernels, forward(): pl.pallas_call(functools.partial(attend_kernel, count, HD ** (-0.5)), gri...  23.5 us
  transfers between devices with their start and end apart: 19, of which 8 were waited for; matrix products, arithmetic and copies ran while one was open for 8% of the time, Pallas kernels for 14%

profile of v4, /device:TPU:0, one launch (start us, length us, event | category | flops | bytes accessed | tf_op | source)
XLA Modules:
  0.0 737.0 jit_solution(3626029544839095484)
XLA Ops:
  7.9 2.6 pack_columns.4
  10.5 2.3 pack_columns.5
  12.8 2.2 pack_columns.3
  15.0 134.6 %start.1 = (bf16[4,2,2,128,1536]{4,3,2,1,0:T(8,128)(2,1)}, bf16[512,2048]{1,0:T(8,128)(2,1)}, bf16[3072,2048]{1,0:T(8,128)(2,1)}, bf16[4,64,2048]{2,1,0:T(8,128)(2,1)}) custom-call(bf16[64,1536]{1,0:T(8,128)(2,1)} %get-tuple-element.63.refs_0_, bf16[64,1536]{1,0:T(8,128)(2,1)} %get-tuple-element.64.refs_1_, bf16[64,1536]{1,0:T(8,128)(2,1)} %get-tuple-element.65.refs_2_, ...), custom_call_target="tpu_custom_call" | custom-call | flops 131999997952 | bytes 120000000 | tf_op jit(solution)/shard_map/start/pallas_call | solution.py:304
  149.6 4.4 collective-permute-start.3
  154.0 1.3 collective-permute-start.4
  155.3 1.7 collective-permute-start.5
  157.6 1.0 constant_dynamic-slice_fusion
  160.4 33.1 %project.1 = (f32[1024,512]{1,0:T(8,128)}, f32[3072,512]{1,0:T(8,128)}, bf16[3072,512]{1,0:T(8,128)(2,1)}, bf16[3072,48]{1,0:T(8,128)(2,1)}, f32[8,1024]{1,0:T(8,128)}, /*index=5*/f32[8,3072]{1,0:T(8,128)}) custom-call(bf16[3072,2048]{1,0:T(8,128)(2,1)} %get-tuple-element.83.x_ref.refs_16_, bf16[2048,1536]{1,0:T(8,128)(2,1)} %bitcast.112, ...), custom_call_target="tpu_custom_call" | custom-call | flops 1100000000 | bytes 1000000 | tf_op jit(solution)/shard_map/project/pallas_call | solution.py:391
  193.5 0.9 slice.151
  195.2 2.4 collective-permute-start
  198.6 1.0 copy.64
  201.0 1.5 dynamic-slice_bitcast_fusion
  202.6 2.0 broadcast_maximum_fusion.refs_6_.refs_4_
  204.5 5.8 fusion
  210.3 1.6 pad_maximum_fusion.1.cos_ref.refs_8_
  212.0 1.6 pad_maximum_fusion.2.sin_ref.refs_9_
  215.2 0.9 collective-permute-start.2
  219.5 1.7 copy.63.inv_k_ref.refs_6_
  221.2 1.0 copy.62.inv_q_ref.refs_5_
  222.2 12.0 %rope_forward.1 = (bf16[1024,512]{1,0:T(8,128)(2,1)}, bf16[3072,512]{1,0:T(8,128)(2,1)}) custom-call(f32[1024,512]{1,0:T(8,128)} %get-tuple-element.85.q_ref.refs_3_, f32[3072,512]{1,0:T(8,128)} %get-tuple-element.86.k_ref.refs_4_, f32[1024,1]{1,0:T(8,128)} %copy.62.inv_q_ref.refs_5_, f32[3072,1]{1,0:T(8,128)} %copy.63.inv_k_ref.refs_6_, ...), custom_call_target="tpu_custom_call" | custom-call | flops 1100000000 | bytes 1000000 | tf_op jit(solution)/shard_map/rope_forward/pallas_call | solution.py:440
  234.2 23.5 %attend_forward.1 = (bf16[2,2,256,512]{3,2,1,0:T(8,128)(2,1)}, f32[8,512,1]{2,1,0:T(8,128)}) custom-call(bf16[2,2,256,512]{3,2,1,0:T(8,128)(2,1)} %bitcast.119, bf16[6,2,256,512]{3,2,1,0:T(8,128)(2,1)} %bitcast.103, bf16[6,2,256,512]{3,2,1,0:T(8,128)(2,1)} %bitcast.104, bf16[6,2,256,512]{3,2,1,0:T(8,128)(2,1)} %bitcast.105, ...), custom_call_target="tpu_custom_call" | custom-call | flops 1100000000 | bytes 1000000 | tf_op jit(solution)/shard_map/attend_forward/pallas_call | solution.py:953
  257.7 1.7 convolution_convert_fusion.1
  259.3 2.1 fusion.9
  261.5 1.5 broadcast_select_fusion.3
  263.2 1.3 fusion.15
  265.3 1.4 copy-done.6
  266.7 1.2 slice.201
  268.6 2.5 collective-permute-done.6
  271.1 1.9 add_convert_fusion.2
  273.0 1.4 collective-permute-start.8
  274.4 1.3 fusion.16
  276.7 1.5 constant_dynamic-slice_fusion.7
  278.1 1.1 collective-permute-done.7.refs_1_
  279.3 19.3 %collective-permute-done.8.refs_2_ = bf16[256,2048]{1,0:T(8,128)(2,1)S(1)} collective-permute-done((bf16[256,2048]{1,0:T(8,128)(2,1)S(1)}, bf16[256,2048]{1,0:T(8,128)(2,1)S(1)}, u32[]{:S(2)}, u32[]{:S(2)}) %collective-permute-start.8) | collective-permute-done | bytes 1048608 | tf_op jit(solution)/shard_map/ppermute | solution.py:51
  298.6 1.0 copy-done.21
  299.6 5.6 after_attention.1
  305.2 1.3 collective-permute-start.10
  307.1 1.6 collective-permute-start.12
  309.3 1.0 constant_dynamic-slice_fusion.8
  310.3 19.7 %collective-permute-done.10 = bf16[256,2048]{1,0:T(8,128)(2,1)S(1)} collective-permute-done((bf16[256,2048]{1,0:T(8,128)(2,1)}, bf16[256,2048]{1,0:T(8,128)(2,1)S(1)}, u32[]{:S(2)}, u32[]{:S(2)}) %collective-permute-start.10) | collective-permute-done | bytes 1048608 | tf_op jit(solution)/shard_map/ppermute | solution.py:51
  331.2 1.2 reshape.554
  332.4 1.3 dynamic-slice_reduce_fusion
  335.4 2.8 reduce.5.refs_16_
  338.2 1.3 collective-permute-start.14
  339.6 1.6 collective-permute-start.15
  341.2 1.3 constant_dynamic-update-slice_fusion.9
  342.6 1.3 constant_dynamic-update-slice_fusion.8
  343.9 8.7 %collective-permute-done.14 = bf16[128,2048]{1,0:T(8,128)(2,1)S(1)} collective-permute-done((bf16[128,2048]{1,0:T(8,128)(2,1)S(1)}, bf16[128,2048]{1,0:T(8,128)(2,1)S(1)}, u32[]{:S(2)}, u32[]{:S(2)}) %collective-permute-start.14) | collective-permute-done | bytes 524320 | tf_op jit(solution)/shard_map/ppermute | solution.py:57
  352.6 1.1 collective-permute-done.15
  353.9 1.3 constant_dynamic-update-slice_fusion.6
  355.4 1.1 collective-permute-done.16
  356.6 3.2 copy-done.2
  359.9 3.2 convolution_convert_fusion.narrow_ref.refs_6_
  363.0 26.9 %gate_up.1 = (bf16[2048,1024]{1,0:T(8,128)(2,1)}, bf16[2048,1024]{1,0:T(8,128)(2,1)}, bf16[2048,1024]{1,0:T(8,128)(2,1)}) custom-call(bf16[2048,2048]{1,0:T(8,128)(2,1)} %copy-done.2, bf16[4,512,2048]{2,1,0:T(8,128)(2,1)} %bitcast.96, bf16[4,512,2048]{2,1,0:T(8,128)(2,1)} %bitcast.97, bf16[2048,32]{1,0:T(8,128)(2,1)} %convolution_convert_fusion.narrow_ref.refs_6_, ...), custom_call_target="tpu_custom_call" | custom-call | flops 1100000000 | bytes 1000000 | tf_op jit(solution)/shard_map/gate_up/pallas_call | solution.py:343
  389.9 187.8 %feed_layer.1 = (bf16[256,2048]{1,0:T(8,128)(2,1)}, f32[256,2048]{1,0:T(8,128)}, bf16[1024,2048]{1,0:T(8,128)(2,1)}, bf16[2048,32]{1,0:T(8,128)(2,1)}, f32[3,16,...) custom-call(bf16[16,1024]{1,0:T(8,128)(2,1)} %bitcast.142, ...), custom_call_target="tpu_custom_call" | custom-call | flops 186999996416 | bytes 170000000 | tf_op jit(solution)/shard_map/feed_layer/pallas_call | solution.py:1326
  577.7 5.3 convolution_multiply_fusion
  583.7 63.5 %attend_backward.1 = (f32[2,2,256,512]{3,2,1,0:T(8,128)}, f32[2,2,256,512]{3,2,1,0:T(8,128)}, f32[2,2,256,512]{3,2,1,0:T(8,128)}, bf16[1024,16]{1,0:T(8,128)(2,1)}) custom-call(bf16[1024,2048]{1,0:T(8,128)(2,1)} %get-tuple-element.105.refs_0_, bf16[512,2048]{1,0:T(8,128)(2,1)} %bitcast.108, bf16[16,512]{1,0:T(8,128)(2,1)} %bitcast.144, ...), custom_call_target="tpu_custom_call" | custom-call | flops 76999999488 | bytes 70000000 | tf_op jit(solution)/shard_map/attend_backward/pallas_call | solution.py:900
  647.2 1.2 convolution_multiply_fusion.2
  648.7 0.9 pad_maximum_fusion.4.refs_13_
  649.6 70.1 %finish.1 = (f32[256,2048]{1,0:T(8,128)}, f32[176,64]{1,0:T(8,128)}, f32[48,256]{1,0:T(8,128)}) custom-call(f32[1024,512]{1,0:T(8,128)} %bitcast.153, f32[1024,512]{1,0:T(8,128)} %bitcast.154, f32[1024,512]{1,0:T(8,128)} %bitcast.155, f32[1024,512]{1,0:T(8,128)} %get-tuple-element.85.q_ref.refs_3_, f32[3072,512]{1,0:T(8,128)} %get-tuple-element.86.k_ref.refs_4_, ...), custom_call_target="tpu_custom_call" | custom-call | flops 65999998976 | bytes 60000000 | tf_op jit(solution)/shard_map/finish/pallas_call | solution.py:698
  719.7 0.9 fusion.10
  726.7 1.0 copy.96
  727.7 1.3 copy.97
  (160 shorter events, 25.6 us)
Async XLA Ops:
  7.2 152.5 %copy-start = (bf16[8,6,16,2048]{3,2,1,0:T(8,128)(2,1)S(1)}, bf16[8,6,16,2048]{3,2,1,0:T(8,128)(2,1)}, u32[]{:S(2)}) copy-start(bf16[8,6,16,2048]{3,2,1,0:T(8,128)(2,1)} %param.34) | copy-start | bytes 9437188
  7.2 355.9 %all-gather.6.cloned.1.call-start = ((), (), s32[]{:S(2)}) async-start(), calls=%async_computation.1 | async-start | bytes 10485760 | tf_op jit(solution)/shard_map/all_gather | solution.py:1443
  149.6 240.3 %all-gather.4.cloned.1.call-start = ((), (), s32[]{:S(2)}) async-start(), calls=%async_computation | async-start | bytes 5242880 | tf_op jit(solution)/shard_map/all_gather | solution.py:1506
  149.6 111.8 %collective-permute-start.3 = (bf16[256,2048]{1,0:T(8,128)(2,1)}, bf16[256,2048]{1,0:T(8,128)(2,1)}, u32[]{:S(2)}, u32[]{:S(2)}) collective-permute-start(bf16[256,2048]{1,0:T(8,128)(2,1)} %bitcast.122), channel_id=1, source_target_pairs={{0,2},{3,1},{4,6},{7,5},{8,10},{11,9},{12,14},{15,13},{16,18},{19,... | collective-permute-start | bytes 3145736 | tf_op jit(solution)/shard_map/ppermute | solution.py:1445
  154.0 107.5 %collective-permute-start.4 = (bf16[256,2048]{1,0:T(8,128)(2,1)}, bf16[256,2048]{1,0:T(8,128)(2,1)}, u32[]{:S(2)}, u32[]{:S(2)}) collective-permute-start(bf16[256,2048]{1,0:T(8,128)(2,1)} %bitcast.123), channel_id=1, source_target_pairs={{1,0},{2,3},{5,4},{6,7},{9,8},{10,11},{13,12},{14,15},{17,16},{18,... | collective-permute-start | bytes 3145736 | tf_op jit(solution)/shard_map/ppermute | solution.py:1445
  155.3 106.2 %collective-permute-start.5 = (bf16[256,2048]{1,0:T(8,128)(2,1)}, bf16[256,2048]{1,0:T(8,128)(2,1)}, u32[]{:S(2)}, u32[]{:S(2)}) collective-permute-start(bf16[256,2048]{1,0:T(8,128)(2,1)} %bitcast.124), channel_id=1, source_target_pairs={{1,2},{2,1},{5,6},{6,5},{9,10},{10,9},{13,14},{14,13},{17,18},{18,... | collective-permute-start | bytes 3145736 | tf_op jit(solution)/shard_map/ppermute | solution.py:1445
  160.4 37.9 %copy-start.20 = (s32[4,8]{1,0:T(4,128)S(1)}, s32[4,8]{1,0:T(4,128)}, u32[]{:S(2)}) copy-start(s32[4,8]{1,0:T(4,128)} %param.21) | copy-start | bytes 388
  195.2 20.1 %collective-permute-start = (f32[1,4096]{1,0:T(1,128)S(1)}, f32[1,4096]{1,0:T(1,128)S(1)}, u32[]{:S(2)}, u32[]{:S(2)}) collective-permute-start(f32[1,4096]{1,0:T(1,128)S(1)} %pad_maximum_fusion.8), channel_id=1, source_target_pairs={{0,1},{1,0},{2,3},{3,2},{4,5},{5,4},{6,7},{7,6},{8,9},{9,8},{10,11... | collective-permute-start | bytes 49160 | tf_op jit(solution)/shard_map/ppermute | solution.py:48
  197.6 19.8 %collective-permute-start.1 = (f32[1,4096]{1,0:T(1,128)S(1)}, f32[1,4096]{1,0:T(1,128)S(1)}, u32[]{:S(2)}, u32[]{:S(2)}) collective-permute-start(f32[1,4096]{1,0:T(1,128)S(1)} %pad_maximum_fusion.8), channel_id=1, source_target_pairs={{0,4},{4,0},{1,5},{5,1},{2,6},{6,2},{3,7},{7,3},{8,12},{12,8},{9,1... | collective-permute-start | bytes 49160 | tf_op jit(solution)/shard_map/ppermute | solution.py:51
  202.6 73.1 %copy-start.13 = (bf16[16,2048]{1,0:T(8,128)(2,1)}, bf16[16,2048]{1,0:T(8,128)(2,1)S(1)}, u32[]{:S(2)}) copy-start(bf16[16,2048]{1,0:T(8,128)(2,1)S(1)} %get-tuple-element.127.refs_3_) | copy-start | bytes 196612
  215.2 3.4 collective-permute-start.2
  257.7 3.8 copy-start.12
  259.3 16.3 %copy-start.14 = (bf16[1024,16]{0,1:T(8,128)(2,1)}, bf16[1024,16]{0,1:T(8,128)(2,1)S(1)}, u32[]{:S(2)}) copy-start(bf16[1024,16]{0,1:T(8,128)(2,1)S(1)} %convolution_convert_fusion.1) | copy-start | bytes 98308
  263.2 1.4 copy-start.3
  265.3 1.4 copy-start.6
  267.8 3.3 collective-permute-start.6
  268.5 5.9 copy-start.4
  268.5 5.9 copy-start.10
  268.6 88.0 %copy-start.17 = (bf16[1,2,16,2048]{3,2,1,0:T(8,128)(2,1)}, bf16[1,2,16,2048]{3,2,1,0:T(8,128)(2,1)S(1)}, u32[]{:S(2)}) copy-start(bf16[1,2,16,2048]{3,2,1,0:T(8,128)(2,1)S(1)} %constant_dynamic-slice_fusion.2) | copy-start | bytes 393220
  273.0 25.5 %collective-permute-start.8 = (bf16[256,2048]{1,0:T(8,128)(2,1)S(1)}, bf16[256,2048]{1,0:T(8,128)(2,1)S(1)}, u32[]{:S(2)}, u32[]{:S(2)}) collective-permute-start(bf16[256,2048]{1,0:T(8,128)(2,1)S(1)} %add_convert_fusion.2), channel_id=1, source_target_pairs={{0,4},{4,0},{1,5},{5,1},{2,6},{6,2},{3,7},{7,3},{8,12},{12,8},{9,1... | collective-permute-start | bytes 3145736 | tf_op jit(solution)/shard_map/ppermute | solution.py:51
  276.4 22.1 %copy-start.7 = (bf16[512,2048]{1,0:T(8,128)(2,1)}, bf16[512,2048]{1,0:T(8,128)(2,1)S(1)}, u32[]{:S(2)}) copy-start(bf16[512,2048]{1,0:T(8,128)(2,1)S(1)} %add_convert_fusion.refs_0_) | copy-start | bytes 6291460
  276.5 2.7 collective-permute-start.7
  279.3 19.3 %copy-start.22 = (bf16[256,2048]{1,0:T(8,128)(2,1)}, bf16[256,2048]{1,0:T(8,128)(2,1)S(1)}, u32[]{:S(2)}) copy-start(bf16[256,2048]{1,0:T(8,128)(2,1)S(1)} %collective-permute-done.7.refs_1_) | copy-start | bytes 3145732
  298.6 1.0 copy-start.21
  305.2 24.8 %collective-permute-start.10 = (bf16[256,2048]{1,0:T(8,128)(2,1)}, bf16[256,2048]{1,0:T(8,128)(2,1)S(1)}, u32[]{:S(2)}, u32[]{:S(2)}) collective-permute-start(bf16[256,2048]{1,0:T(8,128)(2,1)} %get-tuple-element.95), channel_id=1, source_target_pairs={{0,4},{4,0},{1,5},{5,1},{2,6},{6,2},{3,7},{7,3},{8,12},{12,8},{9,1... | collective-permute-start | bytes 3145736 | tf_op jit(solution)/shard_map/ppermute | solution.py:51
  307.1 32.4 %collective-permute-start.12 = (bf16[256,2048]{1,0:T(8,128)(2,1)}, bf16[256,2048]{1,0:T(8,128)(2,1)S(1)}, u32[]{:S(2)}, u32[]{:S(2)}) collective-permute-start(bf16[256,2048]{1,0:T(8,128)(2,1)} %get-tuple-element.95), channel_id=1, source_target_pairs={{0,2},{2,0},{1,3},{3,1},{4,6},{6,4},{5,7},{7,5},{8,10},{10,8},{9,1... | collective-permute-start | bytes 3145736 | tf_op jit(solution)/shard_map/ppermute | solution.py:57
  309.3 33.2 %collective-permute-start.9 = (bf16[256,2048]{1,0:T(8,128)(2,1)}, bf16[256,2048]{1,0:T(8,128)(2,1)}, u32[]{:S(2)}, u32[]{:S(2)}) collective-permute-start(bf16[256,2048]{1,0:T(8,128)(2,1)} %get-tuple-element.95), channel_id=1, source_target_pairs={{0,1},{1,0},{2,3},{3,2},{4,5},{5,4},{6,7},{7,6},{8,9},{9,8},{10,11... | collective-permute-start | bytes 3145736 | tf_op jit(solution)/shard_map/ppermute | solution.py:48
  330.0 23.9 %collective-permute-start.11 = (bf16[256,2048]{1,0:T(8,128)(2,1)S(1)}, bf16[256,2048]{1,0:T(8,128)(2,1)}, u32[]{:S(2)}, u32[]{:S(2)}) collective-permute-start(bf16[256,2048]{1,0:T(8,128)(2,1)S(1)} %collective-permute-done.10), channel_id=1, source_target_pairs={{0,1},{1,0},{2,3},{3,2},{4,5},{5,4},{6,7},{7,6},{8,9},{9,8},{10,11... | collective-permute-start | bytes 3145736 | tf_op jit(solution)/shard_map/ppermute | solution.py:48
  338.2 14.4 %collective-permute-start.14 = (bf16[128,2048]{1,0:T(8,128)(2,1)S(1)}, bf16[128,2048]{1,0:T(8,128)(2,1)S(1)}, u32[]{:S(2)}, u32[]{:S(2)}) collective-permute-start(bf16[128,2048]{1,0:T(8,128)(2,1)S(1)} %slice.204), channel_id=1, source_target_pairs={{0,2},{2,0},{1,3},{3,1},{4,6},{6,4},{5,7},{7,5},{8,10},{10,8},{9,1... | collective-permute-start | bytes 1572872 | tf_op jit(solution)/shard_map/ppermute | solution.py:57
  339.6 14.1 %collective-permute-start.15 = (bf16[128,2048]{1,0:T(8,128)(2,1)S(1)}, bf16[128,2048]{1,0:T(8,128)(2,1)S(1)}, u32[]{:S(2)}, u32[]{:S(2)}) collective-permute-start(bf16[128,2048]{1,0:T(8,128)(2,1)S(1)} %slice.205), channel_id=1, source_target_pairs={{0,4},{4,0},{1,5},{5,1},{2,6},{6,2},{3,7},{7,3},{8,12},{12,8},{9,1... | collective-permute-start | bytes 1572872 | tf_op jit(solution)/shard_map/ppermute | solution.py:51
  342.5 12.8 %collective-permute-start.13 = (bf16[256,2048]{1,0:T(8,128)(2,1)S(1)}, bf16[256,2048]{1,0:T(8,128)(2,1)S(1)}, u32[]{:S(2)}, u32[]{:S(2)}) collective-permute-start(bf16[256,2048]{1,0:T(8,128)(2,1)S(1)} %collective-permute-done.12), channel_id=1, source_target_pairs={{0,1},{1,0},{2,3},{3,2},{4,5},{5,4},{6,7},{7,6},{8,9},{9,8},{10,11... | collective-permute-start | bytes 3145736 | tf_op jit(solution)/shard_map/ppermute | solution.py:48
  353.8 2.7 collective-permute-start.16
  356.6 3.3 copy-start.2
  577.7 5.3 copy-start.8
  577.7 5.3 copy-start.15
  583.7 63.5 %copy-start.5 = (bf16[2,2,256,512]{3,2,1,0:T(8,128)(2,1)S(1)}, bf16[2,2,256,512]{3,2,1,0:T(8,128)(2,1)}, u32[]{:S(2)}) copy-start(bf16[2,2,256,512]{3,2,1,0:T(8,128)(2,1)} %get-tuple-element.92.refs_14_) | copy-start | bytes 3145732
  583.7 64.9 %copy-start.19 = (f32[4]{0:T(128)S(1)}, f32[4]{0:T(128)}, u32[]{:S(2)}) copy-start(f32[4]{0:T(128)} %compare_convert_fusion.1) | copy-start | bytes 52
  583.7 65.0 %copy-start.16 = (f32[16,2048]{1,0:T(8,128)S(1)}, f32[16,2048]{1,0:T(8,128)}, u32[]{:S(2)}) copy-start(f32[16,2048]{1,0:T(8,128)} %get-tuple-element.114) | copy-start | bytes 393220
  649.6 74.0 %copy-start.18 = (f32[8]{0:T(128)S(1)}, f32[8]{0:T(128)}, u32[]{:S(2)}) copy-start(f32[8]{0:T(128)} %compare_convert_fusion) | copy-start | bytes 100
  649.6 77.2 %copy-start.11 = (bf16[256,2048]{1,0:T(8,128)(2,1)S(1)}, bf16[256,2048]{1,0:T(8,128)(2,1)}, u32[]{:S(2)}) copy-start(bf16[256,2048]{1,0:T(8,128)(2,1)} %get-tuple-element.104) | copy-start | bytes 3145732
  719.7 8.0 %copy-start.9 = (f32[256,2048]{1,0:T(8,128)S(1)}, f32[256,2048]{1,0:T(8,128)}, u32[]{:S(2)}) copy-start(f32[256,2048]{1,0:T(8,128)} %get-tuple-element.117) | copy-start | bytes 6291460
  726.7 3.0 copy-start.1
Sparse Core Ops, SparseCore 0:
  149.7 146.8 all-gather.5
  298.2 78.9 all-gather.3

commit v5 on v4

--- a/solution.py
+++ b/solution.py
@@ -1039,8 +1039,8 @@
     p, x, y, c = (lax.axis_index(a) for a in ("p", "x", "y", "c"))
     core, across, over = (p, x, y, 1 - c), (p, 1 - x, y, c), (p, x, 1 - y, c)
     rows, model = result_ref.shape
-    pair = 2 * rows
-    half = rows // 2
+    size = rows // 2
+    quarter = rows // 4
     hidden = down_w.shape[0]
     rank = d_in_ref.shape[0]
     copies = Copies(send_sem, recv_sem)
@@ -1050,18 +1050,42 @@
         copy.start()
         return copy
 
-    def load_acts(turn, kind, k):
-        src = (gated_any, gate_any, up_any)[kind].at[pl.ds(k * pair, pair)]
-        copy = pltpu.make_async_copy(src, acts.at[turn % 2, kind], act_sem.at[turn % 2, kind])
-        copy.start()
-        return copy
-
-    first_order, back_order = (3, 1, 2, 0), (0, 1, 3, 2)
+    halves = (pl.ds(0, size), pl.ds(size, size))
+    top = (pl.ds(0, quarter), pl.ds(size, quarter))
+    low = (pl.ds(quarter, quarter), pl.ds(size + quarter, quarter))
+
+    class Stream:
+        def __init__(self, order, kinds):
+            self.order, self.kinds, self.flight = order, kinds, []
+            for _ in range(min(4, len(order))):
+                self.fetch()
+
+        def fetch(self):
+            n = len(self.flight)
+            if n < len(self.order):
+                k, h = self.order[n]
+                group = []
+                for kind in self.kinds:
+                    src = (gated_any, gate_any, up_any)[kind].at[pl.ds(2 * k, 2), halves[h]]
+                    group.append(pltpu.make_async_copy(src, acts.at[n % 4, kind], act_sem.at[n % 4, kind]))
+                    group[-1].start()
+                self.flight.append(group)
+
+        def slot(self, k, h):
+            n = self.order.index((k, h))
+            for copy in self.flight[n]:
+                copy.wait()
+            return n % 4
+
+    def act(slot, kind, cols=slice(None)):
+        return acts[slot, kind, :, :, cols].reshape(2 * size, -1)
+
+    both = lambda order: [(k, h) for h in range(2) for k in order]
+    stream = Stream(both((3, 1, 2, 0)), (0,))
+    loaded = load(0, down_any, down_w)
     groups = feed_any.shape[0]
     depth = model // groups
     reach = later_any.shape[0]
-    loaded = load(0, down_any, down_w)
-    gated_loads = [load_acts(0, 0, first_order[0]), load_acts(1, 0, first_order[1])]
     middle_load, cot_load = load(1, middle_any, tokens), load(2, cot_any, cot)
     feed_loads = []
     for k in range(groups):
@@ -1079,239 +1103,308 @@
         src = (query_any, log_any) if t == 0 else (later_any.at[t - 1], later_log_any.at[t - 1])
         return [copies.remote(src[0], later_any.at[t], left), copies.remote(src[1], later_log_any.at[t], left)]
 
-    pulls = pull(0)
     maps_ref[...] = jnp.zeros_like(maps_ref)
     gb_d_ref[...] = jnp.zeros_like(gb_d_ref)
 
     def part(k):
         return own_pair if k == 0 else blocks.at[pl.ds(2 * k, 2)]
 
-    def store(k, cols, value):
+    def store(k, h, cols, value):
         dst = part(k)
-        dst[0, :, cols] = value[:rows].astype(BF)
-        dst[1, :, cols] = value[rows:].astype(BF)
+        dst[0, halves[h], cols] = value[:size].astype(BF)
+        dst[1, halves[h], cols] = value[size:].astype(BF)
 
     def columns(n):
         return pl.ds(pl.multiple_of(n * 512, 512), 512)
 
-    def forward(k, slot):
-        here = slice(k * pair, (k + 1) * pair)
-        narrow_d[here, :] = dot_nt(acts[slot, 0], d_in_ref[...]).astype(BF)
+    def forward(k, h):
+        slot = stream.slot(k, h)
+        here = 2 * k + h
+        narrow_d[here] = dot_nt(act(slot, 0), d_in_ref[...]).astype(BF)
 
         def body(n, carry):
             cols = columns(n)
-            value = dot(acts[slot, 0], down_w[:, cols])
-            store(k, cols, value + SCALE_ADAPT * dot(narrow_d[here, :], d_out_ref[:, cols]))
+            value = dot(act(slot, 0), down_w[:, cols])
+            store(k, h, cols, value + SCALE_ADAPT * dot(narrow_d[here], d_out_ref[:, cols]))
             return carry
 
         lax.fori_loop(0, model // 512, body, 0)
-
-    def backward(k, slot):
-        here = slice(k * pair, (k + 1) * pair)
-        grad = blocks[2 * k : 2 * k + 2].reshape(pair, model)
-        low_d = dot_nt(grad, d_out_ref[...]).astype(BF)
-        back_d[here, :] = low_d
-        gb_d_ref[...] += SCALE_ADAPT * dot_tn(narrow_d[here, :], grad)
+        stream.fetch()
+
+    def taken(k, h):
+        return blocks[2 * k : 2 * k + 2, halves[h], :].reshape(2 * size, model)
+
+    def backward(k, h):
+        slot = stream.slot(k, h)
+        here = 2 * k + h
+        low_d = dot_nt(taken(k, h), d_out_ref[...]).astype(BF)
+        back_d[here] = low_d
+        gb_d_ref[...] += SCALE_ADAPT * dot_tn(narrow_d[here], taken(k, h))
 
         def tile(t, carry):
             cols = pl.ds(pl.multiple_of(t * 256, 256), 256)
-            grad = blocks[2 * k : 2 * k + 2].reshape(pair, model)
-            dm = dot_nt(grad, down_w[cols, :]) + SCALE_ADAPT * dot(low_d, d_in_ref[:, cols])
-            gate, up = acts[slot, 1, :, cols].astype(F32), acts[slot, 2, :, cols].astype(F32)
+            dm = dot_nt(taken(k, h), down_w[cols, :]) + SCALE_ADAPT * dot(low_d, d_in_ref[:, cols])
+            gate, up = act(slot, 1, cols).astype(F32), act(slot, 2, cols).astype(F32)
             sig = jax.nn.sigmoid(gate)
             silu = gate * sig
-            dgu[k, 0, :, cols] = (dm * up * (sig + silu * (1.0 - sig))).astype(BF)
-            dgu[k, 1, :, cols] = (dm * silu).astype(BF)
+            dgu[here, 0, :, cols] = (dm * up * (sig + silu * (1.0 - sig))).astype(BF)
+            dgu[here, 1, :, cols] = (dm * silu).astype(BF)
             return carry
 
         lax.fori_loop(0, hidden // 256, tile, 0)
-        back_gu_ref[here, :rank] = dot_nt(dgu[k, 0], gu_out_ref[0]).astype(BF)
-        back_gu_ref[here, rank:] = dot_nt(dgu[k, 1], gu_out_ref[1]).astype(BF)
+        back_g = dot_nt(dgu[here, 0], gu_out_ref[0]).astype(BF)
+        back_u = dot_nt(dgu[here, 1], gu_out_ref[1]).astype(BF)
+        back = jnp.concatenate([back_g, back_u], axis=1)
+        back_gu_ref[2 * k : 2 * k + 2, halves[h], :] = back.reshape(2, size, 2 * rank)
 
         def body(n, carry):
             cols = columns(n)
-            value = dot_nt(dgu[k, 0], gate_w[cols, :]) + dot_nt(dgu[k, 1], up_w[cols, :])
-            store(k, cols, value + SCALE_ADAPT * dot(back_gu_ref[here, :], gu_in_ref[:, cols]))
+            value = dot_nt(dgu[here, 0], gate_w[cols, :]) + dot_nt(dgu[here, 1], up_w[cols, :])
+            store(k, h, cols, value + SCALE_ADAPT * dot(back, gu_in_ref[:, cols]))
             return carry
 
         lax.fori_loop(0, model // 512, body, 0)
+        stream.fetch()
 
     def adapter_maps():
-        turns = [load_acts(k, 0, k) for k in range(2)]
-        for k in range(4):
-            here = slice(k * pair, (k + 1) * pair)
-            turns[k].wait()
-            maps_ref[0] += SCALE_ADAPT * dot_tn(back_d[here, :], acts[k % 2, 0])
-            if k < 2:
-                turns.append(load_acts(k + 2, 0, k + 2))
+        for k, h in stream.order:
+            slot = stream.slot(k, h)
+            here = 2 * k + h
+            maps_ref[0] += SCALE_ADAPT * dot_tn(back_d[here], act(slot, 0))
+            narrow = narrow_gu_ref[2 * k : 2 * k + 2, halves[h], :].reshape(2 * size, 2 * rank)
             for n in range(2):
-                narrow = narrow_gu_ref[here, n * rank : (n + 1) * rank]
-                maps_ref[1 + n] += SCALE_ADAPT * dot_tn(narrow, dgu[k, n])
-
-    def to_core(k):
-        return copies.remote(part(k).at[1], core_in.at[k], core)
-
-    def by_tiles(size, work):
+                maps_ref[1 + n] += SCALE_ADAPT * dot_tn(narrow[:, n * rank : (n + 1) * rank], dgu[here, n])
+            stream.fetch()
+
+    def by_tiles(start, count, work):
         def body(n, carry):
-            work(pl.ds(pl.multiple_of(n * 64, 64), 64))
+            work(pl.multiple_of(n * 32, 32))
             return carry
 
-        lax.fori_loop(0, size // 64, body, 0)
-
-    def meet(k, copy):
-        copy.wait_recv()
-
-        def work(tile):
-            blocks[2 * k, tile, :] = (blocks[2 * k, tile, :].astype(F32) + core_in[k, tile, :].astype(F32)).astype(BF)
-
-        by_tiles(rows, work)
-
-    top, low = pl.ds(0, half), pl.ds(half, half)
-
-    def add(block, start, more):
-        def work(tile):
-            here = pl.ds(tile.start + start, tile.size)
-            blocks[block, here, :] = (blocks[block, here, :].astype(F32) + more[tile, :].astype(F32)).astype(BF)
-
-        by_tiles(half, work)
-
-    def far_halves():
-        return (
-            copies.remote(blocks.at[6, top], by_x, across),
-            copies.remote(blocks.at[6, low], by_y, over),
-        )
-
-    def send_top_across():
-        return copies.remote(blocks.at[2, top], across_in.at[top], across)
-
-    def finish_sum(far, own, parts):
-        far_x, far_y = far
-        parts.append(copies.remote(blocks.at[4, low], over_in.at[low], over))
-        far_y.wait_recv()
-        add(2, half, by_y)
-        parts.append(copies.remote(blocks.at[2, low], across_in.at[low], across))
-        far_x.wait_recv()
-        add(4, 0, by_x)
-        parts.append(copies.remote(blocks.at[4, top], over_in.at[top], over))
-        own.wait_recv()
-        for copy in parts:
-            copy.wait_recv()
-
-    def summed(tile):
-        total = own_pair[0, tile, :].astype(F32) + core_in[0, tile, :].astype(F32)
-        return total + across_in[tile, :].astype(F32) + over_in[tile, :].astype(F32)
-
+        lax.fori_loop(start // 32, (start + count) // 32, body, 0)
+
+    class Half:
+        def __init__(self, h):
+            self.h, self.met, self.parts, self.gone = h, {}, [], []
+
+        def to_core(self, k):
+            here = halves[self.h]
+            self.met[k] = copies.remote(part(k).at[1, here], core_in.at[k, here], core)
+
+        def meet(self, k):
+            self.met[k].wait_recv()
+
+            def work(start):
+                tile = pl.ds(start, 32)
+                blocks[2 * k, tile, :] = (
+                    blocks[2 * k, tile, :].astype(F32) + core_in[k, tile, :].astype(F32)
+                ).astype(BF)
+
+            by_tiles(self.h * size, size, work)
+            h = self.h
+            if k == 3:
+                self.far_x = copies.remote(blocks.at[6, top[h]], by_x.at[h], across)
+                self.far_y = copies.remote(blocks.at[6, low[h]], by_y.at[h], over)
+            if k == 1:
+                self.parts.append(copies.remote(blocks.at[2, top[h]], across_in.at[top[h]], across))
+            if k == 2:
+                self.parts.append(copies.remote(blocks.at[4, low[h]], over_in.at[low[h]], over))
+
+        def pass_far(self):
+            h = self.h
+
+            def add(block, start, more):
+                def work(n):
+                    here = pl.ds(n + start, 32)
+                    blocks[block, here, :] = (
+                        blocks[block, here, :].astype(F32) + more[h, pl.ds(n, 32), :].astype(F32)
+                    ).astype(BF)
+
+                by_tiles(0, quarter, work)
+
+            self.far_y.wait_recv()
+            add(2, h * size + quarter, by_y)
+            self.parts.append(copies.remote(blocks.at[2, low[h]], across_in.at[low[h]], across))
+            self.far_x.wait_recv()
+            add(4, h * size, by_x)
+            self.parts.append(copies.remote(blocks.at[4, top[h]], over_in.at[top[h]], over))
+
+        def close(self, work):
+            self.met[0].wait_recv()
+            for copy in self.parts:
+                copy.wait_recv()
+
+            def body(start):
+                tile = pl.ds(start, 32)
+                total = own_pair[0, tile, :].astype(F32) + core_in[0, tile, :].astype(F32)
+                work(tile, total + across_in[tile, :].astype(F32) + over_in[tile, :].astype(F32))
+
+            by_tiles(self.h * size, size, body)
+
+        def share(self):
+            here = halves[self.h]
+            self.to_x = copies.remote(blocks.at[0, here], blocks.at[2, here], across)
+            self.to_y = copies.remote(blocks.at[0, here], blocks.at[4, here], over)
+            self.to_c = copies.remote(blocks.at[0, here], blocks.at[1, here], core)
+
+        def pass_x(self):
+            h, here = self.h, halves[self.h]
+            self.to_x.wait_recv()
+            self.x_on = copies.remote(blocks.at[2, here], blocks.at[3, here], core)
+            self.x_far = copies.remote(blocks.at[2, top[h]], blocks.at[6, top[h]], over)
+
+        def pass_y(self):
+            h, here = self.h, halves[self.h]
+            self.to_y.wait_recv()
+            self.y_on = copies.remote(blocks.at[4, here], blocks.at[5, here], core)
+            self.y_far = copies.remote(blocks.at[4, low[h]], blocks.at[6, low[h]], across)
+
+        def pass_on(self):
+            here = halves[self.h]
+            self.x_far.wait_recv()
+            self.y_far.wait_recv()
+            self.far_on = copies.remote(blocks.at[6, here], blocks.at[7, here], core)
+
+        def ready(self, k):
+            here = (self.to_c, getattr(self, "x_on", None), getattr(self, "y_on", None), getattr(self, "far_on", None))[k]
+            here.wait_recv()
+            gone = [] if k == 0 else [here]
+            if k in (1, 2):
+                gone.append(self.x_far if k == 1 else self.y_far)
+            for copy in gone:
+                copy.wait_send()
+            self.gone += gone
+
+    first, second = Half(0), Half(1)
     loaded.wait()
-    gated_loads[0].wait()
     forward(3, 0)
-    sent = to_core(3)
-    gated_loads.append(load_acts(2, 0, first_order[2]))
-    gated_loads[1].wait()
+    first.to_core(3)
+    forward(1, 0)
+    first.to_core(1)
+    first.meet(3)
+    forward(2, 0)
+    first.to_core(2)
+    first.meet(1)
+    forward(0, 0)
+    first.to_core(0)
+    first.meet(2)
+    forward(3, 1)
+    second.to_core(3)
+    first.pass_far()
     forward(1, 1)
-    sent1 = to_core(1)
-    meet(3, sent)
-    far = far_halves()
-    gated_loads.append(load_acts(3, 0, first_order[3]))
-    gated_loads[2].wait()
-    forward(2, 0)
-    sent2 = to_core(2)
-    meet(1, sent1)
-    parts = [send_top_across()]
-    gated_loads[3].wait()
+    second.to_core(1)
+    second.meet(3)
+    forward(2, 1)
+    second.to_core(2)
+    second.meet(1)
     forward(0, 1)
-    own = to_core(0)
-    meet(2, sent2)
-    act_loads = [[load_acts(0, kind, 0) for kind in range(3)], [load_acts(1, kind, 1) for kind in range(3)]]
-    finish_sum(far, own, parts)
-    copies.finish()
-    for device in (core, across, over):
-        pl.semaphore_signal(free_sem, inc=1, device_id=device, device_id_type=pl.DeviceIdType.MESH)
+    second.to_core(0)
+    second.meet(2)
+    stream = Stream([(0, 0), (0, 1), (1, 0), (3, 0), (1, 1), (2, 0), (3, 1), (2, 1)], (0, 1, 2))
     middle_load.wait()
     cot_load.wait()
 
-    def close(tile):
-        feed, gain = summed(tile), feed_gain_ref[...]
+    def end(tile, feed):
+        gain = feed_gain_ref[...]
         result_ref[tile, :] = (tokens[tile, :] + feed * rms_inverse(feed) * gain).astype(BF)
         blocks[0, tile, :] = rms_backward(feed, gain, cot[tile, :].astype(F32)).astype(BF)
 
-    by_tiles(rows, close)
-
-    pl.semaphore_wait(free_sem, 3)
-    copies.all = []
-    to_x = copies.remote(blocks.at[0], blocks.at[2], across)
-    to_y = copies.remote(blocks.at[0], blocks.at[4], over)
-    to_c = copies.remote(blocks.at[0], blocks.at[1], core)
+    def free(half):
+        for copy in [*half.met.values(), *half.parts, half.far_x, half.far_y]:
+            copy.wait_send()
+        for device in (core, across, over):
+            pl.semaphore_signal(free_sem.at[half.h], inc=1, device_id=device, device_id_type=pl.DeviceIdType.MESH)
+
+    first.close(end)
+    free(first)
+    pl.semaphore_wait(free_sem.at[0], 3)
+    first.share()
+    second.pass_far()
+    second.close(end)
+    free(second)
+    pl.semaphore_wait(free_sem.at[1], 3)
+    second.share()
+    copies.all = [first.to_x, first.to_y, first.to_c, second.to_x, second.to_y, second.to_c]
     attn_load = load(3, attn_any, tokens)
+    pulls = pull(0)
     for copy in feed_loads:
         copy.wait()
-    to_c.wait_recv()
-    for copy in act_loads[0]:
-        copy.wait()
+    for half in (first, second):
+        half.met, half.parts = {}, []
+
+    first.ready(0)
     backward(0, 0)
-    own = to_core(0)
-    act_loads.append([load_acts(2, kind, 3) for kind in range(3)])
+    first.to_core(0)
+    first.pass_x()
+    first.pass_y()
+    second.ready(0)
+    backward(0, 1)
+    second.to_core(0)
+    first.pass_on()
+    first.ready(1)
+    backward(1, 0)
+    first.to_core(1)
+    second.pass_x()
+    second.pass_y()
+    first.meet(1)
     for t in range(1, reach):
         for copy in pulls:
             copy.wait_recv()
         pulls = pull(t)
-    to_x.wait_recv()
-    x_on = [copies.remote(blocks.at[2], blocks.at[3], core), copies.remote(blocks.at[2, top], blocks.at[6, top], over)]
-    to_y.wait_recv()
-    y_on = [copies.remote(blocks.at[4], blocks.at[5], core), copies.remote(blocks.at[4, low], blocks.at[6, low], across)]
-    x_on[0].wait_recv()
-    for copy in act_loads[1]:
-        copy.wait()
-    for copy in x_on:
-        copy.wait_send()
+    first.ready(3)
+    backward(3, 0)
+    first.to_core(3)
+    second.ready(1)
     backward(1, 1)
-    sent1 = to_core(1)
-    act_loads.append([load_acts(3, kind, 2) for kind in range(3)])
-    x_on[1].wait_recv()
-    y_on[1].wait_recv()
-    far_on = copies.remote(blocks.at[6], blocks.at[7], core)
-    meet(1, sent1)
-    parts = [send_top_across()]
-    far_on.wait_recv()
-    for copy in act_loads[2]:
-        copy.wait()
-    far_on.wait_send()
-    backward(3, 0)
-    sent = to_core(3)
-    meet(3, sent)
-    far = far_halves()
-    y_on[0].wait_recv()
-    for copy in act_loads[3]:
-        copy.wait()
-    for copy in y_on:
-        copy.wait_send()
+    second.to_core(1)
+    first.meet(3)
+    second.pass_on()
+    first.ready(2)
+    backward(2, 0)
+    first.to_core(2)
+    second.meet(1)
+    second.ready(3)
+    first.meet(2)
+    backward(3, 1)
+    second.to_core(3)
+    first.pass_far()
+    second.ready(2)
+    second.meet(3)
     backward(2, 1)
-    sent2 = to_core(2)
-    meet(2, sent2)
-    finish_sum(far, own, parts)
+    second.to_core(2)
+    stream = Stream([(k, h) for k in range(4) for h in range(2)], (0,))
     attn_load.wait()
 
-    def open_attention(tile):
-        mid = cot[tile, :].astype(F32) + summed(tile)
+    def open_attention(tile, total):
+        mid = cot[tile, :].astype(F32) + total
         mid_ref[tile, :] = mid
-        grad_attn_ref[tile, :] = rms_backward(tokens[tile, :], attn_gain_ref[...], mid).astype(BF)
-
-    by_tiles(rows, open_attention)
-
-    def block(k):
-        return grad_attn_ref.at[pl.ds(k * rows, rows)]
-
-    to_x = copies.remote(block(0), block(2), across)
-    to_c = copies.remote(block(0), block(1), core)
-    to_x.wait_recv()
-    on = copies.remote(block(2), block(3), core)
+        grad_attn_ref[0, tile, :] = rms_backward(tokens[tile, :], attn_gain_ref[...], mid).astype(BF)
+
+    def share_attention(h):
+        here = halves[h]
+        block = lambda k: grad_attn_ref.at[k, here]
+        return copies.remote(block(0), block(2), across), copies.remote(block(0), block(1), core)
+
+    def pass_attention(h, to_x):
+        to_x.wait_recv()
+        return copies.remote(grad_attn_ref.at[2, halves[h]], grad_attn_ref.at[3, halves[h]], core)
+
+    second.meet(2)
+    first.close(open_attention)
+    to_x, to_c = share_attention(0)
+    last = [to_c]
+    second.pass_far()
+    last.append(pass_attention(0, to_x))
+    second.close(open_attention)
+    to_x, to_c = share_attention(1)
+    last.append(to_c)
     adapter_maps()
-    to_c.wait_recv()
-    on.wait_recv()
-    for copy in pulls:
+    last.append(pass_attention(1, to_x))
+    for copy in last + pulls:
         copy.wait_recv()
-    done = (*x_on, far_on, *y_on)
+    gone = first.gone + second.gone
     for copy in copies.all:
-        if not any(copy is other for other in done):
+        if not any(copy is other for other in gone):
             copy.wait_send()
 
 
@@ -1322,7 +1415,7 @@
     vm = pl.BlockSpec(memory_space=pltpu.VMEM)
     anywhere = pl.BlockSpec(memory_space=pl.ANY)
     block = lambda *shape: pltpu.VMEM(shape, BF)
-    count = 48 + 2 * reach
+    count = 96 + 2 * reach
     return pl.pallas_call(
         feed_kernel,
         in_specs=[vm] * 7 + [anywhere] * 10,
@@ -1330,8 +1423,8 @@
         out_shape=[
             jax.ShapeDtypeStruct((rows, model), BF),
             jax.ShapeDtypeStruct((rows, model), F32),
-            jax.ShapeDtypeStruct((4 * rows, model), BF),
-            jax.ShapeDtypeStruct((8 * rows, 2 * rank), BF),
+            jax.ShapeDtypeStruct((4, rows, model), BF),
+            jax.ShapeDtypeStruct((8, rows, 2 * rank), BF),
             jax.ShapeDtypeStruct((3, rank, hidden), F32),
             jax.ShapeDtypeStruct((rank, model), F32),
             jax.ShapeDtypeStruct((reach,) + query.shape, BF),
@@ -1341,22 +1434,22 @@
             block(hidden, model),
             block(model, hidden),
             block(model, hidden),
-            block(2, 3, 2 * rows, hidden),
+            block(4, 3, 2, rows // 2, hidden),
             block(8, rows, model),
             block(2, rows, model),
             block(4, rows, model),
-            block(rows // 2, model),
-            block(rows // 2, model),
+            block(2, rows // 4, model),
+            block(2, rows // 4, model),
             block(rows, model),
             block(rows, model),
             pltpu.VMEM((rows, model), F32),
             block(rows, model),
-            block(4, 2, 2 * rows, hidden),
-            block(8 * rows, rank),
-            block(8 * rows, rank),
+            block(8, 2, rows, hidden),
+            block(8, rows, rank),
+            block(8, rows, rank),
             pltpu.SemaphoreType.DMA((2 * groups + 4,)),
-            pltpu.SemaphoreType.DMA((2, 3)),
-            pltpu.SemaphoreType.REGULAR,
+            pltpu.SemaphoreType.DMA((4, 3)),
+            pltpu.SemaphoreType.REGULAR((2,)),
             pltpu.SemaphoreType.DMA((count,)),
             pltpu.SemaphoreType.DMA((count,)),
         ],
@@ -1365,7 +1458,17 @@
         ),
         name="feed_layer",
         cost_estimate=cost(170),
-    )(*maps, narrow_gu, *acts, *weights, middle, cot, attn_out, query, log)
+    )(
+        *maps,
+        narrow_gu.reshape(8, rows, -1),
+        *[v.reshape(8, rows, hidden) for v in acts],
+        *weights,
+        middle,
+        cot,
+        attn_out,
+        query,
+        log,
+    )
 
 
 def by_rows(kernel, name, rows, width, args, dtypes, us):
@@ -1551,7 +1654,7 @@
         heads,
         rows,
         [
-            grad_attn,
+            grad_attn.reshape(4 * rows, width),
             w_o,
             a_o,
             b_o,
@@ -1586,6 +1689,7 @@
     def spread(v):
         return (v.reshape(-1, heads, 1, HD) * mine[:, None]).reshape(-1, width)
 
+    back_gu, grad_attn = back_gu.reshape(8 * rows, -1), grad_attn.reshape(4 * rows, -1)
     ga_gu = SCALE_ADAPT * dot_tn(back_gu, middle_low)
     ga_o = SCALE_ADAPT * dot_tn(back_o, o)
     gb_o = SCALE_ADAPT * dot_tn(narrow_o, grad_attn)

time: 748 us -> 724 us (0.968)
  Pallas kernels: 564 us -> 541 us
    pallas_call x1, Pallas kernels: 188 us -> 161 us  [feed_layer(): pl.pallas_call(feed_kernel, in_specs=[vm] * 7 + [anywhere] * 10, out_spec...]
where the time goes in v5:
time: 724 us; the launch traced here: 714 us
  Pallas kernels  541 us (75%)
  waiting for transfers between devices  53.9 us (7%)
  local copies, waits for them, and re-layouts  39.8 us (5%)
  other arithmetic  27.8 us (4%)
  starting transfers between devices  19.5 us (3%)
  matrix products  16 us (2%)
  between operations  15.9 us (2%)
    pallas_call x1, Pallas kernels, feed_layer(): pl.pallas_call(feed_kernel, in_specs=[vm] * 7 + [anywhere] * 10, out_spec...  161 us
    pallas_call x1, Pallas kernels, start(): pl.pallas_call(functools.partial(start_kernel, groups, reach), in_specs=[...  135 us
    pallas_call x1, Pallas kernels, finish(): pl.pallas_call(functools.partial(finish_kernel, groups, heads, early_rows...  70.3 us
    pallas_call x1, Pallas kernels, attend_back(): pl.pallas_call(functools.partial(attend_back_kernel, groups, reach, heads...  66.5 us
    ppermute x4, waiting for transfers between devices, swap_x(): return lax.ppermute(value, 'x', SWAP)  40.1 us
    pallas_call x1, Pallas kernels, project(): pl.pallas_call(functools.partial(project_kernel, heads, own_tiles), grid=...  33.1 us
    pallas_call x1, Pallas kernels, gate_up(): pl.pallas_call(gate_up_kernel, grid=(steps,), in_specs=[pl.BlockSpec((row...  26.9 us
    pallas_call x1, Pallas kernels, forward(): pl.pallas_call(functools.partial(attend_kernel, count, HD ** (-0.5)), gri...  23.5 us
  transfers between devices with their start and end apart: 19, of which 8 were waited for; matrix products, arithmetic and copies ran while one was open for 8% of the time, Pallas kernels for 14%

profile of v5, /device:TPU:0, one launch (start us, length us, event | category | flops | bytes accessed | tf_op | source)
XLA Modules:
  0.0 713.7 jit_solution(4421436945195162999)
XLA Ops:
  7.9 2.6 pack_columns.4
  10.5 2.3 pack_columns.5
  12.8 2.2 pack_columns.3
  15.0 134.6 %start.1 = (bf16[4,2,2,128,1536]{4,3,2,1,0:T(8,128)(2,1)}, bf16[512,2048]{1,0:T(8,128)(2,1)}, bf16[3072,2048]{1,0:T(8,128)(2,1)}, bf16[4,64,2048]{2,1,0:T(8,128)(2,1)}) custom-call(bf16[64,1536]{1,0:T(8,128)(2,1)} %get-tuple-element.63.refs_0_, bf16[64,1536]{1,0:T(8,128)(2,1)} %get-tuple-element.64.refs_1_, bf16[64,1536]{1,0:T(8,128)(2,1)} %get-tuple-element.65.refs_2_, ...), custom_call_target="tpu_custom_call" | custom-call | flops 131999997952 | bytes 120000000 | tf_op jit(solution)/shard_map/start/pallas_call | solution.py:304
  149.6 4.4 collective-permute-start.3
  154.0 1.3 collective-permute-start.4
  155.3 1.7 collective-permute-start.5
  157.6 1.0 constant_dynamic-slice_fusion
  160.4 33.1 %project.1 = (f32[1024,512]{1,0:T(8,128)}, f32[3072,512]{1,0:T(8,128)}, bf16[3072,512]{1,0:T(8,128)(2,1)}, bf16[3072,48]{1,0:T(8,128)(2,1)}, f32[8,1024]{1,0:T(8,128)}, /*index=5*/f32[8,3072]{1,0:T(8,128)}) custom-call(bf16[3072,2048]{1,0:T(8,128)(2,1)} %get-tuple-element.83.x_ref.refs_16_, bf16[2048,1536]{1,0:T(8,128)(2,1)} %bitcast.118, ...), custom_call_target="tpu_custom_call" | custom-call | flops 1100000000 | bytes 1000000 | tf_op jit(solution)/shard_map/project/pallas_call | solution.py:391
  193.5 0.9 slice.151
  195.2 2.4 collective-permute-start
  198.6 1.0 copy.64
  201.0 1.5 dynamic-slice_bitcast_fusion
  202.6 2.0 broadcast_maximum_fusion.refs_6_.refs_4_
  204.5 5.8 fusion
  210.3 1.6 pad_maximum_fusion.1.cos_ref.refs_8_
  212.0 1.6 pad_maximum_fusion.2.sin_ref.refs_9_
  215.2 0.9 collective-permute-start.2
  219.5 1.7 copy.63.inv_k_ref.refs_6_
  221.2 1.0 copy.62.inv_q_ref.refs_5_
  222.2 12.0 %rope_forward.1 = (bf16[1024,512]{1,0:T(8,128)(2,1)}, bf16[3072,512]{1,0:T(8,128)(2,1)}) custom-call(f32[1024,512]{1,0:T(8,128)} %get-tuple-element.85.q_ref.refs_3_, f32[3072,512]{1,0:T(8,128)} %get-tuple-element.86.k_ref.refs_4_, f32[1024,1]{1,0:T(8,128)} %copy.62.inv_q_ref.refs_5_, f32[3072,1]{1,0:T(8,128)} %copy.63.inv_k_ref.refs_6_, ...), custom_call_target="tpu_custom_call" | custom-call | flops 1100000000 | bytes 1000000 | tf_op jit(solution)/shard_map/rope_forward/pallas_call | solution.py:440
  234.2 23.5 %attend_forward.1 = (bf16[2,2,256,512]{3,2,1,0:T(8,128)(2,1)}, f32[8,512,1]{2,1,0:T(8,128)}) custom-call(bf16[2,2,256,512]{3,2,1,0:T(8,128)(2,1)} %bitcast.128, bf16[6,2,256,512]{3,2,1,0:T(8,128)(2,1)} %bitcast.109, bf16[6,2,256,512]{3,2,1,0:T(8,128)(2,1)} %bitcast.110, bf16[6,2,256,512]{3,2,1,0:T(8,128)(2,1)} %bitcast.111, ...), custom_call_target="tpu_custom_call" | custom-call | flops 1100000000 | bytes 1000000 | tf_op jit(solution)/shard_map/attend_forward/pallas_call | solution.py:953
  257.7 1.7 convolution_convert_fusion.1
  259.3 2.1 fusion.9
  261.5 1.5 broadcast_select_fusion.3
  263.2 1.3 fusion.15
  265.3 1.4 copy-done.6
  266.7 1.2 slice.201
  268.6 2.5 collective-permute-done.6
  271.1 1.9 add_convert_fusion.2
  273.0 1.4 collective-permute-start.8
  274.4 1.3 fusion.16
  276.7 1.5 constant_dynamic-slice_fusion.7
  278.1 1.1 collective-permute-done.7.refs_1_
  279.3 19.3 %collective-permute-done.8.refs_2_ = bf16[256,2048]{1,0:T(8,128)(2,1)S(1)} collective-permute-done((bf16[256,2048]{1,0:T(8,128)(2,1)S(1)}, bf16[256,2048]{1,0:T(8,128)(2,1)S(1)}, u32[]{:S(2)}, u32[]{:S(2)}) %collective-permute-start.8) | collective-permute-done | bytes 1048608 | tf_op jit(solution)/shard_map/ppermute | solution.py:51
  298.6 1.0 copy-done.21
  299.6 5.6 after_attention.1
  305.2 1.3 collective-permute-start.10
  307.1 1.6 collective-permute-start.12
  309.3 1.0 constant_dynamic-slice_fusion.8
  310.3 19.7 %collective-permute-done.10 = bf16[256,2048]{1,0:T(8,128)(2,1)S(1)} collective-permute-done((bf16[256,2048]{1,0:T(8,128)(2,1)}, bf16[256,2048]{1,0:T(8,128)(2,1)S(1)}, u32[]{:S(2)}, u32[]{:S(2)}) %collective-permute-start.10) | collective-permute-done | bytes 1048608 | tf_op jit(solution)/shard_map/ppermute | solution.py:51
  331.2 1.2 reshape.573
  332.4 1.3 dynamic-slice_reduce_fusion
  335.4 2.8 reduce.5.refs_16_
  338.2 1.3 collective-permute-start.14
  339.6 1.6 collective-permute-start.15
  341.2 1.3 constant_dynamic-update-slice_fusion.9
  342.6 1.3 constant_dynamic-update-slice_fusion.8
  343.9 8.7 %collective-permute-done.14 = bf16[128,2048]{1,0:T(8,128)(2,1)S(1)} collective-permute-done((bf16[128,2048]{1,0:T(8,128)(2,1)S(1)}, bf16[128,2048]{1,0:T(8,128)(2,1)S(1)}, u32[]{:S(2)}, u32[]{:S(2)}) %collective-permute-start.14) | collective-permute-done | bytes 524320 | tf_op jit(solution)/shard_map/ppermute | solution.py:57
  352.6 1.1 collective-permute-done.15
  353.9 1.3 constant_dynamic-update-slice_fusion.6
  355.4 1.1 collective-permute-done.16
  356.6 3.2 copy-done.2
  359.9 3.2 convolution_convert_fusion.narrow_ref
  363.0 26.9 %gate_up.1 = (bf16[2048,1024]{1,0:T(8,128)(2,1)}, bf16[2048,1024]{1,0:T(8,128)(2,1)}, bf16[2048,1024]{1,0:T(8,128)(2,1)}) custom-call(bf16[2048,2048]{1,0:T(8,128)(2,1)} %copy-done.2, bf16[4,512,2048]{2,1,0:T(8,128)(2,1)} %bitcast.102, bf16[4,512,2048]{2,1,0:T(8,128)(2,1)} %bitcast.103, bf16[2048,32]{1,0:T(8,128)(2,1)} %convolution_convert_fusion.narrow_ref, ...), custom_call_target="tpu_custom_call" | custom-call | flops 1100000000 | bytes 1000000 | tf_op jit(solution)/shard_map/gate_up/pallas_call | solution.py:343
  389.9 161.3 %feed_layer.1 = (bf16[256,2048]{1,0:T(8,128)(2,1)}, f32[256,2048]{1,0:T(8,128)}, bf16[4,256,2048]{2,1,0:T(8,128)(2,1)}, bf16[8,256,32]{2,1,0:T(8,128)(2,1)}, f32...) custom-call(bf16[16,1024]{1,0:T(8,128)(2,1)} %bitcast.152, ...), custom_call_target="tpu_custom_call" | custom-call | flops 186999996416 | bytes 170000000 | tf_op jit(solution)/shard_map/feed_layer/pallas_call | solution.py:1419
  551.2 5.3 convolution_multiply_fusion
  557.2 66.5 %attend_backward.1 = (f32[2,2,256,512]{3,2,1,0:T(8,128)}, f32[2,2,256,512]{3,2,1,0:T(8,128)}, f32[2,2,256,512]{3,2,1,0:T(8,128)}, bf16[1024,16]{1,0:T(8,128)(2,1)}) custom-call(bf16[1024,2048]{1,0:T(8,128)(2,1)} %bitcast.120, bf16[512,2048]{1,0:T(8,128)(2,1)} %bitcast.114, bf16[16,512]{1,0:T(8,128)(2,1)} %bitcast.154, bf16[16,2048]{1,0:T(8,128)(2,1)} %copy-done.13, ...), custom_call_target="tpu_custom_call" | custom-call | flops 76999999488 | bytes 70000000 | tf_op jit(solution)/shard_map/attend_backward/pallas_call | solution.py:900
  623.7 1.2 convolution_multiply_fusion.2
  625.2 0.9 pad_maximum_fusion.4.refs_13_
  626.1 70.3 %finish.1 = (f32[256,2048]{1,0:T(8,128)}, f32[176,64]{1,0:T(8,128)}, f32[48,256]{1,0:T(8,128)}) custom-call(f32[1024,512]{1,0:T(8,128)} %bitcast.166, f32[1024,512]{1,0:T(8,128)} %bitcast.167, f32[1024,512]{1,0:T(8,128)} %bitcast.168, f32[1024,512]{1,0:T(8,128)} %get-tuple-element.85.q_ref.refs_3_, f32[3072,512]{1,0:T(8,128)} %get-tuple-element.86.k_ref.refs_4_, ...), custom_call_target="tpu_custom_call" | custom-call | flops 65999998976 | bytes 60000000 | tf_op jit(solution)/shard_map/finish/pallas_call | solution.py:698
  696.4 0.9 fusion.10
  703.4 1.0 copy.96
  704.4 1.3 copy.97
  (160 shorter events, 25.6 us)
Async XLA Ops:
  7.2 152.5 %copy-start = (bf16[8,6,16,2048]{3,2,1,0:T(8,128)(2,1)S(1)}, bf16[8,6,16,2048]{3,2,1,0:T(8,128)(2,1)}, u32[]{:S(2)}) copy-start(bf16[8,6,16,2048]{3,2,1,0:T(8,128)(2,1)} %param.34) | copy-start | bytes 9437188
  7.2 355.9 %all-gather.6.cloned.1.call-start = ((), (), s32[]{:S(2)}) async-start(), calls=%async_computation.1 | async-start | bytes 10485760 | tf_op jit(solution)/shard_map/all_gather | solution.py:1546
  149.6 240.3 %all-gather.4.cloned.1.call-start = ((), (), s32[]{:S(2)}) async-start(), calls=%async_computation | async-start | bytes 5242880 | tf_op jit(solution)/shard_map/all_gather | solution.py:1609
  149.6 111.8 %collective-permute-start.3 = (bf16[256,2048]{1,0:T(8,128)(2,1)}, bf16[256,2048]{1,0:T(8,128)(2,1)}, u32[]{:S(2)}, u32[]{:S(2)}) collective-permute-start(bf16[256,2048]{1,0:T(8,128)(2,1)} %bitcast.131), channel_id=1, source_target_pairs={{0,2},{3,1},{4,6},{7,5},{8,10},{11,9},{12,14},{15,13},{16,18},{19,... | collective-permute-start | bytes 3145736 | tf_op jit(solution)/shard_map/ppermute | solution.py:1548
  154.0 107.5 %collective-permute-start.4 = (bf16[256,2048]{1,0:T(8,128)(2,1)}, bf16[256,2048]{1,0:T(8,128)(2,1)}, u32[]{:S(2)}, u32[]{:S(2)}) collective-permute-start(bf16[256,2048]{1,0:T(8,128)(2,1)} %bitcast.132), channel_id=1, source_target_pairs={{1,0},{2,3},{5,4},{6,7},{9,8},{10,11},{13,12},{14,15},{17,16},{18,... | collective-permute-start | bytes 3145736 | tf_op jit(solution)/shard_map/ppermute | solution.py:1548
  155.3 106.2 %collective-permute-start.5 = (bf16[256,2048]{1,0:T(8,128)(2,1)}, bf16[256,2048]{1,0:T(8,128)(2,1)}, u32[]{:S(2)}, u32[]{:S(2)}) collective-permute-start(bf16[256,2048]{1,0:T(8,128)(2,1)} %bitcast.133), channel_id=1, source_target_pairs={{1,2},{2,1},{5,6},{6,5},{9,10},{10,9},{13,14},{14,13},{17,18},{18,... | collective-permute-start | bytes 3145736 | tf_op jit(solution)/shard_map/ppermute | solution.py:1548
  160.4 37.9 %copy-start.20 = (s32[4,8]{1,0:T(4,128)S(1)}, s32[4,8]{1,0:T(4,128)}, u32[]{:S(2)}) copy-start(s32[4,8]{1,0:T(4,128)} %param.21) | copy-start | bytes 388
  195.2 20.1 %collective-permute-start = (f32[1,4096]{1,0:T(1,128)S(1)}, f32[1,4096]{1,0:T(1,128)S(1)}, u32[]{:S(2)}, u32[]{:S(2)}) collective-permute-start(f32[1,4096]{1,0:T(1,128)S(1)} %pad_maximum_fusion.8), channel_id=1, source_target_pairs={{0,1},{1,0},{2,3},{3,2},{4,5},{5,4},{6,7},{7,6},{8,9},{9,8},{10,11... | collective-permute-start | bytes 49160 | tf_op jit(solution)/shard_map/ppermute | solution.py:48
  197.6 19.8 %collective-permute-start.1 = (f32[1,4096]{1,0:T(1,128)S(1)}, f32[1,4096]{1,0:T(1,128)S(1)}, u32[]{:S(2)}, u32[]{:S(2)}) collective-permute-start(f32[1,4096]{1,0:T(1,128)S(1)} %pad_maximum_fusion.8), channel_id=1, source_target_pairs={{0,4},{4,0},{1,5},{5,1},{2,6},{6,2},{3,7},{7,3},{8,12},{12,8},{9,1... | collective-permute-start | bytes 49160 | tf_op jit(solution)/shard_map/ppermute | solution.py:51
  202.6 73.1 %copy-start.13 = (bf16[16,2048]{1,0:T(8,128)(2,1)}, bf16[16,2048]{1,0:T(8,128)(2,1)S(1)}, u32[]{:S(2)}) copy-start(bf16[16,2048]{1,0:T(8,128)(2,1)S(1)} %get-tuple-element.127.refs_3_) | copy-start | bytes 196612
  215.2 3.4 collective-permute-start.2
  257.7 3.8 copy-start.12
  259.3 16.3 %copy-start.14 = (bf16[1024,16]{0,1:T(8,128)(2,1)}, bf16[1024,16]{0,1:T(8,128)(2,1)S(1)}, u32[]{:S(2)}) copy-start(bf16[1024,16]{0,1:T(8,128)(2,1)S(1)} %convolution_convert_fusion.1) | copy-start | bytes 98308
  263.2 1.4 copy-start.3
  265.3 1.4 copy-start.6
  267.8 3.3 collective-permute-start.6
  268.5 5.9 copy-start.4
  268.5 5.9 copy-start.10
  268.6 88.0 %copy-start.17 = (bf16[1,2,16,2048]{3,2,1,0:T(8,128)(2,1)}, bf16[1,2,16,2048]{3,2,1,0:T(8,128)(2,1)S(1)}, u32[]{:S(2)}) copy-start(bf16[1,2,16,2048]{3,2,1,0:T(8,128)(2,1)S(1)} %constant_dynamic-slice_fusion.2) | copy-start | bytes 393220
  273.0 25.5 %collective-permute-start.8 = (bf16[256,2048]{1,0:T(8,128)(2,1)S(1)}, bf16[256,2048]{1,0:T(8,128)(2,1)S(1)}, u32[]{:S(2)}, u32[]{:S(2)}) collective-permute-start(bf16[256,2048]{1,0:T(8,128)(2,1)S(1)} %add_convert_fusion.2), channel_id=1, source_target_pairs={{0,4},{4,0},{1,5},{5,1},{2,6},{6,2},{3,7},{7,3},{8,12},{12,8},{9,1... | collective-permute-start | bytes 3145736 | tf_op jit(solution)/shard_map/ppermute | solution.py:51
  276.4 22.1 %copy-start.7 = (bf16[512,2048]{1,0:T(8,128)(2,1)}, bf16[512,2048]{1,0:T(8,128)(2,1)S(1)}, u32[]{:S(2)}) copy-start(bf16[512,2048]{1,0:T(8,128)(2,1)S(1)} %add_convert_fusion.refs_0_) | copy-start | bytes 6291460
  276.5 2.7 collective-permute-start.7
  279.3 19.3 %copy-start.22 = (bf16[256,2048]{1,0:T(8,128)(2,1)}, bf16[256,2048]{1,0:T(8,128)(2,1)S(1)}, u32[]{:S(2)}) copy-start(bf16[256,2048]{1,0:T(8,128)(2,1)S(1)} %collective-permute-done.7.refs_1_) | copy-start | bytes 3145732
  298.6 1.0 copy-start.21
  305.2 24.8 %collective-permute-start.10 = (bf16[256,2048]{1,0:T(8,128)(2,1)}, bf16[256,2048]{1,0:T(8,128)(2,1)S(1)}, u32[]{:S(2)}, u32[]{:S(2)}) collective-permute-start(bf16[256,2048]{1,0:T(8,128)(2,1)} %get-tuple-element.95), channel_id=1, source_target_pairs={{0,4},{4,0},{1,5},{5,1},{2,6},{6,2},{3,7},{7,3},{8,12},{12,8},{9,1... | collective-permute-start | bytes 3145736 | tf_op jit(solution)/shard_map/ppermute | solution.py:51
  307.1 32.4 %collective-permute-start.12 = (bf16[256,2048]{1,0:T(8,128)(2,1)}, bf16[256,2048]{1,0:T(8,128)(2,1)S(1)}, u32[]{:S(2)}, u32[]{:S(2)}) collective-permute-start(bf16[256,2048]{1,0:T(8,128)(2,1)} %get-tuple-element.95), channel_id=1, source_target_pairs={{0,2},{2,0},{1,3},{3,1},{4,6},{6,4},{5,7},{7,5},{8,10},{10,8},{9,1... | collective-permute-start | bytes 3145736 | tf_op jit(solution)/shard_map/ppermute | solution.py:57
  309.3 33.2 %collective-permute-start.9 = (bf16[256,2048]{1,0:T(8,128)(2,1)}, bf16[256,2048]{1,0:T(8,128)(2,1)}, u32[]{:S(2)}, u32[]{:S(2)}) collective-permute-start(bf16[256,2048]{1,0:T(8,128)(2,1)} %get-tuple-element.95), channel_id=1, source_target_pairs={{0,1},{1,0},{2,3},{3,2},{4,5},{5,4},{6,7},{7,6},{8,9},{9,8},{10,11... | collective-permute-start | bytes 3145736 | tf_op jit(solution)/shard_map/ppermute | solution.py:48
  330.0 23.9 %collective-permute-start.11 = (bf16[256,2048]{1,0:T(8,128)(2,1)S(1)}, bf16[256,2048]{1,0:T(8,128)(2,1)}, u32[]{:S(2)}, u32[]{:S(2)}) collective-permute-start(bf16[256,2048]{1,0:T(8,128)(2,1)S(1)} %collective-permute-done.10), channel_id=1, source_target_pairs={{0,1},{1,0},{2,3},{3,2},{4,5},{5,4},{6,7},{7,6},{8,9},{9,8},{10,11... | collective-permute-start | bytes 3145736 | tf_op jit(solution)/shard_map/ppermute | solution.py:48
  338.2 14.4 %collective-permute-start.14 = (bf16[128,2048]{1,0:T(8,128)(2,1)S(1)}, bf16[128,2048]{1,0:T(8,128)(2,1)S(1)}, u32[]{:S(2)}, u32[]{:S(2)}) collective-permute-start(bf16[128,2048]{1,0:T(8,128)(2,1)S(1)} %slice.204), channel_id=1, source_target_pairs={{0,2},{2,0},{1,3},{3,1},{4,6},{6,4},{5,7},{7,5},{8,10},{10,8},{9,1... | collective-permute-start | bytes 1572872 | tf_op jit(solution)/shard_map/ppermute | solution.py:57
  339.6 14.1 %collective-permute-start.15 = (bf16[128,2048]{1,0:T(8,128)(2,1)S(1)}, bf16[128,2048]{1,0:T(8,128)(2,1)S(1)}, u32[]{:S(2)}, u32[]{:S(2)}) collective-permute-start(bf16[128,2048]{1,0:T(8,128)(2,1)S(1)} %slice.205), channel_id=1, source_target_pairs={{0,4},{4,0},{1,5},{5,1},{2,6},{6,2},{3,7},{7,3},{8,12},{12,8},{9,1... | collective-permute-start | bytes 1572872 | tf_op jit(solution)/shard_map/ppermute | solution.py:51
  342.5 12.8 %collective-permute-start.13 = (bf16[256,2048]{1,0:T(8,128)(2,1)S(1)}, bf16[256,2048]{1,0:T(8,128)(2,1)S(1)}, u32[]{:S(2)}, u32[]{:S(2)}) collective-permute-start(bf16[256,2048]{1,0:T(8,128)(2,1)S(1)} %collective-permute-done.12), channel_id=1, source_target_pairs={{0,1},{1,0},{2,3},{3,2},{4,5},{5,4},{6,7},{7,6},{8,9},{9,8},{10,11... | collective-permute-start | bytes 3145736 | tf_op jit(solution)/shard_map/ppermute | solution.py:48
  353.8 2.7 collective-permute-start.16
  356.6 3.3 copy-start.2
  551.2 5.3 copy-start.8
  551.2 5.3 copy-start.15
  557.2 66.6 %copy-start.5 = (bf16[2,2,256,512]{3,2,1,0:T(8,128)(2,1)S(1)}, bf16[2,2,256,512]{3,2,1,0:T(8,128)(2,1)}, u32[]{:S(2)}) copy-start(bf16[2,2,256,512]{3,2,1,0:T(8,128)(2,1)} %get-tuple-element.92.refs_14_) | copy-start | bytes 3145732
  557.2 67.9 %copy-start.19 = (f32[4]{0:T(128)S(1)}, f32[4]{0:T(128)}, u32[]{:S(2)}) copy-start(f32[4]{0:T(128)} %compare_convert_fusion.1) | copy-start | bytes 52
  557.2 68.0 %copy-start.16 = (f32[16,2048]{1,0:T(8,128)S(1)}, f32[16,2048]{1,0:T(8,128)}, u32[]{:S(2)}) copy-start(f32[16,2048]{1,0:T(8,128)} %get-tuple-element.114) | copy-start | bytes 393220
  626.1 74.1 %copy-start.18 = (f32[8]{0:T(128)S(1)}, f32[8]{0:T(128)}, u32[]{:S(2)}) copy-start(f32[8]{0:T(128)} %compare_convert_fusion) | copy-start | bytes 100
  626.1 77.3 %copy-start.11 = (bf16[256,2048]{1,0:T(8,128)(2,1)S(1)}, bf16[256,2048]{1,0:T(8,128)(2,1)}, u32[]{:S(2)}) copy-start(bf16[256,2048]{1,0:T(8,128)(2,1)} %get-tuple-element.104) | copy-start | bytes 3145732
  696.4 8.0 %copy-start.9 = (f32[256,2048]{1,0:T(8,128)S(1)}, f32[256,2048]{1,0:T(8,128)}, u32[]{:S(2)}) copy-start(f32[256,2048]{1,0:T(8,128)} %get-tuple-element.117) | copy-start | bytes 6291460
  703.4 3.0 copy-start.1
Sparse Core Ops, SparseCore 0:
  149.7 146.8 all-gather.5
  298.2 78.9 all-gather.3

commit v6 on v5

--- a/solution.py
+++ b/solution.py
@@ -183,10 +183,32 @@
 TURNS4 = TURNS8[:4]
 
 
-def start_kernel(groups, reach, *refs):
-    qkv_pack, feed_packs, x_ref, o_ref = refs[0:4], (refs[4:12], refs[12:20]), refs[20], refs[21]
-    w_ref, feed_ref, all_ref, o_all_ref, local_sem, send_sem, recv_sem = refs[22:]
+def start_kernel(groups, reach, raw, *refs):
     p, x, y, c = (lax.axis_index(a) for a in ("p", "x", "y", "c"))
+    if raw:
+        sources, x_ref, o_ref = refs[0:5], refs[5], refs[6]
+        w_ref, feed_ref, all_ref, o_all_ref, local_sem, send_sem, recv_sem = refs[7:14]
+        whole, (qkv_packs, feed_all), load_sem = refs[14:19], refs[19:21], refs[21]
+        loads = [pltpu.make_async_copy(sources[k], whole[k], load_sem.at[k]) for k in range(5)]
+        for load in loads:
+            load.start()
+        qkv_pack = [qkv_packs.at[d] for d in range(4)]
+        feed_packs = [[feed_all.at[k, d] for d in range(8)] for k in range(2)]
+
+        def packed(kinds, offsets, turns, width, dst):
+            for kind in kinds:
+                loads[kind].wait()
+            for d, turn in enumerate(turns):
+                places = offsets(*[(u + t) % 2 for u, t in zip((x, y, c), turn)])
+                for w, kind in enumerate(kinds):
+                    for k, place in enumerate(places):
+                        at = (w * len(places) + k) * width
+                        cut = whole[kind][:, pl.ds(pl.multiple_of(place * width, HD), width)]
+                        dst[d, :, at : at + width] = cut
+
+    else:
+        qkv_pack, feed_packs, x_ref, o_ref = refs[0:4], (refs[4:12], refs[12:20]), refs[20], refs[21]
+        w_ref, feed_ref, all_ref, o_all_ref, local_sem, send_sem, recv_sem = refs[22:]
     turned = lambda u, t: 1 - u if t else u
     group = [(p, turned(x, dx), turned(y, dy), turned(c, dc)) for dx, dy, dc in TURNS8]
     core, across, over = group[1], group[2], group[4]
@@ -234,12 +256,18 @@
         feed_ref.at[pl.ds(pl.multiple_of(slot, 16), depth), pl.ds(hidden, hidden)],
     ]
     firsts = (qkv_pack[0], feed_packs[0][0], feed_packs[1][0])
-    kept = [local(k, firsts[k], mine[k]) for k in range(3)] + [local(3, x_ref, tokens(0, 0))]
+    if raw:
+        packed((0, 1, 2), raw[0], TURNS4, HD, qkv_packs)
+    kept = [local(0, firsts[0], mine[0]), local(3, x_ref, tokens(0, 0))]
     kept.append(local(4, o_ref, o_all_ref.at[p]))
     o_of = lambda q: o_all_ref.at[lax.rem(p + 2 * groups - q, groups)]
     regrouped = [remote(qkv_pack[d], mine[0], group[d]) for d in (1, 2, 3)]
     moves = [remote(x_ref, tokens(1, 0), right)]
     sent = list(regrouped) + moves
+    if raw:
+        for k in range(2):
+            packed((3 + k,), raw[1], TURNS8, feed_all.shape[3] // groups, feed_all.at[k])
+    kept += [local(k, firsts[k], mine[k]) for k in (1, 2)]
     kept[0].wait()
     for copy in regrouped:
         copy.wait_recv()
@@ -295,32 +323,48 @@
         copy.wait()
 
 
-def start(groups, reach, qkv_pack, gate_pack, up_pack, own_inputs, own_o):
-    depth, size = qkv_pack[0].shape
-    rows, width = own_inputs.shape
-    hidden = gate_pack[0].shape[1]
+def start(groups, reach, spot, weights, offsets, width, own_inputs, own_o):
+    depth = weights[0].shape[0]
+    rows, model = own_inputs.shape
+    size = 3 * len(offsets[0](0, 0, 0)) * HD
+    hidden = len(offsets[1](0, 0, 0)) * width
     copies = 3 + 1 + 1 + 1 + 14 + (groups - 1) + (groups - 2) + (groups - 1) + (reach - 1) + 2 * (reach + 1) + (reach + 1)
     anywhere = pl.BlockSpec(memory_space=pl.ANY)
+    scratch = [
+        pltpu.SemaphoreType.DMA((5,)),
+        pltpu.SemaphoreType.DMA((copies,)),
+        pltpu.SemaphoreType.DMA((copies,)),
+    ]
+    raw = None
+    if width % HD == 0:
+        raw = offsets
+        scratch += [pltpu.VMEM(w.shape, BF) for w in weights]
+        scratch += [pltpu.VMEM((4, depth, size), BF), pltpu.VMEM((2, 8, depth, hidden), BF)]
+        scratch.append(pltpu.SemaphoreType.DMA((5,)))
+    else:
+        weights = [
+            *pack(spot, weights[:3], HD, offsets[0], TURNS4),
+            *pack(spot, weights[3:4], width, offsets[1], TURNS8),
+            *pack(spot, weights[4:5], width, offsets[1], TURNS8),
+        ]
     weight, feed, inputs, o_all = pl.pallas_call(
-        functools.partial(start_kernel, groups, reach),
-        in_specs=[anywhere] * 22,
+        functools.partial(start_kernel, groups, reach, raw),
+        in_specs=[anywhere] * (len(weights) + 2),
         out_specs=[anywhere] * 4,
         out_shape=[
             jax.ShapeDtypeStruct((groups, 2, 2, 2 * depth, size), BF),
             jax.ShapeDtypeStruct((8 * depth, 2 * hidden), BF),
-            jax.ShapeDtypeStruct((4 * (reach + 1) * rows, width), BF),
+            jax.ShapeDtypeStruct((4 * (reach + 1) * rows, model), BF),
             jax.ShapeDtypeStruct((groups,) + own_o.shape, BF),
         ],
-        scratch_shapes=[
-            pltpu.SemaphoreType.DMA((5,)),
-            pltpu.SemaphoreType.DMA((copies,)),
-            pltpu.SemaphoreType.DMA((copies,)),
-        ],
-        compiler_params=pltpu.CompilerParams(collective_id=0, has_side_effects=True),
+        scratch_shapes=scratch,
+        compiler_params=pltpu.CompilerParams(
+            collective_id=0, has_side_effects=True, vmem_limit_bytes=VMEM_BYTES
+        ),
         name="start",
         cost_estimate=cost(120),
-    )(*qkv_pack, *gate_pack, *up_pack, own_inputs, own_o)
-    return weight.reshape(-1, size), feed, inputs, o_all.reshape(-1, width)
+    )(*weights, own_inputs, own_o)
+    return weight.reshape(-1, size), feed, inputs, o_all.reshape(-1, model)
 
 
 def gate_up_kernel(x_ref, gate_w_ref, up_w_ref, narrow_ref, maps_ref, gate_ref, up_ref, gated_ref):
@@ -414,9 +458,62 @@
     )(x, weight, in_maps, out_maps)
 
 
-def post_kernel(heads, own_tiles, q_ref, k_ref, inv_q_ref, inv_k_ref, gain_ref, cos_ref, sin_ref, q_out, k_out):
+def scales_kernel(model, q_ref, k_ref, inv_q_ref, inv_k_ref, mine, others, send_sem, recv_sem):
+    p, x, y, c = (lax.axis_index(a) for a in ("p", "x", "y", "c"))
+    devices = ((p, x, y, 1 - c), (p, 1 - x, y, c), (p, 1 - x, y, 1 - c))
+    lines, wide = mine.shape
+    half = wide // 2
+    q_lines = q_ref.shape[1] // wide
+    copies = Copies(send_sem, recv_sem)
+    barrier = pltpu.get_barrier_semaphore()
+    for device in devices:
+        pl.semaphore_signal(barrier, inc=1, device_id=device, device_id_type=pl.DeviceIdType.MESH)
+    for n in range(lines):
+        src, at = (q_ref, n) if n < q_lines else (k_ref, n - q_lines)
+        mine[n : n + 1, :] = src[:1, at * wide : (at + 1) * wide]
+    pl.semaphore_wait(barrier, 3)
+    moves = [copies.remote(mine, others.at[k], device) for k, device in enumerate(devices)]
+    swap_lanes = lambda v: jnp.concatenate([v[:, half:], v[:, :half]], axis=1)
+    swap_lines = lambda v: jnp.concatenate([v[n ^ 1 : (n ^ 1) + 1] for n in range(lines)], axis=0)
+    for move in moves:
+        move.wait_recv()
+    total = mine[...] + swap_lanes(others[0]) + swap_lines(others[1]) + swap_lines(swap_lanes(others[2]))
+    inv = lax.rsqrt(total / model + EPS).T
+    for n in range(lines):
+        out, at = (inv_q_ref, n) if n < q_lines else (inv_k_ref, n - q_lines)
+        out[at * wide : (at + 1) * wide, :] = inv[:, n : n + 1]
+    copies.finish()
+
+
+def scales(square_q, square_k, model, wide):
+    lines = (square_q.shape[1] + square_k.shape[1]) // wide
+    vm = pl.BlockSpec(memory_space=pltpu.VMEM)
+    return pl.pallas_call(
+        functools.partial(scales_kernel, model),
+        in_specs=[vm] * 2,
+        out_specs=[vm] * 2,
+        out_shape=[jax.ShapeDtypeStruct((v.shape[1], 1), F32) for v in (square_q, square_k)],
+        scratch_shapes=[
+            pltpu.VMEM((lines, wide), F32),
+            pltpu.VMEM((3, lines, wide), F32),
+            pltpu.SemaphoreType.DMA((3,)),
+            pltpu.SemaphoreType.DMA((3,)),
+        ],
+        compiler_params=pltpu.CompilerParams(collective_id=4, has_side_effects=True),
+        name="scales",
+        cost_estimate=cost(1),
+    )(square_q, square_k)
+
+
+def rotation(row_ref, block_ref, b):
+    here = slice(b, b + 1) if isinstance(b, int) else pl.ds(b, 1)
+    cos, sin = block_ref[0, here, :], block_ref[1, here, :]
+    return cos * row_ref[0] - sin * row_ref[1], sin * row_ref[2] + cos * row_ref[3]
+
+
+def post_kernel(heads, own_tiles, q_ref, k_ref, inv_q_ref, inv_k_ref, gain_ref, row_ref, block_ref, q_out, k_out):
     width = heads * HD
-    cos, sin = cos_ref[...], sin_ref[...]
+    cos, sin = rotation(row_ref, block_ref, pl.program_id(0))
 
     def turn(pre_ref, inv, part, out_ref):
         for h in range(heads):
@@ -431,9 +528,9 @@
         turn(q_ref, inv_q_ref[...], 0, q_out)
 
 
-def post(pre_q, pre_k, inv_q, inv_k, gain, cos, sin, heads):
+def post(pre_q, pre_k, inv_q, inv_k, gain, row_tables, block_tables, heads):
     rows, width = pre_k.shape
-    tile = 256
+    tile = row_tables.shape[1]
     own_tiles = pre_q.shape[0] // tile
     row = lambda n: pl.BlockSpec((tile, n), lambda r: (r, 0))
     own = lambda n: pl.BlockSpec((tile, n), lambda r: (jnp.minimum(r, own_tiles - 1), 0))
@@ -446,14 +543,14 @@
             own(1),
             row(1),
             pl.BlockSpec((1, 2 * width), lambda r: (0, 0)),
-            row(HD),
-            row(HD),
+            pl.BlockSpec(row_tables.shape, lambda r: (0, 0, 0)),
+            pl.BlockSpec(block_tables.shape, lambda r: (0, 0, 0)),
         ],
         out_specs=[own(width), row(width)],
         out_shape=[jax.ShapeDtypeStruct(pre_q.shape, BF), jax.ShapeDtypeStruct(pre_k.shape, BF)],
         name="rope_forward",
         cost_estimate=cost(1),
-    )(pre_q, pre_k, inv_q, inv_k, gain, cos, sin)
+    )(pre_q, pre_k, inv_q, inv_k, gain, row_tables, block_tables)
 
 
 def unpost_kernel(heads, dq_ref, dk_ref, pre_q_ref, pre_k_ref, gain_ref, cos_ref, sin_ref, turn_ref, inner_ref):
@@ -496,18 +593,19 @@
         inv_q_ref,
         inv_k_ref,
         gain_ref,
-        cos_ref,
-        sin_ref,
+        row_ref,
+        block_ref,
         in_maps_ref,
         out_maps_ref,
         narrow_ref,
         early_ref,
         wide_ref,
+        choose_ref,
         weight_any,
         inputs_any,
         mid_any,
-    ) = refs[:18]
-    out_ref, sums_ref, wide_out_ref = refs[18:21]
+    ) = refs[:19]
+    out_ref, a_model_ref, a_hidden_ref, b_model_ref, b_hidden_ref = refs[19:24]
     (
         weight,
         inputs,
@@ -535,7 +633,7 @@
         local_sem,
         send_sem,
         recv_sem,
-    ) = refs[21:]
+    ) = refs[24:]
     p, x, y, c = (lax.axis_index(a) for a in ("p", "x", "y", "c"))
     core, across, both, over = (p, x, y, 1 - c), (p, 1 - x, y, c), (p, 1 - x, y, 1 - c), (p, x, 1 - y, c)
     others = [lax.rem(p + s, groups) for s in range(1, groups)]
@@ -557,7 +655,7 @@
 
     def unturn(b, carry):
         here = pl.ds(pl.multiple_of(b * rows, rows), rows)
-        cos, sin = cos_ref[here, :], sin_ref[here, :]
+        cos, sin = rotation(row_ref, block_ref, b)
         for part, pre_ref in enumerate((pre_q_ref, pre_k_ref)):
             product = None
             for h in range(heads):
@@ -605,11 +703,14 @@
 
     loads[0].wait()
 
-    def into(start, dst):
+    def backed(start):
         here = slice(start, start + 2 * rows)
         for k in range(3):
             part = dot_nt(grad[here, k * width : (k + 1) * width], out_maps_ref[k])
             back[here, k * rank : (k + 1) * rank] = part.astype(BF)
+
+    def into(start, dst, side):
+        here = slice(start, start + 2 * rows)
 
         def columns(n, carry):
             cols = pl.ds(pl.multiple_of(n * 512, 512), 512)
@@ -617,14 +718,25 @@
             dst[:, cols] = full.astype(BF)
             return carry
 
-        lax.fori_loop(0, model // 512, columns, 0)
-
-    into(2 * rows, far)
-    far_copy = copies.remote(far.at[pl.ds(rows, rows)], core_in, core)
-    far_copy.wait_recv()
-    met[...] = (far[:rows, :].astype(F32) + core_in[...].astype(F32)).astype(BF)
-    across_copy = copies.remote(met, across_in, across)
-    into(0, near)
+        steps = model // 1024
+        lax.fori_loop(side * steps, (side + 1) * steps, columns, 0)
+
+    sides = [pl.ds(k * (model // 2), model // 2) for k in range(2)]
+    backed(2 * rows)
+    far_copies = []
+    for k in range(2):
+        into(2 * rows, far, k)
+        far_copies.append(
+            copies.remote(far.at[pl.ds(rows, rows), sides[k]], core_in.at[:, sides[k]], core)
+        )
+    across_copies = []
+    for k in range(2):
+        far_copies[k].wait_recv()
+        met[:, sides[k]] = (far[:rows, sides[k]].astype(F32) + core_in[:, sides[k]].astype(F32)).astype(BF)
+        across_copies.append(copies.remote(met.at[:, sides[k]], across_in.at[:, sides[k]], across))
+    backed(0)
+    for k in range(2):
+        into(0, near, k)
     near_copy = copies.remote(near.at[pl.ds(rows, rows)], near_in, core)
 
     loads[1].wait()
@@ -663,14 +775,24 @@
     for k, copy in enumerate(wides):
         copy.wait_recv()
         wide_sum = wide_sum + wide_in[k]
-    wide_out_ref[...] = wide_sum
     last.wait_recv()
     summed = summed + own_sum_in[...]
-    sums_ref[...] = jnp.where(c == 0, summed[:, : HD // 2], summed[:, HD // 2 :])
+    summed = jnp.where(c == 0, summed[:, : HD // 2], summed[:, HD // 2 :])
+    for n in range(choose_ref.shape[0]):
+        mask = choose_ref[n : n + 1, :]
+        low = mask[:, : HD // 2]
+        for at, k in enumerate((5, 6, 7, 2, 0, 1)):
+            a_model_ref[n, at] = low * summed[k * rank : (k + 1) * rank, :]
+        for at, k in enumerate((8, 9, 10, 3, 4)):
+            b_model_ref[n, at] = low * summed[k * rank : (k + 1) * rank, :]
+        a_hidden_ref[n] = mask * wide_sum[:rank, :]
+        for at in range(2):
+            b_hidden_ref[n, at] = mask * wide_sum[(1 + at) * rank : (2 + at) * rank, :]
 
     loads[2].wait()
     near_copy.wait_recv()
-    across_copy.wait_recv()
+    for copy in across_copies:
+        copy.wait_recv()
     out_ref[...] = (
         mid[...]
         + near[:rows, :].astype(F32)
@@ -684,26 +806,28 @@
     own, width = args[0].shape
     rows, model = mid.shape
     rank = args[11].shape[1]
-    early_rows, wide_rows = args[13].shape[0], args[14].shape[0]
+    early_rows, wide_rows, adapters = args[13].shape[0], args[14].shape[0], args[15].shape[0]
     total_rows = early_rows + 6 * rank
     late = early_rows + 3 * rank
     vm = pl.BlockSpec(memory_space=pltpu.VMEM)
     anywhere = pl.BlockSpec(memory_space=pl.ANY)
-    count = 3 + groups + (groups - 1) + 3 + 2 * groups + (groups - 1) + 1
+    count = 3 + groups + (groups - 1) + 5 + 2 * groups + (groups - 1) + 1
     block = lambda *shape: pltpu.VMEM(shape, BF)
     full = lambda *shape: pltpu.VMEM(shape, F32)
-    first_rows = lambda v: vm if v.shape[0] <= own else pl.BlockSpec(
+    first_rows = lambda v: vm if v.ndim != 2 or v.shape[0] <= own else pl.BlockSpec(
         (own, v.shape[1]), lambda k: (0, 0), pipeline_mode=pl.Buffered(1)
     )
     return pl.pallas_call(
         functools.partial(finish_kernel, groups, heads, early_rows),
         grid=(1,),
         in_specs=[first_rows(v) for v in args] + [anywhere] * 3,
-        out_specs=[vm] * 3,
+        out_specs=[vm] * 5,
         out_shape=[
             jax.ShapeDtypeStruct((rows, model), F32),
-            jax.ShapeDtypeStruct((total_rows, HD // 2), F32),
-            jax.ShapeDtypeStruct((wide_rows, 256), F32),
+            jax.ShapeDtypeStruct((adapters, 6, rank, HD // 2), F32),
+            jax.ShapeDtypeStruct((adapters, rank, 256), F32),
+            jax.ShapeDtypeStruct((adapters, 5, rank, HD // 2), F32),
+            jax.ShapeDtypeStruct((adapters, 2, rank, 256), F32),
         ],
         scratch_shapes=[
             pltpu.VMEM(weight.shape, BF),
@@ -777,13 +901,15 @@
         query_rows_ref,
         log_ref,
         log_rows_ref,
+        back_gu_ref,
         q_any,
         k_any,
         v_any,
         o_any,
-    ) = refs[:15]
-    later_any = refs[15]
-    dq_ref, dk_ref, dv_ref, back_ref = refs[16:20]
+        later_any,
+        middle_any,
+    ) = refs[:18]
+    dq_ref, dk_ref, dv_ref, back_ref, maps_ref = refs[18:23]
     (
         q_buf,
         k_buf,
@@ -794,10 +920,11 @@
         do_in,
         inner,
         inner_in,
+        middle_buf,
         load_sem,
         send_sem,
         recv_sem,
-    ) = refs[20:]
+    ) = refs[23:]
     p, x, y, c = (lax.axis_index(a) for a in ("p", "x", "y", "c"))
     right, left = (lax.rem(p + 1, groups), x, y, c), (lax.rem(p + groups - 1, groups), x, y, c)
     rows = q_buf.shape[2]
@@ -809,6 +936,15 @@
     for n, (src, dst) in enumerate(sources):
         loads.append(pltpu.make_async_copy(src, dst, load_sem.at[n]))
         loads[-1].start()
+    part = middle_buf.shape[1]
+
+    def load_middle(n):
+        src = middle_any.at[pl.ds(n * part, part)]
+        copy = pltpu.make_async_copy(src, middle_buf.at[n % 2], load_sem.at[5 + n % 2])
+        copy.start()
+        return copy
+
+    middles = [load_middle(n) for n in range(2)]
     barrier = pltpu.get_barrier_semaphore()
     for device in (left, right):
         pl.semaphore_signal(barrier, inc=1, device_id=device, device_id_type=pl.DeviceIdType.MESH)
@@ -819,8 +955,10 @@
         back_ref[here, :] = low
         value = dot_nt(grad_ref[here, :], weight_ref[...]) + SCALE_ADAPT * dot(low, in_maps_ref[...])
         do_buf[b] = value.astype(BF).reshape(2, rows, heads * HD)
-    pl.semaphore_wait(barrier, 2)
-    moves = [copies.remote(do_buf, do_in.at[0], left)]
+        if b == 0:
+            pl.semaphore_wait(barrier, 2)
+            moves = []
+        moves.append(copies.remote(do_buf.at[b], do_in.at[0, b], left))
     for load in loads:
         load.wait()
 
@@ -866,10 +1004,13 @@
     lax.fori_loop(0, 2 * heads, own, 0)
 
     for t in range(1, reach + 1):
-        moves[-1].wait_recv()
+        arrived, moves = moves, []
+        for b in range(2):
+            arrived[b].wait_recv()
+            if t < reach:
+                moves.append(copies.remote(do_in.at[t - 1, b], do_in.at[t, b], left))
         inner_moves[-1].wait_recv()
         if t < reach:
-            moves.append(copies.remote(do_in.at[t - 1], do_in.at[t], left))
             inner_moves.append(copies.remote(inner_in.at[t - 1], inner_in.at[t], left))
 
         def from_later(n, carry, t=t):
@@ -886,23 +1027,31 @@
             return carry
 
         lax.fori_loop(0, 2 * heads, from_later, 0)
+        if t == 1:
+            for n in range(middle_any.shape[0] // part):
+                middles[n].wait()
+                term = SCALE_ADAPT * dot_tn(back_gu_ref[n * part : (n + 1) * part, :], middle_buf[n % 2])
+                maps_ref[...] = term if n == 0 else maps_ref[...] + term
+                if (n + 3) * part <= middle_any.shape[0]:
+                    middles.append(load_middle(n + 2))
     copies.finish()
 
 
-def attend_back(groups, reach, heads, rows, args, later):
+def attend_back(groups, reach, heads, rows, args, later, middle_low):
     own = 4 * rows
     local = heads * HD
     vm = pl.BlockSpec(memory_space=pltpu.VMEM)
     anywhere = pl.BlockSpec(memory_space=pl.ANY)
     block = lambda n: pltpu.VMEM((2 * n, 2, rows, local), BF)
     view = lambda v: v.reshape(-1, 2, rows, local)
-    count = 2 * reach
-    dq, dk, dv, back = pl.pallas_call(
+    count = 3 * reach
+    rank2, model = args[11].shape[1], middle_low.shape[1]
+    dq, dk, dv, back, maps = pl.pallas_call(
         functools.partial(attend_back_kernel, groups, reach, heads, HD**-0.5),
-        in_specs=[vm] * 11 + [anywhere] * 5,
-        out_specs=[vm] * 4,
+        in_specs=[vm] * 12 + [anywhere] * 6,
+        out_specs=[vm] * 5,
         out_shape=[jax.ShapeDtypeStruct((2, 2, rows, local), F32)] * 3
-        + [jax.ShapeDtypeStruct((own, args[2].shape[0]), BF)],
+        + [jax.ShapeDtypeStruct((own, args[2].shape[0]), BF), jax.ShapeDtypeStruct((rank2, model), F32)],
         scratch_shapes=[
             block(1),
             block(reach + 1),
@@ -913,7 +1062,8 @@
             pltpu.VMEM((reach, 2, 2, rows, local), BF),
             pltpu.VMEM((2 * heads, 2 * rows), F32),
             pltpu.VMEM((reach, 2 * heads, 2 * rows), F32),
-            pltpu.SemaphoreType.DMA((5,)),
+            pltpu.VMEM((2, 2 * rows, model), BF),
+            pltpu.SemaphoreType.DMA((7,)),
             pltpu.SemaphoreType.DMA((count,)),
             pltpu.SemaphoreType.DMA((count,)),
         ],
@@ -922,8 +1072,8 @@
         ),
         name="attend_backward",
         cost_estimate=cost(70),
-    )(*args[:11], *[view(v) for v in args[11:]], later.reshape(reach, 2, 2, rows, local))
-    return [v.reshape(own, local) for v in (dq, dk, dv)], back
+    )(*args[:12], *[view(v) for v in args[12:]], later.reshape(reach, 2, 2, rows, local), middle_low)
+    return [v.reshape(own, local) for v in (dq, dk, dv)], back, maps
 
 
 class Attention:
@@ -1537,9 +1687,10 @@
     w_qkv, feed_piece, inputs, o_own = start(
         at.np,
         reach,
-        pack(at.spot, [query_weight, key_weight, value_weight], HD, head_offsets, TURNS4),
-        pack(at.spot, [gate_weight], hidden_rows, feed_offsets, TURNS8),
-        pack(at.spot, [up_weight], hidden_rows, feed_offsets, TURNS8),
+        at.spot,
+        [query_weight, key_weight, value_weight, gate_weight, up_weight],
+        (head_offsets, feed_offsets),
+        hidden_rows,
         own_inputs,
         output_weight,
     )
@@ -1596,21 +1747,23 @@
 
     half_dim = HD // 2
     inv_freq = ROPE_BASE ** (-(jnp.arange(half_dim, dtype=F32) * 2.0 / HD))
-    spots = jnp.concatenate([spot(at.x), spot(at.x), spot(1 - at.x), spot(1 - at.x)])
-    angles = jnp.concatenate([spots - 2 * rows * t for t in range(count)]).astype(F32)[:, None] * inv_freq
-    cos, sin = jnp.cos(angles), jnp.sin(angles)
-    cos = jnp.concatenate([cos, cos], axis=1)
-    sin = jnp.concatenate([-sin, sin], axis=1)
+    first = at.p * 2 * rows
+    starts = jnp.stack([first + xx * rows - 2 * rows * t for t in range(count) for xx in (at.x, at.x, 1 - at.x, 1 - at.x)])
+    wide_freq = jnp.concatenate([inv_freq, inv_freq])[None]
+    sign = jnp.where(jnp.arange(HD) < half_dim, -1.0, 1.0)[None]
+    turn_angle = starts.astype(F32)[:, None] * wide_freq
+    row_angle = step_rows.astype(F32)[:, None] * wide_freq
+    row_cos, row_sin = jnp.cos(row_angle), jnp.sin(row_angle)
+    row_tables = jnp.stack([row_cos, row_sin, sign * row_cos, sign * row_sin])
+    block_tables = jnp.stack([jnp.cos(turn_angle), jnp.sin(turn_angle)])
 
     own = 4 * rows
     pre_q, pre_k, value_all, narrow_qkv, square_q, square_k = project(
         inputs, own, w_qkv, a_qkv, b_qkv, heads
     )
     w_d = lax.all_gather(after(down_weight, square_q), "p", axis=0, tiled=True)
-    squares = jnp.concatenate([square_q[:1], square_k[:1]], axis=1)
-    inv = lax.rsqrt(at.sum4(squares, 2 + reach) / width + EPS).reshape(-1, 1)
-    inv_q, inv_k = inv[:own], inv[own:]
-    query, key_all = post(pre_q, pre_k, inv_q, inv_k, gain, cos, sin, heads)
+    inv_q, inv_k = scales(square_q, square_k, width, 2 * rows)
+    query, key_all = post(pre_q, pre_k, inv_q, inv_k, gain, row_tables, block_tables, heads)
     o, log = attention.forward(query, key_all, value_all)
     narrow_o = dot_nt(o, a_o).astype(BF)
     def attn_part(part, mark=None):
@@ -1648,7 +1801,7 @@
     )
     lo_rows = jnp.stack([lo_of(pos + 2 * rows * t) for t in range(count)])
     query_rows = jnp.stack([pos + 2 * rows * t for t in range(count)])
-    (dq, dk, dv), back_o = attend_back(
+    (dq, dk, dv), back_o, ga_gu = attend_back(
         at.np,
         reach,
         heads,
@@ -1663,12 +1816,14 @@
             query_rows,
             log,
             later_logs,
+            back_gu.reshape(8 * rows, -1),
             query,
             key_all,
             value_all,
             o,
         ],
         later,
+        middle_low,
     )
     def share_y(mine, other):
         return mine + at.swap_y(other)
@@ -1689,14 +1844,14 @@
     def spread(v):
         return (v.reshape(-1, heads, 1, HD) * mine[:, None]).reshape(-1, width)
 
-    back_gu, grad_attn = back_gu.reshape(8 * rows, -1), grad_attn.reshape(4 * rows, -1)
-    ga_gu = SCALE_ADAPT * dot_tn(back_gu, middle_low)
+    grad_attn = grad_attn.reshape(4 * rows, -1)
     ga_o = SCALE_ADAPT * dot_tn(back_o, o)
     gb_o = SCALE_ADAPT * dot_tn(narrow_o, grad_attn)
+    choose = (jnp.arange(adapter_model_input_maps.shape[0], dtype=jnp.int32) == selected).astype(F32)
     early = jnp.concatenate([ga_gu, spread(ga_o), gb_o, gb_d])
     wide = wide.reshape(3 * rank, -1)
     if 2 * depth == HD and hidden_rows == 2 * HD:
-        grad_input, sums, wide = finish(
+        outs = finish(
             at.np,
             heads,
             [
@@ -1708,23 +1863,25 @@
                 inv_q,
                 inv_k,
                 gain,
-                cos,
-                sin,
+                row_tables,
+                block_tables,
                 a_qkv,
                 b_qkv,
                 narrow_qkv,
                 early,
                 wide,
+                jnp.broadcast_to(choose[:, None], (choose.shape[0], 256)),
             ],
             w_qkv,
             inputs,
             grad_mid,
         )
-        sums, wide = sums.reshape(-1, rank, depth), wide.reshape(-1, rank, hidden_rows)
-        early, late = sums[:5], sums[5:]
+        return (result[None], outs[0][None], *outs[1:])
     else:
         early = sum_model(after(early, dq))
-        inputs, narrow_qkv, pre_k, inv_k, cos, sin = (v[:own] for v in (inputs, narrow_qkv, pre_k, inv_k, cos, sin))
+        inputs, narrow_qkv, pre_k, inv_k = (v[:own] for v in (inputs, narrow_qkv, pre_k, inv_k))
+        tables = [jnp.concatenate([rotation(row_tables, block_tables, b)[k] for b in range(4)]) for k in range(2)]
+        cos, sin = tables
         wide = wide.reshape(-1, at.np, hidden_rows)
         dk = after(dk, early)
         turn, inner = unpost(dq, dk, pre_q, pre_k, gain, cos, sin, heads)
@@ -1769,7 +1926,6 @@
         sums = sums.reshape(-1, rank, depth)
         late, early = sums[:6], sums[6:]
         wide = share_p(after(wide, marks[0])).reshape(-1, rank, hidden_rows)
-    choose = (jnp.arange(adapter_model_input_maps.shape[0], dtype=jnp.int32) == selected).astype(F32)
     sum_a_model = choose[:, None, None, None] * jnp.concatenate([late[:3], early[2:3], early[:2]])[None]
     sum_a_hidden = choose[:, None, None] * wide[0][None]
     sum_b_model = choose[:, None, None, None] * jnp.concatenate([late[3:], early[3:]])[None]

time: 724 us -> 696 us (0.961)
  other arithmetic: 27.8 us -> 15.7 us
    slice x14 -> x0, local copies, waits for them, and re-layouts: 8.2 us -> none  [the longest x4 2.69 us: on_device(): inv_q, inv_k = (inv[:own], inv[own:])]
    unnamed x58 -> x64, local copies, waits for them, and re-layouts: 14.2 us -> 17.9 us
    dot_general x9 -> x8, matrix products: 16 us -> 13.9 us  [dot(): return lax.dot_general(a, b, (dims, ((), ())), preferred_element_type=F32)]
    pallas_call x4 -> x2, Pallas kernels: 142 us -> 144 us  [the longest x1 135 us: start(): pl.pallas_call(functools.partial(start_kernel, groups, reach, raw), in_sp...]
    ppermute x4 -> x3, waiting for transfers between devices: 40.1 us -> 40.8 us  [swap_x(): return lax.ppermute(value, 'x', SWAP)]
  transfers between devices with their start and end apart: 19 -> 16, of which waited for: 8 -> 7; matrix products, arithmetic and copies ran while one was open for 8% -> 7% of each run, Pallas kernels for 14% -> 16%
where the time goes in v6:
time: 696 us; the launch traced here: 686 us
  Pallas kernels  537 us (77%)
  waiting for transfers between devices  55.1 us (8%)
  local copies, waits for them, and re-layouts  35.5 us (5%)
  between operations  15.8 us (2%)
  other arithmetic  15.7 us (2%)
  matrix products  13.9 us (2%)
  starting transfers between devices  13.5 us (2%)
    pallas_call x1, Pallas kernels, feed_layer(): pl.pallas_call(feed_kernel, in_specs=[vm] * 7 + [anywhere] * 10, out_spec...  162 us
    pallas_call x1, Pallas kernels, start(): pl.pallas_call(functools.partial(start_kernel, groups, reach, raw), in_sp...  135 us
    pallas_call x1, Pallas kernels, finish(): pl.pallas_call(functools.partial(finish_kernel, groups, heads, early_rows...  68.4 us
    pallas_call x1, Pallas kernels, attend_back(): pl.pallas_call(functools.partial(attend_back_kernel, groups, reach, heads...  61.8 us
    ppermute x3, waiting for transfers between devices, swap_x(): return lax.ppermute(value, 'x', SWAP)  40.8 us
    pallas_call x1, Pallas kernels, project(): pl.pallas_call(functools.partial(project_kernel, heads, own_tiles), grid=...  33.1 us
    pallas_call x1, Pallas kernels, gate_up(): pl.pallas_call(gate_up_kernel, grid=(steps,), in_specs=[pl.BlockSpec((row...  27.3 us
    pallas_call x1, Pallas kernels, forward(): pl.pallas_call(functools.partial(attend_kernel, count, HD ** (-0.5)), gri...  23.5 us
  transfers between devices with their start and end apart: 16, of which 7 were waited for; matrix products, arithmetic and copies ran while one was open for 7% of the time, Pallas kernels for 16%

profile of v6, /device:TPU:0, one launch (start us, length us, event | category | flops | bytes accessed | tf_op | source)
XLA Modules:
  0.0 686.2 jit_solution(6422239394894069219)
XLA Ops:
  7.2 134.9 %start.1 = (bf16[4,2,2,128,1536]{4,3,2,1,0:T(8,128)(2,1)}, bf16[512,2048]{1,0:T(8,128)(2,1)}, bf16[3072,2048]{1,0:T(8,128)(2,1)}, bf16[4,64,2048]{2,1,0:T(8,128)(2,1)}) custom-call(bf16[64,2048]{1,0:T(8,128)(2,1)} %refs_0_.1, bf16[64,2048]{1,0:T(8,128)(2,1)} %refs_1_.1, bf16[64,2048]{1,0:T(8,128)(2,1)} %refs_2_.1, bf16[64,8192]{1,0:T(8,128)(2,1)} %refs_3_.1, ...), custom_call_target="tpu_custom_call" | custom-call | flops 131999997952 | bytes 120000000 | tf_op jit(solution)/shard_map/start/pallas_call | solution.py:350
  142.2 4.4 collective-permute-start
  146.6 1.3 collective-permute-start.1
  147.9 1.7 collective-permute-start.2
  150.2 1.0 constant_dynamic-slice_fusion
  151.7 0.6 reshape.810.out_maps_ref.refs_11_
  152.8 1.0 copy.50
  153.8 0.9 copy.51.refs_7_.refs_5_
  154.9 0.7 constant_dynamic-slice_fusion.1
  155.6 33.1 %project.1 = (f32[1024,512]{1,0:T(8,128)}, f32[3072,512]{1,0:T(8,128)}, bf16[3072,512]{1,0:T(8,128)(2,1)}, bf16[3072,48]{1,0:T(8,128)(2,1)}, f32[8,1024]{1,0:T(8,128)}, /*index=5*/f32[8,3072]{1,0:T(8,128)}) custom-call(bf16[3072,2048]{1,0:T(8,128)(2,1)} %get-tuple-element.48.x_ref.refs_17_, bf16[2048,1536]{1,0:T(8,128)(2,1)} %bitcast.108, ...), custom_call_target="tpu_custom_call" | custom-call | flops 1100000000 | bytes 1000000 | tf_op jit(solution)/shard_map/project/pallas_call | solution.py:435
  188.7 8.8 %scales.1 = (f32[1024,1]{1,0:T(8,128)}, f32[3072,1]{1,0:T(8,128)}) custom-call(f32[8,1024]{1,0:T(8,128)} %get-tuple-element.52.q_ref, f32[8,3072]{1,0:T(8,128)} %get-tuple-element.53.k_ref), custom_call_target="tpu_custom_call" | custom-call | flops 1100000000 | bytes 1000000 | tf_op jit(solution)/shard_map/scales/pallas_call | solution.py:491
  197.5 0.7 fusion.4
  200.1 0.8 pad_maximum_fusion.3.row_ref.refs_8_
  200.9 11.6 %rope_forward.1 = (bf16[1024,512]{1,0:T(8,128)(2,1)}, bf16[3072,512]{1,0:T(8,128)(2,1)}) custom-call(f32[1024,512]{1,0:T(8,128)} %get-tuple-element.50.q_ref.refs_3_, f32[3072,512]{1,0:T(8,128)} %get-tuple-element.51.k_ref.refs_4_, f32[1024,1]{1,0:T(8,128)} %get-tuple-element.54.inv_q_ref.refs_5_, f32[3072,1]{1,0:T(8,128)} %get-tuple-element.55.inv_k_ref.refs_6_, ...), custom_call_target="tpu_custom_call" | custom-call | flops 1100000000 | bytes 1000000 | tf_op jit(solution)/shard_map/rope_forward/pallas_call | solution.py:537
  213.2 2.0 broadcast_maximum_fusion.refs_6_.refs_4_
  215.1 23.5 %attend_forward.1 = (bf16[2,2,256,512]{3,2,1,0:T(8,128)(2,1)}, f32[8,512,1]{2,1,0:T(8,128)}) custom-call(bf16[2,2,256,512]{3,2,1,0:T(8,128)(2,1)} %bitcast.117, bf16[6,2,256,512]{3,2,1,0:T(8,128)(2,1)} %bitcast.99, bf16[6,2,256,512]{3,2,1,0:T(8,128)(2,1)} %bitcast.100, bf16[6,2,256,512]{3,2,1,0:T(8,128)(2,1)} %bitcast.101, ...), custom_call_target="tpu_custom_call" | custom-call | flops 1100000000 | bytes 1000000 | tf_op jit(solution)/shard_map/attend_forward/pallas_call | solution.py:1103
  238.7 1.5 dynamic-slice_bitcast_fusion
  240.2 1.6 convolution_convert_fusion.1
  241.8 2.1 fusion.6
  244.0 1.5 broadcast_select_fusion.3
  245.7 1.3 fusion.7
  246.9 0.7 add_convert_fusion.1
  247.7 1.3 slice.76
  249.4 0.7 collective-permute-start.3
  250.3 2.5 collective-permute-done.3
  252.8 1.9 add_convert_fusion.2
  255.4 2.3 fusion.8
  257.7 0.7 add_convert_fusion.refs_0_
  258.7 1.5 constant_dynamic-slice_fusion.7
  260.2 1.1 collective-permute-done.4.refs_1_
  261.3 19.0 %collective-permute-done.5.refs_2_ = bf16[256,2048]{1,0:T(8,128)(2,1)S(1)} collective-permute-done((bf16[256,2048]{1,0:T(8,128)(2,1)S(1)}, bf16[256,2048]{1,0:T(8,128)(2,1)S(1)}, u32[]{:S(2)}, u32[]{:S(2)}) %collective-permute-start.5) | collective-permute-done | bytes 1048608 | tf_op jit(solution)/shard_map/ppermute | solution.py:51
  280.2 1.0 copy-done.22
  281.3 5.2 after_attention.1
  287.6 1.7 collective-permute-start.9
  289.8 1.0 constant_dynamic-slice_fusion.8
  290.8 20.6 %collective-permute-done.7 = bf16[256,2048]{1,0:T(8,128)(2,1)S(1)} collective-permute-done((bf16[256,2048]{1,0:T(8,128)(2,1)}, bf16[256,2048]{1,0:T(8,128)(2,1)S(1)}, u32[]{:S(2)}, u32[]{:S(2)}) %collective-permute-start.7) | collective-permute-done | bytes 1048608 | tf_op jit(solution)/shard_map/ppermute | solution.py:51
  312.5 1.2 reshape.804
  313.7 1.3 dynamic-slice_reduce_fusion
  315.0 0.6 reshape.805.maps_ref.refs_2_
  316.1 0.6 copy.58
  316.7 2.8 reduce.2.refs_16_
  319.5 1.5 collective-permute-start.11
  321.7 1.3 constant_dynamic-update-slice_fusion.8
  323.1 1.3 constant_dynamic-update-slice_fusion.7
  324.5 9.4 %collective-permute-done.11 = bf16[128,2048]{1,0:T(8,128)(2,1)S(1)} collective-permute-done((bf16[128,2048]{1,0:T(8,128)(2,1)S(1)}, bf16[128,2048]{1,0:T(8,128)(2,1)S(1)}, u32[]{:S(2)}, u32[]{:S(2)}) %collective-permute-start.11) | collective-permute-done | bytes 524320 | tf_op jit(solution)/shard_map/ppermute | solution.py:57
  333.9 1.3 collective-permute-done.12
  335.4 1.3 constant_dynamic-update-slice_fusion.5
  337.0 1.1 collective-permute-done.13
  338.2 3.2 copy-done.4
  341.4 3.2 convolution_convert_fusion.narrow_ref
  344.6 27.3 %gate_up.1 = (bf16[2048,1024]{1,0:T(8,128)(2,1)}, bf16[2048,1024]{1,0:T(8,128)(2,1)}, bf16[2048,1024]{1,0:T(8,128)(2,1)}) custom-call(bf16[2048,2048]{1,0:T(8,128)(2,1)} %copy-done.4, bf16[4,512,2048]{2,1,0:T(8,128)(2,1)} %bitcast.92, bf16[4,512,2048]{2,1,0:T(8,128)(2,1)} %bitcast.93, bf16[2048,32]{1,0:T(8,128)(2,1)} %convolution_convert_fusion.narrow_ref, ...), custom_call_target="tpu_custom_call" | custom-call | flops 1100000000 | bytes 1000000 | tf_op jit(solution)/shard_map/gate_up/pallas_call | solution.py:387
  371.9 162.3 %feed_layer.1 = (bf16[256,2048]{1,0:T(8,128)(2,1)}, f32[256,2048]{1,0:T(8,128)}, bf16[4,256,2048]{2,1,0:T(8,128)(2,1)}, bf16[8,256,32]{2,1,0:T(8,128)(2,1)}, f32...) custom-call(bf16[16,1024]{1,0:T(8,128)(2,1)} %bitcast.135, ...), custom_call_target="tpu_custom_call" | custom-call | flops 186999996416 | bytes 170000000 | tf_op jit(solution)/shard_map/feed_layer/pallas_call | solution.py:1569
  534.2 2.8 convolution_multiply_fusion
  537.1 61.8 %attend_backward.1 = (f32[2,2,256,512]{3,2,1,0:T(8,128)}, f32[2,2,256,512]{3,2,1,0:T(8,128)}, f32[2,2,256,512]{3,2,1,0:T(8,128)}, bf16[1024,16]{1,0:T(8,128)(2,1)}, f32[32,2048]{1,0:T(8,128)}) custom-call(bf16[1024,2048]{1,0:T(8,128)(2,1)} %bitcast.111, bf16[512,2048]{1,0:T(8,128)(2,1)} %bitcast.104, bf16[16,512]{1,0:T(8,128)(2,1)} %bitcast.136, ...), custom_call_target="tpu_custom_call" | custom-call | flops 76999999488 | bytes 70000000 | tf_op jit(solution)/shard_map/attend_backward/pallas_call | solution.py:1049
  598.9 1.2 convolution_multiply_fusion.1
  600.3 1.8 pad_maximum_fusion.2.refs_13_
  602.1 0.7 broadcast_in_dim.82.refs_15_
  602.8 68.4 %finish.1 = (f32[256,2048]{1,0:T(8,128)}, f32[8,6,16,64]{3,2,1,0:T(8,128)}, f32[8,16,256]{2,1,0:T(8,128)}, f32[8,5,16,64]{3,2,1,0:T(8,128)}, f32[8,2,16,256]{3,2,1,0:T(8,128)}) custom-call(f32[1024,512]{1,0:T(8,128)} %bitcast.150, f32[1024,512]{1,0:T(8,128)} %bitcast.151, f32[1024,512]{1,0:T(8,128)} %bitcast.152, ...), custom_call_target="tpu_custom_call" | custom-call | flops 65999998976 | bytes 60000000 | tf_op jit(solution)/shard_map/finish/pallas_call | solution.py:820
  671.3 1.0 copy.78
  672.3 3.8 copy.79
  676.1 0.7 copy.80
  676.8 0.7 copy.81
  677.5 0.7 copy.82
  678.2 0.7 copy.83
  (118 shorter events, 10.1 us)
Async XLA Ops:
  7.2 147.5 %copy-start = (bf16[8,6,16,2048]{3,2,1,0:T(8,128)(2,1)S(1)}, bf16[8,6,16,2048]{3,2,1,0:T(8,128)(2,1)}, u32[]{:S(2)}) copy-start(bf16[8,6,16,2048]{3,2,1,0:T(8,128)(2,1)} %param.34) | copy-start | bytes 9437188
  7.2 337.4 %all-gather.6.cloned.1.call-start = ((), (), s32[]{:S(2)}) async-start(), calls=%async_computation.1 | async-start | bytes 10485760 | tf_op jit(solution)/shard_map/all_gather | solution.py:1697
  7.2 145.2 %copy-start.21 = (s32[4,8]{1,0:T(4,128)S(1)}, s32[4,8]{1,0:T(4,128)}, u32[]{:S(2)}) copy-start(s32[4,8]{1,0:T(4,128)} %param.21) | copy-start | bytes 388
  142.2 229.7 %all-gather.4.cloned.1.call-start = ((), (), s32[]{:S(2)}) async-start(), calls=%async_computation | async-start | bytes 5242880 | tf_op jit(solution)/shard_map/all_gather | solution.py:1764
  142.2 101.7 %collective-permute-start = (bf16[256,2048]{1,0:T(8,128)(2,1)}, bf16[256,2048]{1,0:T(8,128)(2,1)}, u32[]{:S(2)}, u32[]{:S(2)}) collective-permute-start(bf16[256,2048]{1,0:T(8,128)(2,1)} %bitcast.120), channel_id=1, source_target_pairs={{0,2},{3,1},{4,6},{7,5},{8,10},{11,9},{12,14},{15,13},{16,18},{19,... | collective-permute-start | bytes 3145736 | tf_op jit(solution)/shard_map/ppermute | solution.py:1699
  146.6 97.3 %collective-permute-start.1 = (bf16[256,2048]{1,0:T(8,128)(2,1)}, bf16[256,2048]{1,0:T(8,128)(2,1)}, u32[]{:S(2)}, u32[]{:S(2)}) collective-permute-start(bf16[256,2048]{1,0:T(8,128)(2,1)} %bitcast.121), channel_id=1, source_target_pairs={{1,0},{2,3},{5,4},{6,7},{9,8},{10,11},{13,12},{14,15},{17,16},{18,... | collective-permute-start | bytes 3145736 | tf_op jit(solution)/shard_map/ppermute | solution.py:1699
  147.9 96.1 %collective-permute-start.2 = (bf16[256,2048]{1,0:T(8,128)(2,1)}, bf16[256,2048]{1,0:T(8,128)(2,1)}, u32[]{:S(2)}, u32[]{:S(2)}) collective-permute-start(bf16[256,2048]{1,0:T(8,128)(2,1)} %bitcast.122), channel_id=1, source_target_pairs={{1,2},{2,1},{5,6},{6,5},{9,10},{10,9},{13,14},{14,13},{17,18},{18,... | collective-permute-start | bytes 3145736 | tf_op jit(solution)/shard_map/ppermute | solution.py:1699
  215.1 28.8 %copy-start.9 = (bf16[4,64,2048]{2,1,0:T(8,128)(2,1)S(1)}, bf16[4,64,2048]{2,1,0:T(8,128)(2,1)}, u32[]{:S(2)}) copy-start(bf16[4,64,2048]{2,1,0:T(8,128)(2,1)} %get-tuple-element.60) | copy-start | bytes 3145732
  240.2 17.5 %copy-start.10 = (bf16[16,2048]{1,0:T(8,128)(2,1)}, bf16[16,2048]{1,0:T(8,128)(2,1)S(1)}, u32[]{:S(2)}) copy-start(bf16[16,2048]{1,0:T(8,128)(2,1)S(1)} %get-tuple-element.97.refs_3_) | copy-start | bytes 196612
  241.8 15.9 %copy-start.13 = (bf16[1024,16]{0,1:T(8,128)(2,1)}, bf16[1024,16]{0,1:T(8,128)(2,1)S(1)}, u32[]{:S(2)}) copy-start(bf16[1024,16]{0,1:T(8,128)(2,1)S(1)} %convolution_convert_fusion.1) | copy-start | bytes 98308
  245.7 2.0 copy-start.2
  247.7 1.8 copy-start.6
  249.4 3.4 collective-permute-start.3
  250.2 5.2 copy-start.3
  250.3 87.9 %copy-start.17 = (bf16[1,2,16,2048]{3,2,1,0:T(8,128)(2,1)}, bf16[1,2,16,2048]{3,2,1,0:T(8,128)(2,1)S(1)}, u32[]{:S(2)}) copy-start(bf16[1,2,16,2048]{3,2,1,0:T(8,128)(2,1)S(1)} %constant_dynamic-slice_fusion.2) | copy-start | bytes 393220
  254.7 25.5 %collective-permute-start.5 = (bf16[256,2048]{1,0:T(8,128)(2,1)S(1)}, bf16[256,2048]{1,0:T(8,128)(2,1)S(1)}, u32[]{:S(2)}, u32[]{:S(2)}) collective-permute-start(bf16[256,2048]{1,0:T(8,128)(2,1)S(1)} %add_convert_fusion.2), channel_id=1, source_target_pairs={{0,4},{4,0},{1,5},{5,1},{2,6},{6,2},{3,7},{7,3},{8,12},{12,8},{9,1... | collective-permute-start | bytes 3145736 | tf_op jit(solution)/shard_map/ppermute | solution.py:51
  258.5 21.8 %copy-start.7 = (bf16[512,2048]{1,0:T(8,128)(2,1)}, bf16[512,2048]{1,0:T(8,128)(2,1)S(1)}, u32[]{:S(2)}) copy-start(bf16[512,2048]{1,0:T(8,128)(2,1)S(1)} %add_convert_fusion.refs_0_) | copy-start | bytes 6291460
  258.5 2.7 collective-permute-start.4
  261.3 19.0 %copy-start.23 = (bf16[256,2048]{1,0:T(8,128)(2,1)}, bf16[256,2048]{1,0:T(8,128)(2,1)S(1)}, u32[]{:S(2)}) copy-start(bf16[256,2048]{1,0:T(8,128)(2,1)S(1)} %collective-permute-done.4.refs_1_) | copy-start | bytes 3145732
  280.2 1.0 copy-start.22
  286.4 24.9 %collective-permute-start.7 = (bf16[256,2048]{1,0:T(8,128)(2,1)}, bf16[256,2048]{1,0:T(8,128)(2,1)S(1)}, u32[]{:S(2)}, u32[]{:S(2)}) collective-permute-start(bf16[256,2048]{1,0:T(8,128)(2,1)} %get-tuple-element.62), channel_id=1, source_target_pairs={{0,4},{4,0},{1,5},{5,1},{2,6},{6,2},{3,7},{7,3},{8,12},{12,8},{9,1... | collective-permute-start | bytes 3145736 | tf_op jit(solution)/shard_map/ppermute | solution.py:51
  287.6 33.5 %collective-permute-start.9 = (bf16[256,2048]{1,0:T(8,128)(2,1)}, bf16[256,2048]{1,0:T(8,128)(2,1)S(1)}, u32[]{:S(2)}, u32[]{:S(2)}) collective-permute-start(bf16[256,2048]{1,0:T(8,128)(2,1)} %get-tuple-element.62), channel_id=1, source_target_pairs={{0,2},{2,0},{1,3},{3,1},{4,6},{6,4},{5,7},{7,5},{8,10},{10,8},{9,1... | collective-permute-start | bytes 3145736 | tf_op jit(solution)/shard_map/ppermute | solution.py:57
  289.8 33.3 %collective-permute-start.6 = (bf16[256,2048]{1,0:T(8,128)(2,1)}, bf16[256,2048]{1,0:T(8,128)(2,1)}, u32[]{:S(2)}, u32[]{:S(2)}) collective-permute-start(bf16[256,2048]{1,0:T(8,128)(2,1)} %get-tuple-element.62), channel_id=1, source_target_pairs={{0,1},{1,0},{2,3},{3,2},{4,5},{5,4},{6,7},{7,6},{8,9},{9,8},{10,11... | collective-permute-start | bytes 3145736 | tf_op jit(solution)/shard_map/ppermute | solution.py:48
  311.4 24.1 %collective-permute-start.8 = (bf16[256,2048]{1,0:T(8,128)(2,1)S(1)}, bf16[256,2048]{1,0:T(8,128)(2,1)}, u32[]{:S(2)}, u32[]{:S(2)}) collective-permute-start(bf16[256,2048]{1,0:T(8,128)(2,1)S(1)} %collective-permute-done.7), channel_id=1, source_target_pairs={{0,1},{1,0},{2,3},{3,2},{4,5},{5,4},{6,7},{7,6},{8,9},{9,8},{10,11... | collective-permute-start | bytes 3145736 | tf_op jit(solution)/shard_map/ppermute | solution.py:48
  319.5 14.4 %collective-permute-start.11 = (bf16[128,2048]{1,0:T(8,128)(2,1)S(1)}, bf16[128,2048]{1,0:T(8,128)(2,1)S(1)}, u32[]{:S(2)}, u32[]{:S(2)}) collective-permute-start(bf16[128,2048]{1,0:T(8,128)(2,1)S(1)} %slice.79), channel_id=1, source_target_pairs={{0,2},{2,0},{1,3},{3,1},{4,6},{6,4},{5,7},{7,5},{8,10},{10,8},{9,1... | collective-permute-start | bytes 1572872 | tf_op jit(solution)/shard_map/ppermute | solution.py:57
  321.1 14.1 %collective-permute-start.12 = (bf16[128,2048]{1,0:T(8,128)(2,1)S(1)}, bf16[128,2048]{1,0:T(8,128)(2,1)S(1)}, u32[]{:S(2)}, u32[]{:S(2)}) collective-permute-start(bf16[128,2048]{1,0:T(8,128)(2,1)S(1)} %slice.80), channel_id=1, source_target_pairs={{0,4},{4,0},{1,5},{5,1},{2,6},{6,2},{3,7},{7,3},{8,12},{12,8},{9,1... | collective-permute-start | bytes 1572872 | tf_op jit(solution)/shard_map/ppermute | solution.py:51
  323.0 13.8 %collective-permute-start.10 = (bf16[256,2048]{1,0:T(8,128)(2,1)S(1)}, bf16[256,2048]{1,0:T(8,128)(2,1)S(1)}, u32[]{:S(2)}, u32[]{:S(2)}) collective-permute-start(bf16[256,2048]{1,0:T(8,128)(2,1)S(1)} %collective-permute-done.9), channel_id=1, source_target_pairs={{0,1},{1,0},{2,3},{3,2},{4,5},{5,4},{6,7},{7,6},{8,9},{9,8},{10,11... | collective-permute-start | bytes 3145736 | tf_op jit(solution)/shard_map/ppermute | solution.py:48
  335.4 2.7 collective-permute-start.13
  338.2 3.3 copy-start.4
  371.9 162.3 %copy-start.14 = (bf16[1024,16]{0,1:T(8,128)(2,1)S(1)}, bf16[1024,16]{0,1:T(8,128)(2,1)}, u32[]{:S(2)}) copy-start(bf16[1024,16]{0,1:T(8,128)(2,1)} %copy-done.13) | copy-start | bytes 98308
  537.0 61.8 %copy-start.5 = (bf16[2,2,256,512]{3,2,1,0:T(8,128)(2,1)S(1)}, bf16[2,2,256,512]{3,2,1,0:T(8,128)(2,1)}, u32[]{:S(2)}) copy-start(bf16[2,2,256,512]{3,2,1,0:T(8,128)(2,1)} %get-tuple-element.59.refs_15_) | copy-start | bytes 3145732
  537.0 63.1 %copy-start.19 = (f32[4]{0:T(128)S(1)}, f32[4]{0:T(128)}, u32[]{:S(2)}) copy-start(f32[4]{0:T(128)} %compare_convert_fusion.1) | copy-start | bytes 52
  537.1 63.2 %copy-start.16 = (f32[16,2048]{1,0:T(8,128)S(1)}, f32[16,2048]{1,0:T(8,128)}, u32[]{:S(2)}) copy-start(f32[16,2048]{1,0:T(8,128)} %get-tuple-element.82) | copy-start | bytes 393220
  537.1 65.1 %copy-start.20 = (f32[8]{0:T(128)S(1)}, f32[8]{0:T(128)}, u32[]{:S(2)}) copy-start(f32[8]{0:T(128)} %compare_convert_fusion) | copy-start | bytes 100
  602.8 68.5 %copy-start.8 = (bf16[256,2048]{1,0:T(8,128)(2,1)S(1)}, bf16[256,2048]{1,0:T(8,128)(2,1)}, u32[]{:S(2)}) copy-start(bf16[256,2048]{1,0:T(8,128)(2,1)} %get-tuple-element.71) | copy-start | bytes 3145732
  671.3 4.8 copy-start.11
  671.3 5.6 copy-start.18
  671.3 6.2 copy-start.12
  671.3 6.9 %copy-start.15 = (f32[8,2,16,256]{3,2,1,0:T(8,128)S(1)}, f32[8,2,16,256]{3,2,1,0:T(8,128)}, u32[]{:S(2)}) copy-start(f32[8,2,16,256]{3,2,1,0:T(8,128)} %get-tuple-element.135) | copy-start | bytes 786436
  671.3 7.6 %copy-start.1 = (bf16[8,6,16,2048]{3,2,1,0:T(8,128)(2,1)S(1)}, bf16[8,6,16,2048]{3,2,1,0:T(8,128)(2,1)}, u32[]{:S(2)}) copy-start(bf16[8,6,16,2048]{3,2,1,0:T(8,128)(2,1)} %param.34) | copy-start | bytes 9437188
Sparse Core Ops, SparseCore 0:
  142.3 146.8 all-gather.5
  290.8 78.9 all-gather.3

commit v7 on v6

--- a/solution.py
+++ b/solution.py
@@ -243,11 +243,16 @@
     def at(ref, start, size):
         return ref.at[pl.ds(pl.multiple_of(start, 16), size)]
 
-    def tokens(t, block):
-        return all_ref.at[pl.ds((4 * t + block) * rows, rows)]
-
-    def owned(q):
-        return w_ref.at[lax.rem(p + 2 * groups - q, groups), :, y]
+    part = rows // 2
+
+    def tokens(t, block, i):
+        return all_ref.at[pl.ds((4 * t + block) * rows + i * part, part)]
+
+    def own_tokens(i):
+        return x_ref.at[pl.ds(i * part, part)]
+
+    def owned(q, i):
+        return w_ref.at[lax.rem(p + 2 * groups - q, groups), i, y]
 
     slot = (4 * x + 2 * y + c) * depth
     mine = [
@@ -258,12 +263,12 @@
     firsts = (qkv_pack[0], feed_packs[0][0], feed_packs[1][0])
     if raw:
         packed((0, 1, 2), raw[0], TURNS4, HD, qkv_packs)
-    kept = [local(0, firsts[0], mine[0]), local(3, x_ref, tokens(0, 0))]
+    kept = [local(0, firsts[0], mine[0]), local(3, x_ref, all_ref.at[pl.ds(0, rows)])]
     kept.append(local(4, o_ref, o_all_ref.at[p]))
     o_of = lambda q: o_all_ref.at[lax.rem(p + 2 * groups - q, groups)]
     regrouped = [remote(qkv_pack[d], mine[0], group[d]) for d in (1, 2, 3)]
-    moves = [remote(x_ref, tokens(1, 0), right)]
-    sent = list(regrouped) + moves
+    moves = [[remote(own_tokens(i), tokens(1, 0, i), right) for i in range(2)]]
+    sent = regrouped + moves[0]
     if raw:
         for k in range(2):
             packed((3 + k,), raw[1], TURNS8, feed_all.shape[3] // groups, feed_all.at[k])
@@ -271,50 +276,50 @@
     kept[0].wait()
     for copy in regrouped:
         copy.wait_recv()
-    along = remote(owned(0), owned(0), right)
+    along = [remote(owned(0, i), owned(0, i), right) for i in range(2)]
     o_along = remote(o_ref, o_of(0), right)
-    sent.append(o_along)
-    later = [remote(owned(0), owned(0), over)]
-    spread = [(remote(x_ref, tokens(0, 1), core), remote(x_ref, tokens(0, 2), across))]
+    sent += [*along, o_along]
+    later = [remote(owned(0, i), owned(0, i), over) for i in range(2)]
+    spread = [[(remote(own_tokens(i), tokens(0, 1, i), core), remote(own_tokens(i), tokens(0, 2, i), across)) for i in range(2)]]
     for k in (1, 2):
         later += [remote(feed_packs[k - 1][d], mine[k], group[d]) for d in range(1, 8)]
-    sent.append(along)
     step = 1
     ready = 0
-
-    def pass_on(t):
-        spread[t][1].wait_recv()
-        later.append(remote(tokens(t, 2), tokens(t, 3), core))
-
     while step < groups or ready <= reach:
         if ready < reach:
-            moves[ready].wait_recv()
-            if ready + 1 < reach:
-                moves.append(remote(tokens(ready + 1, 0), tokens(ready + 2, 0), right))
-                sent.append(moves[-1])
-            spread.append(
-                (
-                    remote(tokens(ready + 1, 0), tokens(ready + 1, 1), core),
-                    remote(tokens(ready + 1, 0), tokens(ready + 1, 2), across),
+            moves.append([])
+            spread.append([])
+            for i in range(2):
+                moves[ready][i].wait_recv()
+                src = tokens(ready + 1, 0, i)
+                if ready + 1 < reach:
+                    moves[-1].append(remote(src, tokens(ready + 2, 0, i), right))
+                spread[-1].append(
+                    (remote(src, tokens(ready + 1, 1, i), core), remote(src, tokens(ready + 1, 2, i), across))
                 )
-            )
+            sent += moves[-1]
         if step < groups:
-            along.wait_recv()
-            if step < groups - 1:
-                along = remote(owned(step), owned(step), right)
-                sent.append(along)
-            later.append(remote(owned(step), owned(step), over))
+            arrived, along = along, []
+            for i in range(2):
+                arrived[i].wait_recv()
+                if step < groups - 1:
+                    along.append(remote(owned(step, i), owned(step, i), right))
+                later.append(remote(owned(step, i), owned(step, i), over))
+            sent += along
             o_along.wait_recv()
             if step < groups - 1:
                 o_along = remote(o_of(step), o_of(step), right)
                 sent.append(o_along)
             step += 1
         if ready <= reach:
-            pass_on(ready)
+            for i in range(2):
+                spread[ready][i][1].wait_recv()
+                later.append(remote(tokens(ready, 2, i), tokens(ready, 3, i), core))
             ready += 1
-    for near, far in spread:
-        near.wait_recv()
-        sent += [near, far]
+    for pairs in spread:
+        for near, far in pairs:
+            near.wait_recv()
+            sent += [near, far]
     for copy in later:
         copy.wait_recv()
     for copy in sent + later:
@@ -328,7 +333,7 @@
     rows, model = own_inputs.shape
     size = 3 * len(offsets[0](0, 0, 0)) * HD
     hidden = len(offsets[1](0, 0, 0)) * width
-    copies = 3 + 1 + 1 + 1 + 14 + (groups - 1) + (groups - 2) + (groups - 1) + (reach - 1) + 2 * (reach + 1) + (reach + 1)
+    copies = 3 + 14 + 2 * reach + 2 * (groups - 1) + 2 * groups + (groups - 1) + 6 * (reach + 1)
     anywhere = pl.BlockSpec(memory_space=pl.ANY)
     scratch = [
         pltpu.SemaphoreType.DMA((5,)),
@@ -701,6 +706,31 @@
             scale = inv * inv * inv * inner[:, part : part + 1]
             grad[here, cols] = (inv * turn[here, cols] - pre_ref[here, :] * scale).astype(BF)
 
+    lanes = lambda side: pl.ds(pl.multiple_of(side * HD, HD), HD)
+
+    def over_y(start, count):
+        return [
+            copies.remote(
+                by_x.at[q, pl.ds(start, count), lanes(1 - y)], by_y_in.at[q, pl.ds(start, count)], over
+            )
+            for q in range(groups)
+        ]
+
+    def over_p(start, count, arriving):
+        here = slice(start, start + count)
+        for q, copy in enumerate(arriving):
+            copy.wait_recv()
+            by_y[q, here, :] = by_x[q, here, lanes(y)] + by_y_in[q, here, :]
+        return [
+            copies.remote(by_y.at[q, pl.ds(start, count)], by_p_in.at[k, pl.ds(start, count)], (q, x, y, c))
+            for k, q in enumerate(others)
+        ]
+
+    for copy in exchanged:
+        copy.wait_recv()
+    for q in range(groups):
+        by_x[q, :early_rows, :] = maps[2 * q + x, :early_rows, :] + maps_in[q, :early_rows, :]
+    early_moves = over_y(0, early_rows)
     loads[0].wait()
 
     def backed(start):
@@ -729,46 +759,43 @@
         far_copies.append(
             copies.remote(far.at[pl.ds(rows, rows), sides[k]], core_in.at[:, sides[k]], core)
         )
+    backed(0)
+
+    loads[1].wait()
+    late = early_rows + 3 * rank
+    full_maps = SCALE_ADAPT * dot_tn(back[...], inputs[...])
+    for b in range(2 * groups):
+        maps[b, early_rows:late, :] = full_maps[:, b * 256 : (b + 1) * 256]
+    send_late = pl.ds(early_rows, 3 * rank)
+    exchanged = [
+        copies.remote(maps.at[2 * q + 1 - x, send_late], maps_in.at[q, send_late], across) for q in range(groups)
+    ]
     across_copies = []
     for k in range(2):
         far_copies[k].wait_recv()
         met[:, sides[k]] = (far[:rows, sides[k]].astype(F32) + core_in[:, sides[k]].astype(F32)).astype(BF)
         across_copies.append(copies.remote(met.at[:, sides[k]], across_in.at[:, sides[k]], across))
-    backed(0)
+    early_moves = over_p(0, early_rows, early_moves)
     for k in range(2):
         into(0, near, k)
     near_copy = copies.remote(near.at[pl.ds(rows, rows)], near_in, core)
-
-    loads[1].wait()
-    late = early_rows + 3 * rank
-    for b in range(2 * groups):
-        cols = slice(b * 256, (b + 1) * 256)
-        maps[b, early_rows:late, :] = SCALE_ADAPT * dot_tn(back[...], inputs[:, cols])
-    send_late = pl.ds(early_rows, 3 * rank)
-    exchanged += [
-        copies.remote(maps.at[2 * q + 1 - x, send_late], maps_in.at[q, send_late], across) for q in range(groups)
-    ]
     for q in range(groups):
         by_x[q, late:, :] = jnp.zeros_like(by_x[q, late:, :])
+    outs = SCALE_ADAPT * dot_tn(narrow_ref[...], grad[...])
     for k in range(3):
-        own = SCALE_ADAPT * dot_tn(narrow_ref[:, k * rank : (k + 1) * rank], grad[:, k * width : (k + 1) * width])
         here = slice(late + k * rank, late + (k + 1) * rank)
         for q in range(groups):
-            by_x[q, here, pl.ds(pl.multiple_of(c * HD, HD), HD)] = own[:, q * HD : (q + 1) * HD]
-    for copy in exchanged:
-        copy.wait_recv()
-    for q in range(groups):
-        by_x[q, :late, :] = maps[2 * q + x, :late, :] + maps_in[q]
-    halves = lambda ref, q, side: ref.at[q, :, pl.ds(pl.multiple_of(side * HD, HD), HD)]
-    exchanged = [copies.remote(halves(by_x, q, 1 - y), by_y_in.at[q], over) for q in range(groups)]
+            cols = slice(k * width + q * HD, k * width + (q + 1) * HD)
+            by_x[q, here, pl.ds(pl.multiple_of(c * HD, HD), HD)] = outs[k * rank : (k + 1) * rank, cols]
     for q, copy in enumerate(exchanged):
         copy.wait_recv()
-        by_y[q] = by_x[q, :, pl.ds(pl.multiple_of(y * HD, HD), HD)] + by_y_in[q]
-    exchanged = [copies.remote(by_y.at[q], by_p_in.at[k], (q, x, y, c)) for k, q in enumerate(others)]
+        by_x[q, early_rows:late, :] = maps[2 * q + x, early_rows:late, :] + maps_in[q, early_rows:late, :]
+    late_moves = over_p(early_rows, 6 * rank, over_y(early_rows, 6 * rank))
     summed = by_y[p]
     wide_sum = wide_ref[:, pl.ds(pl.multiple_of(p * 256, 256), 256)]
-    for k, copy in enumerate(exchanged):
-        copy.wait_recv()
+    for k in range(groups - 1):
+        early_moves[k].wait_recv()
+        late_moves[k].wait_recv()
         summed = summed + by_p_in[k]
     own_sum[...] = summed
     last = copies.remote(own_sum, own_sum_in, core)
@@ -811,7 +838,7 @@
     late = early_rows + 3 * rank
     vm = pl.BlockSpec(memory_space=pltpu.VMEM)
     anywhere = pl.BlockSpec(memory_space=pl.ANY)
-    count = 3 + groups + (groups - 1) + 5 + 2 * groups + (groups - 1) + 1
+    count = 3 + groups + (groups - 1) + 5 + groups + 2 * groups + 2 * (groups - 1) + 1
     block = lambda *shape: pltpu.VMEM(shape, BF)
     full = lambda *shape: pltpu.VMEM(shape, F32)
     first_rows = lambda v: vm if v.ndim != 2 or v.shape[0] <= own else pl.BlockSpec(
@@ -1009,24 +1036,27 @@
             arrived[b].wait_recv()
             if t < reach:
                 moves.append(copies.remote(do_in.at[t - 1, b], do_in.at[t, b], left))
-        inner_moves[-1].wait_recv()
-        if t < reach:
-            inner_moves.append(copies.remote(inner_in.at[t - 1], inner_in.at[t], left))
-
-        def from_later(n, carry, t=t):
-            s, cols = n // heads, pl.ds(pl.multiple_of(n % heads * HD, HD), HD)
-            k, v = piece(k_buf, s, cols), piece(v_buf, s, cols)
-            q, do = piece(later_buf.at[t - 1], s, cols), piece(do_in.at[t - 1], s, cols)
-            score = dot_nt(k, q) * scale
-            key = pos_ref[...]
-            lo, pos = lo_rows_ref[t, pl.ds(s, 1), :], query_rows_ref[t : t + 1, :]
-            probs = jnp.where((key >= lo) & (key <= pos), jnp.exp(score - log_rows_ref[t - 1, pl.ds(n, 1), :]), 0.0)
-            ds = (probs * (dot_nt(v, do) - inner_in[t - 1, pl.ds(n, 1), :])).astype(BF)
-            put(dv_ref, s, cols, piece(dv_ref, s, cols) + dot(probs.astype(BF), do))
-            put(dk_ref, s, cols, piece(dk_ref, s, cols) + dot(ds, q) * scale)
-            return carry
-
-        lax.fori_loop(0, 2 * heads, from_later, 0)
+            if b == 0:
+                inner_moves[-1].wait_recv()
+                if t < reach:
+                    inner_moves.append(copies.remote(inner_in.at[t - 1], inner_in.at[t], left))
+
+            def from_later(n, carry, t=t, b=b):
+                s, cols = n // heads, pl.ds(pl.multiple_of(n % heads * HD, HD), HD)
+                lanes = slice(b * rows, (b + 1) * rows)
+                k, v = piece(k_buf, s, cols), piece(v_buf, s, cols)
+                q, do = later_buf[t - 1, b, s, :, cols], do_in[t - 1, b, s, :, cols]
+                score = dot_nt(k, q) * scale
+                key = pos_ref[...]
+                lo, pos = lo_rows_ref[t, pl.ds(s, 1), lanes], query_rows_ref[t : t + 1, lanes]
+                log_row = log_rows_ref[t - 1, pl.ds(n, 1), lanes]
+                probs = jnp.where((key >= lo) & (key <= pos), jnp.exp(score - log_row), 0.0)
+                ds = (probs * (dot_nt(v, do) - inner_in[t - 1, pl.ds(n, 1), lanes])).astype(BF)
+                put(dv_ref, s, cols, piece(dv_ref, s, cols) + dot(probs.astype(BF), do))
+                put(dk_ref, s, cols, piece(dk_ref, s, cols) + dot(ds, q) * scale)
+                return carry
+
+            lax.fori_loop(0, 2 * heads, from_later, 0)
         if t == 1:
             for n in range(middle_any.shape[0] // part):
                 middles[n].wait()

time: 696 us -> 673 us (0.967)
  Pallas kernels: 537 us -> 514 us
    pallas_call x1, Pallas kernels: 68.4 us -> 56.4 us  [finish(): pl.pallas_call(functools.partial(finish_kernel, groups, heads, early_rows...]
    pallas_call x1, Pallas kernels: 135 us -> 127 us  [start(): pl.pallas_call(functools.partial(start_kernel, groups, reach, raw), in_sp...]
where the time goes in v7:
time: 673 us; the launch traced here: 664 us
  Pallas kernels  514 us (76%)
  waiting for transfers between devices  55.1 us (8%)
  local copies, waits for them, and re-layouts  35.5 us (5%)
  between operations  15.8 us (2%)
  other arithmetic  15.7 us (2%)
  matrix products  13.9 us (2%)
  starting transfers between devices  13.4 us (2%)
    pallas_call x1, Pallas kernels, feed_layer(): pl.pallas_call(feed_kernel, in_specs=[vm] * 7 + [anywhere] * 10, out_spec...  162 us
    pallas_call x1, Pallas kernels, start(): pl.pallas_call(functools.partial(start_kernel, groups, reach, raw), in_sp...  127 us
    pallas_call x1, Pallas kernels, attend_back(): pl.pallas_call(functools.partial(attend_back_kernel, groups, reach, heads...  59.6 us
    pallas_call x1, Pallas kernels, finish(): pl.pallas_call(functools.partial(finish_kernel, groups, heads, early_rows...  56.4 us
    ppermute x3, waiting for transfers between devices, swap_x(): return lax.ppermute(value, 'x', SWAP)  40.8 us
    pallas_call x1, Pallas kernels, project(): pl.pallas_call(functools.partial(project_kernel, heads, own_tiles), grid=...  33.1 us
    pallas_call x1, Pallas kernels, gate_up(): pl.pallas_call(gate_up_kernel, grid=(steps,), in_specs=[pl.BlockSpec((row...  27.3 us
    pallas_call x1, Pallas kernels, forward(): pl.pallas_call(functools.partial(attend_kernel, count, HD ** (-0.5)), gri...  23.5 us
  transfers between devices with their start and end apart: 16, of which 7 were waited for; matrix products, arithmetic and copies ran while one was open for 7% of the time, Pallas kernels for 16%

profile of v7, /device:TPU:0, one launch (start us, length us, event | category | flops | bytes accessed | tf_op | source)
XLA Modules:
  0.0 663.9 jit_solution(18186390293436407947)
XLA Ops:
  7.2 126.8 %start.1 = (bf16[4,2,2,128,1536]{4,3,2,1,0:T(8,128)(2,1)}, bf16[512,2048]{1,0:T(8,128)(2,1)}, bf16[3072,2048]{1,0:T(8,128)(2,1)}, bf16[4,64,2048]{2,1,0:T(8,128)(2,1)}) custom-call(bf16[64,2048]{1,0:T(8,128)(2,1)} %refs_0_.1, bf16[64,2048]{1,0:T(8,128)(2,1)} %refs_1_.1, bf16[64,2048]{1,0:T(8,128)(2,1)} %refs_2_.1, bf16[64,8192]{1,0:T(8,128)(2,1)} %refs_3_.1, ...), custom_call_target="tpu_custom_call" | custom-call | flops 131999997952 | bytes 120000000 | tf_op jit(solution)/shard_map/start/pallas_call | solution.py:355
  134.2 4.4 collective-permute-start
  138.5 1.3 collective-permute-start.1
  139.8 1.7 collective-permute-start.2
  142.2 1.0 constant_dynamic-slice_fusion
  143.6 0.6 reshape.810.out_maps_ref.refs_11_
  144.7 1.0 copy.50
  145.8 0.9 copy.51.refs_7_.refs_5_
  146.8 0.7 constant_dynamic-slice_fusion.1
  147.5 33.1 %project.1 = (f32[1024,512]{1,0:T(8,128)}, f32[3072,512]{1,0:T(8,128)}, bf16[3072,512]{1,0:T(8,128)(2,1)}, bf16[3072,48]{1,0:T(8,128)(2,1)}, f32[8,1024]{1,0:T(8,128)}, /*index=5*/f32[8,3072]{1,0:T(8,128)}) custom-call(bf16[3072,2048]{1,0:T(8,128)(2,1)} %get-tuple-element.48.x_ref.refs_17_, bf16[2048,1536]{1,0:T(8,128)(2,1)} %bitcast.108, ...), custom_call_target="tpu_custom_call" | custom-call | flops 1100000000 | bytes 1000000 | tf_op jit(solution)/shard_map/project/pallas_call | solution.py:440
  180.6 8.8 %scales.1 = (f32[1024,1]{1,0:T(8,128)}, f32[3072,1]{1,0:T(8,128)}) custom-call(f32[8,1024]{1,0:T(8,128)} %get-tuple-element.52.q_ref, f32[8,3072]{1,0:T(8,128)} %get-tuple-element.53.k_ref), custom_call_target="tpu_custom_call" | custom-call | flops 1100000000 | bytes 1000000 | tf_op jit(solution)/shard_map/scales/pallas_call | solution.py:496
  189.5 0.7 fusion.4
  192.0 0.8 pad_maximum_fusion.3.row_ref.refs_8_
  192.9 11.6 %rope_forward.1 = (bf16[1024,512]{1,0:T(8,128)(2,1)}, bf16[3072,512]{1,0:T(8,128)(2,1)}) custom-call(f32[1024,512]{1,0:T(8,128)} %get-tuple-element.50.q_ref.refs_3_, f32[3072,512]{1,0:T(8,128)} %get-tuple-element.51.k_ref.refs_4_, f32[1024,1]{1,0:T(8,128)} %get-tuple-element.54.inv_q_ref.refs_5_, f32[3072,1]{1,0:T(8,128)} %get-tuple-element.55.inv_k_ref.refs_6_, ...), custom_call_target="tpu_custom_call" | custom-call | flops 1100000000 | bytes 1000000 | tf_op jit(solution)/shard_map/rope_forward/pallas_call | solution.py:542
  205.1 2.0 broadcast_maximum_fusion.refs_6_.refs_4_
  207.1 23.5 %attend_forward.1 = (bf16[2,2,256,512]{3,2,1,0:T(8,128)(2,1)}, f32[8,512,1]{2,1,0:T(8,128)}) custom-call(bf16[2,2,256,512]{3,2,1,0:T(8,128)(2,1)} %bitcast.117, bf16[6,2,256,512]{3,2,1,0:T(8,128)(2,1)} %bitcast.99, bf16[6,2,256,512]{3,2,1,0:T(8,128)(2,1)} %bitcast.100, bf16[6,2,256,512]{3,2,1,0:T(8,128)(2,1)} %bitcast.101, ...), custom_call_target="tpu_custom_call" | custom-call | flops 1100000000 | bytes 1000000 | tf_op jit(solution)/shard_map/attend_forward/pallas_call | solution.py:1133
  230.6 1.5 dynamic-slice_bitcast_fusion
  232.1 1.6 convolution_convert_fusion.1
  233.7 2.1 fusion.6
  235.9 1.5 broadcast_select_fusion.3
  237.6 1.3 fusion.7
  238.9 0.7 add_convert_fusion.1
  239.6 1.3 slice.76
  241.4 0.7 collective-permute-start.3
  242.2 2.5 collective-permute-done.3
  244.7 1.9 add_convert_fusion.2
  247.3 2.3 fusion.8
  249.6 0.7 add_convert_fusion.refs_0_
  250.6 1.5 constant_dynamic-slice_fusion.7
  252.1 1.1 collective-permute-done.4.refs_1_
  253.2 19.0 %collective-permute-done.5.refs_2_ = bf16[256,2048]{1,0:T(8,128)(2,1)S(1)} collective-permute-done((bf16[256,2048]{1,0:T(8,128)(2,1)S(1)}, bf16[256,2048]{1,0:T(8,128)(2,1)S(1)}, u32[]{:S(2)}, u32[]{:S(2)}) %collective-permute-start.5) | collective-permute-done | bytes 1048608 | tf_op jit(solution)/shard_map/ppermute | solution.py:51
  272.2 1.0 copy-done.22
  273.2 5.2 after_attention.1
  279.5 1.7 collective-permute-start.9
  281.8 1.0 constant_dynamic-slice_fusion.8
  282.7 20.6 %collective-permute-done.7 = bf16[256,2048]{1,0:T(8,128)(2,1)S(1)} collective-permute-done((bf16[256,2048]{1,0:T(8,128)(2,1)}, bf16[256,2048]{1,0:T(8,128)(2,1)S(1)}, u32[]{:S(2)}, u32[]{:S(2)}) %collective-permute-start.7) | collective-permute-done | bytes 1048608 | tf_op jit(solution)/shard_map/ppermute | solution.py:51
  304.4 1.2 reshape.804
  305.6 1.3 dynamic-slice_reduce_fusion
  307.0 0.6 reshape.805.maps_ref.refs_2_
  308.0 0.6 copy.58
  308.6 2.8 reduce.2.refs_16_
  311.5 1.5 collective-permute-start.11
  313.7 1.3 constant_dynamic-update-slice_fusion.8
  315.1 1.3 constant_dynamic-update-slice_fusion.7
  316.4 9.4 %collective-permute-done.11 = bf16[128,2048]{1,0:T(8,128)(2,1)S(1)} collective-permute-done((bf16[128,2048]{1,0:T(8,128)(2,1)S(1)}, bf16[128,2048]{1,0:T(8,128)(2,1)S(1)}, u32[]{:S(2)}, u32[]{:S(2)}) %collective-permute-start.11) | collective-permute-done | bytes 524320 | tf_op jit(solution)/shard_map/ppermute | solution.py:57
  325.9 1.3 collective-permute-done.12
  327.4 1.3 constant_dynamic-update-slice_fusion.5
  328.9 1.1 collective-permute-done.13
  330.1 3.2 copy-done.4
  333.3 3.2 convolution_convert_fusion.narrow_ref
  336.5 27.3 %gate_up.1 = (bf16[2048,1024]{1,0:T(8,128)(2,1)}, bf16[2048,1024]{1,0:T(8,128)(2,1)}, bf16[2048,1024]{1,0:T(8,128)(2,1)}) custom-call(bf16[2048,2048]{1,0:T(8,128)(2,1)} %copy-done.4, bf16[4,512,2048]{2,1,0:T(8,128)(2,1)} %bitcast.92, bf16[4,512,2048]{2,1,0:T(8,128)(2,1)} %bitcast.93, bf16[2048,32]{1,0:T(8,128)(2,1)} %convolution_convert_fusion.narrow_ref, ...), custom_call_target="tpu_custom_call" | custom-call | flops 1100000000 | bytes 1000000 | tf_op jit(solution)/shard_map/gate_up/pallas_call | solution.py:392
  363.8 162.3 %feed_layer.1 = (bf16[256,2048]{1,0:T(8,128)(2,1)}, f32[256,2048]{1,0:T(8,128)}, bf16[4,256,2048]{2,1,0:T(8,128)(2,1)}, bf16[8,256,32]{2,1,0:T(8,128)(2,1)}, f32...) custom-call(bf16[16,1024]{1,0:T(8,128)(2,1)} %bitcast.135, ...), custom_call_target="tpu_custom_call" | custom-call | flops 186999996416 | bytes 170000000 | tf_op jit(solution)/shard_map/feed_layer/pallas_call | solution.py:1599
  526.1 2.8 convolution_multiply_fusion
  529.0 59.6 %attend_backward.1 = (f32[2,2,256,512]{3,2,1,0:T(8,128)}, f32[2,2,256,512]{3,2,1,0:T(8,128)}, f32[2,2,256,512]{3,2,1,0:T(8,128)}, bf16[1024,16]{1,0:T(8,128)(2,1)}, f32[32,2048]{1,0:T(8,128)}) custom-call(bf16[1024,2048]{1,0:T(8,128)(2,1)} %bitcast.111, bf16[512,2048]{1,0:T(8,128)(2,1)} %bitcast.104, bf16[16,512]{1,0:T(8,128)(2,1)} %bitcast.136, ...), custom_call_target="tpu_custom_call" | custom-call | flops 76999999488 | bytes 70000000 | tf_op jit(solution)/shard_map/attend_backward/pallas_call | solution.py:1079
  588.6 1.2 convolution_multiply_fusion.1
  590.0 1.8 pad_maximum_fusion.2.refs_13_
  591.9 0.7 broadcast_in_dim.82.refs_15_
  592.6 56.4 %finish.1 = (f32[256,2048]{1,0:T(8,128)}, f32[8,6,16,64]{3,2,1,0:T(8,128)}, f32[8,16,256]{2,1,0:T(8,128)}, f32[8,5,16,64]{3,2,1,0:T(8,128)}, f32[8,2,16,256]{3,2,1,0:T(8,128)}) custom-call(f32[1024,512]{1,0:T(8,128)} %bitcast.150, f32[1024,512]{1,0:T(8,128)} %bitcast.151, f32[1024,512]{1,0:T(8,128)} %bitcast.152, ...), custom_call_target="tpu_custom_call" | custom-call | flops 65999998976 | bytes 60000000 | tf_op jit(solution)/shard_map/finish/pallas_call | solution.py:847
  649.0 1.0 copy.78
  650.0 3.8 copy.79
  653.8 0.7 copy.80
  654.5 0.7 copy.81
  655.2 0.7 copy.82
  655.9 0.7 copy.83
  (118 shorter events, 10.1 us)
Async XLA Ops:
  7.2 139.5 %copy-start = (bf16[8,6,16,2048]{3,2,1,0:T(8,128)(2,1)S(1)}, bf16[8,6,16,2048]{3,2,1,0:T(8,128)(2,1)}, u32[]{:S(2)}) copy-start(bf16[8,6,16,2048]{3,2,1,0:T(8,128)(2,1)} %param.34) | copy-start | bytes 9437188
  7.2 329.4 %all-gather.6.cloned.1.call-start = ((), (), s32[]{:S(2)}) async-start(), calls=%async_computation.1 | async-start | bytes 10485760 | tf_op jit(solution)/shard_map/all_gather | solution.py:1727
  7.2 137.1 %copy-start.21 = (s32[4,8]{1,0:T(4,128)S(1)}, s32[4,8]{1,0:T(4,128)}, u32[]{:S(2)}) copy-start(s32[4,8]{1,0:T(4,128)} %param.21) | copy-start | bytes 388
  134.1 229.7 %all-gather.4.cloned.1.call-start = ((), (), s32[]{:S(2)}) async-start(), calls=%async_computation | async-start | bytes 5242880 | tf_op jit(solution)/shard_map/all_gather | solution.py:1794
  134.2 101.7 %collective-permute-start = (bf16[256,2048]{1,0:T(8,128)(2,1)}, bf16[256,2048]{1,0:T(8,128)(2,1)}, u32[]{:S(2)}, u32[]{:S(2)}) collective-permute-start(bf16[256,2048]{1,0:T(8,128)(2,1)} %bitcast.120), channel_id=1, source_target_pairs={{0,2},{3,1},{4,6},{7,5},{8,10},{11,9},{12,14},{15,13},{16,18},{19,... | collective-permute-start | bytes 3145736 | tf_op jit(solution)/shard_map/ppermute | solution.py:1729
  138.5 97.3 %collective-permute-start.1 = (bf16[256,2048]{1,0:T(8,128)(2,1)}, bf16[256,2048]{1,0:T(8,128)(2,1)}, u32[]{:S(2)}, u32[]{:S(2)}) collective-permute-start(bf16[256,2048]{1,0:T(8,128)(2,1)} %bitcast.121), channel_id=1, source_target_pairs={{1,0},{2,3},{5,4},{6,7},{9,8},{10,11},{13,12},{14,15},{17,16},{18,... | collective-permute-start | bytes 3145736 | tf_op jit(solution)/shard_map/ppermute | solution.py:1729
  139.8 96.1 %collective-permute-start.2 = (bf16[256,2048]{1,0:T(8,128)(2,1)}, bf16[256,2048]{1,0:T(8,128)(2,1)}, u32[]{:S(2)}, u32[]{:S(2)}) collective-permute-start(bf16[256,2048]{1,0:T(8,128)(2,1)} %bitcast.122), channel_id=1, source_target_pairs={{1,2},{2,1},{5,6},{6,5},{9,10},{10,9},{13,14},{14,13},{17,18},{18,... | collective-permute-start | bytes 3145736 | tf_op jit(solution)/shard_map/ppermute | solution.py:1729
  207.1 28.8 %copy-start.9 = (bf16[4,64,2048]{2,1,0:T(8,128)(2,1)S(1)}, bf16[4,64,2048]{2,1,0:T(8,128)(2,1)}, u32[]{:S(2)}) copy-start(bf16[4,64,2048]{2,1,0:T(8,128)(2,1)} %get-tuple-element.60) | copy-start | bytes 3145732
  232.1 17.5 %copy-start.10 = (bf16[16,2048]{1,0:T(8,128)(2,1)}, bf16[16,2048]{1,0:T(8,128)(2,1)S(1)}, u32[]{:S(2)}) copy-start(bf16[16,2048]{1,0:T(8,128)(2,1)S(1)} %get-tuple-element.97.refs_3_) | copy-start | bytes 196612
  233.7 15.9 %copy-start.13 = (bf16[1024,16]{0,1:T(8,128)(2,1)}, bf16[1024,16]{0,1:T(8,128)(2,1)S(1)}, u32[]{:S(2)}) copy-start(bf16[1024,16]{0,1:T(8,128)(2,1)S(1)} %convolution_convert_fusion.1) | copy-start | bytes 98308
  237.6 2.0 copy-start.2
  239.6 1.8 copy-start.6
  241.4 3.4 collective-permute-start.3
  242.1 5.2 copy-start.3
  242.2 87.9 %copy-start.17 = (bf16[1,2,16,2048]{3,2,1,0:T(8,128)(2,1)}, bf16[1,2,16,2048]{3,2,1,0:T(8,128)(2,1)S(1)}, u32[]{:S(2)}) copy-start(bf16[1,2,16,2048]{3,2,1,0:T(8,128)(2,1)S(1)} %constant_dynamic-slice_fusion.2) | copy-start | bytes 393220
  246.7 25.5 %collective-permute-start.5 = (bf16[256,2048]{1,0:T(8,128)(2,1)S(1)}, bf16[256,2048]{1,0:T(8,128)(2,1)S(1)}, u32[]{:S(2)}, u32[]{:S(2)}) collective-permute-start(bf16[256,2048]{1,0:T(8,128)(2,1)S(1)} %add_convert_fusion.2), channel_id=1, source_target_pairs={{0,4},{4,0},{1,5},{5,1},{2,6},{6,2},{3,7},{7,3},{8,12},{12,8},{9,1... | collective-permute-start | bytes 3145736 | tf_op jit(solution)/shard_map/ppermute | solution.py:51
  250.4 21.8 %copy-start.7 = (bf16[512,2048]{1,0:T(8,128)(2,1)}, bf16[512,2048]{1,0:T(8,128)(2,1)S(1)}, u32[]{:S(2)}) copy-start(bf16[512,2048]{1,0:T(8,128)(2,1)S(1)} %add_convert_fusion.refs_0_) | copy-start | bytes 6291460
  250.5 2.7 collective-permute-start.4
  253.2 19.0 %copy-start.23 = (bf16[256,2048]{1,0:T(8,128)(2,1)}, bf16[256,2048]{1,0:T(8,128)(2,1)S(1)}, u32[]{:S(2)}) copy-start(bf16[256,2048]{1,0:T(8,128)(2,1)S(1)} %collective-permute-done.4.refs_1_) | copy-start | bytes 3145732
  272.2 1.0 copy-start.22
  278.4 24.9 %collective-permute-start.7 = (bf16[256,2048]{1,0:T(8,128)(2,1)}, bf16[256,2048]{1,0:T(8,128)(2,1)S(1)}, u32[]{:S(2)}, u32[]{:S(2)}) collective-permute-start(bf16[256,2048]{1,0:T(8,128)(2,1)} %get-tuple-element.62), channel_id=1, source_target_pairs={{0,4},{4,0},{1,5},{5,1},{2,6},{6,2},{3,7},{7,3},{8,12},{12,8},{9,1... | collective-permute-start | bytes 3145736 | tf_op jit(solution)/shard_map/ppermute | solution.py:51
  279.5 33.5 %collective-permute-start.9 = (bf16[256,2048]{1,0:T(8,128)(2,1)}, bf16[256,2048]{1,0:T(8,128)(2,1)S(1)}, u32[]{:S(2)}, u32[]{:S(2)}) collective-permute-start(bf16[256,2048]{1,0:T(8,128)(2,1)} %get-tuple-element.62), channel_id=1, source_target_pairs={{0,2},{2,0},{1,3},{3,1},{4,6},{6,4},{5,7},{7,5},{8,10},{10,8},{9,1... | collective-permute-start | bytes 3145736 | tf_op jit(solution)/shard_map/ppermute | solution.py:57
  281.8 33.3 %collective-permute-start.6 = (bf16[256,2048]{1,0:T(8,128)(2,1)}, bf16[256,2048]{1,0:T(8,128)(2,1)}, u32[]{:S(2)}, u32[]{:S(2)}) collective-permute-start(bf16[256,2048]{1,0:T(8,128)(2,1)} %get-tuple-element.62), channel_id=1, source_target_pairs={{0,1},{1,0},{2,3},{3,2},{4,5},{5,4},{6,7},{7,6},{8,9},{9,8},{10,11... | collective-permute-start | bytes 3145736 | tf_op jit(solution)/shard_map/ppermute | solution.py:48
  303.3 24.1 %collective-permute-start.8 = (bf16[256,2048]{1,0:T(8,128)(2,1)S(1)}, bf16[256,2048]{1,0:T(8,128)(2,1)}, u32[]{:S(2)}, u32[]{:S(2)}) collective-permute-start(bf16[256,2048]{1,0:T(8,128)(2,1)S(1)} %collective-permute-done.7), channel_id=1, source_target_pairs={{0,1},{1,0},{2,3},{3,2},{4,5},{5,4},{6,7},{7,6},{8,9},{9,8},{10,11... | collective-permute-start | bytes 3145736 | tf_op jit(solution)/shard_map/ppermute | solution.py:48
  311.5 14.4 %collective-permute-start.11 = (bf16[128,2048]{1,0:T(8,128)(2,1)S(1)}, bf16[128,2048]{1,0:T(8,128)(2,1)S(1)}, u32[]{:S(2)}, u32[]{:S(2)}) collective-permute-start(bf16[128,2048]{1,0:T(8,128)(2,1)S(1)} %slice.79), channel_id=1, source_target_pairs={{0,2},{2,0},{1,3},{3,1},{4,6},{6,4},{5,7},{7,5},{8,10},{10,8},{9,1... | collective-permute-start | bytes 1572872 | tf_op jit(solution)/shard_map/ppermute | solution.py:57
  313.1 14.1 %collective-permute-start.12 = (bf16[128,2048]{1,0:T(8,128)(2,1)S(1)}, bf16[128,2048]{1,0:T(8,128)(2,1)S(1)}, u32[]{:S(2)}, u32[]{:S(2)}) collective-permute-start(bf16[128,2048]{1,0:T(8,128)(2,1)S(1)} %slice.80), channel_id=1, source_target_pairs={{0,4},{4,0},{1,5},{5,1},{2,6},{6,2},{3,7},{7,3},{8,12},{12,8},{9,1... | collective-permute-start | bytes 1572872 | tf_op jit(solution)/shard_map/ppermute | solution.py:51
  315.0 13.8 %collective-permute-start.10 = (bf16[256,2048]{1,0:T(8,128)(2,1)S(1)}, bf16[256,2048]{1,0:T(8,128)(2,1)S(1)}, u32[]{:S(2)}, u32[]{:S(2)}) collective-permute-start(bf16[256,2048]{1,0:T(8,128)(2,1)S(1)} %collective-permute-done.9), channel_id=1, source_target_pairs={{0,1},{1,0},{2,3},{3,2},{4,5},{5,4},{6,7},{7,6},{8,9},{9,8},{10,11... | collective-permute-start | bytes 3145736 | tf_op jit(solution)/shard_map/ppermute | solution.py:48
  327.3 2.7 collective-permute-start.13
  330.1 3.3 copy-start.4
  363.8 162.3 %copy-start.14 = (bf16[1024,16]{0,1:T(8,128)(2,1)S(1)}, bf16[1024,16]{0,1:T(8,128)(2,1)}, u32[]{:S(2)}) copy-start(bf16[1024,16]{0,1:T(8,128)(2,1)} %copy-done.13) | copy-start | bytes 98308
  529.0 59.6 %copy-start.5 = (bf16[2,2,256,512]{3,2,1,0:T(8,128)(2,1)S(1)}, bf16[2,2,256,512]{3,2,1,0:T(8,128)(2,1)}, u32[]{:S(2)}) copy-start(bf16[2,2,256,512]{3,2,1,0:T(8,128)(2,1)} %get-tuple-element.59.refs_15_) | copy-start | bytes 3145732
  529.0 61.0 %copy-start.19 = (f32[4]{0:T(128)S(1)}, f32[4]{0:T(128)}, u32[]{:S(2)}) copy-start(f32[4]{0:T(128)} %compare_convert_fusion.1) | copy-start | bytes 52
  529.0 61.1 %copy-start.16 = (f32[16,2048]{1,0:T(8,128)S(1)}, f32[16,2048]{1,0:T(8,128)}, u32[]{:S(2)}) copy-start(f32[16,2048]{1,0:T(8,128)} %get-tuple-element.82) | copy-start | bytes 393220
  529.0 62.9 %copy-start.20 = (f32[8]{0:T(128)S(1)}, f32[8]{0:T(128)}, u32[]{:S(2)}) copy-start(f32[8]{0:T(128)} %compare_convert_fusion) | copy-start | bytes 100
  592.6 56.4 %copy-start.8 = (bf16[256,2048]{1,0:T(8,128)(2,1)S(1)}, bf16[256,2048]{1,0:T(8,128)(2,1)}, u32[]{:S(2)}) copy-start(bf16[256,2048]{1,0:T(8,128)(2,1)} %get-tuple-element.71) | copy-start | bytes 3145732
  648.9 4.8 copy-start.11
  648.9 5.6 copy-start.18
  649.0 6.2 copy-start.12
  649.0 6.9 %copy-start.15 = (f32[8,2,16,256]{3,2,1,0:T(8,128)S(1)}, f32[8,2,16,256]{3,2,1,0:T(8,128)}, u32[]{:S(2)}) copy-start(f32[8,2,16,256]{3,2,1,0:T(8,128)} %get-tuple-element.135) | copy-start | bytes 786436
  649.0 7.6 %copy-start.1 = (bf16[8,6,16,2048]{3,2,1,0:T(8,128)(2,1)S(1)}, bf16[8,6,16,2048]{3,2,1,0:T(8,128)(2,1)}, u32[]{:S(2)}) copy-start(bf16[8,6,16,2048]{3,2,1,0:T(8,128)(2,1)} %param.34) | copy-start | bytes 9437188
Sparse Core Ops, SparseCore 0:
  134.2 146.8 all-gather.5
  282.7 78.9 all-gather.3

commit v8 on v7

--- a/solution.py
+++ b/solution.py
@@ -1028,18 +1028,27 @@
         put(dq_ref, s, cols, dq * scale)
         return carry
 
-    lax.fori_loop(0, 2 * heads, own, 0)
+    def pass_on(t, b):
+        moves[t - 1][b].wait_recv()
+        if b == 0:
+            moves.append([])
+        if t < reach:
+            moves[t].append(copies.remote(do_in.at[t - 1, b], do_in.at[t, b], left))
+        if b == 0:
+            inner_moves[-1].wait_recv()
+            if t < reach:
+                inner_moves.append(copies.remote(inner_in.at[t - 1], inner_in.at[t], left))
+
+    moves = [moves]
+    lax.fori_loop(0, heads, own, 0)
+    pass_on(1, 0)
+    lax.fori_loop(heads, 2 * heads, own, 0)
+    pass_on(1, 1)
 
     for t in range(1, reach + 1):
-        arrived, moves = moves, []
         for b in range(2):
-            arrived[b].wait_recv()
-            if t < reach:
-                moves.append(copies.remote(do_in.at[t - 1, b], do_in.at[t, b], left))
-            if b == 0:
-                inner_moves[-1].wait_recv()
-                if t < reach:
-                    inner_moves.append(copies.remote(inner_in.at[t - 1], inner_in.at[t], left))
+            if t > 1:
+                pass_on(t, b)
 
             def from_later(n, carry, t=t, b=b):
                 s, cols = n // heads, pl.ds(pl.multiple_of(n % heads * HD, HD), HD)

time: 673 us -> 674 us (level)
  no operation moved by 1% of the time
where the time goes in v8:
time: 674 us; the launch traced here: 665 us
  Pallas kernels  515 us (76%)
  waiting for transfers between devices  55.1 us (8%)
  local copies, waits for them, and re-layouts  35.5 us (5%)
  between operations  15.8 us (2%)
  other arithmetic  15.7 us (2%)
  matrix products  13.9 us (2%)
  starting transfers between devices  13.4 us (2%)
    pallas_call x1, Pallas kernels, feed_layer(): pl.pallas_call(feed_kernel, in_specs=[vm] * 7 + [anywhere] * 10, out_spec...  162 us
    pallas_call x1, Pallas kernels, start(): pl.pallas_call(functools.partial(start_kernel, groups, reach, raw), in_sp...  127 us
    pallas_call x1, Pallas kernels, attend_back(): pl.pallas_call(functools.partial(attend_back_kernel, groups, reach, heads...  61.1 us
    pallas_call x1, Pallas kernels, finish(): pl.pallas_call(functools.partial(finish_kernel, groups, heads, early_rows...  55.7 us
    ppermute x3, waiting for transfers between devices, swap_x(): return lax.ppermute(value, 'x', SWAP)  40.8 us
    pallas_call x1, Pallas kernels, project(): pl.pallas_call(functools.partial(project_kernel, heads, own_tiles), grid=...  33.1 us
    pallas_call x1, Pallas kernels, gate_up(): pl.pallas_call(gate_up_kernel, grid=(steps,), in_specs=[pl.BlockSpec((row...  27.3 us
    pallas_call x1, Pallas kernels, forward(): pl.pallas_call(functools.partial(attend_kernel, count, HD ** (-0.5)), gri...  23.5 us
  transfers between devices with their start and end apart: 16, of which 7 were waited for; matrix products, arithmetic and copies ran while one was open for 7% of the time, Pallas kernels for 16%

profile of v8, /device:TPU:0, one launch (start us, length us, event | category | flops | bytes accessed | tf_op | source)
XLA Modules:
  0.0 664.7 jit_solution(3481603421541523785)
XLA Ops:
  7.2 126.8 %start.1 = (bf16[4,2,2,128,1536]{4,3,2,1,0:T(8,128)(2,1)}, bf16[512,2048]{1,0:T(8,128)(2,1)}, bf16[3072,2048]{1,0:T(8,128)(2,1)}, bf16[4,64,2048]{2,1,0:T(8,128)(2,1)}) custom-call(bf16[64,2048]{1,0:T(8,128)(2,1)} %refs_0_.1, bf16[64,2048]{1,0:T(8,128)(2,1)} %refs_1_.1, bf16[64,2048]{1,0:T(8,128)(2,1)} %refs_2_.1, bf16[64,8192]{1,0:T(8,128)(2,1)} %refs_3_.1, ...), custom_call_target="tpu_custom_call" | custom-call | flops 131999997952 | bytes 120000000 | tf_op jit(solution)/shard_map/start/pallas_call | solution.py:355
  134.2 4.4 collective-permute-start
  138.5 1.3 collective-permute-start.1
  139.8 1.7 collective-permute-start.2
  142.2 1.0 constant_dynamic-slice_fusion
  143.6 0.6 reshape.810.out_maps_ref.refs_11_
  144.7 1.0 copy.50
  145.8 0.9 copy.51.refs_7_.refs_5_
  146.8 0.7 constant_dynamic-slice_fusion.1
  147.5 33.1 %project.1 = (f32[1024,512]{1,0:T(8,128)}, f32[3072,512]{1,0:T(8,128)}, bf16[3072,512]{1,0:T(8,128)(2,1)}, bf16[3072,48]{1,0:T(8,128)(2,1)}, f32[8,1024]{1,0:T(8,128)}, /*index=5*/f32[8,3072]{1,0:T(8,128)}) custom-call(bf16[3072,2048]{1,0:T(8,128)(2,1)} %get-tuple-element.48.x_ref.refs_17_, bf16[2048,1536]{1,0:T(8,128)(2,1)} %bitcast.108, ...), custom_call_target="tpu_custom_call" | custom-call | flops 1100000000 | bytes 1000000 | tf_op jit(solution)/shard_map/project/pallas_call | solution.py:440
  180.6 8.8 %scales.1 = (f32[1024,1]{1,0:T(8,128)}, f32[3072,1]{1,0:T(8,128)}) custom-call(f32[8,1024]{1,0:T(8,128)} %get-tuple-element.52.q_ref, f32[8,3072]{1,0:T(8,128)} %get-tuple-element.53.k_ref), custom_call_target="tpu_custom_call" | custom-call | flops 1100000000 | bytes 1000000 | tf_op jit(solution)/shard_map/scales/pallas_call | solution.py:496
  189.5 0.7 fusion.4
  192.0 0.8 pad_maximum_fusion.3.row_ref.refs_8_
  192.9 11.6 %rope_forward.1 = (bf16[1024,512]{1,0:T(8,128)(2,1)}, bf16[3072,512]{1,0:T(8,128)(2,1)}) custom-call(f32[1024,512]{1,0:T(8,128)} %get-tuple-element.50.q_ref.refs_3_, f32[3072,512]{1,0:T(8,128)} %get-tuple-element.51.k_ref.refs_4_, f32[1024,1]{1,0:T(8,128)} %get-tuple-element.54.inv_q_ref.refs_5_, f32[3072,1]{1,0:T(8,128)} %get-tuple-element.55.inv_k_ref.refs_6_, ...), custom_call_target="tpu_custom_call" | custom-call | flops 1100000000 | bytes 1000000 | tf_op jit(solution)/shard_map/rope_forward/pallas_call | solution.py:542
  205.1 2.0 broadcast_maximum_fusion.refs_6_.refs_4_
  207.1 23.5 %attend_forward.1 = (bf16[2,2,256,512]{3,2,1,0:T(8,128)(2,1)}, f32[8,512,1]{2,1,0:T(8,128)}) custom-call(bf16[2,2,256,512]{3,2,1,0:T(8,128)(2,1)} %bitcast.117, bf16[6,2,256,512]{3,2,1,0:T(8,128)(2,1)} %bitcast.99, bf16[6,2,256,512]{3,2,1,0:T(8,128)(2,1)} %bitcast.100, bf16[6,2,256,512]{3,2,1,0:T(8,128)(2,1)} %bitcast.101, ...), custom_call_target="tpu_custom_call" | custom-call | flops 1100000000 | bytes 1000000 | tf_op jit(solution)/shard_map/attend_forward/pallas_call | solution.py:1142
  230.6 1.5 dynamic-slice_bitcast_fusion
  232.1 1.6 convolution_convert_fusion.1
  233.7 2.1 fusion.6
  235.9 1.5 broadcast_select_fusion.3
  237.6 1.3 fusion.7
  238.9 0.7 add_convert_fusion.1
  239.6 1.3 slice.76
  241.4 0.7 collective-permute-start.3
  242.2 2.5 collective-permute-done.3
  244.7 1.9 add_convert_fusion.2
  247.3 2.3 fusion.8
  249.6 0.7 add_convert_fusion.refs_0_
  250.6 1.5 constant_dynamic-slice_fusion.7
  252.1 1.1 collective-permute-done.4.refs_1_
  253.2 19.0 %collective-permute-done.5.refs_2_ = bf16[256,2048]{1,0:T(8,128)(2,1)S(1)} collective-permute-done((bf16[256,2048]{1,0:T(8,128)(2,1)S(1)}, bf16[256,2048]{1,0:T(8,128)(2,1)S(1)}, u32[]{:S(2)}, u32[]{:S(2)}) %collective-permute-start.5) | collective-permute-done | bytes 1048608 | tf_op jit(solution)/shard_map/ppermute | solution.py:51
  272.2 1.0 copy-done.22
  273.2 5.2 after_attention.1
  279.5 1.7 collective-permute-start.9
  281.8 1.0 constant_dynamic-slice_fusion.8
  282.7 20.6 %collective-permute-done.7 = bf16[256,2048]{1,0:T(8,128)(2,1)S(1)} collective-permute-done((bf16[256,2048]{1,0:T(8,128)(2,1)}, bf16[256,2048]{1,0:T(8,128)(2,1)S(1)}, u32[]{:S(2)}, u32[]{:S(2)}) %collective-permute-start.7) | collective-permute-done | bytes 1048608 | tf_op jit(solution)/shard_map/ppermute | solution.py:51
  304.4 1.2 reshape.804
  305.6 1.3 dynamic-slice_reduce_fusion
  307.0 0.6 reshape.805.maps_ref.refs_2_
  308.0 0.6 copy.58
  308.6 2.8 reduce.2.refs_16_
  311.5 1.5 collective-permute-start.11
  313.7 1.3 constant_dynamic-update-slice_fusion.8
  315.1 1.3 constant_dynamic-update-slice_fusion.7
  316.4 9.4 %collective-permute-done.11 = bf16[128,2048]{1,0:T(8,128)(2,1)S(1)} collective-permute-done((bf16[128,2048]{1,0:T(8,128)(2,1)S(1)}, bf16[128,2048]{1,0:T(8,128)(2,1)S(1)}, u32[]{:S(2)}, u32[]{:S(2)}) %collective-permute-start.11) | collective-permute-done | bytes 524320 | tf_op jit(solution)/shard_map/ppermute | solution.py:57
  325.9 1.3 collective-permute-done.12
  327.4 1.3 constant_dynamic-update-slice_fusion.5
  328.9 1.1 collective-permute-done.13
  330.1 3.2 copy-done.4
  333.3 3.2 convolution_convert_fusion.narrow_ref
  336.5 27.3 %gate_up.1 = (bf16[2048,1024]{1,0:T(8,128)(2,1)}, bf16[2048,1024]{1,0:T(8,128)(2,1)}, bf16[2048,1024]{1,0:T(8,128)(2,1)}) custom-call(bf16[2048,2048]{1,0:T(8,128)(2,1)} %copy-done.4, bf16[4,512,2048]{2,1,0:T(8,128)(2,1)} %bitcast.92, bf16[4,512,2048]{2,1,0:T(8,128)(2,1)} %bitcast.93, bf16[2048,32]{1,0:T(8,128)(2,1)} %convolution_convert_fusion.narrow_ref, ...), custom_call_target="tpu_custom_call" | custom-call | flops 1100000000 | bytes 1000000 | tf_op jit(solution)/shard_map/gate_up/pallas_call | solution.py:392
  363.8 162.3 %feed_layer.1 = (bf16[256,2048]{1,0:T(8,128)(2,1)}, f32[256,2048]{1,0:T(8,128)}, bf16[4,256,2048]{2,1,0:T(8,128)(2,1)}, bf16[8,256,32]{2,1,0:T(8,128)(2,1)}, f32...) custom-call(bf16[16,1024]{1,0:T(8,128)(2,1)} %bitcast.135, ...), custom_call_target="tpu_custom_call" | custom-call | flops 186999996416 | bytes 170000000 | tf_op jit(solution)/shard_map/feed_layer/pallas_call | solution.py:1608
  526.1 2.8 convolution_multiply_fusion
  529.0 61.1 %attend_backward.1 = (f32[2,2,256,512]{3,2,1,0:T(8,128)}, f32[2,2,256,512]{3,2,1,0:T(8,128)}, f32[2,2,256,512]{3,2,1,0:T(8,128)}, bf16[1024,16]{1,0:T(8,128)(2,1)}, f32[32,2048]{1,0:T(8,128)}) custom-call(bf16[1024,2048]{1,0:T(8,128)(2,1)} %bitcast.111, bf16[512,2048]{1,0:T(8,128)(2,1)} %bitcast.104, bf16[16,512]{1,0:T(8,128)(2,1)} %bitcast.136, ...), custom_call_target="tpu_custom_call" | custom-call | flops 76999999488 | bytes 70000000 | tf_op jit(solution)/shard_map/attend_backward/pallas_call | solution.py:1088
  590.1 1.2 convolution_multiply_fusion.1
  591.6 1.8 pad_maximum_fusion.2.refs_13_
  593.4 0.7 broadcast_in_dim.82.refs_15_
  594.1 55.7 %finish.1 = (f32[256,2048]{1,0:T(8,128)}, f32[8,6,16,64]{3,2,1,0:T(8,128)}, f32[8,16,256]{2,1,0:T(8,128)}, f32[8,5,16,64]{3,2,1,0:T(8,128)}, f32[8,2,16,256]{3,2,1,0:T(8,128)}) custom-call(f32[1024,512]{1,0:T(8,128)} %bitcast.150, f32[1024,512]{1,0:T(8,128)} %bitcast.151, f32[1024,512]{1,0:T(8,128)} %bitcast.152, ...), custom_call_target="tpu_custom_call" | custom-call | flops 65999998976 | bytes 60000000 | tf_op jit(solution)/shard_map/finish/pallas_call | solution.py:847
  649.8 1.0 copy.78
  650.8 3.8 copy.79
  654.5 0.7 copy.80
  655.3 0.7 copy.81
  656.0 0.7 copy.82
  656.7 0.7 copy.83
  (118 shorter events, 10.1 us)
Async XLA Ops:
  7.2 139.5 %copy-start = (bf16[8,6,16,2048]{3,2,1,0:T(8,128)(2,1)S(1)}, bf16[8,6,16,2048]{3,2,1,0:T(8,128)(2,1)}, u32[]{:S(2)}) copy-start(bf16[8,6,16,2048]{3,2,1,0:T(8,128)(2,1)} %param.34) | copy-start | bytes 9437188
  7.2 329.4 %all-gather.6.cloned.1.call-start = ((), (), s32[]{:S(2)}) async-start(), calls=%async_computation.1 | async-start | bytes 10485760 | tf_op jit(solution)/shard_map/all_gather | solution.py:1736
  7.2 137.1 %copy-start.21 = (s32[4,8]{1,0:T(4,128)S(1)}, s32[4,8]{1,0:T(4,128)}, u32[]{:S(2)}) copy-start(s32[4,8]{1,0:T(4,128)} %param.21) | copy-start | bytes 388
  134.1 229.7 %all-gather.4.cloned.1.call-start = ((), (), s32[]{:S(2)}) async-start(), calls=%async_computation | async-start | bytes 5242880 | tf_op jit(solution)/shard_map/all_gather | solution.py:1803
  134.2 101.7 %collective-permute-start = (bf16[256,2048]{1,0:T(8,128)(2,1)}, bf16[256,2048]{1,0:T(8,128)(2,1)}, u32[]{:S(2)}, u32[]{:S(2)}) collective-permute-start(bf16[256,2048]{1,0:T(8,128)(2,1)} %bitcast.120), channel_id=1, source_target_pairs={{0,2},{3,1},{4,6},{7,5},{8,10},{11,9},{12,14},{15,13},{16,18},{19,... | collective-permute-start | bytes 3145736 | tf_op jit(solution)/shard_map/ppermute | solution.py:1738
  138.5 97.3 %collective-permute-start.1 = (bf16[256,2048]{1,0:T(8,128)(2,1)}, bf16[256,2048]{1,0:T(8,128)(2,1)}, u32[]{:S(2)}, u32[]{:S(2)}) collective-permute-start(bf16[256,2048]{1,0:T(8,128)(2,1)} %bitcast.121), channel_id=1, source_target_pairs={{1,0},{2,3},{5,4},{6,7},{9,8},{10,11},{13,12},{14,15},{17,16},{18,... | collective-permute-start | bytes 3145736 | tf_op jit(solution)/shard_map/ppermute | solution.py:1738
  139.8 96.1 %collective-permute-start.2 = (bf16[256,2048]{1,0:T(8,128)(2,1)}, bf16[256,2048]{1,0:T(8,128)(2,1)}, u32[]{:S(2)}, u32[]{:S(2)}) collective-permute-start(bf16[256,2048]{1,0:T(8,128)(2,1)} %bitcast.122), channel_id=1, source_target_pairs={{1,2},{2,1},{5,6},{6,5},{9,10},{10,9},{13,14},{14,13},{17,18},{18,... | collective-permute-start | bytes 3145736 | tf_op jit(solution)/shard_map/ppermute | solution.py:1738
  207.1 28.8 %copy-start.9 = (bf16[4,64,2048]{2,1,0:T(8,128)(2,1)S(1)}, bf16[4,64,2048]{2,1,0:T(8,128)(2,1)}, u32[]{:S(2)}) copy-start(bf16[4,64,2048]{2,1,0:T(8,128)(2,1)} %get-tuple-element.60) | copy-start | bytes 3145732
  232.1 17.5 %copy-start.10 = (bf16[16,2048]{1,0:T(8,128)(2,1)}, bf16[16,2048]{1,0:T(8,128)(2,1)S(1)}, u32[]{:S(2)}) copy-start(bf16[16,2048]{1,0:T(8,128)(2,1)S(1)} %get-tuple-element.97.refs_3_) | copy-start | bytes 196612
  233.7 15.9 %copy-start.13 = (bf16[1024,16]{0,1:T(8,128)(2,1)}, bf16[1024,16]{0,1:T(8,128)(2,1)S(1)}, u32[]{:S(2)}) copy-start(bf16[1024,16]{0,1:T(8,128)(2,1)S(1)} %convolution_convert_fusion.1) | copy-start | bytes 98308
  237.6 2.0 copy-start.2
  239.6 1.8 copy-start.6
  241.4 3.4 collective-permute-start.3
  242.1 5.2 copy-start.3
  242.2 87.9 %copy-start.17 = (bf16[1,2,16,2048]{3,2,1,0:T(8,128)(2,1)}, bf16[1,2,16,2048]{3,2,1,0:T(8,128)(2,1)S(1)}, u32[]{:S(2)}) copy-start(bf16[1,2,16,2048]{3,2,1,0:T(8,128)(2,1)S(1)} %constant_dynamic-slice_fusion.2) | copy-start | bytes 393220
  246.7 25.5 %collective-permute-start.5 = (bf16[256,2048]{1,0:T(8,128)(2,1)S(1)}, bf16[256,2048]{1,0:T(8,128)(2,1)S(1)}, u32[]{:S(2)}, u32[]{:S(2)}) collective-permute-start(bf16[256,2048]{1,0:T(8,128)(2,1)S(1)} %add_convert_fusion.2), channel_id=1, source_target_pairs={{0,4},{4,0},{1,5},{5,1},{2,6},{6,2},{3,7},{7,3},{8,12},{12,8},{9,1... | collective-permute-start | bytes 3145736 | tf_op jit(solution)/shard_map/ppermute | solution.py:51
  250.4 21.8 %copy-start.7 = (bf16[512,2048]{1,0:T(8,128)(2,1)}, bf16[512,2048]{1,0:T(8,128)(2,1)S(1)}, u32[]{:S(2)}) copy-start(bf16[512,2048]{1,0:T(8,128)(2,1)S(1)} %add_convert_fusion.refs_0_) | copy-start | bytes 6291460
  250.5 2.7 collective-permute-start.4
  253.2 19.0 %copy-start.23 = (bf16[256,2048]{1,0:T(8,128)(2,1)}, bf16[256,2048]{1,0:T(8,128)(2,1)S(1)}, u32[]{:S(2)}) copy-start(bf16[256,2048]{1,0:T(8,128)(2,1)S(1)} %collective-permute-done.4.refs_1_) | copy-start | bytes 3145732
  272.2 1.0 copy-start.22
  278.4 24.9 %collective-permute-start.7 = (bf16[256,2048]{1,0:T(8,128)(2,1)}, bf16[256,2048]{1,0:T(8,128)(2,1)S(1)}, u32[]{:S(2)}, u32[]{:S(2)}) collective-permute-start(bf16[256,2048]{1,0:T(8,128)(2,1)} %get-tuple-element.62), channel_id=1, source_target_pairs={{0,4},{4,0},{1,5},{5,1},{2,6},{6,2},{3,7},{7,3},{8,12},{12,8},{9,1... | collective-permute-start | bytes 3145736 | tf_op jit(solution)/shard_map/ppermute | solution.py:51
  279.5 33.5 %collective-permute-start.9 = (bf16[256,2048]{1,0:T(8,128)(2,1)}, bf16[256,2048]{1,0:T(8,128)(2,1)S(1)}, u32[]{:S(2)}, u32[]{:S(2)}) collective-permute-start(bf16[256,2048]{1,0:T(8,128)(2,1)} %get-tuple-element.62), channel_id=1, source_target_pairs={{0,2},{2,0},{1,3},{3,1},{4,6},{6,4},{5,7},{7,5},{8,10},{10,8},{9,1... | collective-permute-start | bytes 3145736 | tf_op jit(solution)/shard_map/ppermute | solution.py:57
  281.8 33.3 %collective-permute-start.6 = (bf16[256,2048]{1,0:T(8,128)(2,1)}, bf16[256,2048]{1,0:T(8,128)(2,1)}, u32[]{:S(2)}, u32[]{:S(2)}) collective-permute-start(bf16[256,2048]{1,0:T(8,128)(2,1)} %get-tuple-element.62), channel_id=1, source_target_pairs={{0,1},{1,0},{2,3},{3,2},{4,5},{5,4},{6,7},{7,6},{8,9},{9,8},{10,11... | collective-permute-start | bytes 3145736 | tf_op jit(solution)/shard_map/ppermute | solution.py:48
  303.3 24.1 %collective-permute-start.8 = (bf16[256,2048]{1,0:T(8,128)(2,1)S(1)}, bf16[256,2048]{1,0:T(8,128)(2,1)}, u32[]{:S(2)}, u32[]{:S(2)}) collective-permute-start(bf16[256,2048]{1,0:T(8,128)(2,1)S(1)} %collective-permute-done.7), channel_id=1, source_target_pairs={{0,1},{1,0},{2,3},{3,2},{4,5},{5,4},{6,7},{7,6},{8,9},{9,8},{10,11... | collective-permute-start | bytes 3145736 | tf_op jit(solution)/shard_map/ppermute | solution.py:48
  311.5 14.4 %collective-permute-start.11 = (bf16[128,2048]{1,0:T(8,128)(2,1)S(1)}, bf16[128,2048]{1,0:T(8,128)(2,1)S(1)}, u32[]{:S(2)}, u32[]{:S(2)}) collective-permute-start(bf16[128,2048]{1,0:T(8,128)(2,1)S(1)} %slice.79), channel_id=1, source_target_pairs={{0,2},{2,0},{1,3},{3,1},{4,6},{6,4},{5,7},{7,5},{8,10},{10,8},{9,1... | collective-permute-start | bytes 1572872 | tf_op jit(solution)/shard_map/ppermute | solution.py:57
  313.1 14.1 %collective-permute-start.12 = (bf16[128,2048]{1,0:T(8,128)(2,1)S(1)}, bf16[128,2048]{1,0:T(8,128)(2,1)S(1)}, u32[]{:S(2)}, u32[]{:S(2)}) collective-permute-start(bf16[128,2048]{1,0:T(8,128)(2,1)S(1)} %slice.80), channel_id=1, source_target_pairs={{0,4},{4,0},{1,5},{5,1},{2,6},{6,2},{3,7},{7,3},{8,12},{12,8},{9,1... | collective-permute-start | bytes 1572872 | tf_op jit(solution)/shard_map/ppermute | solution.py:51
  315.0 13.8 %collective-permute-start.10 = (bf16[256,2048]{1,0:T(8,128)(2,1)S(1)}, bf16[256,2048]{1,0:T(8,128)(2,1)S(1)}, u32[]{:S(2)}, u32[]{:S(2)}) collective-permute-start(bf16[256,2048]{1,0:T(8,128)(2,1)S(1)} %collective-permute-done.9), channel_id=1, source_target_pairs={{0,1},{1,0},{2,3},{3,2},{4,5},{5,4},{6,7},{7,6},{8,9},{9,8},{10,11... | collective-permute-start | bytes 3145736 | tf_op jit(solution)/shard_map/ppermute | solution.py:48
  327.3 2.7 collective-permute-start.13
  330.1 3.3 copy-start.4
  363.8 162.3 %copy-start.14 = (bf16[1024,16]{0,1:T(8,128)(2,1)S(1)}, bf16[1024,16]{0,1:T(8,128)(2,1)}, u32[]{:S(2)}) copy-start(bf16[1024,16]{0,1:T(8,128)(2,1)} %copy-done.13) | copy-start | bytes 98308
  529.0 61.1 %copy-start.5 = (bf16[2,2,256,512]{3,2,1,0:T(8,128)(2,1)S(1)}, bf16[2,2,256,512]{3,2,1,0:T(8,128)(2,1)}, u32[]{:S(2)}) copy-start(bf16[2,2,256,512]{3,2,1,0:T(8,128)(2,1)} %get-tuple-element.59.refs_15_) | copy-start | bytes 3145732
  529.0 62.5 %copy-start.19 = (f32[4]{0:T(128)S(1)}, f32[4]{0:T(128)}, u32[]{:S(2)}) copy-start(f32[4]{0:T(128)} %compare_convert_fusion.1) | copy-start | bytes 52
  529.0 62.6 %copy-start.16 = (f32[16,2048]{1,0:T(8,128)S(1)}, f32[16,2048]{1,0:T(8,128)}, u32[]{:S(2)}) copy-start(f32[16,2048]{1,0:T(8,128)} %get-tuple-element.82) | copy-start | bytes 393220
  529.0 64.4 %copy-start.20 = (f32[8]{0:T(128)S(1)}, f32[8]{0:T(128)}, u32[]{:S(2)}) copy-start(f32[8]{0:T(128)} %compare_convert_fusion) | copy-start | bytes 100
  594.1 55.7 %copy-start.8 = (bf16[256,2048]{1,0:T(8,128)(2,1)S(1)}, bf16[256,2048]{1,0:T(8,128)(2,1)}, u32[]{:S(2)}) copy-start(bf16[256,2048]{1,0:T(8,128)(2,1)} %get-tuple-element.71) | copy-start | bytes 3145732
  649.7 4.8 copy-start.11
  649.7 5.6 copy-start.18
  649.7 6.2 copy-start.12
  649.8 6.9 %copy-start.15 = (f32[8,2,16,256]{3,2,1,0:T(8,128)S(1)}, f32[8,2,16,256]{3,2,1,0:T(8,128)}, u32[]{:S(2)}) copy-start(f32[8,2,16,256]{3,2,1,0:T(8,128)} %get-tuple-element.135) | copy-start | bytes 786436
  649.8 7.6 %copy-start.1 = (bf16[8,6,16,2048]{3,2,1,0:T(8,128)(2,1)S(1)}, bf16[8,6,16,2048]{3,2,1,0:T(8,128)(2,1)}, u32[]{:S(2)}) copy-start(bf16[8,6,16,2048]{3,2,1,0:T(8,128)(2,1)} %param.34) | copy-start | bytes 9437188
Sparse Core Ops, SparseCore 0:
  134.2 146.8 all-gather.5
  282.7 78.9 all-gather.3
